TPU v7x, 32 devices: a whole 2x2x4 slice. The times are simulated.
32 devices in a mesh: dp: 4 (over y, x), seq: 8 (over z, core).
Axes of the slice: x: 2, y: 2, z: 4, core: 2. Of those that a mesh axis runs over, the one named last changes fastest.
Arguments:
- latents: bfloat16 [4, 1024, 1536], P('dp', 'seq'), may hold values from -6 to 6
- context: bfloat16 [4, 128, 768], P('dp'), may hold values from -6 to 6
- clip_starts: int32 [4, 4], P('dp'), may hold values from 0 to 1023, as said below
- buckets: int32 [4], replicated, may hold values from 0 to 4
- owners: int32 [32], replicated, may hold values from 0 to 31, each once
- cotangent: bfloat16 [4, 1024, 1536], P('dp', 'seq'), may hold values from -6 to 6
- sheet: float32 [1536, 29192], P(('dp', 'seq')), may hold values from -2 to 2, as said below
- first: float32 [1536, 29192], P(('dp', 'seq')), may hold values from -0.00059735496 to 0.00059735496
- second: float32 [1536, 29192], P(('dp', 'seq')), may hold values from 2.2302057e-08 to 8.920823e-08
Outputs:
- output: bfloat16 [4, 1024, 1536], P('dp', 'seq')
- latent_grad: float32 [4, 1024, 1536], P('dp', 'seq')
- grad_norm: float32 [], replicated
- sheet_grad: float32 [1536, 29192], P(('dp', 'seq'))
- gain_grad: float32 [1536, 8], P(('dp', 'seq'))
- first_new: float32 [1536, 29192], P(('dp', 'seq'))
- second_new: float32 [1536, 29192], P(('dp', 'seq'))
- sheet_new: float32 [1536, 29192], P(('dp', 'seq'))
- sheet_copy: bfloat16 [1536, 29192], P(('dp', 'seq'))
Inputs may be any that keep to these rules, and one draw needn't show every extreme that they name: `clip_starts`: in each row the starts rise; the first is 0, the second lies in 1 to 64, the last two lie in the last 64 frames. `sheet`: columns from 29184 on are positive.
All inputs are finite; a program needn't handle non-finite values.
Results may differ from a plain program's by a relative error of at most 0.02.
Values may be sent and summed in bfloat16 or wider, within the bound.
A program may use at most 960 MiB of HBM per device.

v0:
```python
import math

import jax
import jax.numpy as jnp
from jax import lax
from jax.sharding import PartitionSpec as P

D = 1536
FF = 6144
HEAD = 64
CTXW = 768
CTX = 128
NB = 5
STEP = 10
SHEET = 29192


HIGHEST = lax.Precision.HIGHEST
EPS_NORM = 1e-05
EPS_ADAM = 1e-08
MASKED_SCORE = -1e30
BETA_ONE = 0.5
BETA_TWO = 0.5
WEIGHT_DECAY = 0.01


def reorder(values, ordering):
    leading = values.shape[:-1]
    groups = ordering.shape[0]
    blocks = values.reshape(leading + (groups, values.shape[-1] // groups))
    return jnp.take(blocks, ordering, axis=-2).reshape(values.shape)


def norm_parts(values):
    average = jnp.mean(values, axis=-1, keepdims=True)
    centered = values - average
    variance = jnp.mean(centered * centered, axis=-1, keepdims=True)
    inverse_std = lax.rsqrt(variance + EPS_NORM)
    return (centered * inverse_std, inverse_std)


def norm_back(grad_normed, normed, inverse_std):
    return inverse_std * (
        grad_normed
        - jnp.mean(grad_normed, axis=-1, keepdims=True)
        - normed * jnp.mean(grad_normed * normed, axis=-1, keepdims=True)
    )


def softmax_rows(scores):
    row_max = jnp.max(scores, axis=-1, keepdims=True)
    exponent = jnp.exp(scores - row_max)
    return exponent / jnp.sum(exponent, axis=-1, keepdims=True)


def rope_tables(positions, head_dim):
    half_dim = head_dim // 2
    frequency = jnp.exp(-math.log(10000.0) * jnp.arange(half_dim, dtype=jnp.float32) / half_dim)
    angles = positions.astype(jnp.float32)[:, None] * frequency[None, :]
    return (jnp.cos(angles)[:, None, :], jnp.sin(angles)[:, None, :])


def rotate(values, cosine, sine_table):
    half_dim = values.shape[-1] // 2
    first_half = values[..., :half_dim]
    second_half = values[..., half_dim:]
    return jnp.concatenate(
        [
            first_half * cosine - second_half * sine_table,
            second_half * cosine + first_half * sine_table,
        ],
        axis=-1,
    )


def unrotate(grads, cosine, sine_table):
    half_dim = grads.shape[-1] // 2
    first_half = grads[..., :half_dim]
    second_half = grads[..., half_dim:]
    return jnp.concatenate(
        [
            first_half * cosine + second_half * sine_table,
            second_half * cosine - first_half * sine_table,
        ],
        axis=-1,
    )


def segment_ids(starts, positions):
    return jnp.sum((starts[None, :] <= positions[:, None]).astype(jnp.int32), axis=1) - 1


def column_spread(length):
    column = jnp.arange(SHEET, dtype=jnp.int32)
    base_std = D ** (-0.5)
    spread = jnp.full((SHEET,), base_std, jnp.float32)
    spread = jnp.where(
        (column >= 3 * D) & (column < 4 * D), base_std * math.sqrt(length) / 4.0, spread
    )
    spread = jnp.where((column >= 5 * D) & (column < 6 * D), base_std * math.sqrt(CTX), spread)
    spread = jnp.where((column >= 6 * D + 2 * FF) & (column < 6 * D + 3 * FF), FF ** (-0.5), spread)
    spread = jnp.where(
        (column >= 6 * D + 3 * FF) & (column < 6 * D + 3 * FF + 2 * CTXW), CTXW ** (-0.5), spread
    )
    spread = jnp.where(column >= 6 * D + 3 * FF + 2 * CTXW, 0.3, spread)
    return spread


def inner_rows(left, right):
    return lax.dot_general(
        left, right, (((0,), (0,)), ((), ())), preferred_element_type=jnp.float32
    )


def inner_rows_high(left, right):
    return lax.dot_general(
        left, right, (((0,), (0,)), ((), ())), precision=HIGHEST, preferred_element_type=jnp.float32
    )


def per_device(latents, context, clip_starts, buckets, owners, cotangent, sheet, first, second):
    frames = latents.shape[1]
    seq_count = lax.axis_size("seq")
    length = frames * seq_count
    head_count = D // HEAD
    score_scale = HEAD ** (-0.5)
    group_ids = jnp.arange(owners.shape[0], dtype=jnp.int32)
    inverse = jnp.sum(
        jnp.where(owners[None, :] == group_ids[:, None], group_ids[None, :], 0), axis=1
    )
    gathered = lax.all_gather(sheet.astype(jnp.bfloat16), ("dp", "seq"), axis=0, tiled=True)
    tail_col = 6 * D + 3 * FF
    gain_col = tail_col + 2 * CTXW
    gain_rows = reorder(gathered[:, gain_col:].astype(jnp.float32).T, inverse)
    row_index = lax.axis_index("dp")
    bucket_ids = jnp.arange(NB, dtype=jnp.int32)
    bucket_pick = (bucket_ids == buckets[row_index]).astype(jnp.float32)
    counts = jnp.sum((buckets[:, None] == bucket_ids[None, :]).astype(jnp.float32), axis=0)
    row_weight = buckets.shape[0] / (NB * jnp.sum(bucket_pick * counts))
    gain_one = gain_rows[0]
    gain_two = gain_rows[1]
    gain_three = gain_rows[2]
    time_gain = jnp.sum(gain_rows[3:] * bucket_pick[:, None], axis=0)
    tokens = latents[0].astype(jnp.float32)
    positions = lax.axis_index("seq") * frames + jnp.arange(frames, dtype=jnp.int32)
    all_positions = jnp.arange(length, dtype=jnp.int32)
    starts = clip_starts[0]
    same_clip = (
        segment_ids(starts, positions)[:, None] == segment_ids(starts, all_positions)[None, :]
    )[None]
    cosine, sine_table = rope_tables(positions, HEAD)
    normed_one, inverse_one = norm_parts(tokens)
    scaled_one = gain_one * time_gain
    h_one_st = reorder((normed_one * scaled_one).astype(jnp.bfloat16), owners)
    joint_qkv = jnp.dot(h_one_st, gathered[:, : 3 * D], preferred_element_type=jnp.float32)
    queries = rotate(joint_qkv[:, :D].reshape(frames, head_count, HEAD), cosine, sine_table).astype(
        jnp.bfloat16
    )
    key_local = rotate(
        joint_qkv[:, D : 2 * D].reshape(frames, head_count, HEAD), cosine, sine_table
    ).astype(jnp.bfloat16)
    value_local = joint_qkv[:, 2 * D :].reshape(frames, head_count, HEAD).astype(jnp.bfloat16)
    key_all, value_all = (
        lax.all_gather(key_local, "seq", axis=0, tiled=True),
        lax.all_gather(value_local, "seq", axis=0, tiled=True),
    )
    scores = (
        jnp.einsum("qhd,khd->hqk", queries, key_all, preferred_element_type=jnp.float32)
        * score_scale
    )
    attn_probs = softmax_rows(jnp.where(same_clip, scores, MASKED_SCORE))
    probs_low = attn_probs.astype(jnp.bfloat16)
    attn_out = (
        jnp.einsum("hqk,khd->qhd", probs_low, value_all, preferred_element_type=jnp.float32)
        .reshape(frames, D)
        .astype(jnp.bfloat16)
    )
    attn_st = reorder(attn_out, owners)
    x_one = tokens + jnp.dot(
        attn_st, gathered[:, 3 * D : 4 * D], preferred_element_type=jnp.float32
    )
    normed_two, inverse_two = norm_parts(x_one)
    h_two_st = reorder((normed_two * gain_two).astype(jnp.bfloat16), owners)
    cross_q = (
        jnp.dot(h_two_st, gathered[:, 4 * D : 5 * D], preferred_element_type=jnp.float32)
        .astype(jnp.bfloat16)
        .reshape(frames, head_count, HEAD)
    )
    text_tokens = context[0]
    text_kv = jnp.einsum(
        "tc,dec->etd",
        text_tokens,
        gathered[:, tail_col:gain_col].reshape(D, 2, CTXW),
        preferred_element_type=jnp.float32,
    )
    text_kv = reorder(text_kv, inverse).astype(jnp.bfloat16).reshape(2, CTX, head_count, HEAD)
    text_keys = text_kv[0]
    text_values = text_kv[1]
    cross_scores = (
        jnp.einsum("qhd,khd->hqk", cross_q, text_keys, preferred_element_type=jnp.float32)
        * score_scale
    )
    cross_probs = softmax_rows(cross_scores)
    cross_low = cross_probs.astype(jnp.bfloat16)
    cross_out = (
        jnp.einsum("hqk,khd->qhd", cross_low, text_values, preferred_element_type=jnp.float32)
        .reshape(frames, D)
        .astype(jnp.bfloat16)
    )
    cross_st = reorder(cross_out, owners)
    x_two = x_one + jnp.dot(
        cross_st, gathered[:, 5 * D : 6 * D], preferred_element_type=jnp.float32
    )
    normed_three, inverse_three = norm_parts(x_two)
    h_three_st = reorder((normed_three * gain_three).astype(jnp.bfloat16), owners)
    grad_out = cotangent[0].astype(jnp.float32) * row_weight
    grad_ff_st = reorder(grad_out.astype(jnp.bfloat16), owners)
    gate_weight = gathered[:, 6 * D : 6 * D + 2 * FF]
    down_weight = gathered[:, 6 * D + 2 * FF : 6 * D + 3 * FF]
    units = down_weight.shape[1]
    gate_up = jnp.dot(h_three_st, gate_weight, preferred_element_type=jnp.float32)
    gate_pre = gate_up[:, :units]
    up_part = gate_up[:, units:]
    sigmoid_gate = jax.nn.sigmoid(gate_pre)
    silu_gate = gate_pre * sigmoid_gate
    hidden = (silu_gate * up_part).astype(jnp.bfloat16)
    ff_out = reorder(
        jnp.einsum("nf,df->nd", hidden, down_weight, preferred_element_type=jnp.float32), inverse
    )
    result = x_two + ff_out
    grad_hidden = jnp.dot(grad_ff_st, down_weight, preferred_element_type=jnp.float32)
    grad_gate = grad_hidden * up_part * (sigmoid_gate * (1.0 + gate_pre * (1.0 - sigmoid_gate)))
    grad_up = grad_hidden * silu_gate
    grad_gu = jnp.concatenate([grad_gate, grad_up], axis=1).astype(jnp.bfloat16)
    grad_h_three = reorder(
        jnp.einsum("nf,df->nd", grad_gu, gate_weight, preferred_element_type=jnp.float32), inverse
    )
    grad_gain_three = jnp.sum(grad_h_three * normed_three, axis=0)
    grad_x_two = grad_out + norm_back(grad_h_three * gain_three, normed_three, inverse_three)
    grad_cross = grad_x_two.astype(jnp.bfloat16)
    grad_cross_out = (
        reorder(
            jnp.einsum(
                "nd,ed->ne",
                grad_cross,
                gathered[:, 5 * D : 6 * D],
                preferred_element_type=jnp.float32,
            ),
            inverse,
        )
        .astype(jnp.bfloat16)
        .reshape(frames, head_count, HEAD)
    )
    grad_cross_probs = jnp.einsum(
        "qhd,khd->hqk", grad_cross_out, text_values, preferred_element_type=jnp.float32
    )
    grad_cross_scores = (
        cross_probs
        * (grad_cross_probs - jnp.sum(cross_probs * grad_cross_probs, axis=-1, keepdims=True))
    ).astype(jnp.bfloat16)
    grad_cross_q = (
        (
            jnp.einsum(
                "hqk,khd->qhd", grad_cross_scores, text_keys, preferred_element_type=jnp.float32
            )
            * score_scale
        )
        .reshape(frames, D)
        .astype(jnp.bfloat16)
    )
    grad_text_keys = (
        jnp.einsum("hqk,qhd->khd", grad_cross_scores, cross_q, preferred_element_type=jnp.float32)
        * score_scale
    )
    grad_text_values = jnp.einsum(
        "hqk,qhd->khd", cross_low, grad_cross_out, preferred_element_type=jnp.float32
    )
    grad_text = reorder(
        jnp.stack([grad_text_keys.reshape(CTX, D), grad_text_values.reshape(CTX, D)]), owners
    )
    grad_h_two = reorder(
        jnp.einsum(
            "ne,de->nd",
            grad_cross_q,
            gathered[:, 4 * D : 5 * D],
            preferred_element_type=jnp.float32,
        ),
        inverse,
    )
    grad_gain_two = jnp.sum(grad_h_two * normed_two, axis=0)
    grad_x_one = grad_x_two + norm_back(grad_h_two * gain_two, normed_two, inverse_two)
    grad_attn = grad_x_one.astype(jnp.bfloat16)
    grad_attn_out = (
        reorder(
            jnp.einsum(
                "nd,ed->ne",
                grad_attn,
                gathered[:, 3 * D : 4 * D],
                preferred_element_type=jnp.float32,
            ),
            inverse,
        )
        .astype(jnp.bfloat16)
        .reshape(frames, head_count, HEAD)
    )
    key_back, value_back = (key_all, value_all)

    def head_grads(head_items):
        head_probs, head_grad_out, head_values = head_items
        grad_probs = jnp.einsum(
            "qd,kd->qk", head_grad_out, head_values, preferred_element_type=jnp.float32
        )
        return (
            head_probs * (grad_probs - jnp.sum(head_probs * grad_probs, axis=-1, keepdims=True))
        ).astype(jnp.bfloat16)

    grad_scores_low = lax.map(
        head_grads, (attn_probs, jnp.swapaxes(grad_attn_out, 0, 1), jnp.swapaxes(value_back, 0, 1))
    )
    grad_queries = (
        jnp.einsum("hqk,khd->qhd", grad_scores_low, key_back, preferred_element_type=jnp.float32)
        * score_scale
    )
    grad_keys = (
        jnp.einsum("hqk,qhd->khd", grad_scores_low, queries, preferred_element_type=jnp.float32)
        * score_scale
    )
    grad_values = jnp.einsum(
        "hqk,qhd->khd", probs_low, grad_attn_out, preferred_element_type=jnp.float32
    )
    key_sums = lax.psum_scatter(
        jnp.concatenate(
            [
                grad_keys.reshape(frames * lax.axis_size("seq"), D),
                grad_values.reshape(frames * lax.axis_size("seq"), D),
            ],
            axis=1,
        ).astype(jnp.bfloat16),
        "seq",
        scatter_dimension=0,
        tiled=True,
    ).astype(jnp.float32)
    grad_q_raw = unrotate(grad_queries, cosine, sine_table).reshape(frames, D)
    grad_k_raw = unrotate(
        key_sums[:, :D].reshape(frames, head_count, HEAD), cosine, sine_table
    ).reshape(frames, D)
    grad_qkv = jnp.concatenate([grad_q_raw, grad_k_raw, key_sums[:, D:]], axis=1).astype(
        jnp.bfloat16
    )
    grad_h_one = reorder(
        jnp.einsum("ne,de->nd", grad_qkv, gathered[:, : 3 * D], preferred_element_type=jnp.float32),
        inverse,
    )
    grad_gain_one = jnp.sum(grad_h_one * normed_one * time_gain, axis=0)
    grad_time = jnp.sum(grad_h_one * normed_one * gain_one, axis=0)
    latent_grad = grad_x_one + norm_back(grad_h_one * scaled_one, normed_one, inverse_one)
    gain_grads = jnp.concatenate(
        [
            jnp.stack([grad_gain_one, grad_gain_two, grad_gain_three]),
            bucket_pick[:, None] * grad_time[None, :],
        ],
        axis=0,
    )
    gain_grads = reorder(gain_grads, owners).T
    text_float = text_tokens.astype(jnp.float32)
    pieces = [
        inner_rows(h_one_st, grad_qkv),
        inner_rows(attn_st, grad_attn),
        inner_rows(h_two_st, grad_cross_q),
        inner_rows(cross_st, grad_cross),
    ]
    pieces = pieces + [inner_rows(h_three_st, grad_gu), inner_rows(grad_ff_st, hidden)]
    pieces = pieces + [
        inner_rows_high(grad_text[0], text_float),
        inner_rows_high(grad_text[1], text_float),
        gain_grads,
    ]
    other_shard = lax.psum_scatter(
        jnp.concatenate(pieces, axis=1), ("dp", "seq"), scatter_dimension=0, tiled=True
    )
    total_squares = lax.psum(jnp.sum(other_shard * other_shard), ("dp", "seq"))
    grad_norm = jnp.sqrt(total_squares)
    clipped = other_shard / jnp.maximum(grad_norm, 1.0)
    gain_grad = clipped[:, 6 * D + 3 * FF + 2 * CTXW :]
    first_new = BETA_ONE * first + (1.0 - BETA_ONE) * clipped
    second_new = BETA_TWO * second + (1.0 - BETA_TWO) * clipped * clipped
    mean_hat = first_new / (1.0 - BETA_ONE**STEP)
    square_hat = second_new / (1.0 - BETA_TWO**STEP)
    rates = column_spread(length)[None, :]
    sheet_new = sheet - rates * (
        mean_hat / (jnp.sqrt(square_hat) + EPS_ADAM) + WEIGHT_DECAY * sheet
    )
    return (
        result.astype(jnp.bfloat16)[None],
        latent_grad[None],
        grad_norm,
        clipped,
        gain_grad,
        first_new,
        second_new,
        sheet_new,
        sheet_new.astype(jnp.bfloat16),
    )


def solution(mesh):
    in_specs = (
        P("dp", "seq", None),
        P("dp", None, None),
        P("dp", None),
        P(),
        P(),
        P("dp", "seq", None),
        P(("dp", "seq"), None),
        P(("dp", "seq"), None),
        P(("dp", "seq"), None),
    )
    out_specs = (
        P("dp", "seq", None),
        P("dp", "seq", None),
        P(),
        P(("dp", "seq"), None),
        P(("dp", "seq"), None),
        P(("dp", "seq"), None),
        P(("dp", "seq"), None),
        P(("dp", "seq"), None),
        P(("dp", "seq"), None),
    )
    return jax.shard_map(
        per_device, mesh=mesh, in_specs=in_specs, out_specs=out_specs, check_vma=False
    )
```

profile of v0, /device:TPU:0, one launch (start us, length us, event | category | flops | bytes accessed | tf_op | source)
XLA Modules:
  0.0 3527.8 jit_solution(12075099092220191973)
XLA Ops:
  18.3 462.6 %all-gather.4.cloned.1.call-done = bf16[1536,29192]{1,0:T(8,128)(2,1)} async-done(((bf16[48,29192]{1,0:T(8,128)(2,1)}), bf16[1536,29192]{1,0:T(8,128)(2,1)}) %all-gather.4.cloned.1.call-update) | async-done | bytes 89677840 | tf_op jit(solution)/shard_map/all_gather | solution.py:131
  486.8 6.2 fusion.22
  502.4 8.4 fusion.100
  510.8 6.7 copy.211
  523.2 11.0 all-gather.8.cloned.1.call-done
  534.2 11.1 fusion.105
  545.2 10.7 broadcast_divide_fusion
  556.0 17.8 all-gather.6.cloned.1.call-done
  573.8 7.8 fusion.55
  601.0 14.0 fusion.14
  615.1 9.9 multiply_convert_fusion.2
  624.9 17.5 fusion.12
  649.0 10.3 fusion.18
  692.7 79.6 %while.10 = (s32[]{:T(128)}, bf16[24,128,1024]{2,1,0:T(8,128)(2,1)}, f32[24,128,1024]{2,1,0:T(8,128)}, bf16[24,128,64]{1,2,0:T(8,128)(2,1)S(1)}, bf16[24,1024,64]{1,2,0:T(8,128)(2,1)}, /*index=5*/s32[]{:T(128)}) while((s32[]{:T(128)}, bf16[24,128,1024]{2,1,0:T(8,128)(2,1)}, f32[24,128,1024]{2,1,0:T(8,128)}, ...), condition=%wide.region_23.28_spmd, body=%wide.region_21.27_spmd.sunk | while | flops 17432448 | bytes 2509393 | solution.py:317
  785.0 8.7 copy.207
  805.0 56.9 %reduce-scatter.4.cloned.1.call-done = bf16[128,3072]{1,0:T(8,128)(2,1)} async-done(((bf16[1024,3072]{1,0:T(8,128)(2,1)}), bf16[128,3072]{1,0:T(8,128)(2,1)}) %reduce-scatter.4.cloned.1.call-update) | async-done | bytes 786448
  864.0 13.0 convolution_dynamic-update-slice_fusion.2
  877.0 7.1 fusion.20
  887.9 6.2 convolution_dynamic-update-slice_fusion.5
  904.3 29.1 convolution_dynamic-update-slice_fusion
  933.4 16.2 convolution_dynamic-update-slice_fusion.1
  960.3 2491.9 %all-reduce.3.cloned.1.call-done = f32[1536,29192]{1,0:T(8,128)} async-done(((f32[1536,29192]{1,0:T(8,128)}), f32[1536,29192]{1,0:T(8,128)}) %all-reduce.3.cloned.1.call-update) | async-done | bytes 179355664
  3458.0 42.8 %psum.7 = f32[]{:T(128)} all-reduce(f32[]{:T(128)} %multiply_reduce_fusion), channel_id=1, replica_groups=mesh['dp'=4,'seq'=8] {'dp','seq'}, use_global_device_ids=true, to_apply=%region_33.38 | all-reduce | flops 1 | bytes 8 | tf_op jit(solution)/shard_map/psum | solution.py:381
  3501.5 15.3 fusion.98
  (360 shorter events, 228.6 us)
Async XLA Ops:
  7.2 510.3 %copy-start = (bf16[1,128,768]{2,1,0:T(8,128)(2,1)S(1)}, bf16[1,128,768]{2,1,0:T(8,128)(2,1)}, u32[]{:S(2)}) copy-start(bf16[1,128,768]{2,1,0:T(8,128)(2,1)} %param.20) | copy-start | bytes 589828
  7.2 473.7 %all-gather.4.cloned.1.call-start = ((), (), s32[]{:S(2)}) async-start(), calls=%async_computation.1 | async-start | bytes 92860416 | tf_op jit(solution)/shard_map/all_gather | solution.py:131
  11.8 522.3 %all-gather.8.cloned.1.call-start = ((), (), s32[]{:S(2)}) async-start(), calls=%async_computation.3 | async-start | bytes 3538944 | tf_op jit(solution)/shard_map/all_gather | solution.py:164
  15.0 471.0 %copy-start.3 = (f32[1,128,1536]{1,2,0:T(8,128)}, f32[1,128,1536]{1,2,0:T(8,128)S(1)}, u32[]{:S(2)}) copy-start(f32[1,128,1536]{1,2,0:T(8,128)S(1)} %copy.151) | copy-start | bytes 2359300
  15.0 471.0 %copy-start.61 = (s32[1024]{0:T(1024)}, s32[1024]{0:T(1024)S(1)}, u32[]{:S(2)}) copy-start(s32[1024]{0:T(1024)S(1)} %pad_clamp_fusion) | copy-start | bytes 12292
  16.3 468.0 %copy-start.72 = (f32[5]{0:T(128)}, f32[5]{0:T(128)S(1)}, u32[]{:S(2)}) copy-start(f32[5]{0:T(128)S(1)} %compare_convert_fusion) | copy-start | bytes 64
  17.0 467.3 %copy-start.62 = (s32[1024]{0:T(1024)}, s32[1024]{0:T(1024)S(1)}, u32[]{:S(2)}) copy-start(s32[1024]{0:T(1024)S(1)} %pad_clamp_fusion.1) | copy-start | bytes 12292
  17.2 467.2 %copy-start.64 = (f32[128]{0:T(128)}, f32[128]{0:T(128)S(1)}, u32[]{:S(2)}) copy-start(f32[128]{0:T(128)S(1)} %broadcast_multiply_fusion.9) | copy-start | bytes 1540
  17.4 475.5 %copy-start.56 = (pred[32]{0:T(512)(128)(4,1)}, pred[32]{0:T(512)(128)(4,1)S(1)}, u32[]{:S(2)}) copy-start(pred[32]{0:T(512)(128)(4,1)S(1)} %compare_and_fusion) | copy-start | bytes 100
  17.5 466.9 %copy-start.52 = (pred[32]{0:T(512)(128)(4,1)}, pred[32]{0:T(512)(128)(4,1)S(1)}, u32[]{:S(2)}) copy-start(pred[32]{0:T(512)(128)(4,1)S(1)} %compare_and_fusion.1) | copy-start | bytes 100
  17.5 466.9 %copy-start.68 = (f32[128]{0:T(128)}, f32[128]{0:T(128)S(1)}, u32[]{:S(2)}) copy-start(f32[128]{0:T(128)S(1)} %add_rsqrt_fusion.2) | copy-start | bytes 1540
  18.2 476.6 %copy-start.45 = (f32[128,32]{0,1:T(8,128)}, f32[128,32]{0,1:T(8,128)S(1)}, u32[]{:S(2)}) copy-start(f32[128,32]{0,1:T(8,128)S(1)} %get-tuple-element.174) | copy-start | bytes 49156
  486.0 129.0 %copy-start.19 = (bf16[32,128,48]{1,2,0:T(8,128)(2,1)}, bf16[32,128,48]{1,2,0:T(8,128)(2,1)S(1)}, u32[]{:S(2)}) copy-start(bf16[32,128,48]{1,2,0:T(8,128)(2,1)S(1)} %get-tuple-element.176) | copy-start | bytes 1179652
  495.8 38.4 %copy-start.35 = (bf16[128,24,32]{0,2,1:T(8,128)(2,1)}, bf16[128,24,32]{0,2,1:T(8,128)(2,1)S(1)}, u32[]{:S(2)}) copy-start(bf16[128,24,32]{0,2,1:T(8,128)(2,1)S(1)} %get-tuple-element.158) | copy-start | bytes 589828
  496.7 77.1 %all-gather.6.cloned.1.call-start = ((), (), s32[]{:S(2)}) async-start(), calls=%async_computation.2 | async-start | bytes 3538944 | tf_op jit(solution)/shard_map/all_gather | solution.py:165
  498.8 363.1 %reduce-scatter.4.cloned.1.call-start = ((), (), s32[]{:S(2)}) async-start(), calls=%async_computation.4 | async-start | bytes 7077888
  523.2 67.8 %copy-start.30 = (bf16[1,128,32,48]{1,3,0,2:T(8,128)(2,1)}, bf16[1,128,32,48]{1,3,0,2:T(8,128)(2,1)S(1)}, u32[]{:S(2)}) copy-start(bf16[1,128,32,48]{1,3,0,2:T(8,128)(2,1)S(1)} %get-tuple-element.165) | copy-start | bytes 1179652
  692.7 79.6 %copy-start.36 = (bf16[128,24,32]{0,2,1:T(8,128)(2,1)S(1)}, bf16[128,24,32]{0,2,1:T(8,128)(2,1)}, u32[]{:S(2)}) copy-start(bf16[128,24,32]{0,2,1:T(8,128)(2,1)} %copy-done.35) | copy-start | bytes 589828
  793.7 2658.4 %all-reduce.3.cloned.1.call-start = ((), (), s32[]{:S(2)}) async-start(), calls=%async_computation.5 | async-start | bytes 360185856
  799.7 63.9 %copy-start.46 = (f32[128,32]{0,1:T(8,128)S(1)}, f32[128,32]{0,1:T(8,128)}, u32[]{:S(2)}) copy-start(f32[128,32]{0,1:T(8,128)} %copy-done.45) | copy-start | bytes 49156
  799.7 63.9 %copy-start.47 = (f32[128,32]{0,1:T(8,128)S(1)}, f32[128,32]{0,1:T(8,128)}, u32[]{:S(2)}) copy-start(f32[128,32]{0,1:T(8,128)} %get-tuple-element.175) | copy-start | bytes 49156
  805.0 59.0 %copy-start.22 = (bf16[32,128,48]{1,2,0:T(8,128)(2,1)S(1)}, bf16[32,128,48]{1,2,0:T(8,128)(2,1)}, u32[]{:S(2)}) copy-start(bf16[32,128,48]{1,2,0:T(8,128)(2,1)} %copy-done.21) | copy-start | bytes 1179652
  904.3 29.2 copy-start.20
  959.2 2497.6 %copy-start.2 = (bf16[1,128,1536]{2,1,0:T(8,128)(2,1)S(1)}, bf16[1,128,1536]{2,1,0:T(8,128)(2,1)}, u32[]{:S(2)}) copy-start(bf16[1,128,1536]{2,1,0:T(8,128)(2,1)} %param.19) | copy-start | bytes 1179652
  (59 other events, 294.0 us)
Sparse Core Ops, SparseCore 0:
  12.0 468.9 all-gather.3
  496.8 37.3 all-gather.7
  536.3 37.4 all-gather.5
  793.9 68.0 reduce-scatter.3
  959.3 2492.8 all-reduce.2
where the time goes:
time: 3540 us; the launch traced here: 3530 us
  waiting for transfers between devices  3040 us (86%)
  matrix products  248 us (7%)
  other arithmetic  112 us (3%)
  local copies, waits for them, and re-layouts  66.2 us (2%)
  blocking collectives  42.8 us (1%)
    unnamed x7, waiting for transfers between devices  2550 us
    all_gather x1, waiting for transfers between devices, per_device(): lax.all_gather(sheet.astype(jnp.bfloat16), ('dp', 'seq'), axis=0, tiled=T...  463 us
    dot_general x6, matrix products, inner_rows(): lax.dot_general(left, right, (((0,), (0,)), ((), ())), preferred_element_...  74.7 us
  transfers between devices with their start and end apart: 5, of which 5 were waited for; matrix products, arithmetic and copies ran while one was open for 2% of the time, Pallas kernels for 0%

commit v1 on v0

--- a/solution.py
+++ b/solution.py
@@ -3,6 +3,7 @@
 import jax
 import jax.numpy as jnp
 from jax import lax
+from jax.sharding import Mesh
 from jax.sharding import PartitionSpec as P
 
 D = 1536
@@ -118,7 +119,7 @@
     )
 
 
-def per_device(latents, context, clip_starts, buckets, owners, cotangent, sheet, first, second):
+def gather_plan(latents, context, clip_starts, buckets, owners, cotangent, sheet, first, second):
     frames = latents.shape[1]
     seq_count = lax.axis_size("seq")
     length = frames * seq_count
@@ -403,29 +404,448 @@
     )
 
 
+PLANE = ("dp", "core")
+
+
+def norm_columns(values):
+    average = jnp.mean(values, axis=0, keepdims=True)
+    centered = values - average
+    variance = jnp.mean(centered * centered, axis=0, keepdims=True)
+    inverse_std = lax.rsqrt(variance + EPS_NORM)
+    return (centered * inverse_std, inverse_std)
+
+
+def norm_columns_back(grad_normed, normed, inverse_std):
+    return inverse_std * (
+        grad_normed
+        - jnp.mean(grad_normed, axis=0, keepdims=True)
+        - normed * jnp.mean(grad_normed * normed, axis=0, keepdims=True)
+    )
+
+
+def rotate_columns(values, cosine, sine_table):
+    half_dim = HEAD // 2
+    first_half = values[:, :half_dim]
+    second_half = values[:, half_dim:]
+    return jnp.concatenate(
+        [
+            first_half * cosine - second_half * sine_table,
+            second_half * cosine + first_half * sine_table,
+        ],
+        axis=1,
+    )
+
+
+def contract_rows(left, right):
+    return lax.dot_general(
+        left, right, (((0,), (0,)), ((), ())), preferred_element_type=jnp.float32
+    )
+
+
+def contract_last(left, right):
+    return lax.dot_general(
+        left, right, (((1,), (1,)), ((), ())), preferred_element_type=jnp.float32
+    )
+
+
+def matmul(left, right):
+    return jnp.dot(left, right, preferred_element_type=jnp.float32)
+
+
+def plane_gather(shard):
+    return lax.all_gather(shard, PLANE, axis=1, tiled=True)
+
+
+def plane_gather_rows(shard):
+    return lax.all_gather(shard, PLANE, axis=0, tiled=True)
+
+
+def plane_scatter_frames(partial):
+    return lax.psum_scatter(partial, PLANE, scatter_dimension=1, tiled=True)
+
+
+def plane_scatter_rows(partial):
+    return lax.psum_scatter(partial, PLANE, scatter_dimension=0, tiled=True)
+
+
+def to_frames(rows):
+    return lax.all_to_all(rows, PLANE, split_axis=1, concat_axis=0, tiled=True)
+
+
+def to_rows(frames):
+    return lax.all_to_all(frames, PLANE, split_axis=0, concat_axis=1, tiled=True)
+
+
+def row_to_plane(local):
+    groups = lax.axis_size("dp")
+    frames, width = local.shape
+    pieces = lax.all_to_all(local, "dp", split_axis=0, concat_axis=0, tiled=True)
+    return lax.all_to_all(pieces, "z", split_axis=0, concat_axis=0, tiled=True)
+
+
+def plane_to_row(local):
+    pieces = lax.all_to_all(local, "z", split_axis=0, concat_axis=0, tiled=True)
+    return lax.all_to_all(pieces, "dp", split_axis=0, concat_axis=0, tiled=True)
+
+
+def split_columns(block, members):
+    rows, columns = block.shape
+    return block.reshape(rows, members, columns // members)
+
+
+def gather_columns(block, order):
+    rows, members, width = block.shape
+    mine = lax.all_to_all(jnp.swapaxes(block, 0, 1), PLANE, split_axis=0, concat_axis=0, tiled=True)
+    blocks = lax.all_gather(mine, "z", axis=0, tiled=True)
+    return jnp.take(blocks, order, axis=0).reshape(-1, width)
+
+
+def scatter_columns(grad, order, planes):
+    blocks = grad.astype(jnp.bfloat16).reshape(order.shape[0], -1, grad.shape[-1])
+    blocks = jnp.take(blocks, order, axis=0)
+    mine = lax.psum_scatter(blocks, "z", scatter_dimension=0, tiled=True)
+    return jnp.swapaxes(lax.all_to_all(mine, PLANE, split_axis=0, concat_axis=0, tiled=True), 0, 1)
+
+
+def plane_plan(latents, context, clip_starts, buckets, owners, cotangent, sheet, first, second):
+    groups = lax.axis_size("dp")
+    planes = lax.axis_size("z")
+    cores = lax.axis_size("core")
+    members = groups * cores
+    frames = latents.shape[1]
+    length = frames * members
+    rows = sheet.shape[0]
+    blocks = owners.shape[0]
+    head_count = D // HEAD // members
+    span = D // members
+    units = FF // members
+    score_scale = HEAD ** (-0.5)
+    tail_col = 6 * D + 3 * FF
+    gain_col = tail_col + 2 * CTXW
+    plane = lax.axis_index("z")
+
+    group_ids = jnp.arange(blocks, dtype=jnp.int32)
+    inverse = jnp.sum(
+        jnp.where(owners[None, :] == group_ids[:, None], group_ids[None, :], 0), axis=1
+    )
+    slot = group_ids.reshape(groups, planes, cores).swapaxes(0, 1).reshape(-1)
+    slot_of = jnp.sum(
+        jnp.where(slot[None, :] == group_ids[:, None], group_ids[None, :], 0), axis=1
+    )
+    to_logical = jnp.take(slot_of, inverse)
+    to_slots = jnp.take(owners, slot)
+
+    low_sheet = sheet.astype(jnp.bfloat16)
+
+    def columns_of(start, width):
+        return split_columns(low_sheet[:, start : start + width], members)
+
+    gains = lax.all_gather(low_sheet[:, gain_col:], ("z", "dp", "core"), axis=0, tiled=True)
+    gains = jnp.take(gains.reshape(blocks, rows, 8), to_logical, axis=0).reshape(D, 8)
+    gains = gains.astype(jnp.float32)
+    weight_one = gather_columns(
+        jnp.concatenate([columns_of(k * D, D) for k in range(4)], axis=2), to_logical
+    )
+    weight_two = gather_columns(
+        jnp.concatenate(
+            [
+                columns_of(4 * D, D),
+                columns_of(5 * D, D),
+                columns_of(tail_col, CTXW),
+                columns_of(tail_col + CTXW, CTXW),
+            ],
+            axis=2,
+        ),
+        to_logical,
+    )
+    weight_gu = gather_columns(
+        jnp.concatenate([columns_of(6 * D, FF), columns_of(6 * D + FF, FF)], axis=2), to_logical
+    )
+    weight_down = gather_columns(columns_of(6 * D + 2 * FF, FF), to_logical)
+    weight_qkv = weight_one[:, : 3 * span]
+    weight_ao = weight_one[:, 3 * span :]
+    weight_cq = weight_two[:, :span]
+    weight_co = weight_two[:, span : 2 * span]
+    weight_text = weight_two[:, 2 * span :]
+
+    bucket_ids = jnp.arange(NB, dtype=jnp.int32)
+    bucket_pick = (bucket_ids == buckets[plane]).astype(jnp.float32)
+    counts = jnp.sum((buckets[:, None] == bucket_ids[None, :]).astype(jnp.float32), axis=0)
+    row_weight = buckets.shape[0] / (NB * jnp.sum(bucket_pick * counts))
+    gain_one = gains[:, 0:1]
+    gain_two = gains[:, 1:2]
+    gain_three = gains[:, 2:3]
+    time_gain = jnp.sum(gains[:, 3:] * bucket_pick[None, :], axis=1, keepdims=True)
+
+    both = row_to_plane(jnp.concatenate([latents[0], cotangent[0]], axis=1))
+    tokens = both[:, :D].astype(jnp.float32).T
+    grad_out = both[:, D:].astype(jnp.float32).T * row_weight
+
+    rest = frames // planes
+    place = jnp.arange(length, dtype=jnp.int32).reshape(planes, cores, groups, rest)
+    positions = place.transpose(2, 1, 0, 3).reshape(-1)
+    starts = lax.all_gather(clip_starts, "dp", axis=0, tiled=True)[plane]
+    segments = segment_ids(starts, positions)
+    same_clip = segments[:, None] == segments[None, :]
+    frequency = jnp.exp(
+        -math.log(10000.0) * jnp.arange(HEAD // 2, dtype=jnp.float32) / (HEAD // 2)
+    )
+    angles = frequency[:, None] * positions.astype(jnp.float32)[None, :]
+    cosine = jnp.cos(angles)[None]
+    sine_table = jnp.sin(angles)[None]
+
+    grad_ff = plane_gather(grad_out.astype(jnp.bfloat16))
+    normed_one, inverse_one = norm_columns(tokens)
+    scaled_one = gain_one * time_gain
+    h_one = plane_gather((normed_one * scaled_one).astype(jnp.bfloat16))
+
+    joint = contract_rows(weight_qkv, h_one).reshape(3, head_count, HEAD, length)
+    queries = rotate_columns(joint[0], cosine, sine_table).astype(jnp.bfloat16)
+    keys = rotate_columns(joint[1], cosine, sine_table).astype(jnp.bfloat16)
+    values = joint[2].astype(jnp.bfloat16)
+    scores = (
+        jnp.einsum("hdq,hdk->hqk", queries, keys, preferred_element_type=jnp.float32) * score_scale
+    )
+    attn_probs = softmax_rows(jnp.where(same_clip[None], scores, MASKED_SCORE))
+    probs_low = attn_probs.astype(jnp.bfloat16)
+    attn_out = jnp.einsum("hqk,hdk->hdq", probs_low, values, preferred_element_type=jnp.float32)
+    attn_out = plane_gather_rows(attn_out.reshape(span, length).astype(jnp.bfloat16))
+    x_one = tokens + to_frames(contract_rows(weight_ao, attn_out).astype(jnp.bfloat16)).astype(
+        jnp.float32
+    )
+
+    text_part = lax.dynamic_index_in_dim(
+        lax.all_gather(context, "dp", axis=0, tiled=True), plane, 0, keepdims=False
+    )
+    member = lax.axis_index("dp") * cores + lax.axis_index("core")
+    text_width = CTXW // members
+    text_mine = lax.dynamic_slice_in_dim(text_part, member * text_width, text_width, axis=1)
+    text_kv = jnp.stack(
+        [
+            contract_last(weight_text[:, :text_width], text_mine),
+            contract_last(weight_text[:, text_width:], text_mine),
+        ],
+        axis=1,
+    ).reshape(D, 2 * CTX)
+    text_kv = plane_scatter_rows(text_kv.astype(jnp.bfloat16)).reshape(head_count, HEAD, 2, CTX)
+    text_keys = text_kv[:, :, 0]
+    text_values = text_kv[:, :, 1]
+    normed_two, inverse_two = norm_columns(x_one)
+    h_two = plane_gather((normed_two * gain_two).astype(jnp.bfloat16))
+    cross_q = contract_rows(weight_cq, h_two).astype(jnp.bfloat16).reshape(head_count, HEAD, length)
+    cross_scores = (
+        jnp.einsum("hdq,hdk->hqk", cross_q, text_keys, preferred_element_type=jnp.float32)
+        * score_scale
+    )
+    cross_probs = softmax_rows(cross_scores)
+    cross_low = cross_probs.astype(jnp.bfloat16)
+    cross_out = jnp.einsum(
+        "hqk,hdk->hdq", cross_low, text_values, preferred_element_type=jnp.float32
+    )
+    cross_out = plane_gather_rows(cross_out.reshape(span, length).astype(jnp.bfloat16))
+    x_two = x_one + to_frames(contract_rows(weight_co, cross_out).astype(jnp.bfloat16)).astype(
+        jnp.float32
+    )
+
+    normed_three, inverse_three = norm_columns(x_two)
+    h_three = plane_gather((normed_three * gain_three).astype(jnp.bfloat16))
+    gate_up = contract_rows(weight_gu, h_three)
+    gate_pre = gate_up[:units]
+    up_part = gate_up[units:]
+    sigmoid_gate = jax.nn.sigmoid(gate_pre)
+    silu_gate = gate_pre * sigmoid_gate
+    hidden = (silu_gate * up_part).astype(jnp.bfloat16)
+    ff_out = plane_scatter_frames(matmul(weight_down, hidden).astype(jnp.bfloat16))
+    result = x_two + ff_out.astype(jnp.float32)
+    output = plane_to_row(result.astype(jnp.bfloat16).T)
+
+    grad_hidden = contract_rows(weight_down, grad_ff)
+    grad_gate = grad_hidden * up_part * (sigmoid_gate * (1.0 + gate_pre * (1.0 - sigmoid_gate)))
+    grad_up = grad_hidden * silu_gate
+    grad_gu = jnp.concatenate([grad_gate, grad_up], axis=0).astype(jnp.bfloat16)
+    grad_weight_gu = contract_last(h_three, grad_gu)
+    grad_weight_down = contract_last(grad_ff, hidden)
+    sums_gu = scatter_columns(grad_weight_gu, to_slots, planes)
+    sums_down = scatter_columns(grad_weight_down, to_slots, planes)
+    grad_h_three = plane_scatter_frames(matmul(weight_gu, grad_gu).astype(jnp.bfloat16)).astype(
+        jnp.float32
+    )
+    grad_gain_three = jnp.sum(grad_h_three * normed_three, axis=1)
+    grad_x_two = grad_out + norm_columns_back(
+        grad_h_three * gain_three, normed_three, inverse_three
+    )
+    grad_cross = to_rows(grad_x_two.astype(jnp.bfloat16))
+    grad_weight_co = contract_last(cross_out, grad_cross)
+    grad_cross_out = plane_scatter_rows(
+        matmul(weight_co, grad_cross).astype(jnp.bfloat16)
+    ).reshape(head_count, HEAD, length)
+    grad_cross_probs = jnp.einsum(
+        "hdq,hdk->hqk", grad_cross_out, text_values, preferred_element_type=jnp.float32
+    )
+    grad_cross_scores = (
+        cross_probs
+        * (grad_cross_probs - jnp.sum(cross_probs * grad_cross_probs, axis=-1, keepdims=True))
+    ).astype(jnp.bfloat16)
+    grad_cross_q = (
+        jnp.einsum("hqk,hdk->hdq", grad_cross_scores, text_keys, preferred_element_type=jnp.float32)
+        * score_scale
+    )
+    grad_cross_q = grad_cross_q.reshape(span, length).astype(jnp.bfloat16)
+    grad_text_keys = (
+        jnp.einsum("hqk,hdq->hdk", grad_cross_scores, cross_q, preferred_element_type=jnp.float32)
+        * score_scale
+    )
+    grad_text_values = jnp.einsum(
+        "hqk,hdq->hdk", cross_low, grad_cross_out, preferred_element_type=jnp.float32
+    )
+    grad_text = jnp.concatenate(
+        [grad_text_keys.reshape(span, CTX), grad_text_values.reshape(span, CTX)], axis=1
+    )
+    grad_text = plane_gather_rows(grad_text.astype(jnp.bfloat16))
+    grad_weight_cq = contract_last(h_two, grad_cross_q)
+    grad_weight_text = [
+        matmul(grad_text[:, :CTX], text_mine),
+        matmul(grad_text[:, CTX:], text_mine),
+    ]
+    sums_two = scatter_columns(
+        jnp.concatenate([grad_weight_cq, grad_weight_co] + grad_weight_text, axis=1),
+        to_slots,
+        planes,
+    )
+    grad_h_two = plane_scatter_frames(
+        matmul(weight_cq, grad_cross_q).astype(jnp.bfloat16)
+    ).astype(jnp.float32)
+    grad_gain_two = jnp.sum(grad_h_two * normed_two, axis=1)
+    grad_x_one = grad_x_two + norm_columns_back(grad_h_two * gain_two, normed_two, inverse_two)
+    grad_attn = to_rows(grad_x_one.astype(jnp.bfloat16))
+    grad_weight_ao = contract_last(attn_out, grad_attn)
+    grad_attn_out = plane_scatter_rows(matmul(weight_ao, grad_attn).astype(jnp.bfloat16)).reshape(
+        head_count, HEAD, length
+    )
+    grad_probs = jnp.einsum(
+        "hdq,hdk->hqk", grad_attn_out, values, preferred_element_type=jnp.float32
+    )
+    grad_scores = (
+        attn_probs * (grad_probs - jnp.sum(attn_probs * grad_probs, axis=-1, keepdims=True))
+    ).astype(jnp.bfloat16)
+    grad_queries = (
+        jnp.einsum("hqk,hdk->hdq", grad_scores, keys, preferred_element_type=jnp.float32)
+        * score_scale
+    )
+    grad_keys = (
+        jnp.einsum("hqk,hdq->hdk", grad_scores, queries, preferred_element_type=jnp.float32)
+        * score_scale
+    )
+    grad_values = jnp.einsum(
+        "hqk,hdq->hdk", probs_low, grad_attn_out, preferred_element_type=jnp.float32
+    )
+    grad_qkv = jnp.stack(
+        [
+            rotate_columns(grad_queries, cosine, -sine_table),
+            rotate_columns(grad_keys, cosine, -sine_table),
+            grad_values,
+        ]
+    )
+    grad_qkv = grad_qkv.reshape(3 * span, length).astype(jnp.bfloat16)
+    grad_weight_qkv = contract_last(h_one, grad_qkv)
+    sums_one = scatter_columns(
+        jnp.concatenate([grad_weight_qkv, grad_weight_ao], axis=1), to_slots, planes
+    )
+    grad_h_one = plane_scatter_frames(matmul(weight_qkv, grad_qkv).astype(jnp.bfloat16)).astype(
+        jnp.float32
+    )
+    grad_gain_one = jnp.sum(grad_h_one * normed_one * time_gain, axis=1)
+    grad_time = jnp.sum(grad_h_one * normed_one * gain_one, axis=1)
+    latent_grad = grad_x_one + norm_columns_back(grad_h_one * scaled_one, normed_one, inverse_one)
+    latent_grad = plane_to_row(latent_grad.astype(jnp.bfloat16).T).astype(jnp.float32)
+    gain_grads = jnp.concatenate(
+        [
+            jnp.stack([grad_gain_one, grad_gain_two, grad_gain_three], axis=1),
+            grad_time[:, None] * bucket_pick[None, :],
+        ],
+        axis=1,
+    )
+    gain_grads = jnp.take(gain_grads.reshape(blocks, rows, 8), to_slots, axis=0)
+    gain_sums = lax.psum_scatter(
+        gain_grads.reshape(D, 8), ("z", "dp", "core"), scatter_dimension=0, tiled=True
+    )
+
+    def joined(part):
+        return part.reshape(rows, -1)
+
+    grad_sheet = jnp.concatenate(
+        [joined(sums_one[:, :, k * span : (k + 1) * span]) for k in range(4)]
+        + [joined(sums_two[:, :, :span]), joined(sums_two[:, :, span : 2 * span])]
+        + [joined(sums_gu[:, :, :units]), joined(sums_gu[:, :, units:]), joined(sums_down)]
+        + [
+            joined(sums_two[:, :, 2 * span : 2 * span + text_width]),
+            joined(sums_two[:, :, 2 * span + text_width :]),
+        ],
+        axis=1,
+    ).astype(jnp.float32)
+    grad_sheet = jnp.concatenate([grad_sheet, gain_sums], axis=1)
+    total_squares = lax.psum(jnp.sum(grad_sheet * grad_sheet), ("dp", "z", "core"))
+    return (output[None], latent_grad[None]) + update(
+        grad_sheet, total_squares, sheet, first, second, length
+    )
+
+
+def update(grad_sheet, total_squares, sheet, first, second, length):
+    grad_norm = jnp.sqrt(total_squares)
+    clipped = grad_sheet / jnp.maximum(grad_norm, 1.0)
+    gain_grad = clipped[:, 6 * D + 3 * FF + 2 * CTXW :]
+    first_new = BETA_ONE * first + (1.0 - BETA_ONE) * clipped
+    second_new = BETA_TWO * second + (1.0 - BETA_TWO) * clipped * clipped
+    mean_hat = first_new / (1.0 - BETA_ONE**STEP)
+    square_hat = second_new / (1.0 - BETA_TWO**STEP)
+    rates = column_spread(length)[None, :]
+    sheet_new = sheet - rates * (
+        mean_hat / (jnp.sqrt(square_hat) + EPS_ADAM) + WEIGHT_DECAY * sheet
+    )
+    return (
+        grad_norm,
+        clipped,
+        gain_grad,
+        first_new,
+        second_new,
+        sheet_new,
+        sheet_new.astype(jnp.bfloat16),
+    )
+
+
 def solution(mesh):
+    groups, seq_count = mesh.shape["dp"], mesh.shape["seq"]
+    by_plane = seq_count == 2 * groups and (D // HEAD) % seq_count == 0
+    if by_plane:
+        mesh = Mesh(mesh.devices.reshape(groups, seq_count // 2, 2), ("dp", "z", "core"))
+    seq = ("z", "core") if by_plane else "seq"
+    both = ("dp", "z", "core") if by_plane else ("dp", "seq")
     in_specs = (
-        P("dp", "seq", None),
+        P("dp", seq, None),
         P("dp", None, None),
         P("dp", None),
         P(),
         P(),
-        P("dp", "seq", None),
-        P(("dp", "seq"), None),
-        P(("dp", "seq"), None),
-        P(("dp", "seq"), None),
+        P("dp", seq, None),
+        P(both, None),
+        P(both, None),
+        P(both, None),
     )
     out_specs = (
-        P("dp", "seq", None),
-        P("dp", "seq", None),
+        P("dp", seq, None),
+        P("dp", seq, None),
         P(),
-        P(("dp", "seq"), None),
-        P(("dp", "seq"), None),
-        P(("dp", "seq"), None),
-        P(("dp", "seq"), None),
-        P(("dp", "seq"), None),
-        P(("dp", "seq"), None),
+        P(both, None),
+        P(both, None),
+        P(both, None),
+        P(both, None),
+        P(both, None),
+        P(both, None),
     )
     return jax.shard_map(
-        per_device, mesh=mesh, in_specs=in_specs, out_specs=out_specs, check_vma=False
-    )
+        plane_plan if by_plane else gather_plan,
+        mesh=mesh,
+        in_specs=in_specs,
+        out_specs=out_specs,
+        check_vma=False,
+    )

time: 3540 us -> 1330 us (0.38)
  waiting for transfers between devices: 3040 us -> 696 us
  blocking collectives: 42.8 us -> 219 us
  matrix products: 248 us -> 131 us
  local copies, waits for them, and re-layouts: 66.2 us -> 123 us
  starting transfers between devices: 0.71 us -> 49.3 us
    unnamed x7 -> x26, waiting for transfers between devices: 2550 us -> 166 us
    all_gather x3 -> x10, waiting for transfers between devices: 491 us -> 215 us  [the longest x4 91.9 us: plane_gather(): return lax.all_gather(shard, PLANE, axis=1, tiled=True)]
    reduce_scatter x0 -> x8, waiting for transfers between devices: none -> 247 us  [the longest x4 108 us: scatter_columns(): mine = lax.psum_scatter(blocks, 'z', scatter_dimension=0, tiled=True)]
    dot_general x54 -> x32, matrix products: 234 us -> 120 us  [the longest x6 34.1 us: contract_rows(): lax.dot_general(left, right, (((0,), (0,)), ((), ())), preferred_element_...]
    all_to_all x0 -> x6, blocking collectives: none -> 89.9 us  [the longest x2 37 us: gather_columns(): lax.all_to_all(jnp.swapaxes(block, 0, 1), PLANE, split_axis=0, concat_axi...]
    all_gather x0 -> x4, blocking collectives: none -> 88.6 us  [the longest x1 55 us: plane_plan(): lax.all_gather(low_sheet[:, gain_col:], ('z', 'dp', 'core'), axis=0, tile...]
    all_to_all x0 -> x12, waiting for transfers between devices: none -> 67.9 us  [the longest x3 25.1 us: scatter_columns(): lax.all_to_all(mine, PLANE, split_axis=0, concat_axis=0, tiled=True)]
    all_to_all x0 -> x12, starting transfers between devices: none -> 47 us  [the longest x3 10.9 us: scatter_columns(): lax.all_to_all(mine, PLANE, split_axis=0, concat_axis=0, tiled=True)]
  transfers between devices with their start and end apart: 5 -> 34, of which waited for: 5 -> 27; matrix products, arithmetic and copies ran while one was open for 2% -> 19% of each run, Pallas kernels for 0% -> 0%
where the time goes in v1:
time: 1330 us
  waiting for transfers between devices  696 us (52%)
  blocking collectives  219 us (16%)
  matrix products  131 us (10%)
  local copies, waits for them, and re-layouts  123 us (9%)
  other arithmetic  89.8 us (7%)
  starting transfers between devices  49.3 us (4%)
  between operations  18.9 us (1%)
    unnamed x26, waiting for transfers between devices  166 us
    reduce_scatter x4, waiting for transfers between devices, scatter_columns(): mine = lax.psum_scatter(blocks, 'z', scatter_dimension=0, tiled=True)  108 us
    all_gather x4, waiting for transfers between devices, plane_gather(): return lax.all_gather(shard, PLANE, axis=1, tiled=True)  91.9 us
    all_gather x4, waiting for transfers between devices, gather_columns(): blocks = lax.all_gather(mine, 'z', axis=0, tiled=True)  87 us
    reduce_scatter x3, waiting for transfers between devices, plane_scatter_rows(): return lax.psum_scatter(partial, PLANE, scatter_dimension=0, tiled=True)  72.2 us
    reduce_scatter x1, waiting for transfers between devices, plane_plan(): lax.psum_scatter(gain_grads.reshape(D, 8), ('z', 'dp', 'core'), scatter_d...  67.1 us
    all_gather x1, blocking collectives, plane_plan(): lax.all_gather(low_sheet[:, gain_col:], ('z', 'dp', 'core'), axis=0, tile...  55 us
    unnamed x174, local copies, waits for them, and re-layouts  49.5 us
  transfers between devices with their start and end apart: 34, of which 27 were waited for; matrix products, arithmetic and copies ran while one was open for 19% of the time, Pallas kernels for 0%

profile of v1, /device:TPU:0, one launch (start us, length us, event | category | flops | bytes accessed | tf_op | source)
XLA Modules:
  0.0 1325.7 jit_solution(7354228151506770985)
XLA Ops:
  19.2 15.5 %all_to_all.149 = bf16[8,48,768]{2,1,0:T(8,128)(2,1)} all-to-all(bf16[8,48,768]{2,1,0:T(8,128)(2,1)S(1)} %copy.303), channel_id=1, replica_groups=mesh['dp'=4,'z'=4,'core'=2] {'dp','core'}, dimensions={0} | all-to-all | bytes 1179648 | tf_op jit(solution)/shard_map/all_to_all | solution.py:498
  73.8 55.0 %all-gather = bf16[32,48,8]{1,2,0:T(8,128)(2,1)S(1)} all-gather(bf16[1,48,8]{1,2,0:T(8,128)(2,1)S(1)} %slice_bitcast_fusion.2), channel_id=1, replica_groups=mesh['dp'=4,'z'=4,'core'=2] {'z','dp','core'}, dimensions={0}, use_global_device_ids=true | all-gather | bytes 25344 | tf_op jit(solution)/shard_map/all_gather | solution.py:543
  168.6 13.1 all-gather.15.cloned.1.call-done
  234.1 26.1 %all-gather.17.cloned.1.call-done = bf16[1536,1024]{1,0:T(8,128)(2,1)} async-done(((bf16[192,1024]{1,0:T(8,128)(2,1)}), bf16[1536,1024]{1,0:T(8,128)(2,1)}) %all-gather.17.cloned.1.call-update) | async-done | bytes 3145744 | tf_op jit(solution)/shard_map/all_gather | solution.py:460
  282.0 26.8 %reduce-scatter.23.cloned.1.call-done = bf16[192,256]{1,0:T(8,128)(2,1)} async-done(((bf16[1536,256]{1,0:T(8,128)(2,1)}), bf16[192,256]{1,0:T(8,128)(2,1)}) %reduce-scatter.23.cloned.1.call-update) | async-done | bytes 98320 | tf_op jit(solution)/shard_map/reduce_scatter | solution.py:468
  312.2 31.4 %all-gather.21.cloned.1.call-done = bf16[1536,1024]{0,1:T(8,128)(2,1)} async-done(((bf16[1536,128]{0,1:T(8,128)(2,1)}), bf16[1536,1024]{0,1:T(8,128)(2,1)}) %all-gather.21.cloned.1.call-update) | async-done | bytes 3145744 | tf_op jit(solution)/shard_map/all_gather | solution.py:456
  360.1 21.5 %all_to_all.150 = bf16[8,48,1536]{2,1,0:T(8,128)(2,1)} all-to-all(bf16[8,48,1536]{2,1,0:T(8,128)(2,1)S(1)} %copy.324), channel_id=1, replica_groups=mesh['dp'=4,'z'=4,'core'=2] {'dp','core'}, dimensions={0} | all-to-all | bytes 2359296 | tf_op jit(solution)/shard_map/all_to_all | solution.py:498
  407.4 74.5 %all-gather.27.cloned.1.call-done = bf16[32,48,1536]{2,1,0:T(8,128)(2,1)} async-done(((bf16[8,48,1536]{2,1,0:T(8,128)(2,1)}), bf16[32,48,1536]{2,1,0:T(8,128)(2,1)}) %all-gather.27.cloned.1.call-update) | async-done | bytes 4718608 | tf_op jit(solution)/shard_map/all_gather | solution.py:499
  492.5 22.5 %all-gather.29.cloned.1.call-done = bf16[1536,1024]{0,1:T(8,128)(2,1)} async-done(((bf16[1536,128]{0,1:T(8,128)(2,1)}), bf16[1536,1024]{0,1:T(8,128)(2,1)}) %all-gather.29.cloned.1.call-update) | async-done | bytes 3145744 | tf_op jit(solution)/shard_map/all_gather | solution.py:456
  524.9 25.0 %all-gather.31.cloned.1.call-done = bf16[1536,1024]{0,1:T(8,128)(2,1)} async-done(((bf16[1536,128]{0,1:T(8,128)(2,1)}), bf16[1536,1024]{0,1:T(8,128)(2,1)}) %all-gather.31.cloned.1.call-update) | async-done | bytes 3145744 | tf_op jit(solution)/shard_map/all_gather | solution.py:456
  583.8 34.7 %reduce-scatter.39.cloned.1.call-done = bf16[128,1536]{1,0:T(8,128)(2,1)} async-done(((bf16[1024,1536]{1,0:T(8,128)(2,1)}), bf16[128,1536]{1,0:T(8,128)(2,1)}) %reduce-scatter.39.cloned.1.call-update) | async-done | bytes 393232
  621.0 48.1 %reduce-scatter.37.cloned.1.call-done = bf16[128,1536]{1,0:T(8,128)(2,1)} async-done(((bf16[1024,1536]{1,0:T(8,128)(2,1)}), bf16[128,1536]{1,0:T(8,128)(2,1)}) %reduce-scatter.37.cloned.1.call-update) | async-done | bytes 393232
  686.6 45.4 %reduce-scatter.25.cloned.1.call-done = bf16[192,1024]{1,0:T(8,128)(2,1)} async-done(((bf16[1536,1024]{1,0:T(8,128)(2,1)}), bf16[192,1024]{1,0:T(8,128)(2,1)}) %reduce-scatter.25.cloned.1.call-update) | async-done | bytes 393232 | tf_op jit(solution)/shard_map/reduce_scatter | solution.py:468
  744.6 46.3 %reduce-scatter.41.cloned.1.call-done = bf16[128,1536]{1,0:T(8,128)(2,1)} async-done(((bf16[1024,1536]{1,0:T(8,128)(2,1)}), bf16[128,1536]{1,0:T(8,128)(2,1)}) %reduce-scatter.41.cloned.1.call-update) | async-done | bytes 393232
  925.2 19.7 %reduce-scatter.33.cloned.1.call-done = bf16[8,48,1536]{2,1,0:T(8,128)(2,1)} async-done(((bf16[32,48,1536]{2,1,0:T(8,128)(2,1)}), bf16[8,48,1536]{2,1,0:T(8,128)(2,1)}) %reduce-scatter.33.cloned.1.call-update) | async-done | bytes 1179664 | tf_op jit(solution)/shard_map/reduce_scatter | solution.py:506
  944.8 20.4 %all_to_all.154 = bf16[8,48,1536]{2,1,0:T(8,128)(2,1)S(1)} all-to-all(bf16[8,48,1536]{2,1,0:T(8,128)(2,1)} %reduce-scatter.33.cloned.1.call-done), channel_id=1, replica_groups=mesh['dp'=4,'z'=4,'core'=2] {'dp','core'}, dimensions={0} | all-to-all | bytes 2359296 | tf_op jit(solution)/shard_map/all_to_all | solution.py:507
  965.2 23.9 %reduce-scatter.31.cloned.1.call-done = bf16[8,48,576]{2,1,0:T(8,128)(2,1)} async-done(((bf16[32,48,576]{2,1,0:T(8,128)(2,1)}), bf16[8,48,576]{2,1,0:T(8,128)(2,1)}) %reduce-scatter.31.cloned.1.call-update) | async-done | bytes 442384 | tf_op jit(solution)/shard_map/reduce_scatter | solution.py:506
  1004.6 34.4 %reduce-scatter.43.cloned.1.call-done = bf16[128,1536]{1,0:T(8,128)(2,1)} async-done(((bf16[1024,1536]{1,0:T(8,128)(2,1)}), bf16[128,1536]{1,0:T(8,128)(2,1)}) %reduce-scatter.43.cloned.1.call-update) | async-done | bytes 393232
  1041.6 48.2 %reduce-scatter.29.cloned.1.call-done = bf16[8,48,768]{2,1,0:T(8,128)(2,1)} async-done(((bf16[32,48,768]{2,1,0:T(8,128)(2,1)}), bf16[8,48,768]{2,1,0:T(8,128)(2,1)}) %reduce-scatter.29.cloned.1.call-update) | async-done | bytes 589840 | tf_op jit(solution)/shard_map/reduce_scatter | solution.py:506
  1113.5 16.6 %all-to-all-done.8 = bf16[4,32,1536]{2,1,0:T(8,128)(2,1)} async-done(((bf16[4,32,1536]{2,1,0:T(8,128)(2,1)}), bf16[4,32,1536]{2,1,0:T(8,128)(2,1)}, u32[]{:S(2)}, u32[]{:S(2)}) %all-to-all-start.8) | async-done | bytes 393248 | tf_op jit(solution)/shard_map/all_to_all | solution.py:487
  1130.1 16.3 %reduce-scatter.35.cloned.1.call-done = bf16[8,48,768]{2,1,0:T(8,128)(2,1)} async-done(((bf16[32,48,768]{2,1,0:T(8,128)(2,1)}), bf16[8,48,768]{2,1,0:T(8,128)(2,1)}) %reduce-scatter.35.cloned.1.call-update) | async-done | bytes 589840 | tf_op jit(solution)/shard_map/reduce_scatter | solution.py:506
  1180.7 67.1 %reduce-scatter.45.cloned.1.call-done = f32[48,8]{1,0:T(8,128)} async-done(((f32[1536,8]{1,0:T(8,128)}), f32[48,8]{1,0:T(8,128)}) %reduce-scatter.45.cloned.1.call-update) | async-done | bytes 1552 | tf_op jit(solution)/shard_map/reduce_scatter | solution.py:769
  1252.5 40.2 %psum.7 = f32[]{:T(128)} all-reduce(f32[]{:T(128)} %multiply_reduce_fusion.1), channel_id=1, replica_groups=mesh['dp'=4,'z'=4,'core'=2] {'dp','z','core'}, use_global_device_ids=true, to_apply=%region_41.46 | all-reduce | flops 1 | bytes 8 | tf_op jit(solution)/shard_map/psum | solution.py:787
  1297.2 15.2 %fusion.111 = (bf16[48,29192]{1,0:T(8,128)(2,1)}, f32[48,29192]{1,0:T(8,128)}, f32[48,29192]{1,0:T(8,128)}, f32[48,29192]{1,0:T(8,128)}, f32[48,29192]{1,0:T(8,128)S(1)}) fusion(f32[48,29192]{1,0:T(8,128)} %param.23, f32[29192]{0:T(1024)S(1)} %copy-done.31, f32[48,29192]{1,0:T(8,128)} %param.25, f32[48,29192]{1,0:T(8,128)} %param.24, f32[]{:T(128)S(6)} %max.3, ...), kind=kLoop, calls=%fused_computation.288 | loop fusion | flops 23820672 | bytes 47758116 | tf_op jit(solution)/shard_map/convert_element_type | solution.py:812
  (454 shorter events, 519.1 us)
Async XLA Ops:
  7.2 150.7 %all-gather.13.cloned.1.call-start = ((), (), s32[]{:S(2)}) async-start(), calls=%async_computation.30 | async-start | bytes 2949120 | tf_op jit(solution)/shard_map/all_gather | solution.py:499
  58.7 101.6 %all-gather.25.cloned.1.call-start = ((), (), s32[]{:S(2)}) async-start(), calls=%async_computation.37 | async-start | bytes 2949120 | tf_op jit(solution)/shard_map/all_gather | solution.py:499
  68.9 64.8 %all-to-all-start.1 = ((bf16[4,32,3072]{2,1,0:T(8,128)(2,1)}), bf16[4,32,3072]{2,1,0:T(8,128)(2,1)S(1)}, u32[]{:S(2)}, u32[]{:S(2)}) async-start(bf16[4,32,3072]{2,1,0:T(8,128)(2,1)} %all-to-all-done), calls=%async_computation.1 | async-start | bytes 1572864 | tf_op jit(solution)/shard_map/all_to_all | solution.py:483
  73.8 107.9 %all-gather.15.cloned.1.call-start = ((), (), s32[]{:S(2)}) async-start(), calls=%async_computation.31 | async-start | bytes 3538944 | tf_op jit(solution)/shard_map/all_gather | solution.py:456
  142.4 84.9 %all-gather.19.cloned.1.call-start = ((), (), s32[]{:S(2)}) async-start(), calls=%async_computation.33 | async-start | bytes 2457600 | tf_op jit(solution)/shard_map/all_gather | solution.py:499
  157.7 102.5 %all-gather.17.cloned.1.call-start = ((), (), s32[]{:S(2)}) async-start(), calls=%async_computation.32 | async-start | bytes 3538944 | tf_op jit(solution)/shard_map/all_gather | solution.py:460
  268.2 40.6 %reduce-scatter.23.cloned.1.call-start = ((), (), s32[]{:S(2)}) async-start(), calls=%async_computation.34 | async-start | bytes 884736 | tf_op jit(solution)/shard_map/reduce_scatter | solution.py:468
  270.9 72.7 %all-gather.21.cloned.1.call-start = ((), (), s32[]{:S(2)}) async-start(), calls=%async_computation.35 | async-start | bytes 3538944 | tf_op jit(solution)/shard_map/all_gather | solution.py:456
  281.8 109.4 %all-gather.23.cloned.1.call-start = ((), (), s32[]{:S(2)}) async-start(), calls=%async_computation.36 | async-start | bytes 3538944 | tf_op jit(solution)/shard_map/all_gather | solution.py:460
  353.4 128.5 %all-gather.27.cloned.1.call-start = ((), (), s32[]{:S(2)}) async-start(), calls=%async_computation.38 | async-start | bytes 5898240 | tf_op jit(solution)/shard_map/all_gather | solution.py:499
  381.6 133.4 %all-gather.29.cloned.1.call-start = ((), (), s32[]{:S(2)}) async-start(), calls=%async_computation.39 | async-start | bytes 3538944 | tf_op jit(solution)/shard_map/all_gather | solution.py:456
  406.6 143.2 %all-gather.31.cloned.1.call-start = ((), (), s32[]{:S(2)}) async-start(), calls=%async_computation.40 | async-start | bytes 3538944 | tf_op jit(solution)/shard_map/all_gather | solution.py:456
  407.4 211.2 %reduce-scatter.39.cloned.1.call-start = ((), (), s32[]{:S(2)}) async-start(), calls=%async_computation.48 | async-start | bytes 3538944
  572.1 97.0 %reduce-scatter.37.cloned.1.call-start = ((), (), s32[]{:S(2)}) async-start(), calls=%async_computation.47 | async-start | bytes 3538944
  583.8 148.3 %reduce-scatter.25.cloned.1.call-start = ((), (), s32[]{:S(2)}) async-start(), calls=%async_computation.41 | async-start | bytes 3538944 | tf_op jit(solution)/shard_map/reduce_scatter | solution.py:468
  686.6 104.3 %reduce-scatter.41.cloned.1.call-start = ((), (), s32[]{:S(2)}) async-start(), calls=%async_computation.49 | async-start | bytes 3538944
  744.5 116.4 %reduce-scatter.27.cloned.1.call-start = ((), (), s32[]{:S(2)}) async-start(), calls=%async_computation.42 | async-start | bytes 3538944 | tf_op jit(solution)/shard_map/reduce_scatter | solution.py:468
  811.2 133.6 %reduce-scatter.33.cloned.1.call-start = ((), (), s32[]{:S(2)}) async-start(), calls=%async_computation.45 | async-start | bytes 5898240 | tf_op jit(solution)/shard_map/reduce_scatter | solution.py:506
  832.0 157.1 %reduce-scatter.31.cloned.1.call-start = ((), (), s32[]{:S(2)}) async-start(), calls=%async_computation.44 | async-start | bytes 2457600 | tf_op jit(solution)/shard_map/reduce_scatter | solution.py:506
  860.7 178.3 %reduce-scatter.43.cloned.1.call-start = ((), (), s32[]{:S(2)}) async-start(), calls=%async_computation.50 | async-start | bytes 3538944
  895.3 194.4 %reduce-scatter.29.cloned.1.call-start = ((), (), s32[]{:S(2)}) async-start(), calls=%async_computation.43 | async-start | bytes 2949120 | tf_op jit(solution)/shard_map/reduce_scatter | solution.py:506
  924.4 222.0 %reduce-scatter.35.cloned.1.call-start = ((), (), s32[]{:S(2)}) async-start(), calls=%async_computation.46 | async-start | bytes 2949120 | tf_op jit(solution)/shard_map/reduce_scatter | solution.py:506
  1093.4 154.4 %reduce-scatter.45.cloned.1.call-start = ((), (), s32[]{:S(2)}) async-start(), calls=%async_computation.51 | async-start | bytes 811008 | tf_op jit(solution)/shard_map/reduce_scatter | solution.py:769
  1169.8 123.6 %all-to-all-start.12 = ((bf16[4,32,1536]{2,1,0:T(8,128)(2,1)}), bf16[4,32,1536]{2,1,0:T(8,128)(2,1)}, u32[]{:S(2)}, u32[]{:S(2)}) async-start(bf16[4,32,1536]{2,1,0:T(8,128)(2,1)} %bitcast.60), calls=%async_computation.15 | async-start | bytes 786432 | tf_op jit(solution)/shard_map/all_to_all | solution.py:487
  (87 other events, 2088.9 us)
Sparse Core Ops, SparseCore 0:
  34.8 58.8 all-gather.12
  95.8 52.7 all-gather.24
  150.5 31.1 all-gather.14
  183.7 43.5 all-gather.18
  229.0 31.1 all-gather.16
  272.4 36.3 reduce-scatter.22
  311.3 32.2 all-gather.20
  353.5 37.6 all-gather.22
  392.8 89.0 all-gather.26
  484.2 30.7 all-gather.28
  517.5 32.3 all-gather.30
  572.2 46.2 reduce-scatter.38
  622.9 46.2 reduce-scatter.36
  686.7 45.3 reduce-scatter.24
  744.6 46.2 reduce-scatter.40
  811.4 45.3 reduce-scatter.26
  859.6 85.2 reduce-scatter.32
  947.1 41.9 reduce-scatter.30
  993.5 45.4 reduce-scatter.42
  1041.7 48.0 reduce-scatter.28
  1092.6 53.7 reduce-scatter.34
  1152.1 95.6 reduce-scatter.44

commit v2 on v1

--- a/solution.py
+++ b/solution.py
@@ -1,8 +1,11 @@
+import functools
 import math
 
 import jax
 import jax.numpy as jnp
 from jax import lax
+from jax.experimental import pallas as pl
+from jax.experimental.pallas import tpu as pltpu
 from jax.sharding import Mesh
 from jax.sharding import PartitionSpec as P
 
@@ -452,40 +455,780 @@
     return jnp.dot(left, right, preferred_element_type=jnp.float32)
 
 
-def plane_gather(shard):
-    return lax.all_gather(shard, PLANE, axis=1, tiled=True)
-
-
-def plane_gather_rows(shard):
-    return lax.all_gather(shard, PLANE, axis=0, tiled=True)
-
-
-def plane_scatter_frames(partial):
-    return lax.psum_scatter(partial, PLANE, scatter_dimension=1, tiled=True)
-
-
-def plane_scatter_rows(partial):
-    return lax.psum_scatter(partial, PLANE, scatter_dimension=0, tiled=True)
-
-
-def to_frames(rows):
-    return lax.all_to_all(rows, PLANE, split_axis=1, concat_axis=0, tiled=True)
-
-
-def to_rows(frames):
-    return lax.all_to_all(frames, PLANE, split_axis=0, concat_axis=1, tiled=True)
-
-
-def row_to_plane(local):
-    groups = lax.axis_size("dp")
-    frames, width = local.shape
-    pieces = lax.all_to_all(local, "dp", split_axis=0, concat_axis=0, tiled=True)
-    return lax.all_to_all(pieces, "z", split_axis=0, concat_axis=0, tiled=True)
-
-
-def plane_to_row(local):
-    pieces = lax.all_to_all(local, "z", split_axis=0, concat_axis=0, tiled=True)
-    return lax.all_to_all(pieces, "dp", split_axis=0, concat_axis=0, tiled=True)
+MESH_ID = pl.DeviceIdType.MESH
+IDENTITIES = {}
+
+
+def identity_of(name, *arrays):
+    key = (name,) + tuple((array.shape, str(array.dtype)) for array in arrays)
+    return IDENTITIES.setdefault(key, len(IDENTITIES))
+
+
+IN_HBM = pl.BlockSpec(memory_space=pl.ANY)
+IN_VMEM = pl.BlockSpec(memory_space=pltpu.VMEM)
+BRIEF = pl.CostEstimate(flops=0, bytes_accessed=1024, transcendentals=0)
+
+
+def greet(peers):
+    barrier = pltpu.get_barrier_semaphore()
+    for peer in peers:
+        pl.semaphore_signal(barrier, inc=1, device_id=peer, device_id_type=MESH_ID)
+    pl.semaphore_wait(barrier, len(peers))
+
+
+def near():
+    group, core = lax.axis_index("dp"), lax.axis_index("core")
+    across = group + 1 - 2 * lax.rem(group, 2)
+    along = lax.rem(group + 2, 4)
+    return group, core, across, along
+
+
+def member_rows(width):
+    def place(ref, member, start, count):
+        first_row = pl.multiple_of(member * width + start, 16)
+        return ref.at[pl.ds(first_row, count), :]
+
+    return place
+
+
+def member_lanes(width):
+    def place(ref, member, start, count):
+        return ref.at[pl.ds(start, count), pl.ds(pl.multiple_of(member * width, 128), width)]
+
+    return place
+
+
+def mover(send_sem, recv_sem, first=0):
+    def copy(k, source, target, peer):
+        return pltpu.make_async_remote_copy(
+            src_ref=source,
+            dst_ref=target,
+            send_sem=send_sem.at[first + k],
+            recv_sem=recv_sem.at[first + k],
+            device_id=peer,
+            device_id_type=MESH_ID,
+        )
+
+    return copy
+
+
+def member_at(member):
+    return {"dp": lax.div(member, 2), "core": lax.rem(member, 2)}
+
+
+def plane_peers():
+    group, core, _, _ = near()
+    member = group * 2 + core
+    return [lax.rem(member + step, 8) for step in range(1, 8)]
+
+
+def gather_steps(place, x_ref, o_ref, local_sem, copy):
+    group, core, across, along = near()
+    beyond = across + along - group
+    other = 1 - core
+    sibling, by_x, by_y = {"core": other}, {"dp": across}, {"dp": along}
+    half = x_ref.shape[0] // 2
+
+    def part(owner, owner_core, piece):
+        return place(o_ref, owner * 2 + owner_core, piece * half, half)
+
+    sent = []
+
+    def send(k, source, target, peer):
+        moving = copy(k, source, target, peer)
+        moving.start()
+        sent.append(moving)
+
+    def own(k, piece, peer):
+        send(k, x_ref.at[pl.ds(piece * half, half), :], part(group, core, piece), peer)
+
+    def relay(k, owner, piece, peer):
+        send(k, part(owner, core, piece), part(owner, core, piece), peer)
+
+    def arrived(k, owner, owner_core, piece):
+        landed = part(owner, owner_core, piece)
+        copy(k, landed, landed, sibling).wait_recv()
+
+    local = pltpu.make_async_copy(
+        x_ref, place(o_ref, group * 2 + core, 0, 2 * half), local_sem
+    )
+    local.start()
+    own(0, 0, by_x)
+    own(1, 1, by_y)
+    own(2, 1, by_x)
+    own(3, 0, by_y)
+    own(4, 0, sibling)
+    own(5, 1, sibling)
+
+    def finish():
+        arrived(0, across, core, 0)
+        relay(6, across, 0, by_y)
+        relay(7, across, 0, sibling)
+        arrived(1, along, core, 1)
+        relay(8, along, 1, by_x)
+        relay(9, along, 1, sibling)
+        arrived(2, across, core, 1)
+        relay(10, across, 1, sibling)
+        arrived(3, along, core, 0)
+        relay(11, along, 0, sibling)
+        arrived(6, beyond, core, 0)
+        relay(12, beyond, 0, sibling)
+        arrived(8, beyond, core, 1)
+        relay(13, beyond, 1, sibling)
+        arrived(4, group, other, 0)
+        arrived(5, group, other, 1)
+        arrived(7, across, other, 0)
+        arrived(9, along, other, 1)
+        arrived(10, across, other, 1)
+        arrived(11, along, other, 0)
+        arrived(12, beyond, other, 0)
+        arrived(13, beyond, other, 1)
+        local.wait()
+        for moving in sent:
+            moving.wait_send()
+
+    return finish
+
+
+def exchange_steps(source, target, x_ref, o_ref, local_sem, copy):
+    group, core, _, _ = near()
+    member = group * 2 + core
+    local = pltpu.make_async_copy(source(x_ref, member), target(o_ref, member), local_sem)
+    local.start()
+    sent = []
+    for k, peer in enumerate(plane_peers()):
+        sent.append(copy(k, source(x_ref, peer), target(o_ref, member), member_at(peer)))
+        sent[-1].start()
+
+    def finish():
+        for k in range(7):
+            sender = lax.rem(member + 7 - k, 8)
+            landed = target(o_ref, sender)
+            copy(k, landed, landed, member_at(sender)).wait_recv()
+        local.wait()
+        for moving in sent:
+            moving.wait_send()
+
+    return finish
+
+
+def gather_kernel(place, x_ref, *refs):
+    o_ref, local_sem, send_sem, recv_sem = refs[-4:]
+    _, core, across, along = near()
+    greet([{"dp": across}, {"dp": along}, {"core": 1 - core}])
+    gather_steps(place, x_ref, o_ref, local_sem, mover(send_sem, recv_sem))()
+
+
+def plane_gather_call(shard, shape, place, kind, after):
+    return pl.pallas_call(
+        functools.partial(gather_kernel, place),
+        out_shape=jax.ShapeDtypeStruct(shape, shard.dtype),
+        in_specs=[IN_HBM] * (1 + len(after)),
+        out_specs=IN_HBM,
+        scratch_shapes=[
+            pltpu.SemaphoreType.DMA,
+            pltpu.SemaphoreType.DMA((14,)),
+            pltpu.SemaphoreType.DMA((14,)),
+        ],
+        compiler_params=pltpu.CompilerParams(
+            collective_id=identity_of(kind, shard, *after), has_side_effects=True
+        ),
+        cost_estimate=BRIEF,
+        name="plane_gather",
+    )(shard, *after)
+
+
+def plane_gather(shard, after=()):
+    rows, width = shard.shape
+    return plane_gather_call(shard, (rows, 8 * width), member_lanes(width), "gather lanes", after)
+
+
+def plane_gather_rows(shard, after=()):
+    rows, width = shard.shape
+    return plane_gather_call(shard, (8 * rows, width), member_rows(rows), "gather rows", after)
+
+
+def scatter_kernel(place, p_ref, *refs):
+    o_ref, pair, total, from_x, from_y, relay, send_sem, recv_sem = refs[-8:]
+    group, core, across, along = near()
+    beyond = across + along - group
+    other = 1 - core
+    sibling, by_x, by_y = {"core": other}, {"dp": across}, {"dp": along}
+    rows = o_ref.shape[0]
+    half = rows // 2
+    low, high = pl.ds(0, half), pl.ds(half, half)
+
+    copy = mover(send_sem, recv_sem)
+    sent = []
+
+    def send(k, source, target, peer):
+        moving = copy(k, source, target, peer)
+        moving.start()
+        sent.append(moving)
+
+    def arrived(k, target):
+        copy(k, target, target, sibling).wait_recv()
+
+    def wide(ref):
+        return ref[...].astype(jnp.float32)
+
+    def both_cores(k, owner):
+        arrived(k, pair.at[k])
+        summed = wide(place(p_ref, owner * 2 + core, 0, rows)) + wide(pair.at[k])
+        total[k] = summed.astype(total.dtype)
+
+    greet([by_x, by_y, sibling])
+    for k, owner in enumerate((beyond, across, along, group)):
+        send(k, place(p_ref, owner * 2 + other, 0, rows), pair.at[k], sibling)
+    both_cores(0, beyond)
+    send(4, total.at[0, low], relay.at[0], by_x)
+    send(5, total.at[0, high], relay.at[1], by_y)
+    both_cores(1, across)
+    send(6, total.at[1, low], from_x.at[low], by_x)
+    both_cores(2, along)
+    send(7, total.at[2, high], from_y.at[high], by_y)
+    both_cores(3, group)
+    arrived(5, relay.at[1])
+    total[1, high] = (wide(total.at[1, high]) + wide(relay.at[1])).astype(total.dtype)
+    send(8, total.at[1, high], from_x.at[high], by_x)
+    arrived(4, relay.at[0])
+    total[2, low] = (wide(total.at[2, low]) + wide(relay.at[0])).astype(total.dtype)
+    send(9, total.at[2, low], from_y.at[low], by_y)
+    arrived(6, from_x.at[low])
+    arrived(7, from_y.at[high])
+    arrived(8, from_x.at[high])
+    arrived(9, from_y.at[low])
+    o_ref[...] = (wide(total.at[3]) + wide(from_x) + wide(from_y)).astype(o_ref.dtype)
+    for moving in sent:
+        moving.wait_send()
+
+
+def plane_scatter_call(partial, shape, place, dtype, kind, after):
+    rows, width = shape
+    slot = pltpu.VMEM((rows, width), jnp.bfloat16)
+    return pl.pallas_call(
+        functools.partial(scatter_kernel, place),
+        out_shape=jax.ShapeDtypeStruct(shape, dtype),
+        in_specs=[IN_VMEM] + [IN_HBM] * len(after),
+        out_specs=IN_VMEM,
+        scratch_shapes=[
+            pltpu.VMEM((4, rows, width), jnp.bfloat16),
+            pltpu.VMEM((4, rows, width), jnp.bfloat16),
+            slot,
+            slot,
+            pltpu.VMEM((2, rows // 2, width), jnp.bfloat16),
+            pltpu.SemaphoreType.DMA((10,)),
+            pltpu.SemaphoreType.DMA((10,)),
+        ],
+        compiler_params=pltpu.CompilerParams(
+            collective_id=identity_of(kind, partial, *after),
+            has_side_effects=True,
+            vmem_limit_bytes=24 * 2**20,
+        ),
+        cost_estimate=BRIEF,
+        name="plane_scatter",
+    )(partial, *after)
+
+
+def plane_scatter_frames(partial, after=()):
+    rows, width = partial.shape[0], partial.shape[1] // 8
+    place = member_lanes(width)
+    return plane_scatter_call(partial, (rows, width), place, jnp.float32, "scatter lanes", after)
+
+
+def plane_scatter_rows(partial, after=()):
+    rows, width = partial.shape[0] // 8, partial.shape[1]
+    place = member_rows(rows)
+    return plane_scatter_call(partial, (rows, width), place, jnp.bfloat16, "scatter rows", after)
+
+
+def exchange_kernel(source, target, x_ref, *refs):
+    o_ref, local_sem, send_sem, recv_sem = refs[-4:]
+    greet([member_at(peer) for peer in plane_peers()])
+    exchange_steps(source, target, x_ref, o_ref, local_sem, mover(send_sem, recv_sem))()
+
+
+def exchange(array, shape, source, target, kind, after=()):
+    return pl.pallas_call(
+        functools.partial(exchange_kernel, source, target),
+        out_shape=jax.ShapeDtypeStruct(shape, array.dtype),
+        in_specs=[IN_HBM] * (1 + len(after)),
+        out_specs=IN_HBM,
+        scratch_shapes=[
+            pltpu.SemaphoreType.DMA,
+            pltpu.SemaphoreType.DMA((7,)),
+            pltpu.SemaphoreType.DMA((7,)),
+        ],
+        compiler_params=pltpu.CompilerParams(
+            collective_id=identity_of(kind, array, *after), has_side_effects=True
+        ),
+        cost_estimate=BRIEF,
+        name="plane_exchange",
+    )(array, *after)
+
+
+def whole_rows(rows):
+    place = member_rows(rows)
+    return lambda ref, member: place(ref, member, 0, rows)
+
+
+def whole_lanes(rows, width):
+    place = member_lanes(width)
+    return lambda ref, member: place(ref, member, 0, rows)
+
+
+def to_frames(part):
+    rows, width = part.shape[0], part.shape[1] // 8
+    return exchange(part, (8 * rows, width), whole_lanes(rows, width), whole_rows(rows), "to frames")
+
+
+def to_rows(part):
+    rows, width = part.shape[0] // 8, part.shape[1]
+    return exchange(part, (rows, 8 * width), whole_rows(rows), whole_lanes(rows, width), "to rows")
+
+
+def block(ref, member):
+    return ref.at[member]
+
+
+def exchange_blocks(blocks, after=()):
+    return exchange(blocks, blocks.shape, block, block, "blocks", after)
+
+
+def lanes(ref, start, width):
+    return ref.at[:, pl.ds(pl.multiple_of(start, 128), width)]
+
+
+def sheet_part(start, width):
+    return lambda ref, member: lanes(ref, start + member * width, width)
+
+
+def block_part(start, width):
+    return lambda ref, member: lanes(ref.at[member], start, width)
+
+
+def feed_kernel(count, *refs):
+    gu_ref, down_ref = refs[:2]
+    o_ref, local_sem, send_sem, recv_sem = refs[-4:]
+    width = down_ref.shape[-1]
+    greet([member_at(peer) for peer in plane_peers()])
+    finish = []
+    for k, (ref, start) in enumerate(((gu_ref, 0), (gu_ref, width), (down_ref, 0))):
+        source, target = block_part(start, width), sheet_part(8 * k * width, width)
+        copy = mover(send_sem, recv_sem, 7 * k)
+        finish.append(exchange_steps(source, target, ref, o_ref, local_sem.at[k], copy))
+    for end in finish:
+        end()
+
+
+def feed(gu, down, after=()):
+    return pl.pallas_call(
+        functools.partial(feed_kernel, len(after)),
+        out_shape=jax.ShapeDtypeStruct((gu.shape[1], 24 * down.shape[-1]), gu.dtype),
+        in_specs=[IN_HBM] * (2 + len(after)),
+        out_specs=IN_HBM,
+        scratch_shapes=[
+            pltpu.SemaphoreType.DMA((3,)),
+            pltpu.SemaphoreType.DMA((21,)),
+            pltpu.SemaphoreType.DMA((21,)),
+        ],
+        compiler_params=pltpu.CompilerParams(
+            collective_id=identity_of("feed", gu, down, *after), has_side_effects=True
+        ),
+        cost_estimate=BRIEF,
+        name="feed",
+    )(gu, down, *after)
+
+
+def opening_kernel(
+    x_ref,
+    small_ref,
+    text_ref,
+    w_ref,
+    v_ref,
+    t_ref,
+    all_ref,
+    mine_ref,
+    wo_ref,
+    vo_ref,
+    held,
+    local_sem,
+    send_sem,
+    recv_sem,
+):
+    group, core, _, _ = near()
+    member = group * 2 + core
+    plane = lax.axis_index("z")
+    step = x_ref.shape[0] // 4
+    text_rows = mine_ref.shape[0]
+    teacher = jnp.logical_and(group == plane, core == 0)
+
+    def frames(ref, j):
+        return ref.at[pl.ds(pl.multiple_of(j * step, 16), step), :]
+
+    peers = plane_peers()
+    line = [lax.rem(plane + k, 4) for k in range(1, 4)]
+    greet([member_at(peer) for peer in peers] + [{"z": there} for there in line])
+
+    near_copy = mover(send_sem, recv_sem)
+    line_copy = mover(send_sem, recv_sem, 7)
+    small_local = pltpu.make_async_copy(small_ref, all_ref.at[plane, member], local_sem.at[0])
+    small_local.start()
+    first = [
+        near_copy(k, small_ref, all_ref.at[plane, member], member_at(peer))
+        for k, peer in enumerate(peers)
+    ]
+    for moving in first:
+        moving.start()
+
+    others = [lax.rem(group + k, 4) for k in range(1, 4)]
+    keep = pltpu.make_async_copy(frames(x_ref, group), frames(held, group), local_sem.at[1])
+    keep.start()
+
+    def spread(owner, landing):
+        return pltpu.make_async_remote_copy(
+            src_ref=frames(x_ref, owner),
+            dst_ref=frames(held, landing),
+            send_sem=send_sem.at[10 + owner],
+            recv_sem=recv_sem.at[10 + landing],
+            device_id={"dp": owner},
+            device_id_type=MESH_ID,
+        )
+
+    for owner in others:
+        spread(owner, group).start()
+
+    def rise(row):
+        return pltpu.make_async_remote_copy(
+            src_ref=frames(held, row),
+            dst_ref=frames(t_ref, plane),
+            send_sem=send_sem.at[28 + row],
+            recv_sem=recv_sem.at[28 + plane],
+            device_id={"z": row},
+            device_id_type=MESH_ID,
+        )
+
+    stay = pltpu.make_async_copy(frames(held, plane), frames(t_ref, plane), local_sem.at[4])
+
+    def pass_on(row):
+        pl.when(row == plane)(stay.start)
+        pl.when(row != plane)(rise(row).start)
+
+    first_done = exchange_steps(
+        block, block, w_ref, wo_ref, local_sem.at[2], mover(send_sem, recv_sem, 14)
+    )
+    second_done = exchange_steps(
+        block, block, v_ref, vo_ref, local_sem.at[5], mover(send_sem, recv_sem, 32)
+    )
+
+    def text_copy(k, peer):
+        return pltpu.make_async_remote_copy(
+            src_ref=text_ref.at[pl.ds(pl.multiple_of(peer * text_rows, 16), text_rows), :],
+            dst_ref=mine_ref,
+            send_sem=send_sem.at[21 + k],
+            recv_sem=recv_sem.at[21],
+            device_id=member_at(peer),
+            device_id_type=MESH_ID,
+        )
+
+    own_text = text_ref.at[pl.ds(pl.multiple_of(member * text_rows, 16), text_rows), :]
+    text_local = pltpu.make_async_copy(own_text, mine_ref, local_sem.at[3])
+
+    @pl.when(teacher)
+    def _():
+        text_local.start()
+        for k, peer in enumerate(peers):
+            text_copy(k, peer).start()
+
+    keep.wait()
+    pass_on(group)
+    for owner in others:
+        spread(owner, owner).wait_recv()
+        pass_on(owner)
+
+    for k in range(7):
+        landed = all_ref.at[plane, lax.rem(member + 7 - k, 8)]
+        near_copy(k, landed, landed, member_at(peers[k])).wait_recv()
+    small_local.wait()
+    second = [
+        line_copy(k, all_ref.at[plane], all_ref.at[plane], {"z": there})
+        for k, there in enumerate(line)
+    ]
+    for moving in second:
+        moving.start()
+    for k in range(3):
+        landed = all_ref.at[lax.rem(plane + 3 - k, 4)]
+        line_copy(k, landed, landed, {"z": line[k]}).wait_recv()
+
+    for there in line:
+        landed = frames(t_ref, there)
+        pltpu.make_async_remote_copy(
+            src_ref=landed,
+            dst_ref=landed,
+            send_sem=send_sem.at[28 + there],
+            recv_sem=recv_sem.at[28 + there],
+            device_id={"z": there},
+            device_id_type=MESH_ID,
+        ).wait_recv()
+    stay.wait()
+    first_done()
+    second_done()
+
+    @pl.when(teacher)
+    def _():
+        text_local.wait()
+        for k, peer in enumerate(peers):
+            text_copy(k, peer).wait_send()
+
+    @pl.when(jnp.logical_not(teacher))
+    def _():
+        text_copy(0, peers[0]).wait_recv()
+
+    for moving in first + second:
+        moving.wait_send()
+    for owner in others:
+        spread(owner, group).wait_send()
+    for there in line:
+        rise(there).wait_send()
+
+
+def opening(local, small, text, first, second):
+    return pl.pallas_call(
+        opening_kernel,
+        out_shape=(
+            jax.ShapeDtypeStruct(local.shape, local.dtype),
+            jax.ShapeDtypeStruct((4, 8) + small.shape, small.dtype),
+            jax.ShapeDtypeStruct((text.shape[0] // 8, text.shape[1]), text.dtype),
+            jax.ShapeDtypeStruct(first.shape, first.dtype),
+            jax.ShapeDtypeStruct(second.shape, second.dtype),
+        ),
+        in_specs=[IN_HBM] * 5,
+        out_specs=(IN_HBM,) * 5,
+        scratch_shapes=[
+            pltpu.VMEM(local.shape, local.dtype),
+            pltpu.SemaphoreType.DMA((6,)),
+            pltpu.SemaphoreType.DMA((39,)),
+            pltpu.SemaphoreType.DMA((39,)),
+        ],
+        compiler_params=pltpu.CompilerParams(
+            collective_id=identity_of("opening", local), has_side_effects=True
+        ),
+        cost_estimate=BRIEF,
+        name="opening",
+    )(local, small, text, first, second)
+
+
+def first_gather_kernel(x_ref, y_ref, sheet_ref, ox_ref, oy_ref, w_ref, local_sem, send_sem, recv_sem):
+    place = member_lanes(x_ref.shape[1])
+    width = FF // 8
+    greet([member_at(peer) for peer in plane_peers()])
+    finish = [
+        gather_steps(place, x_ref, ox_ref, local_sem.at[0], mover(send_sem, recv_sem)),
+        gather_steps(place, y_ref, oy_ref, local_sem.at[1], mover(send_sem, recv_sem, 14)),
+    ]
+    for k in range(3):
+        source, target = sheet_part(6 * D + k * FF, width), block_part(k * width, width)
+        copy = mover(send_sem, recv_sem, 28 + 7 * k)
+        finish.append(exchange_steps(source, target, sheet_ref, w_ref, local_sem.at[2 + k], copy))
+    for end in finish:
+        end()
+
+
+def first_gather(shard, other, sheet):
+    rows, width = shard.shape
+    whole = jax.ShapeDtypeStruct((rows, 8 * width), shard.dtype)
+    return pl.pallas_call(
+        first_gather_kernel,
+        out_shape=(
+            whole,
+            whole,
+            jax.ShapeDtypeStruct((8, sheet.shape[0], 3 * FF // 8), sheet.dtype),
+        ),
+        in_specs=[IN_HBM] * 3,
+        out_specs=(IN_HBM,) * 3,
+        scratch_shapes=[
+            pltpu.SemaphoreType.DMA((5,)),
+            pltpu.SemaphoreType.DMA((49,)),
+            pltpu.SemaphoreType.DMA((49,)),
+        ],
+        compiler_params=pltpu.CompilerParams(
+            collective_id=identity_of("first gather", shard, sheet), has_side_effects=True
+        ),
+        cost_estimate=BRIEF,
+        name="first_gather",
+    )(shard, other, sheet)
+
+
+def closing_kernel(
+    x_ref, w_ref, g_ref, _, t_ref, o_ref, s_ref, held, tall, local_sem, send_sem, recv_sem
+):
+    group, core, _, _ = near()
+    member = group * 2 + core
+    plane = lax.axis_index("z")
+    step = x_ref.shape[0] // 4
+    line = [lax.rem(plane + k, 4) for k in range(1, 4)]
+    back = [lax.rem(plane + 3 - k, 4) for k in range(3)]
+    groups = [lax.rem(group + k, 4) for k in range(1, 4)]
+    peers = plane_peers()
+    greet([member_at(peer) for peer in peers] + [{"z": there} for there in line])
+
+    def frames(ref, j):
+        return ref.at[pl.ds(pl.multiple_of(j * step, 16), step), :]
+
+    copy = mover(send_sem, recv_sem)
+    gain_line = mover(send_sem, recv_sem, 14)
+    gain_plane = mover(send_sem, recv_sem, 17)
+    gain_local = pltpu.make_async_copy(g_ref, tall.at[plane], local_sem.at[3])
+    gain_local.start()
+    sent = [gain_line(k, g_ref, tall.at[plane], {"z": there}) for k, there in enumerate(line)]
+    local = pltpu.make_async_copy(frames(x_ref, plane), frames(held, plane), local_sem.at[0])
+    local.start()
+    sent += [
+        copy(k, frames(x_ref, there), frames(held, plane), {"z": there})
+        for k, there in enumerate(line)
+    ]
+    for moving in sent:
+        moving.start()
+    weights_done = exchange_steps(
+        block, block, w_ref, o_ref, local_sem.at[1], mover(send_sem, recv_sem, 7)
+    )
+
+    gain_local.wait()
+    for k, origin in enumerate(back):
+        gain_line(k, tall.at[origin], tall.at[origin], {"z": origin}).wait_recv()
+    tall[4] = tall[0] + tall[1] + tall[2] + tall[3]
+    gain_keep = pltpu.make_async_copy(tall.at[4], s_ref.at[member], local_sem.at[4])
+    gain_keep.start()
+    given = [
+        gain_plane(k, tall.at[4], s_ref.at[member], member_at(peer)) for k, peer in enumerate(peers)
+    ]
+    for moving in given:
+        moving.start()
+
+    def onward(owner):
+        return pltpu.make_async_remote_copy(
+            src_ref=frames(held, owner),
+            dst_ref=frames(t_ref, group),
+            send_sem=send_sem.at[3 + owner],
+            recv_sem=recv_sem.at[3 + group],
+            device_id={"dp": owner},
+            device_id_type=MESH_ID,
+        )
+
+    keep = pltpu.make_async_copy(frames(held, group), frames(t_ref, group), local_sem.at[2])
+
+    def pass_on(owner):
+        pl.when(owner == group)(keep.start)
+        pl.when(owner != group)(onward(owner).start)
+
+    local.wait()
+    pass_on(plane)
+    for k, origin in enumerate(back):
+        landed = frames(held, origin)
+        copy(k, landed, landed, {"z": origin}).wait_recv()
+        pass_on(origin)
+    for origin in groups:
+        landed = frames(t_ref, origin)
+        pltpu.make_async_remote_copy(
+            src_ref=landed,
+            dst_ref=landed,
+            send_sem=send_sem.at[3 + origin],
+            recv_sem=recv_sem.at[3 + origin],
+            device_id={"dp": origin},
+            device_id_type=MESH_ID,
+        ).wait_recv()
+    keep.wait()
+    weights_done()
+    gain_keep.wait()
+    for k in range(7):
+        landed = s_ref.at[lax.rem(member + 7 - k, 8)]
+        gain_plane(k, landed, landed, member_at(peers[k])).wait_recv()
+    for moving in sent + given:
+        moving.wait_send()
+    for origin in groups:
+        onward(origin).wait_send()
+
+
+def closing(local, weights, gains, after):
+    return pl.pallas_call(
+        closing_kernel,
+        out_shape=(
+            jax.ShapeDtypeStruct(local.shape, local.dtype),
+            jax.ShapeDtypeStruct(weights.shape, weights.dtype),
+            jax.ShapeDtypeStruct((8,) + gains.shape, gains.dtype),
+        ),
+        in_specs=[IN_HBM] * 4,
+        out_specs=(IN_HBM,) * 3,
+        scratch_shapes=[
+            pltpu.VMEM(local.shape, local.dtype),
+            pltpu.VMEM((5,) + gains.shape, gains.dtype),
+            pltpu.SemaphoreType.DMA((5,)),
+            pltpu.SemaphoreType.DMA((24,)),
+            pltpu.SemaphoreType.DMA((24,)),
+        ],
+        compiler_params=pltpu.CompilerParams(
+            collective_id=identity_of("closing", local), has_side_effects=True
+        ),
+        cost_estimate=BRIEF,
+        name="closing",
+    )(local, weights, gains, after)
+
+
+def everywhere_kernel(x_ref, o_ref, local_sem, send_sem, recv_sem):
+    group, core, _, _ = near()
+    member = group * 2 + core
+    plane = lax.axis_index("z")
+    peers = [lax.rem(member + step, 8) for step in range(1, 8)]
+    places = [{"dp": lax.div(peer, 2), "core": lax.rem(peer, 2)} for peer in peers]
+    places = places + [{"z": lax.rem(plane + step, 4)} for step in range(1, 4)]
+    greet(places)
+
+    def copy(k, source, target):
+        return pltpu.make_async_remote_copy(
+            src_ref=source,
+            dst_ref=target,
+            send_sem=send_sem.at[k],
+            recv_sem=recv_sem.at[k],
+            device_id=places[k],
+            device_id_type=MESH_ID,
+        )
+
+    local = pltpu.make_async_copy(x_ref, o_ref.at[plane, member], local_sem)
+    local.start()
+    copies = [copy(k, x_ref, o_ref.at[plane, member]) for k in range(7)]
+    for moving in copies:
+        moving.start()
+    for k in range(7):
+        landed = o_ref.at[plane, lax.rem(member + 7 - k, 8)]
+        copy(k, landed, landed).wait_recv()
+    local.wait()
+    between = [copy(7 + k, o_ref.at[plane], o_ref.at[plane]) for k in range(3)]
+    for moving in between:
+        moving.start()
+    for k in range(3):
+        landed = o_ref.at[lax.rem(plane + 3 - k, 4)]
+        copy(7 + k, landed, landed).wait_recv()
+    for moving in copies + between:
+        moving.wait_send()
+
+
+def gather_everywhere(block):
+    return pl.pallas_call(
+        everywhere_kernel,
+        out_shape=jax.ShapeDtypeStruct((4, 8) + block.shape, block.dtype),
+        in_specs=[IN_VMEM],
+        out_specs=IN_VMEM,
+        scratch_shapes=[
+            pltpu.SemaphoreType.DMA,
+            pltpu.SemaphoreType.DMA((10,)),
+            pltpu.SemaphoreType.DMA((10,)),
+        ],
+        compiler_params=pltpu.CompilerParams(
+            collective_id=identity_of("everywhere", block), has_side_effects=True
+        ),
+        cost_estimate=BRIEF,
+        name="gather_everywhere",
+    )(block)
 
 
 def split_columns(block, members):
@@ -493,18 +1236,22 @@
     return block.reshape(rows, members, columns // members)
 
 
-def gather_columns(block, order):
-    rows, members, width = block.shape
-    mine = lax.all_to_all(jnp.swapaxes(block, 0, 1), PLANE, split_axis=0, concat_axis=0, tiled=True)
+def pick_blocks(blocks, order):
+    return blocks.at[order].get(mode="promise_in_bounds")
+
+
+def gather_line(mine, order):
     blocks = lax.all_gather(mine, "z", axis=0, tiled=True)
-    return jnp.take(blocks, order, axis=0).reshape(-1, width)
-
-
-def scatter_columns(grad, order, planes):
+    return pick_blocks(blocks, order).reshape(-1, mine.shape[-1])
+
+
+def grad_blocks(grad, order):
     blocks = grad.astype(jnp.bfloat16).reshape(order.shape[0], -1, grad.shape[-1])
-    blocks = jnp.take(blocks, order, axis=0)
-    mine = lax.psum_scatter(blocks, "z", scatter_dimension=0, tiled=True)
-    return jnp.swapaxes(lax.all_to_all(mine, PLANE, split_axis=0, concat_axis=0, tiled=True), 0, 1)
+    return pick_blocks(blocks, order)
+
+
+def scatter_line(blocks):
+    return lax.psum_scatter(blocks, "z", scatter_dimension=0, tiled=True)
 
 
 def plane_plan(latents, context, clip_starts, buckets, owners, cotangent, sheet, first, second):
@@ -540,33 +1287,43 @@
     def columns_of(start, width):
         return split_columns(low_sheet[:, start : start + width], members)
 
-    gains = lax.all_gather(low_sheet[:, gain_col:], ("z", "dp", "core"), axis=0, tiled=True)
-    gains = jnp.take(gains.reshape(blocks, rows, 8), to_logical, axis=0).reshape(D, 8)
-    gains = gains.astype(jnp.float32)
-    weight_one = gather_columns(
-        jnp.concatenate([columns_of(k * D, D) for k in range(4)], axis=2), to_logical
-    )
-    weight_two = gather_columns(
-        jnp.concatenate(
-            [
-                columns_of(4 * D, D),
-                columns_of(5 * D, D),
-                columns_of(tail_col, CTXW),
-                columns_of(tail_col + CTXW, CTXW),
-            ],
-            axis=2,
-        ),
-        to_logical,
-    )
-    weight_gu = gather_columns(
-        jnp.concatenate([columns_of(6 * D, FF), columns_of(6 * D + FF, FF)], axis=2), to_logical
-    )
-    weight_down = gather_columns(columns_of(6 * D + 2 * FF, FF), to_logical)
-    weight_qkv = weight_one[:, : 3 * span]
-    weight_ao = weight_one[:, 3 * span :]
-    weight_cq = weight_two[:, :span]
-    weight_co = weight_two[:, span : 2 * span]
-    weight_text = weight_two[:, 2 * span :]
+    def member_blocks(*pieces):
+        return jnp.swapaxes(jnp.concatenate(pieces, axis=2), 0, 1)
+
+    blocks_qkv = member_blocks(*[columns_of(k * D, D) for k in range(3)])
+    blocks_two = member_blocks(
+        columns_of(3 * D, D),
+        columns_of(4 * D, D),
+        columns_of(5 * D, D),
+        columns_of(tail_col, CTXW),
+        columns_of(tail_col + CTXW, CTXW),
+    )
+    small = jnp.concatenate(
+        [
+            jnp.pad(low_sheet[:, gain_col:].astype(jnp.float32).T, ((0, 0), (0, 64 - rows))),
+            jnp.pad(clip_starts.astype(jnp.float32), ((0, 7), (0, 64 - clip_starts.shape[1]))),
+        ],
+        axis=1,
+    )
+    both, small, text_mine, mine_qkv, mine_two = opening(
+        jnp.concatenate([latents[0], cotangent[0]], axis=1),
+        small,
+        context[0].T,
+        blocks_qkv,
+        blocks_two,
+    )
+    weight_qkv = gather_line(mine_qkv, to_logical)
+    weight_two = gather_line(mine_two, to_logical)
+    weight_ao = weight_two[:, :span]
+    weight_cq = weight_two[:, span : 2 * span]
+    weight_co = weight_two[:, 2 * span : 3 * span]
+    weight_text = weight_two[:, 3 * span :]
+    gains = pick_blocks(small[..., :rows].reshape(blocks, 8, rows), to_logical)
+    gains = gains.swapaxes(1, 2).reshape(D, 8)
+    starts = lax.dynamic_index_in_dim(
+        small[0, :, 0, 64 : 64 + clip_starts.shape[1]], plane * cores, 0, False
+    )
+    starts = starts.astype(jnp.int32)
 
     bucket_ids = jnp.arange(NB, dtype=jnp.int32)
     bucket_pick = (bucket_ids == buckets[plane]).astype(jnp.float32)
@@ -577,14 +1334,12 @@
     gain_three = gains[:, 2:3]
     time_gain = jnp.sum(gains[:, 3:] * bucket_pick[None, :], axis=1, keepdims=True)
 
-    both = row_to_plane(jnp.concatenate([latents[0], cotangent[0]], axis=1))
     tokens = both[:, :D].astype(jnp.float32).T
     grad_out = both[:, D:].astype(jnp.float32).T * row_weight
 
     rest = frames // planes
     place = jnp.arange(length, dtype=jnp.int32).reshape(planes, cores, groups, rest)
     positions = place.transpose(2, 1, 0, 3).reshape(-1)
-    starts = lax.all_gather(clip_starts, "dp", axis=0, tiled=True)[plane]
     segments = segment_ids(starts, positions)
     same_clip = segments[:, None] == segments[None, :]
     frequency = jnp.exp(
@@ -594,10 +1349,14 @@
     cosine = jnp.cos(angles)[None]
     sine_table = jnp.sin(angles)[None]
 
-    grad_ff = plane_gather(grad_out.astype(jnp.bfloat16))
     normed_one, inverse_one = norm_columns(tokens)
     scaled_one = gain_one * time_gain
-    h_one = plane_gather((normed_one * scaled_one).astype(jnp.bfloat16))
+    h_one, grad_ff, mine_feed = first_gather(
+        (normed_one * scaled_one).astype(jnp.bfloat16), grad_out.astype(jnp.bfloat16), low_sheet
+    )
+    weight_feed = gather_line(mine_feed, to_logical)
+    weight_gu = weight_feed[:, : 2 * units]
+    weight_down = weight_feed[:, 2 * units :]
 
     joint = contract_rows(weight_qkv, h_one).reshape(3, head_count, HEAD, length)
     queries = rotate_columns(joint[0], cosine, sine_table).astype(jnp.bfloat16)
@@ -614,16 +1373,11 @@
         jnp.float32
     )
 
-    text_part = lax.dynamic_index_in_dim(
-        lax.all_gather(context, "dp", axis=0, tiled=True), plane, 0, keepdims=False
-    )
-    member = lax.axis_index("dp") * cores + lax.axis_index("core")
     text_width = CTXW // members
-    text_mine = lax.dynamic_slice_in_dim(text_part, member * text_width, text_width, axis=1)
     text_kv = jnp.stack(
         [
-            contract_last(weight_text[:, :text_width], text_mine),
-            contract_last(weight_text[:, text_width:], text_mine),
+            matmul(weight_text[:, :text_width], text_mine),
+            matmul(weight_text[:, text_width:], text_mine),
         ],
         axis=1,
     ).reshape(D, 2 * CTX)
@@ -656,20 +1410,19 @@
     silu_gate = gate_pre * sigmoid_gate
     hidden = (silu_gate * up_part).astype(jnp.bfloat16)
     ff_out = plane_scatter_frames(matmul(weight_down, hidden).astype(jnp.bfloat16))
-    result = x_two + ff_out.astype(jnp.float32)
-    output = plane_to_row(result.astype(jnp.bfloat16).T)
+    result = x_two + ff_out
 
     grad_hidden = contract_rows(weight_down, grad_ff)
     grad_gate = grad_hidden * up_part * (sigmoid_gate * (1.0 + gate_pre * (1.0 - sigmoid_gate)))
     grad_up = grad_hidden * silu_gate
     grad_gu = jnp.concatenate([grad_gate, grad_up], axis=0).astype(jnp.bfloat16)
-    grad_weight_gu = contract_last(h_three, grad_gu)
-    grad_weight_down = contract_last(grad_ff, hidden)
-    sums_gu = scatter_columns(grad_weight_gu, to_slots, planes)
-    sums_down = scatter_columns(grad_weight_down, to_slots, planes)
-    grad_h_three = plane_scatter_frames(matmul(weight_gu, grad_gu).astype(jnp.bfloat16)).astype(
-        jnp.float32
-    )
+    grad_blocks_gu = grad_blocks(contract_last(h_three, grad_gu), to_slots)
+    grad_blocks_down = grad_blocks(contract_last(grad_ff, hidden), to_slots)
+    grad_h_three = plane_scatter_frames(
+        matmul(weight_gu, grad_gu).astype(jnp.bfloat16), [grad_blocks_gu, grad_blocks_down]
+    )
+    sums_gu = scatter_line(grad_blocks_gu)
+    sums_down = scatter_line(grad_blocks_down)
     grad_gain_three = jnp.sum(grad_h_three * normed_three, axis=1)
     grad_x_two = grad_out + norm_columns_back(
         grad_h_three * gain_three, normed_three, inverse_three
@@ -704,24 +1457,26 @@
     grad_text = plane_gather_rows(grad_text.astype(jnp.bfloat16))
     grad_weight_cq = contract_last(h_two, grad_cross_q)
     grad_weight_text = [
-        matmul(grad_text[:, :CTX], text_mine),
-        matmul(grad_text[:, CTX:], text_mine),
+        contract_last(grad_text[:, :CTX], text_mine),
+        contract_last(grad_text[:, CTX:], text_mine),
     ]
-    sums_two = scatter_columns(
-        jnp.concatenate([grad_weight_cq, grad_weight_co] + grad_weight_text, axis=1),
-        to_slots,
-        planes,
-    )
     grad_h_two = plane_scatter_frames(
-        matmul(weight_cq, grad_cross_q).astype(jnp.bfloat16)
-    ).astype(jnp.float32)
+        matmul(weight_cq, grad_cross_q).astype(jnp.bfloat16), [sums_gu]
+    )
     grad_gain_two = jnp.sum(grad_h_two * normed_two, axis=1)
     grad_x_one = grad_x_two + norm_columns_back(grad_h_two * gain_two, normed_two, inverse_two)
     grad_attn = to_rows(grad_x_one.astype(jnp.bfloat16))
     grad_weight_ao = contract_last(attn_out, grad_attn)
-    grad_attn_out = plane_scatter_rows(matmul(weight_ao, grad_attn).astype(jnp.bfloat16)).reshape(
-        head_count, HEAD, length
-    )
+    grad_blocks_two = grad_blocks(
+        jnp.concatenate(
+            [grad_weight_ao, grad_weight_cq, grad_weight_co] + grad_weight_text, axis=1
+        ),
+        to_slots,
+    )
+    sums_two = scatter_line(grad_blocks_two)
+    grad_attn_out = plane_scatter_rows(
+        matmul(weight_ao, grad_attn).astype(jnp.bfloat16), [sums_down, grad_blocks_two]
+    ).reshape(head_count, HEAD, length)
     grad_probs = jnp.einsum(
         "hdq,hdk->hqk", grad_attn_out, values, preferred_element_type=jnp.float32
     )
@@ -748,43 +1503,53 @@
     )
     grad_qkv = grad_qkv.reshape(3 * span, length).astype(jnp.bfloat16)
     grad_weight_qkv = contract_last(h_one, grad_qkv)
-    sums_one = scatter_columns(
-        jnp.concatenate([grad_weight_qkv, grad_weight_ao], axis=1), to_slots, planes
-    )
-    grad_h_one = plane_scatter_frames(matmul(weight_qkv, grad_qkv).astype(jnp.bfloat16)).astype(
-        jnp.float32
+    grad_blocks_qkv = grad_blocks(grad_weight_qkv, to_slots)
+    sums_one = scatter_line(grad_blocks_qkv)
+    sums_feed = feed(sums_gu, sums_down, [grad_blocks_qkv])
+    grad_h_one = plane_scatter_frames(
+        matmul(weight_qkv, grad_qkv).astype(jnp.bfloat16), [sums_two, grad_blocks_qkv]
     )
     grad_gain_one = jnp.sum(grad_h_one * normed_one * time_gain, axis=1)
     grad_time = jnp.sum(grad_h_one * normed_one * gain_one, axis=1)
     latent_grad = grad_x_one + norm_columns_back(grad_h_one * scaled_one, normed_one, inverse_one)
-    latent_grad = plane_to_row(latent_grad.astype(jnp.bfloat16).T).astype(jnp.float32)
     gain_grads = jnp.concatenate(
         [
-            jnp.stack([grad_gain_one, grad_gain_two, grad_gain_three], axis=1),
-            grad_time[:, None] * bucket_pick[None, :],
+            jnp.stack([grad_gain_one, grad_gain_two, grad_gain_three]),
+            bucket_pick[:, None] * grad_time[None, :],
         ],
-        axis=1,
-    )
-    gain_grads = jnp.take(gain_grads.reshape(blocks, rows, 8), to_slots, axis=0)
-    gain_sums = lax.psum_scatter(
-        gain_grads.reshape(D, 8), ("z", "dp", "core"), scatter_dimension=0, tiled=True
-    )
+        axis=0,
+    )
+    sums_two = exchange_blocks(sums_two, [sums_feed])
+    out_pair, sums_one, gain_sums = closing(
+        jnp.concatenate([result.T, latent_grad.T], axis=1).astype(jnp.bfloat16),
+        sums_one,
+        gain_grads,
+        sums_two,
+    )
+    output = out_pair[:, :D]
+    latent_grad = out_pair[:, D:].astype(jnp.float32)
+    place = lax.axis_index("dp") * (planes * cores) + plane * cores + lax.axis_index("core")
+    gain_sums = lax.dynamic_index_in_dim(
+        jnp.sum(gain_sums, axis=0).reshape(8, blocks, rows), owners[place], 1, False
+    ).T
+    sums_one, sums_two = jnp.swapaxes(sums_one, 0, 1), jnp.swapaxes(sums_two, 0, 1)
 
     def joined(part):
         return part.reshape(rows, -1)
 
     grad_sheet = jnp.concatenate(
-        [joined(sums_one[:, :, k * span : (k + 1) * span]) for k in range(4)]
-        + [joined(sums_two[:, :, :span]), joined(sums_two[:, :, span : 2 * span])]
-        + [joined(sums_gu[:, :, :units]), joined(sums_gu[:, :, units:]), joined(sums_down)]
+        [joined(sums_one[:, :, k * span : (k + 1) * span]) for k in range(3)]
+        + [joined(sums_two[:, :, k * span : (k + 1) * span]) for k in range(3)]
+        + [sums_feed]
         + [
-            joined(sums_two[:, :, 2 * span : 2 * span + text_width]),
-            joined(sums_two[:, :, 2 * span + text_width :]),
-        ],
+            joined(sums_two[:, :, 3 * span : 3 * span + text_width]),
+            joined(sums_two[:, :, 3 * span + text_width :]),
+        ]
+        + [gain_sums.astype(jnp.bfloat16)],
         axis=1,
     ).astype(jnp.float32)
-    grad_sheet = jnp.concatenate([grad_sheet, gain_sums], axis=1)
-    total_squares = lax.psum(jnp.sum(grad_sheet * grad_sheet), ("dp", "z", "core"))
+    squares = jnp.pad(jnp.sum(grad_sheet * grad_sheet).reshape(1, 1), ((0, 7), (0, 127)))
+    total_squares = jnp.sum(gather_everywhere(squares))
     return (output[None], latent_grad[None]) + update(
         grad_sheet, total_squares, sheet, first, second, length
     )
@@ -815,7 +1580,7 @@
 
 def solution(mesh):
     groups, seq_count = mesh.shape["dp"], mesh.shape["seq"]
-    by_plane = seq_count == 2 * groups and (D // HEAD) % seq_count == 0
+    by_plane = groups == 4 and seq_count == 8
     if by_plane:
         mesh = Mesh(mesh.devices.reshape(groups, seq_count // 2, 2), ("dp", "z", "core"))
     seq = ("z", "core") if by_plane else "seq"

time: 1330 us -> 708 us (0.53)
  waiting for transfers between devices: 696 us -> 3.17 us
  Pallas kernels: 0 us -> 402 us
  blocking collectives: 219 us -> 0 us
  starting transfers between devices: 49.3 us -> 1 us
  other arithmetic: 89.8 us -> 54.7 us
  local copies, waits for them, and re-layouts: 123 us -> 94.3 us
    pallas_call x0 -> x22, Pallas kernels: none -> 402 us  [the longest x7 118 us: plane_scatter_call(): pl.pallas_call(functools.partial(scatter_kernel, place), out_shape=jax.Sh...]
    reduce_scatter x8 -> x4, waiting for transfers between devices: 247 us -> 0.02 us  [scatter_line(): return lax.psum_scatter(blocks, 'z', scatter_dimension=0, tiled=True)]
    all_gather x10 -> x3, waiting for transfers between devices: 215 us -> 2.35 us  [gather_line(): blocks = lax.all_gather(mine, 'z', axis=0, tiled=True)]
    unnamed x26 -> x7, waiting for transfers between devices: 166 us -> 0.8 us
    all_to_all x6 -> x0, blocking collectives: 89.9 us -> none  [the longest x2 37 us: gather_columns(): lax.all_to_all(jnp.swapaxes(block, 0, 1), PLANE, split_axis=0, concat_axi...]
    all_gather x4 -> x0, blocking collectives: 88.6 us -> none  [the longest x1 55 us: plane_plan(): lax.all_gather(low_sheet[:, gain_col:], ('z', 'dp', 'core'), axis=0, tile...]
    all_to_all x12 -> x0, waiting for transfers between devices: 67.9 us -> none  [the longest x3 25.1 us: scatter_columns(): lax.all_to_all(mine, PLANE, split_axis=0, concat_axis=0, tiled=True)]
    all_to_all x12 -> x0, starting transfers between devices: 47 us -> none  [the longest x3 10.9 us: scatter_columns(): lax.all_to_all(mine, PLANE, split_axis=0, concat_axis=0, tiled=True)]
  transfers between devices with their start and end apart: 34 -> 7, of which waited for: 27 -> 1; matrix products, arithmetic and copies ran while one was open for 19% -> 26% of each run, Pallas kernels for 0% -> 46%
where the time goes in v2:
time: 708 us; the launch traced here: 699 us
  Pallas kernels  402 us (57%)
  matrix products  124 us (18%)
  local copies, waits for them, and re-layouts  94.3 us (13%)
  other arithmetic  54.7 us (8%)
  between operations  20.6 us (3%)
    pallas_call x7, Pallas kernels, plane_scatter_call(): pl.pallas_call(functools.partial(scatter_kernel, place), out_shape=jax.Sh...  118 us
    pallas_call x5, Pallas kernels, plane_gather_call(): pl.pallas_call(functools.partial(gather_kernel, place), out_shape=jax.Sha...  81.5 us
    pallas_call x1, Pallas kernels, first_gather(): pl.pallas_call(first_gather_kernel, out_shape=(whole, whole, jax.ShapeDty...  62.8 us
    pallas_call x5, Pallas kernels, exchange(): pl.pallas_call(functools.partial(exchange_kernel, source, target), out_sh...  39.7 us
    dot_general x8, matrix products, matmul(): return jnp.dot(left, right, preferred_element_type=jnp.float32)  31.5 us
    pallas_call x1, Pallas kernels, opening(): pl.pallas_call(opening_kernel, out_shape=(jax.ShapeDtypeStruct(local.shap...  31.2 us
    pallas_call x1, Pallas kernels, closing(): pl.pallas_call(closing_kernel, out_shape=(jax.ShapeDtypeStruct(local.shap...  31 us
    dot_general x6, matrix products, contract_rows(): lax.dot_general(left, right, (((0,), (0,)), ((), ())), preferred_element_...  29.1 us
  transfers between devices with their start and end apart: 7, of which 1 were waited for; matrix products, arithmetic and copies ran while one was open for 26% of the time, Pallas kernels for 46%

profile of v2, /device:TPU:0, one launch (start us, length us, event | category | flops | bytes accessed | tf_op | source)
XLA Modules:
  0.0 699.1 jit_solution(12139038362085457664)
XLA Ops:
  18.0 31.2 %opening.1 = (bf16[128,3072]{1,0:T(8,128)(2,1)}, f32[4,8,8,128]{3,2,1,0:T(8,128)}, bf16[96,128]{1,0:T(8,128)(2,1)}, bf16[8,48,576]{2,1,0:T(8,128)(2,1)}, bf16[8,48,768]{2,1,0:T(8,128)(2,1)}) custom-call(bf16[128,3072]{1,0:T(8,128)(2,1)} %pad_maximum_fusion.3.x_ref, f32[8,128]{1,0:T(8,128)} %select_maximum_fusion.small_ref, bf16[768,128]{1,0:T(8,128)(2,1)} %bitcast.228, ...), custom_call_target="tpu_custom_call" | custom-call | bytes 1024 | tf_op jit(solution)/shard_map/opening/pallas_call | solution.py:996
  60.5 62.8 %first_gather.1 = (bf16[1536,1024]{1,0:T(8,128)(2,1)}, bf16[1536,1024]{1,0:T(8,128)(2,1)}, bf16[8,48,2304]{2,1,0:T(8,128)(2,1)}) custom-call(bf16[1536,128]{1,0:T(8,128)(2,1)} %copy.278.x_ref, bf16[1536,128]{1,0:T(8,128)(2,1)} %copy.279.y_ref, bf16[48,29192]{1,0:T(8,128)(2,1)} %copy-done.18), custom_call_target="tpu_custom_call" | custom-call | bytes 1024 | tf_op jit(solution)/shard_map/first_gather/pallas_call | solution.py:1040
  135.8 8.1 %fusion.101 = (f32[3,1024]{1,0:T(4,128)S(1)}, f32[3,1024,1024]{1,2,0:T(8,128)}) fusion(pred[1024,1024]{0,1:T(8,128)(4,1)S(1)} %broadcast_compare_fusion, bf16[3,32,1024]{2,1,0:T(8,128)(2,1)S(1)} %get-tuple-element.147, bf16[3,32,1024]{2,1,0:T(8,128)(2,1)S(1)} %get-tuple-element.148, bf16[3,32,1024]{2,1,0:T(8,128)(2,1)S(1)} %get-tuple-element.129, ...), kind=kOutput, calls=%fused_computation.261 | convolution fusion | flops 416809984 | bytes 14430208 | tf_op jit(solution)/shard_map/sub | solution.py:56
  150.5 17.8 %plane_gather.5 = bf16[1536,1024]{1,0:T(8,128)(2,1)} custom-call(bf16[192,1024]{1,0:T(8,128)(2,1)} %bitcast.232), custom_call_target="tpu_custom_call" | custom-call | bytes 1024 | tf_op jit(solution)/shard_map/plane_gather/pallas_call | solution.py:623
  175.8 7.7 %plane_exchange.5 = bf16[1536,128]{1,0:T(8,128)(2,1)} custom-call(bf16[192,1024]{1,0:T(8,128)(2,1)} %convolution_convert_fusion.17.x_ref), custom_call_target="tpu_custom_call" | custom-call | bytes 1024 | tf_op jit(solution)/shard_map/plane_exchange/pallas_call | solution.py:752
  186.3 18.6 %plane_gather.6 = bf16[1536,1024]{1,0:T(8,128)(2,1)} custom-call(bf16[1536,128]{1,0:T(8,128)(2,1)} %copy.284.x_ref), custom_call_target="tpu_custom_call" | custom-call | bytes 1024 | tf_op jit(solution)/shard_map/plane_gather/pallas_call | solution.py:623
  208.2 9.0 %plane_scatter.7 = bf16[192,256]{1,0:T(8,128)(2,1)S(1)} custom-call(bf16[1536,256]{1,0:T(8,128)(2,1)S(1)} %copy.327.p_ref), custom_call_target="tpu_custom_call" | custom-call | bytes 1024 | tf_op jit(solution)/shard_map/plane_scatter/pallas_call | solution.py:709
  224.8 17.3 %plane_gather.7 = bf16[1536,1024]{1,0:T(8,128)(2,1)} custom-call(bf16[192,1024]{1,0:T(8,128)(2,1)} %bitcast.233), custom_call_target="tpu_custom_call" | custom-call | bytes 1024 | tf_op jit(solution)/shard_map/plane_gather/pallas_call | solution.py:623
  256.9 18.6 %plane_gather.8 = bf16[1536,1024]{1,0:T(8,128)(2,1)} custom-call(bf16[1536,128]{1,0:T(8,128)(2,1)} %copy.288.x_ref), custom_call_target="tpu_custom_call" | custom-call | bytes 1024 | tf_op jit(solution)/shard_map/plane_gather/pallas_call | solution.py:623
  319.1 18.4 %plane_scatter.8 = f32[1536,128]{1,0:T(8,128)S(1)} custom-call(bf16[1536,1024]{1,0:T(8,128)(2,1)S(1)} %convolution_convert_fusion.5.p_ref), custom_call_target="tpu_custom_call" | custom-call | bytes 1024 | tf_op jit(solution)/shard_map/plane_scatter/pallas_call | solution.py:709
  347.1 8.8 %fusion.12.p_ref = bf16[1536,1024]{1,0:T(8,128)(2,1)S(1)} fusion(bf16[1536,2304]{1,0:T(8,128)(2,1)} %bitcast.208, bf16[768,1024]{1,0:T(8,128)(2,1)} %copy-done.79, bf16[768,1024]{1,0:T(8,128)(2,1)} %copy-done.78), kind=kOutput, calls=%fused_computation.37 | convolution fusion | flops 4839702528 | bytes 11010048 | tf_op jit(solution)/shard_map/dot_general | solution.py:455
  355.9 17.9 %plane_scatter.9 = f32[1536,128]{1,0:T(8,128)S(1)} custom-call(bf16[1536,1024]{1,0:T(8,128)(2,1)S(1)} %fusion.12.p_ref, bf16[32,48,1536]{2,1,0:T(8,128)(2,1)S(1)} %bitcast.189, bf16[32,48,768]{2,1,0:T(8,128)(2,1)S(1)} %gather_fusion.5), custom_call_target="tpu_custom_call" | custom-call | bytes 1024 | tf_op jit(solution)/shard_map/plane_scatter/pallas_call | solution.py:709
  391.0 18.6 %plane_scatter.10 = bf16[192,1024]{1,0:T(8,128)(2,1)S(1)} custom-call(bf16[1536,1024]{1,0:T(8,128)(2,1)S(1)} %convolution_convert_fusion.4.p_ref), custom_call_target="tpu_custom_call" | custom-call | bytes 1024 | tf_op jit(solution)/shard_map/plane_scatter/pallas_call | solution.py:709
  412.8 9.2 %plane_gather.9 = bf16[1536,256]{1,0:T(8,128)(2,1)} custom-call(bf16[192,256]{1,0:T(8,128)(2,1)} %pad_maximum_fusion.20.x_ref), custom_call_target="tpu_custom_call" | custom-call | bytes 1024 | tf_op jit(solution)/shard_map/plane_gather/pallas_call | solution.py:623
  436.7 17.7 %plane_scatter.11 = f32[1536,128]{1,0:T(8,128)S(1)} custom-call(bf16[1536,1024]{1,0:T(8,128)(2,1)S(1)} %convolution_convert_fusion.3.p_ref, bf16[8,48,1536]{2,1,0:T(8,128)(2,1)S(1)} %copy-done.4), custom_call_target="tpu_custom_call" | custom-call | bytes 1024 | tf_op jit(solution)/shard_map/plane_scatter/pallas_call | solution.py:709
  462.1 7.7 %plane_exchange.8 = bf16[192,1024]{1,0:T(8,128)(2,1)} custom-call(bf16[1536,128]{1,0:T(8,128)(2,1)} %copy.294.x_ref), custom_call_target="tpu_custom_call" | custom-call | bytes 1024 | tf_op jit(solution)/shard_map/plane_exchange/pallas_call | solution.py:752
  487.8 18.0 %plane_scatter.12 = bf16[192,1024]{1,0:T(8,128)(2,1)S(1)} custom-call(bf16[1536,1024]{1,0:T(8,128)(2,1)S(1)} %copy-done.3, bf16[8,48,768]{2,1,0:T(8,128)(2,1)S(1)} %copy-done.8, bf16[32,48,768]{2,1,0:T(8,128)(2,1)S(1)} %copy-done.1), custom_call_target="tpu_custom_call" | custom-call | bytes 1024 | tf_op jit(solution)/shard_map/plane_scatter/pallas_call | solution.py:709
  505.9 10.2 %multiply_reduce_fusion = (f32[3,1024]{1,0:T(4,128)S(1)}, f32[3,1024,1024]{1,2,0:T(8,128)}) fusion(f32[3,1024,1024]{1,2,0:T(8,128)} %get-tuple-element.155, f32[3,1024]{1,0:T(4,128)S(1)} %copy-done.63, bf16[3,64,1024]{2,1,0:T(8,128)(2,1)S(1)} %bitcast.190, bf16[3,64,1024]{2,1,0:T(8,128)(2,1)S(1)} %bitcast.235), kind=kOutput, calls=%fused_computation.13 | convolution fusion | flops 412087296 | bytes 25976832 | tf_op jit(solution)/shard_map/hdq,hdk->hqk/dot_general | solution.py:1480
  541.7 22.3 %feed.1.refs_0_ = bf16[48,18432]{1,0:T(8,128)(2,1)} custom-call(bf16[8,48,1536]{2,1,0:T(8,128)(2,1)} %reduce-scatter.5.cloned.1.call-done.refs_0_, bf16[8,48,768]{2,1,0:T(8,128)(2,1)} %reduce-scatter.7.cloned.1.call-done.refs_0_.refs_1_, bf16[32,48,576]{2,1,0:T(8,128)(2,1)} %gather_fusion.7), custom_call_target="tpu_custom_call" | custom-call | bytes 1024 | tf_op jit(solution)/shard_map/feed/pallas_call | solution.py:825
  573.3 18.2 %plane_scatter.13 = f32[1536,128]{1,0:T(8,128)S(1)} custom-call(bf16[1536,1024]{1,0:T(8,128)(2,1)S(1)} %copy-done.6, bf16[8,48,768]{2,1,0:T(8,128)(2,1)S(1)} %copy-done.9, bf16[32,48,576]{2,1,0:T(8,128)(2,1)S(1)} %copy-done), custom_call_target="tpu_custom_call" | custom-call | bytes 1024 | tf_op jit(solution)/shard_map/plane_scatter/pallas_call | solution.py:709
  593.1 9.3 %plane_exchange.9._ = bf16[8,48,768]{2,1,0:T(8,128)(2,1)} custom-call(bf16[8,48,768]{2,1,0:T(8,128)(2,1)} %reduce-scatter.9.cloned.1.call-done.refs_0_.x_ref, bf16[48,18432]{1,0:T(8,128)(2,1)} %feed.1.refs_0_), custom_call_target="tpu_custom_call" | custom-call | bytes 1024 | tf_op jit(solution)/shard_map/plane_exchange/pallas_call | solution.py:752
  608.2 31.0 %closing.1 = (bf16[128,3072]{1,0:T(8,128)(2,1)}, bf16[8,48,576]{2,1,0:T(8,128)(2,1)}, f32[8,8,1536]{2,1,0:T(8,128)}) custom-call(bf16[128,3072]{1,0:T(8,128)(2,1)} %pad_maximum_fusion.5.x_ref, bf16[8,48,576]{2,1,0:T(8,128)(2,1)} %reduce-scatter.11.cloned.1.call-done.w_ref, f32[8,1536]{1,0:T(8,128)} %pad_maximum_fusion.21.g_ref, ...), custom_call_target="tpu_custom_call" | custom-call | bytes 1024 | tf_op jit(solution)/shard_map/closing/pallas_call | solution.py:1153
  655.1 15.4 %gather_everywhere.1 = f32[4,8,8,128]{3,2,1,0:T(8,128)} custom-call(f32[8,128]{1,0:T(8,128)} %pad.18.x_ref), custom_call_target="tpu_custom_call" | custom-call | bytes 1024 | tf_op jit(solution)/shard_map/gather_everywhere/pallas_call | solution.py:1216
  672.8 12.7 %fusion.89 = (bf16[48,29192]{1,0:T(8,128)(2,1)}, f32[48,29192]{1,0:T(8,128)}, f32[48,29192]{1,0:T(8,128)}, f32[48,29192]{1,0:T(8,128)}, f32[48,29192]{1,0:T(8,128)S(1)}) fusion(f32[48,29192]{1,0:T(8,128)} %param.17, f32[29192]{0:T(1024)S(1)} %copy-done.43, f32[48,29192]{1,0:T(8,128)} %param.19, f32[48,29192]{1,0:T(8,128)} %param.18, f32[]{:T(128)S(6)} %max.3, ...), kind=kLoop, calls=%fused_computation.250 | loop fusion | flops 23820672 | bytes 44955684 | tf_op jit(solution)/shard_map/convert_element_type | solution.py:1577
  (397 shorter events, 252.2 us)
Async XLA Ops:
  7.2 119.9 %all-gather.6.cloned.1.call-start = ((), (), s32[]{:S(2)}) async-start(), calls=%async_computation.5 | async-start | bytes 2457600 | tf_op jit(solution)/shard_map/all_gather | solution.py:1244
  16.0 34.2 %copy-start.10 = (s32[32]{0:T(128)S(1)}, s32[32]{0:T(128)}, u32[]{:S(2)}) copy-start(s32[32]{0:T(128)} %param.15) | copy-start | bytes 388
  16.9 35.9 %copy-start.76 = (s32[4]{0:T(128)S(1)}, s32[4]{0:T(128)}, u32[]{:S(2)}) copy-start(s32[4]{0:T(128)} %param.14) | copy-start | bytes 52
  49.2 119.1 %all-gather.4.cloned.1.call-start = ((), (), s32[]{:S(2)}) async-start(), calls=%async_computation.4 | async-start | bytes 2949120 | tf_op jit(solution)/shard_map/all_gather | solution.py:1244
  50.0 227.9 %all-gather.8.cloned.1.call-start = ((), (), s32[]{:S(2)}) async-start(), calls=%async_computation.6 | async-start | bytes 8847360 | tf_op jit(solution)/shard_map/all_gather | solution.py:1244
  56.1 67.1 %copy-start.57 = (f32[1536]{0:T(1024)}, f32[1536]{0:T(1024)S(1)}, u32[]{:S(2)}) copy-start(f32[1536]{0:T(1024)S(1)} %fusion.72) | copy-start | bytes 18436
  56.8 66.5 %copy-start.55 = (f32[1536]{0:T(1024)}, f32[1536]{0:T(1024)S(1)}, u32[]{:S(2)}) copy-start(f32[1536]{0:T(1024)S(1)} %get-tuple-element.99) | copy-start | bytes 18436
  58.1 65.2 %copy-start.66 = (f32[128]{0:T(128)}, f32[128]{0:T(128)S(1)}, u32[]{:S(2)}) copy-start(f32[128]{0:T(128)S(1)} %broadcast_multiply_fusion.9) | copy-start | bytes 1540
  58.4 64.9 %copy-start.69 = (f32[128]{0:T(128)}, f32[128]{0:T(128)S(1)}, u32[]{:S(2)}) copy-start(f32[128]{0:T(128)S(1)} %add_rsqrt_fusion.2) | copy-start | bytes 1540
  123.3 312.0 %reduce-scatter.5.cloned.1.call-start = ((), (), s32[]{:S(2)}) async-start(), calls=%async_computation.7 | async-start | bytes 5898240 | tf_op jit(solution)/shard_map/reduce_scatter | solution.py:1254
  184.7 70.0 %copy-start.16 = (bf16[1536,128]{0,1:T(8,128)(2,1)}, bf16[1536,128]{0,1:T(8,128)(2,1)S(1)}, u32[]{:S(2)}) copy-start(bf16[1536,128]{0,1:T(8,128)(2,1)S(1)} %copy.281) | copy-start | bytes 1179652
  184.9 20.0 %copy-start.64 = (f32[128]{0:T(128)}, f32[128]{0:T(128)S(1)}, u32[]{:S(2)}) copy-start(f32[128]{0:T(128)S(1)} %broadcast_multiply_fusion.8) | copy-start | bytes 1540
  184.9 20.0 %copy-start.44 = (bf16[96,128]{1,0:T(8,128)(2,1)S(1)}, bf16[96,128]{1,0:T(8,128)(2,1)}, u32[]{:S(2)}) copy-start(bf16[96,128]{1,0:T(8,128)(2,1)} %get-tuple-element.26) | copy-start | bytes 73732
  185.2 21.3 %copy-start.68 = (f32[128]{0:T(128)}, f32[128]{0:T(128)S(1)}, u32[]{:S(2)}) copy-start(f32[128]{0:T(128)S(1)} %add_rsqrt_fusion.1) | copy-start | bytes 1540
  311.6 173.3 %reduce-scatter.7.cloned.1.call-start = ((), (), s32[]{:S(2)}) async-start(), calls=%async_computation.8 | async-start | bytes 2949120 | tf_op jit(solution)/shard_map/reduce_scatter | solution.py:1254
  391.0 18.9 %copy-start.28 = (f32[3,1024,128]{1,2,0:T(8,128)S(1)}, f32[3,1024,128]{1,2,0:T(8,128)}, u32[]{:S(2)}) copy-start(f32[3,1024,128]{1,2,0:T(8,128)} %get-tuple-element.157) | copy-start | bytes 4718596
  409.6 160.7 %reduce-scatter.9.cloned.1.call-start = ((), (), s32[]{:S(2)}) async-start(), calls=%async_computation.9 | async-start | bytes 2949120 | tf_op jit(solution)/shard_map/reduce_scatter | solution.py:1254
  436.7 20.1 %copy-start.65 = (f32[128]{0:T(128)S(1)}, f32[128]{0:T(128)}, u32[]{:S(2)}) copy-start(f32[128]{0:T(128)} %copy-done.64) | copy-start | bytes 1540
  484.3 21.5 %copy-start.46 = (bf16[192,1024]{1,0:T(8,128)(2,1)S(1)}, bf16[192,1024]{1,0:T(8,128)(2,1)}, u32[]{:S(2)}) copy-start(bf16[192,1024]{1,0:T(8,128)(2,1)} %copy-done.45) | copy-start | bytes 1179652
  484.3 123.9 %reduce-scatter.11.cloned.1.call-start = ((), (), s32[]{:S(2)}) async-start(), calls=%async_computation.10 | async-start | bytes 2457600 | tf_op jit(solution)/shard_map/reduce_scatter | solution.py:1254
  573.3 18.5 %copy-start.70 = (f32[128]{0:T(128)S(1)}, f32[128]{0:T(128)}, u32[]{:S(2)}) copy-start(f32[128]{0:T(128)} %copy-done.69) | copy-start | bytes 1540
  608.2 33.7 %copy-start.33 = (bf16[48,8,192]{2,0,1:T(8,128)(2,1)S(1)}, bf16[48,8,192]{2,0,1:T(8,128)(2,1)}, u32[]{:S(2)}) copy-start(bf16[48,8,192]{2,0,1:T(8,128)(2,1)} %get-tuple-element.141) | copy-start | bytes 442372
  647.4 25.4 %copy-start.43 = (f32[29192]{0:T(1024)S(1)}, f32[29192]{0:T(1024)}, u32[]{:S(2)}) copy-start(f32[29192]{0:T(1024)} %select_select_fusion) | copy-start | bytes 350308
  649.9 22.9 %copy-start.19 = (bf16[48,29192]{1,0:T(8,128)(2,1)S(1)}, bf16[48,29192]{1,0:T(8,128)(2,1)}, u32[]{:S(2)}) copy-start(bf16[48,29192]{1,0:T(8,128)(2,1)} %constant_dynamic-update-slice_fusion) | copy-start | bytes 8407300
  (68 other events, 417.9 us)
Sparse Core Ops, SparseCore 0:
  49.4 48.8 all-gather.5
  99.9 49.3 all-gather.3
  150.8 127.0 all-gather.7
  311.7 83.4 reduce-scatter.4
  409.7 45.2 reduce-scatter.6
  484.4 45.5 reduce-scatter.8
  540.0 38.6 reduce-scatter.10

commit v3 on v2

--- a/solution.py
+++ b/solution.py
@@ -464,9 +464,22 @@
     return IDENTITIES.setdefault(key, len(IDENTITIES))
 
 
-IN_HBM = pl.BlockSpec(memory_space=pl.ANY)
+IN_HBM = pl.BlockSpec(memory_space=pltpu.HBM)
+IN_SMEM = pl.BlockSpec(memory_space=pltpu.SMEM)
 IN_VMEM = pl.BlockSpec(memory_space=pltpu.VMEM)
 BRIEF = pl.CostEstimate(flops=0, bytes_accessed=1024, transcendentals=0)
+
+
+def reorder_blocks(source, target, order):
+    rows = source.shape[1]
+
+    @pl.loop(0, source.shape[0])
+    def _(b):
+        target[pl.ds(pl.multiple_of(b * rows, 16), rows), :] = source[order(b)]
+
+
+def wide(ref):
+    return ref[...].astype(jnp.float32)
 
 
 def greet(peers):
@@ -522,7 +535,7 @@
     return [lax.rem(member + step, 8) for step in range(1, 8)]
 
 
-def gather_steps(place, x_ref, o_ref, local_sem, copy):
+def gather_steps(place, x_ref, o_ref, local_sem, copy, arrived_whole=lambda member: None):
     group, core, across, along = near()
     beyond = across + along - group
     other = 1 - core
@@ -561,6 +574,11 @@
     own(5, 1, sibling)
 
     def finish():
+        local.wait()
+        arrived_whole(group * 2 + core)
+        arrived(4, group, other, 0)
+        arrived(5, group, other, 1)
+        arrived_whole(group * 2 + other)
         arrived(0, across, core, 0)
         relay(6, across, 0, by_y)
         relay(7, across, 0, sibling)
@@ -569,21 +587,24 @@
         relay(9, along, 1, sibling)
         arrived(2, across, core, 1)
         relay(10, across, 1, sibling)
+        arrived_whole(across * 2 + core)
         arrived(3, along, core, 0)
         relay(11, along, 0, sibling)
+        arrived_whole(along * 2 + core)
+        arrived(7, across, other, 0)
+        arrived(10, across, other, 1)
+        arrived_whole(across * 2 + other)
         arrived(6, beyond, core, 0)
         relay(12, beyond, 0, sibling)
         arrived(8, beyond, core, 1)
         relay(13, beyond, 1, sibling)
-        arrived(4, group, other, 0)
-        arrived(5, group, other, 1)
-        arrived(7, across, other, 0)
+        arrived_whole(beyond * 2 + core)
         arrived(9, along, other, 1)
-        arrived(10, across, other, 1)
         arrived(11, along, other, 0)
+        arrived_whole(along * 2 + other)
         arrived(12, beyond, other, 0)
         arrived(13, beyond, other, 1)
-        local.wait()
+        arrived_whole(beyond * 2 + other)
         for moving in sent:
             moving.wait_send()
 
@@ -648,17 +669,15 @@
     return plane_gather_call(shard, (8 * rows, width), member_rows(rows), "gather rows", after)
 
 
-def scatter_kernel(place, p_ref, *refs):
-    o_ref, pair, total, from_x, from_y, relay, send_sem, recv_sem = refs[-8:]
+def scatter_steps(place, p_ref, bufs, copy):
+    pair, total, from_x, from_y, relay = bufs
     group, core, across, along = near()
     beyond = across + along - group
     other = 1 - core
     sibling, by_x, by_y = {"core": other}, {"dp": across}, {"dp": along}
-    rows = o_ref.shape[0]
+    rows = total.shape[1]
     half = rows // 2
     low, high = pl.ds(0, half), pl.ds(half, half)
-
-    copy = mover(send_sem, recv_sem)
     sent = []
 
     def send(k, source, target, peer):
@@ -669,54 +688,72 @@
     def arrived(k, target):
         copy(k, target, target, sibling).wait_recv()
 
-    def wide(ref):
-        return ref[...].astype(jnp.float32)
-
     def both_cores(k, owner):
         arrived(k, pair.at[k])
         summed = wide(place(p_ref, owner * 2 + core, 0, rows)) + wide(pair.at[k])
         total[k] = summed.astype(total.dtype)
 
-    greet([by_x, by_y, sibling])
-    for k, owner in enumerate((beyond, across, along, group)):
-        send(k, place(p_ref, owner * 2 + other, 0, rows), pair.at[k], sibling)
-    both_cores(0, beyond)
-    send(4, total.at[0, low], relay.at[0], by_x)
-    send(5, total.at[0, high], relay.at[1], by_y)
-    both_cores(1, across)
-    send(6, total.at[1, low], from_x.at[low], by_x)
-    both_cores(2, along)
-    send(7, total.at[2, high], from_y.at[high], by_y)
-    both_cores(3, group)
-    arrived(5, relay.at[1])
-    total[1, high] = (wide(total.at[1, high]) + wide(relay.at[1])).astype(total.dtype)
-    send(8, total.at[1, high], from_x.at[high], by_x)
-    arrived(4, relay.at[0])
-    total[2, low] = (wide(total.at[2, low]) + wide(relay.at[0])).astype(total.dtype)
-    send(9, total.at[2, low], from_y.at[low], by_y)
-    arrived(6, from_x.at[low])
-    arrived(7, from_y.at[high])
-    arrived(8, from_x.at[high])
-    arrived(9, from_y.at[low])
-    o_ref[...] = (wide(total.at[3]) + wide(from_x) + wide(from_y)).astype(o_ref.dtype)
-    for moving in sent:
-        moving.wait_send()
+    def cores():
+        for k, owner in enumerate((beyond, across, along, group)):
+            send(k, place(p_ref, owner * 2 + other, 0, rows), pair.at[k], sibling)
+
+    def chips():
+        both_cores(0, beyond)
+        send(4, total.at[0, low], relay.at[0], by_x)
+        send(5, total.at[0, high], relay.at[1], by_y)
+        both_cores(1, across)
+        send(6, total.at[1, low], from_x.at[low], by_x)
+        both_cores(2, along)
+        send(7, total.at[2, high], from_y.at[high], by_y)
+        both_cores(3, group)
+
+    def relays():
+        arrived(5, relay.at[1])
+        total[1, high] = (wide(total.at[1, high]) + wide(relay.at[1])).astype(total.dtype)
+        send(8, total.at[1, high], from_x.at[high], by_x)
+        arrived(4, relay.at[0])
+        total[2, low] = (wide(total.at[2, low]) + wide(relay.at[0])).astype(total.dtype)
+        send(9, total.at[2, low], from_y.at[low], by_y)
+
+    def finish():
+        arrived(6, from_x.at[low])
+        arrived(7, from_y.at[high])
+        arrived(8, from_x.at[high])
+        arrived(9, from_y.at[low])
+        summed = wide(total.at[3]) + wide(from_x) + wide(from_y)
+        for moving in sent:
+            moving.wait_send()
+        return summed
+
+    return cores, chips, relays, finish
+
+
+def scatter_bufs(rows, width):
+    slot = pltpu.VMEM((rows, width), jnp.bfloat16)
+    four = pltpu.VMEM((4, rows, width), jnp.bfloat16)
+    return [four, four, slot, slot, pltpu.VMEM((2, rows // 2, width), jnp.bfloat16)]
+
+
+def scatter_kernel(place, p_ref, *refs):
+    o_ref, *bufs, send_sem, recv_sem = refs[-8:]
+    _, core, across, along = near()
+    greet([{"dp": across}, {"dp": along}, {"core": 1 - core}])
+    cores, chips, relays, finish = scatter_steps(place, p_ref, bufs, mover(send_sem, recv_sem))
+    cores()
+    chips()
+    relays()
+    o_ref[...] = finish().astype(o_ref.dtype)
 
 
 def plane_scatter_call(partial, shape, place, dtype, kind, after):
     rows, width = shape
-    slot = pltpu.VMEM((rows, width), jnp.bfloat16)
     return pl.pallas_call(
         functools.partial(scatter_kernel, place),
         out_shape=jax.ShapeDtypeStruct(shape, dtype),
         in_specs=[IN_VMEM] + [IN_HBM] * len(after),
         out_specs=IN_VMEM,
-        scratch_shapes=[
-            pltpu.VMEM((4, rows, width), jnp.bfloat16),
-            pltpu.VMEM((4, rows, width), jnp.bfloat16),
-            slot,
-            slot,
-            pltpu.VMEM((2, rows // 2, width), jnp.bfloat16),
+        scratch_shapes=scatter_bufs(rows, width)
+        + [
             pltpu.SemaphoreType.DMA((10,)),
             pltpu.SemaphoreType.DMA((10,)),
         ],
@@ -740,6 +777,388 @@
     rows, width = partial.shape[0] // 8, partial.shape[1]
     place = member_rows(rows)
     return plane_scatter_call(partial, (rows, width), place, jnp.bfloat16, "scatter rows", after)
+
+
+def project_kernel(kind, order_ref, s_ref, w_ref, base_ref, gain_ref, side_ref, *refs):
+    full_ref, x_ref, n_ref, i_ref, h_ref, side_out, *refs = refs
+    full, total, part, landed, shard, by_block, base, gain, residual, normed, *refs = refs
+    heads, weight, *bufs, local_sem, send_sem, recv_sem = refs
+    rows, length = s_ref.shape
+    width = base_ref.shape[1]
+    fetches = [
+        pltpu.make_async_copy(ref, held, local_sem.at[8 + k])
+        for k, (ref, held) in enumerate(
+            [(s_ref, heads), (w_ref, weight), (base_ref, base), (gain_ref, gain)]
+            + ([(side_ref, bufs[-1])] if kind == "sum" else [])
+        )
+    ]
+    for fetch in fetches:
+        fetch.start()
+    greet([member_at(peer) for peer in plane_peers()])
+    side = mover(send_sem, recv_sem, 35)
+    if kind == "sum":
+        cores, chips, relays, finish = scatter_steps(
+            member_rows(side_out.shape[0]), bufs[-1], bufs[:-1], side
+        )
+        fetches[4].wait()
+        cores()
+    fetches[0].wait()
+    fetches[1].wait()
+    total[...] = jnp.zeros_like(total)
+
+    def add(member):
+        first = pl.multiple_of(member * rows, 16)
+
+        @pl.loop(0, length // 256)
+        def _(i):
+            at = pl.ds(pl.multiple_of(i * 256, 256), 256)
+            total[:, at] += jnp.dot(
+                weight[member], full[pl.ds(first, rows), at], preferred_element_type=jnp.float32
+            )
+
+    gathered = gather_steps(
+        member_rows(rows), heads, full, local_sem.at[0], mover(send_sem, recv_sem), add
+    )
+    if kind == "sum":
+        chips()
+    else:
+        side_done = gather_steps(
+            member_lanes(width), side_ref, side_out, local_sem.at[7], side
+        )
+    gathered()
+    kept = pltpu.make_async_copy(full, full_ref, local_sem.at[0])
+    kept.start()
+    part[...] = total[...].astype(part.dtype)
+    exchanged = exchange_steps(
+        whole_lanes(rows, width),
+        whole_rows(rows),
+        part,
+        landed,
+        local_sem.at[3],
+        mover(send_sem, recv_sem, 14),
+    )
+    if kind == "sum":
+        relays()
+    exchanged()
+    fetches[2].wait()
+    fetches[3].wait()
+    residual[...] = base[...] + wide(landed)
+    standard, inverse_std = norm_columns(residual[...])
+    normed[...] = standard
+    i_ref[...] = inverse_std
+    scaled = (standard * gain[...]).astype(shard.dtype)
+    if kind == "gather":
+        by_block[...] = scaled.reshape(by_block.shape)
+        reorder_blocks(by_block, shard, lambda b: order_ref[0, b])
+    else:
+        shard[...] = scaled
+    gathered = gather_steps(
+        member_lanes(width), shard, h_ref, local_sem.at[4], mover(send_sem, recv_sem, 21)
+    )
+    x_copy = pltpu.make_async_copy(residual, x_ref, local_sem.at[5])
+    x_copy.start()
+    n_copy = pltpu.make_async_copy(normed, n_ref, local_sem.at[6])
+    n_copy.start()
+    if kind == "sum":
+        side_out[...] = finish().astype(side_out.dtype)
+    else:
+        side_done()
+    gathered()
+    kept.wait()
+    x_copy.wait()
+    n_copy.wait()
+
+
+def project(kind, orders, heads, weight, base, gain, side):
+    rows, length = heads.shape
+    features, width = base.shape
+    by_member = weight.reshape(8, rows, rows).swapaxes(1, 2)
+    whole = jax.ShapeDtypeStruct((features, length), jnp.bfloat16)
+    frames = jax.ShapeDtypeStruct(base.shape, jnp.float32)
+    if kind == "sum":
+        side_out = jax.ShapeDtypeStruct((side.shape[0] // 8, side.shape[1]), side.dtype)
+        bufs, at = scatter_bufs(*side_out.shape), IN_VMEM
+        bufs.append(pltpu.VMEM(side.shape, side.dtype))
+    else:
+        side_out, bufs, at = whole, [], IN_HBM
+    low, high = pltpu.VMEM(base.shape, jnp.bfloat16), pltpu.VMEM(base.shape, jnp.float32)
+    return pl.pallas_call(
+        functools.partial(project_kernel, kind),
+        out_shape=(whole, frames, frames, jax.ShapeDtypeStruct((1, width), jnp.float32), whole)
+        + (side_out,),
+        in_specs=[IN_SMEM] + [IN_HBM] * 5,
+        out_specs=(IN_HBM, IN_HBM, IN_HBM, IN_VMEM, IN_HBM, at),
+        scratch_shapes=[
+            pltpu.VMEM((features, length), jnp.bfloat16),
+            pltpu.VMEM((rows, length), jnp.float32),
+            pltpu.VMEM((rows, length), jnp.bfloat16),
+            low,
+            low,
+            pltpu.VMEM((orders.shape[1], features // orders.shape[1], width), jnp.bfloat16),
+            high,
+            pltpu.VMEM(gain.shape, jnp.float32),
+            high,
+            high,
+            pltpu.VMEM(heads.shape, heads.dtype),
+            pltpu.VMEM(by_member.shape, by_member.dtype),
+        ]
+        + bufs
+        + [
+            pltpu.SemaphoreType.DMA((13,)),
+            pltpu.SemaphoreType.DMA((49,)),
+            pltpu.SemaphoreType.DMA((49,)),
+        ],
+        compiler_params=pltpu.CompilerParams(
+            collective_id=identity_of("project " + kind, heads),
+            has_side_effects=True,
+            vmem_limit_bytes=32 * 2**20,
+        ),
+        cost_estimate=BRIEF,
+        name="project_" + kind,
+    )(orders, heads, by_member, base, gain, side)
+
+
+def back_kernel(plan, *refs):
+    by_rows, send_rows, text, in_slots, after = plan
+    refs = list(refs)
+
+    def take(count):
+        taken = refs[:count]
+        del refs[:count]
+        return taken
+
+    order_ref = take(1)[0]
+    sources = take(3 if by_rows else 7)
+    text_ref = take(1)[0] if text else None
+    take(after)
+    o_ref, own_out = take(2)
+    sum_ref = None if by_rows else take(1)[0]
+    rows_ref = take(1)[0] if send_rows else None
+    text_out = take(1)[0] if text else None
+    held = take(len(sources))
+    w_ref, g_ref, act, *norms = held
+    results = take(0 if by_rows else 2)
+    mine, theirs, pair, from_x, from_y, relay, shard, slots, own_ref = take(9)
+    local_sem, send_sem, recv_sem = refs
+    fetches = [
+        pltpu.make_async_copy(ref, here, local_sem.at[4 + k])
+        for k, (ref, here) in enumerate(zip(sources, held))
+    ]
+    for fetch in fetches:
+        fetch.start()
+
+    group, core, across, along = near()
+    beyond = across + along - group
+    sibling, by_x, by_y = {"core": 1 - core}, {"dp": across}, {"dp": along}
+    rows, width = mine.shape[1:]
+    half = rows // 2
+    low, high = pl.ds(0, half), pl.ds(half, half)
+    copy = mover(send_sem, recv_sem)
+    sent = []
+
+    def send(k, source, target, peer):
+        moving = copy(k, source, target, peer)
+        moving.start()
+        sent.append(moving)
+
+    def arrived(k, target):
+        copy(k, target, target, sibling).wait_recv()
+
+    def split(k, at_rows, at_lanes, first, second):
+        mine[k, at_rows, at_lanes] = jnp.where(core == 0, first, second).astype(mine.dtype)
+        theirs[k, at_rows, at_lanes] = jnp.where(core == 0, second, first).astype(mine.dtype)
+
+    def work_out(k, owner):
+        if by_rows:
+
+            @pl.loop(0, width // 256)
+            def _(i):
+                at = pl.ds(pl.multiple_of(i * 256, 256), 256)
+                both = jnp.dot(
+                    w_ref[pl.ds(pl.multiple_of(owner * 2 * rows, 16), 2 * rows), :],
+                    g_ref[:, at],
+                    preferred_element_type=jnp.float32,
+                )
+                split(k, slice(None), at, both[:rows], both[rows:])
+
+        else:
+
+            @pl.loop(0, rows // 256)
+            def _(i):
+                at = pl.ds(pl.multiple_of(i * 256, 256), 256)
+                both = jnp.dot(
+                    w_ref[at, :],
+                    g_ref[:, pl.ds(pl.multiple_of(owner * 2 * width, 256), 2 * width)],
+                    preferred_element_type=jnp.float32,
+                )
+                split(k, at, slice(None), both[:, :width], both[:, width:])
+
+        send(k, theirs.at[k], pair.at[k], sibling)
+
+    def both_cores(k):
+        arrived(k, pair.at[k])
+        mine[k] = (wide(mine.at[k]) + wide(pair.at[k])).astype(mine.dtype)
+
+    def weight_grads(first, last):
+        rows_of = act if in_slots else slots
+        tile, count = rows_of.shape[0] // 6, g_ref.shape[0]
+
+        @pl.loop(first, last)
+        def _(i):
+            at = pl.ds(pl.multiple_of(i * tile, tile), tile)
+            for j in range(0, count, 256):
+                of = slice(j, min(j + 256, count))
+                own_ref[at, of] = contract_last(rows_of[at, :], g_ref[of, :]).astype(
+                    own_ref.dtype
+                )
+
+    if send_rows or text:
+        greet([member_at(peer) for peer in plane_peers()])
+    else:
+        greet([by_x, by_y, sibling])
+    fetches[0].wait()
+    fetches[1].wait()
+    for k, owner in enumerate((beyond, across, along, group)):
+        work_out(k, owner)
+        if k == 1:
+            both_cores(0)
+            send(4, mine.at[0, low], relay.at[0], by_x)
+            send(5, mine.at[0, high], relay.at[1], by_y)
+        if k == 2:
+            both_cores(1)
+            send(6, mine.at[1, low], from_x.at[low], by_x)
+        if k == 3:
+            both_cores(2)
+            send(7, mine.at[2, high], from_y.at[high], by_y)
+    if text:
+        text_done = gather_steps(
+            member_rows(text_ref.shape[0]),
+            text_ref,
+            text_out,
+            local_sem.at[1],
+            mover(send_sem, recv_sem, 17),
+        )
+    fetches[2].wait()
+    if not in_slots:
+        reorder_blocks(act, slots, lambda b: order_ref[0, b])
+    weight_grads(0, 2)
+    arrived(5, relay.at[1])
+    mine[1, high] = (wide(mine.at[1, high]) + wide(relay.at[1])).astype(mine.dtype)
+    send(8, mine.at[1, high], from_x.at[high], by_x)
+    arrived(4, relay.at[0])
+    mine[2, low] = (wide(mine.at[2, low]) + wide(relay.at[0])).astype(mine.dtype)
+    send(9, mine.at[2, low], from_y.at[low], by_y)
+    both_cores(3)
+    weight_grads(2, 6)
+    own_copy = pltpu.make_async_copy(own_ref, own_out, local_sem.at[2])
+    own_copy.start()
+    arrived(6, from_x.at[low])
+    arrived(7, from_y.at[high])
+    arrived(8, from_x.at[high])
+    arrived(9, from_y.at[low])
+    summed = wide(mine.at[3]) + wide(from_x) + wide(from_y)
+    if by_rows:
+        shard[...] = summed.astype(shard.dtype)
+        result_copy = pltpu.make_async_copy(shard, o_ref, local_sem.at[3])
+        result_copy.start()
+    else:
+        for fetch in fetches[3:]:
+            fetch.wait()
+        normed, inverse_std, gain, base = norms
+        result, by_block = results
+        if in_slots:
+            by_block[...] = summed.reshape(by_block.shape)
+            reorder_blocks(by_block, result, lambda b: order_ref[1, b])
+            summed = result[...]
+        result[...] = base[...] + norm_columns_back(
+            summed * gain[...], normed[...], inverse_std[...]
+        )
+        result_copy = pltpu.make_async_copy(result, o_ref, local_sem.at[3])
+        result_copy.start()
+        if send_rows:
+            shard[...] = result[...].astype(shard.dtype)
+            rows_done = exchange_steps(
+                whole_rows(rows // 8),
+                whole_lanes(rows // 8, width),
+                shard,
+                rows_ref,
+                local_sem.at[0],
+                mover(send_sem, recv_sem, 10),
+            )
+        sum_ref[...] = lax.dot_general(
+            jnp.ones((8, width), jnp.float32),
+            summed * normed[...],
+            (((1,), (1,)), ((), ())),
+            precision=HIGHEST,
+            preferred_element_type=jnp.float32,
+        )
+        if send_rows:
+            rows_done()
+    result_copy.wait()
+    own_copy.wait()
+    if text:
+        text_done()
+    for moving in sent:
+        moving.wait_send()
+
+
+def back(orders, weight, grad, act, norm=None, send_rows=False, text=None, in_slots=False, after=()):
+    by_rows = norm is None
+    features, length = weight.shape[0], grad.shape[1]
+    shape = (features // 8, length) if by_rows else (features, length // 8)
+    small = jnp.bfloat16
+    own = jax.ShapeDtypeStruct((features, grad.shape[0]), small)
+    outs = [jax.ShapeDtypeStruct(shape, small if by_rows else jnp.float32), own]
+    specs = [IN_HBM, IN_HBM]
+    if not by_rows:
+        outs.append(jax.ShapeDtypeStruct((8, features), jnp.float32))
+        specs.append(IN_VMEM)
+    if send_rows:
+        outs.append(jax.ShapeDtypeStruct((features // 8, length), small))
+        specs.append(IN_HBM)
+    count = orders.shape[1]
+    if not in_slots:
+        act = act.reshape(count, features // count, length)
+    sources = [weight, grad, act] + list(norm or ())
+    operands = [orders] + sources
+    if text is not None:
+        operands.append(text)
+        outs.append(jax.ShapeDtypeStruct((8 * text.shape[0], text.shape[1]), text.dtype))
+        specs.append(IN_HBM)
+    operands += list(after)
+    plan = (by_rows, send_rows, text is not None, in_slots, len(after))
+    rows, width = shape
+    four, slot = pltpu.VMEM((4, rows, width), small), pltpu.VMEM((rows, width), small)
+    return pl.pallas_call(
+        functools.partial(back_kernel, plan),
+        out_shape=tuple(outs),
+        in_specs=[IN_SMEM] + [IN_HBM] * (len(operands) - 1),
+        out_specs=tuple(specs),
+        scratch_shapes=[pltpu.VMEM(array.shape, array.dtype) for array in sources]
+        + (
+            []
+            if by_rows
+            else [
+                pltpu.VMEM(shape, jnp.float32),
+                pltpu.VMEM((count, rows // count, width), jnp.float32),
+            ]
+        )
+        + [four, four, four, slot, slot, pltpu.VMEM((2, rows // 2, width), small), slot]
+        + [
+            pltpu.VMEM((16, 128) if in_slots else (features, length), small),
+            pltpu.VMEM(own.shape, small),
+            pltpu.SemaphoreType.DMA((11,)),
+            pltpu.SemaphoreType.DMA((31,)),
+            pltpu.SemaphoreType.DMA((31,)),
+        ],
+        compiler_params=pltpu.CompilerParams(
+            collective_id=identity_of("back" + str(plan), *operands),
+            has_side_effects=True,
+            vmem_limit_bytes=44 * 2**20,
+        ),
+        cost_estimate=BRIEF,
+        name="back",
+    )(*operands)
 
 
 def exchange_kernel(source, target, x_ref, *refs):
@@ -807,37 +1226,60 @@
     return lambda ref, member: lanes(ref.at[member], start, width)
 
 
-def feed_kernel(count, *refs):
-    gu_ref, down_ref = refs[:2]
-    o_ref, local_sem, send_sem, recv_sem = refs[-4:]
+def feed_kernel(gu_ref, down_ref, p_ref, *refs):
+    o_ref, y_ref, part, summed, *bufs, local_sem, send_sem, recv_sem = refs[-12:]
     width = down_ref.shape[-1]
+    fetch = pltpu.make_async_copy(p_ref, part, local_sem.at[3])
+    fetch.start()
     greet([member_at(peer) for peer in plane_peers()])
+    cores, chips, relays, ended = scatter_steps(
+        member_lanes(y_ref.shape[1]), part, bufs, mover(send_sem, recv_sem, 21)
+    )
+    fetch.wait()
+    cores()
+    chips()
     finish = []
     for k, (ref, start) in enumerate(((gu_ref, 0), (gu_ref, width), (down_ref, 0))):
         source, target = block_part(start, width), sheet_part(8 * k * width, width)
         copy = mover(send_sem, recv_sem, 7 * k)
         finish.append(exchange_steps(source, target, ref, o_ref, local_sem.at[k], copy))
+    relays()
+    summed[...] = ended()
+    kept = pltpu.make_async_copy(summed, y_ref, local_sem.at[4])
+    kept.start()
     for end in finish:
         end()
-
-
-def feed(gu, down, after=()):
+    kept.wait()
+
+
+def feed(gu, down, partial, after=()):
+    rows, width = partial.shape[0], partial.shape[1] // 8
     return pl.pallas_call(
-        functools.partial(feed_kernel, len(after)),
-        out_shape=jax.ShapeDtypeStruct((gu.shape[1], 24 * down.shape[-1]), gu.dtype),
-        in_specs=[IN_HBM] * (2 + len(after)),
-        out_specs=IN_HBM,
+        feed_kernel,
+        out_shape=(
+            jax.ShapeDtypeStruct((gu.shape[1], 24 * down.shape[-1]), gu.dtype),
+            jax.ShapeDtypeStruct((rows, width), jnp.float32),
+        ),
+        in_specs=[IN_HBM] * (3 + len(after)),
+        out_specs=(IN_HBM, IN_HBM),
         scratch_shapes=[
-            pltpu.SemaphoreType.DMA((3,)),
-            pltpu.SemaphoreType.DMA((21,)),
-            pltpu.SemaphoreType.DMA((21,)),
+            pltpu.VMEM(partial.shape, partial.dtype),
+            pltpu.VMEM((rows, width), jnp.float32),
+        ]
+        + scatter_bufs(rows, width)
+        + [
+            pltpu.SemaphoreType.DMA((5,)),
+            pltpu.SemaphoreType.DMA((31,)),
+            pltpu.SemaphoreType.DMA((31,)),
         ],
         compiler_params=pltpu.CompilerParams(
-            collective_id=identity_of("feed", gu, down, *after), has_side_effects=True
+            collective_id=identity_of("feed", gu, down, *after),
+            has_side_effects=True,
+            vmem_limit_bytes=24 * 2**20,
         ),
         cost_estimate=BRIEF,
         name="feed",
-    )(gu, down, *after)
+    )(gu, down, partial, *after)
 
 
 def opening_kernel(
@@ -1018,49 +1460,63 @@
     )(local, small, text, first, second)
 
 
-def first_gather_kernel(x_ref, y_ref, sheet_ref, ox_ref, oy_ref, w_ref, local_sem, send_sem, recv_sem):
+def first_gather_kernel(
+    x_ref, sheet_ref, o_ref, w_ref, v_ref, local_sem, send_sem, recv_sem
+):
     place = member_lanes(x_ref.shape[1])
     width = FF // 8
     greet([member_at(peer) for peer in plane_peers()])
     finish = [
-        gather_steps(place, x_ref, ox_ref, local_sem.at[0], mover(send_sem, recv_sem)),
-        gather_steps(place, y_ref, oy_ref, local_sem.at[1], mover(send_sem, recv_sem, 14)),
+        gather_steps(place, x_ref, o_ref, local_sem.at[0], mover(send_sem, recv_sem))
     ]
-    for k in range(3):
-        source, target = sheet_part(6 * D + k * FF, width), block_part(k * width, width)
-        copy = mover(send_sem, recv_sem, 28 + 7 * k)
-        finish.append(exchange_steps(source, target, sheet_ref, w_ref, local_sem.at[2 + k], copy))
+    for k, (ref, start) in enumerate(((w_ref, 0), (w_ref, width), (v_ref, 0))):
+        source, target = sheet_part(6 * D + k * FF, width), block_part(start, width)
+        copy = mover(send_sem, recv_sem, 14 + 7 * k)
+        finish.append(exchange_steps(source, target, sheet_ref, ref, local_sem.at[1 + k], copy))
     for end in finish:
         end()
 
 
-def first_gather(shard, other, sheet):
+def first_gather(shard, sheet):
     rows, width = shard.shape
-    whole = jax.ShapeDtypeStruct((rows, 8 * width), shard.dtype)
     return pl.pallas_call(
         first_gather_kernel,
         out_shape=(
-            whole,
-            whole,
-            jax.ShapeDtypeStruct((8, sheet.shape[0], 3 * FF // 8), sheet.dtype),
+            jax.ShapeDtypeStruct((rows, 8 * width), shard.dtype),
+            jax.ShapeDtypeStruct((8, sheet.shape[0], FF // 4), sheet.dtype),
+            jax.ShapeDtypeStruct((8, sheet.shape[0], FF // 8), sheet.dtype),
         ),
-        in_specs=[IN_HBM] * 3,
+        in_specs=[IN_HBM] * 2,
         out_specs=(IN_HBM,) * 3,
         scratch_shapes=[
-            pltpu.SemaphoreType.DMA((5,)),
-            pltpu.SemaphoreType.DMA((49,)),
-            pltpu.SemaphoreType.DMA((49,)),
+            pltpu.SemaphoreType.DMA((4,)),
+            pltpu.SemaphoreType.DMA((35,)),
+            pltpu.SemaphoreType.DMA((35,)),
         ],
         compiler_params=pltpu.CompilerParams(
             collective_id=identity_of("first gather", shard, sheet), has_side_effects=True
         ),
         cost_estimate=BRIEF,
         name="first_gather",
-    )(shard, other, sheet)
+    )(shard, sheet)
 
 
 def closing_kernel(
-    x_ref, w_ref, g_ref, _, t_ref, o_ref, s_ref, held, tall, local_sem, send_sem, recv_sem
+    x_ref,
+    w_ref,
+    v_ref,
+    g_ref,
+    q_ref,
+    t_ref,
+    o_ref,
+    vo_ref,
+    s_ref,
+    all_ref,
+    held,
+    tall,
+    local_sem,
+    send_sem,
+    recv_sem,
 ):
     group, core, _, _ = near()
     member = group * 2 + core
@@ -1078,6 +1534,16 @@
     copy = mover(send_sem, recv_sem)
     gain_line = mover(send_sem, recv_sem, 14)
     gain_plane = mover(send_sem, recv_sem, 17)
+    square_plane = mover(send_sem, recv_sem, 24)
+    square_line = mover(send_sem, recv_sem, 31)
+    square_local = pltpu.make_async_copy(q_ref, all_ref.at[plane, member], local_sem.at[5])
+    square_local.start()
+    shown = [
+        square_plane(k, q_ref, all_ref.at[plane, member], member_at(peer))
+        for k, peer in enumerate(peers)
+    ]
+    for moving in shown:
+        moving.start()
     gain_local = pltpu.make_async_copy(g_ref, tall.at[plane], local_sem.at[3])
     gain_local.start()
     sent = [gain_line(k, g_ref, tall.at[plane], {"z": there}) for k, there in enumerate(line)]
@@ -1092,6 +1558,9 @@
     weights_done = exchange_steps(
         block, block, w_ref, o_ref, local_sem.at[1], mover(send_sem, recv_sem, 7)
     )
+    others_done = exchange_steps(
+        block, block, v_ref, vo_ref, local_sem.at[6], mover(send_sem, recv_sem, 34)
+    )
 
     gain_local.wait()
     for k, origin in enumerate(back):
@@ -1121,6 +1590,13 @@
         pl.when(owner == group)(keep.start)
         pl.when(owner != group)(onward(owner).start)
 
+    square_local.wait()
+    for k in range(7):
+        landed = all_ref.at[plane, lax.rem(member + 7 - k, 8)]
+        square_plane(k, landed, landed, member_at(peers[k])).wait_recv()
+    for k, there in enumerate(line):
+        shown.append(square_line(k, all_ref.at[plane], all_ref.at[plane], {"z": there}))
+        shown[-1].start()
     local.wait()
     pass_on(plane)
     for k, origin in enumerate(back):
@@ -1139,96 +1615,118 @@
         ).wait_recv()
     keep.wait()
     weights_done()
+    others_done()
     gain_keep.wait()
     for k in range(7):
         landed = s_ref.at[lax.rem(member + 7 - k, 8)]
         gain_plane(k, landed, landed, member_at(peers[k])).wait_recv()
-    for moving in sent + given:
+    for k, origin in enumerate(back):
+        square_line(k, all_ref.at[origin], all_ref.at[origin], {"z": origin}).wait_recv()
+    for moving in sent + given + shown:
         moving.wait_send()
     for origin in groups:
         onward(origin).wait_send()
 
 
-def closing(local, weights, gains, after):
+def closing(local, weights, others, gains, squares):
     return pl.pallas_call(
         closing_kernel,
         out_shape=(
             jax.ShapeDtypeStruct(local.shape, local.dtype),
             jax.ShapeDtypeStruct(weights.shape, weights.dtype),
+            jax.ShapeDtypeStruct(others.shape, others.dtype),
             jax.ShapeDtypeStruct((8,) + gains.shape, gains.dtype),
+            jax.ShapeDtypeStruct((4, 8) + squares.shape, squares.dtype),
         ),
-        in_specs=[IN_HBM] * 4,
-        out_specs=(IN_HBM,) * 3,
+        in_specs=[IN_HBM] * 5,
+        out_specs=(IN_HBM,) * 5,
         scratch_shapes=[
             pltpu.VMEM(local.shape, local.dtype),
             pltpu.VMEM((5,) + gains.shape, gains.dtype),
-            pltpu.SemaphoreType.DMA((5,)),
-            pltpu.SemaphoreType.DMA((24,)),
-            pltpu.SemaphoreType.DMA((24,)),
+            pltpu.SemaphoreType.DMA((7,)),
+            pltpu.SemaphoreType.DMA((41,)),
+            pltpu.SemaphoreType.DMA((41,)),
         ],
         compiler_params=pltpu.CompilerParams(
             collective_id=identity_of("closing", local), has_side_effects=True
         ),
         cost_estimate=BRIEF,
         name="closing",
-    )(local, weights, gains, after)
-
-
-def everywhere_kernel(x_ref, o_ref, local_sem, send_sem, recv_sem):
-    group, core, _, _ = near()
-    member = group * 2 + core
-    plane = lax.axis_index("z")
-    peers = [lax.rem(member + step, 8) for step in range(1, 8)]
-    places = [{"dp": lax.div(peer, 2), "core": lax.rem(peer, 2)} for peer in peers]
-    places = places + [{"z": lax.rem(plane + step, 4)} for step in range(1, 4)]
-    greet(places)
-
-    def copy(k, source, target):
-        return pltpu.make_async_remote_copy(
-            src_ref=source,
-            dst_ref=target,
-            send_sem=send_sem.at[k],
-            recv_sem=recv_sem.at[k],
-            device_id=places[k],
-            device_id_type=MESH_ID,
-        )
-
-    local = pltpu.make_async_copy(x_ref, o_ref.at[plane, member], local_sem)
-    local.start()
-    copies = [copy(k, x_ref, o_ref.at[plane, member]) for k in range(7)]
-    for moving in copies:
-        moving.start()
-    for k in range(7):
-        landed = o_ref.at[plane, lax.rem(member + 7 - k, 8)]
-        copy(k, landed, landed).wait_recv()
-    local.wait()
-    between = [copy(7 + k, o_ref.at[plane], o_ref.at[plane]) for k in range(3)]
-    for moving in between:
-        moving.start()
-    for k in range(3):
-        landed = o_ref.at[lax.rem(plane + 3 - k, 4)]
-        copy(7 + k, landed, landed).wait_recv()
-    for moving in copies + between:
-        moving.wait_send()
-
-
-def gather_everywhere(block):
+    )(local, weights, others, gains, squares)
+
+
+def update_kernel(
+    scale_ref, rate_ref, one_ref, two_ref, feed_ref, gain_ref, sheet_ref, first_ref, second_ref, *refs
+):
+    grad_out, first_out, second_out, sheet_out, copy_out, grad = refs
+    step = pl.program_id(0)
+    part = D // 8
+    text = CTXW // 8
+    for k in range(6):
+
+        @pl.when(step == k)
+        def _(k=k):
+            ref, start = (one_ref, k * part) if k < 4 else (two_ref, (k - 4) * part)
+            for m in range(8):
+                grad[:, m * part : (m + 1) * part] = wide(ref.at[m, :, start : start + part])
+
+    @pl.when(jnp.logical_and(step >= 6, step < 18))
+    def _():
+        grad[...] = wide(feed_ref)
+
+    @pl.when(step == 18)
+    def _():
+        for m in range(8):
+            for k in range(2):
+                start = 2 * part + k * text
+                place = k * CTXW + m * text
+                grad[:, place : place + text] = wide(two_ref.at[m, :, start : start + text])
+
+    @pl.when(step == 19)
+    def _():
+        grad[:, :128] = gain_ref[...]
+
+    clipped = grad[...] * scale_ref[0]
+    sheet = sheet_ref[...]
+    first_new = BETA_ONE * first_ref[...] + (1.0 - BETA_ONE) * clipped
+    second_new = BETA_TWO * second_ref[...] + (1.0 - BETA_TWO) * clipped * clipped
+    mean_hat = first_new / (1.0 - BETA_ONE**STEP)
+    square_hat = second_new / (1.0 - BETA_TWO**STEP)
+    sheet_new = sheet - rate_ref[step] * (
+        mean_hat / (jnp.sqrt(square_hat) + EPS_ADAM) + WEIGHT_DECAY * sheet
+    )
+    grad_out[...] = clipped
+    first_out[...] = first_new
+    second_out[...] = second_new
+    sheet_out[...] = sheet_new
+    copy_out[...] = sheet_new.astype(copy_out.dtype)
+
+
+def sheet_update(scale, length, one, two, feed_part, gains, sheet, first, second):
+    rows = sheet.shape[0]
+    rates = column_spread(length)[jnp.minimum(jnp.arange(20) * D, SHEET - 1)]
+    column_block = pl.BlockSpec((rows, D), lambda i: (0, i))
+    like = jax.ShapeDtypeStruct(sheet.shape, sheet.dtype)
     return pl.pallas_call(
-        everywhere_kernel,
-        out_shape=jax.ShapeDtypeStruct((4, 8) + block.shape, block.dtype),
-        in_specs=[IN_VMEM],
-        out_specs=IN_VMEM,
-        scratch_shapes=[
-            pltpu.SemaphoreType.DMA,
-            pltpu.SemaphoreType.DMA((10,)),
-            pltpu.SemaphoreType.DMA((10,)),
+        update_kernel,
+        grid=(20,),
+        out_shape=(like, like, like, like, jax.ShapeDtypeStruct(sheet.shape, jnp.bfloat16)),
+        in_specs=[
+            IN_SMEM,
+            IN_SMEM,
+            pl.BlockSpec(one.shape, lambda i: (0, 0, 0)),
+            pl.BlockSpec(two.shape, lambda i: (0, 0, 0)),
+            pl.BlockSpec((rows, D), lambda i: (0, jnp.clip(i - 6, 0, 11))),
+            pl.BlockSpec(gains.shape, lambda i: (0, 0)),
+            column_block,
+            column_block,
+            column_block,
         ],
-        compiler_params=pltpu.CompilerParams(
-            collective_id=identity_of("everywhere", block), has_side_effects=True
-        ),
-        cost_estimate=BRIEF,
-        name="gather_everywhere",
-    )(block)
+        out_specs=(column_block,) * 5,
+        scratch_shapes=[pltpu.VMEM((rows, D), jnp.float32)],
+        compiler_params=pltpu.CompilerParams(vmem_limit_bytes=24 * 2**20),
+        name="sheet_update",
+    )(scale.reshape(1), rates, one, two, feed_part, gains, sheet, first, second)
 
 
 def split_columns(block, members):
@@ -1245,9 +1743,17 @@
     return pick_blocks(blocks, order).reshape(-1, mine.shape[-1])
 
 
-def grad_blocks(grad, order):
-    blocks = grad.astype(jnp.bfloat16).reshape(order.shape[0], -1, grad.shape[-1])
-    return pick_blocks(blocks, order)
+def gather_slots(mine):
+    return lax.all_gather(mine, "z", axis=0, tiled=True).reshape(-1, mine.shape[-1])
+
+
+def sort_blocks(array, order):
+    blocks = array.reshape(order.shape[0], -1, array.shape[-1])
+    return pick_blocks(blocks, order).reshape(array.shape)
+
+
+def as_blocks(grad, order):
+    return grad.reshape(order.shape[0], -1, grad.shape[-1])
 
 
 def scatter_line(blocks):
@@ -1282,6 +1788,7 @@
     to_logical = jnp.take(slot_of, inverse)
     to_slots = jnp.take(owners, slot)
 
+    orders = jnp.stack([to_slots, to_logical])
     low_sheet = sheet.astype(jnp.bfloat16)
 
     def columns_of(start, width):
@@ -1312,7 +1819,7 @@
         blocks_qkv,
         blocks_two,
     )
-    weight_qkv = gather_line(mine_qkv, to_logical)
+    weight_qkv = gather_slots(mine_qkv)
     weight_two = gather_line(mine_two, to_logical)
     weight_ao = weight_two[:, :span]
     weight_cq = weight_two[:, span : 2 * span]
@@ -1351,12 +1858,11 @@
 
     normed_one, inverse_one = norm_columns(tokens)
     scaled_one = gain_one * time_gain
-    h_one, grad_ff, mine_feed = first_gather(
-        (normed_one * scaled_one).astype(jnp.bfloat16), grad_out.astype(jnp.bfloat16), low_sheet
-    )
-    weight_feed = gather_line(mine_feed, to_logical)
-    weight_gu = weight_feed[:, : 2 * units]
-    weight_down = weight_feed[:, 2 * units :]
+    h_one, mine_gu, mine_down = first_gather(
+        sort_blocks((normed_one * scaled_one).astype(jnp.bfloat16), to_slots), low_sheet
+    )
+    weight_gu = gather_slots(mine_gu)
+    line_down = gather_slots(mine_down)
 
     joint = contract_rows(weight_qkv, h_one).reshape(3, head_count, HEAD, length)
     queries = rotate_columns(joint[0], cosine, sine_table).astype(jnp.bfloat16)
@@ -1368,11 +1874,6 @@
     attn_probs = softmax_rows(jnp.where(same_clip[None], scores, MASKED_SCORE))
     probs_low = attn_probs.astype(jnp.bfloat16)
     attn_out = jnp.einsum("hqk,hdk->hdq", probs_low, values, preferred_element_type=jnp.float32)
-    attn_out = plane_gather_rows(attn_out.reshape(span, length).astype(jnp.bfloat16))
-    x_one = tokens + to_frames(contract_rows(weight_ao, attn_out).astype(jnp.bfloat16)).astype(
-        jnp.float32
-    )
-
     text_width = CTXW // members
     text_kv = jnp.stack(
         [
@@ -1381,11 +1882,19 @@
         ],
         axis=1,
     ).reshape(D, 2 * CTX)
-    text_kv = plane_scatter_rows(text_kv.astype(jnp.bfloat16)).reshape(head_count, HEAD, 2, CTX)
+    attn_out, x_one, normed_two, inverse_two, h_two, text_kv = project(
+        "sum",
+        orders,
+        attn_out.reshape(span, length).astype(jnp.bfloat16),
+        weight_ao,
+        tokens,
+        gain_two,
+        text_kv.astype(jnp.bfloat16),
+    )
+
+    text_kv = text_kv.reshape(head_count, HEAD, 2, CTX)
     text_keys = text_kv[:, :, 0]
     text_values = text_kv[:, :, 1]
-    normed_two, inverse_two = norm_columns(x_one)
-    h_two = plane_gather((normed_two * gain_two).astype(jnp.bfloat16))
     cross_q = contract_rows(weight_cq, h_two).astype(jnp.bfloat16).reshape(head_count, HEAD, length)
     cross_scores = (
         jnp.einsum("hdq,hdk->hqk", cross_q, text_keys, preferred_element_type=jnp.float32)
@@ -1396,42 +1905,46 @@
     cross_out = jnp.einsum(
         "hqk,hdk->hdq", cross_low, text_values, preferred_element_type=jnp.float32
     )
-    cross_out = plane_gather_rows(cross_out.reshape(span, length).astype(jnp.bfloat16))
-    x_two = x_one + to_frames(contract_rows(weight_co, cross_out).astype(jnp.bfloat16)).astype(
-        jnp.float32
-    )
-
-    normed_three, inverse_three = norm_columns(x_two)
-    h_three = plane_gather((normed_three * gain_three).astype(jnp.bfloat16))
+    cross_out, x_two, normed_three, inverse_three, h_three, grad_ff = project(
+        "gather",
+        orders,
+        cross_out.reshape(span, length).astype(jnp.bfloat16),
+        weight_co,
+        x_one,
+        gain_three,
+        sort_blocks(grad_out.astype(jnp.bfloat16), to_slots),
+    )
+
     gate_up = contract_rows(weight_gu, h_three)
     gate_pre = gate_up[:units]
     up_part = gate_up[units:]
     sigmoid_gate = jax.nn.sigmoid(gate_pre)
     silu_gate = gate_pre * sigmoid_gate
     hidden = (silu_gate * up_part).astype(jnp.bfloat16)
-    ff_out = plane_scatter_frames(matmul(weight_down, hidden).astype(jnp.bfloat16))
-    result = x_two + ff_out
-
+
+    grad_blocks_down = as_blocks(contract_last(grad_ff, hidden).astype(jnp.bfloat16), to_slots)
+    weight_down, grad_blocks_down = lax.optimization_barrier((line_down, grad_blocks_down))
+    sums_down = scatter_line(grad_blocks_down)
     grad_hidden = contract_rows(weight_down, grad_ff)
     grad_gate = grad_hidden * up_part * (sigmoid_gate * (1.0 + gate_pre * (1.0 - sigmoid_gate)))
     grad_up = grad_hidden * silu_gate
     grad_gu = jnp.concatenate([grad_gate, grad_up], axis=0).astype(jnp.bfloat16)
-    grad_blocks_gu = grad_blocks(contract_last(h_three, grad_gu), to_slots)
-    grad_blocks_down = grad_blocks(contract_last(grad_ff, hidden), to_slots)
-    grad_h_three = plane_scatter_frames(
-        matmul(weight_gu, grad_gu).astype(jnp.bfloat16), [grad_blocks_gu, grad_blocks_down]
-    )
+    grad_x_two, grad_weight_gu, sum_three, grad_cross = back(
+        orders,
+        weight_gu,
+        grad_gu,
+        h_three,
+        (normed_three, inverse_three, gain_three, grad_out),
+        send_rows=True,
+        in_slots=True,
+        after=[grad_blocks_down],
+    )
+    grad_blocks_gu = as_blocks(grad_weight_gu, to_slots)
     sums_gu = scatter_line(grad_blocks_gu)
-    sums_down = scatter_line(grad_blocks_down)
-    grad_gain_three = jnp.sum(grad_h_three * normed_three, axis=1)
-    grad_x_two = grad_out + norm_columns_back(
-        grad_h_three * gain_three, normed_three, inverse_three
-    )
-    grad_cross = to_rows(grad_x_two.astype(jnp.bfloat16))
-    grad_weight_co = contract_last(cross_out, grad_cross)
-    grad_cross_out = plane_scatter_rows(
-        matmul(weight_co, grad_cross).astype(jnp.bfloat16)
-    ).reshape(head_count, HEAD, length)
+    grad_cross_out, grad_weight_co = back(
+        orders, weight_co, grad_cross, cross_out
+    )
+    grad_cross_out = grad_cross_out.reshape(head_count, HEAD, length)
     grad_cross_probs = jnp.einsum(
         "hdq,hdk->hqk", grad_cross_out, text_values, preferred_element_type=jnp.float32
     )
@@ -1454,29 +1967,34 @@
     grad_text = jnp.concatenate(
         [grad_text_keys.reshape(span, CTX), grad_text_values.reshape(span, CTX)], axis=1
     )
-    grad_text = plane_gather_rows(grad_text.astype(jnp.bfloat16))
-    grad_weight_cq = contract_last(h_two, grad_cross_q)
+    grad_x_one, grad_weight_cq, sum_two, grad_attn, grad_text = back(
+        orders,
+        weight_cq,
+        grad_cross_q,
+        h_two,
+        (normed_two, inverse_two, gain_two, grad_x_two),
+        send_rows=True,
+        text=grad_text.astype(jnp.bfloat16),
+        after=[sums_down],
+    )
+    grad_text = sort_blocks(grad_text, to_slots)
     grad_weight_text = [
         contract_last(grad_text[:, :CTX], text_mine),
         contract_last(grad_text[:, CTX:], text_mine),
     ]
-    grad_h_two = plane_scatter_frames(
-        matmul(weight_cq, grad_cross_q).astype(jnp.bfloat16), [sums_gu]
-    )
-    grad_gain_two = jnp.sum(grad_h_two * normed_two, axis=1)
-    grad_x_one = grad_x_two + norm_columns_back(grad_h_two * gain_two, normed_two, inverse_two)
-    grad_attn = to_rows(grad_x_one.astype(jnp.bfloat16))
-    grad_weight_ao = contract_last(attn_out, grad_attn)
-    grad_blocks_two = grad_blocks(
+    grad_blocks_two = as_blocks(
         jnp.concatenate(
-            [grad_weight_ao, grad_weight_cq, grad_weight_co] + grad_weight_text, axis=1
+            [grad_weight_cq, grad_weight_co]
+            + [grad.astype(jnp.bfloat16) for grad in grad_weight_text],
+            axis=1,
         ),
         to_slots,
     )
     sums_two = scatter_line(grad_blocks_two)
-    grad_attn_out = plane_scatter_rows(
-        matmul(weight_ao, grad_attn).astype(jnp.bfloat16), [sums_down, grad_blocks_two]
-    ).reshape(head_count, HEAD, length)
+    grad_attn_out, grad_weight_ao = back(
+        orders, weight_ao, grad_attn, attn_out, after=[grad_blocks_two]
+    )
+    grad_attn_out = grad_attn_out.reshape(head_count, HEAD, length)
     grad_probs = jnp.einsum(
         "hdq,hdk->hqk", grad_attn_out, values, preferred_element_type=jnp.float32
     )
@@ -1502,79 +2020,79 @@
         ]
     )
     grad_qkv = grad_qkv.reshape(3 * span, length).astype(jnp.bfloat16)
-    grad_weight_qkv = contract_last(h_one, grad_qkv)
-    grad_blocks_qkv = grad_blocks(grad_weight_qkv, to_slots)
-    sums_one = scatter_line(grad_blocks_qkv)
-    sums_feed = feed(sums_gu, sums_down, [grad_blocks_qkv])
-    grad_h_one = plane_scatter_frames(
-        matmul(weight_qkv, grad_qkv).astype(jnp.bfloat16), [sums_two, grad_blocks_qkv]
-    )
-    grad_gain_one = jnp.sum(grad_h_one * normed_one * time_gain, axis=1)
-    grad_time = jnp.sum(grad_h_one * normed_one * gain_one, axis=1)
-    latent_grad = grad_x_one + norm_columns_back(grad_h_one * scaled_one, normed_one, inverse_one)
+    latent_grad, grad_weight_qkv, sum_one = back(
+        orders,
+        weight_qkv,
+        grad_qkv,
+        h_one,
+        (normed_one, inverse_one, scaled_one, grad_x_one),
+        in_slots=True,
+        after=[sums_gu],
+    )
+    grad_blocks_one = as_blocks(
+        jnp.concatenate([grad_weight_qkv, grad_weight_ao], axis=1), to_slots
+    )
+    sums_one = scatter_line(grad_blocks_one)
+    sums_feed, ff_out = feed(
+        sums_gu,
+        sums_down,
+        matmul(weight_down, hidden).astype(jnp.bfloat16),
+        [grad_blocks_one],
+    )
+    result = x_two + sort_blocks(ff_out, to_logical)
+    sum_one = sum_one[0:1]
+    grad_gain_one = sum_one * time_gain.T
+    grad_time = sum_one * gain_one.T
     gain_grads = jnp.concatenate(
         [
-            jnp.stack([grad_gain_one, grad_gain_two, grad_gain_three]),
-            bucket_pick[:, None] * grad_time[None, :],
+            grad_gain_one,
+            sum_two[0:1],
+            sum_three[0:1],
+            bucket_pick[:, None] * grad_time,
         ],
         axis=0,
     )
-    sums_two = exchange_blocks(sums_two, [sums_feed])
-    out_pair, sums_one, gain_sums = closing(
+    squares = sum(
+        jnp.sum(jnp.square(part.astype(jnp.float32)))
+        for part in (sums_gu, sums_down, sums_two, sums_one)
+    )
+    out_pair, sums_one, sums_two, gain_sums, squares = closing(
         jnp.concatenate([result.T, latent_grad.T], axis=1).astype(jnp.bfloat16),
         sums_one,
+        sums_two,
         gain_grads,
-        sums_two,
+        jnp.pad(squares.reshape(1, 1), ((0, 7), (0, 127))),
     )
     output = out_pair[:, :D]
     latent_grad = out_pair[:, D:].astype(jnp.float32)
     place = lax.axis_index("dp") * (planes * cores) + plane * cores + lax.axis_index("core")
+    gain_sums = jnp.sum(gain_sums, axis=0)
+    grad_norm = jnp.sqrt(jnp.sum(squares) + jnp.sum(gain_sums * gain_sums))
+    scale = 1.0 / jnp.maximum(grad_norm, 1.0)
     gain_sums = lax.dynamic_index_in_dim(
-        jnp.sum(gain_sums, axis=0).reshape(8, blocks, rows), owners[place], 1, False
+        gain_sums.reshape(8, blocks, rows), owners[place], 1, False
     ).T
-    sums_one, sums_two = jnp.swapaxes(sums_one, 0, 1), jnp.swapaxes(sums_two, 0, 1)
-
-    def joined(part):
-        return part.reshape(rows, -1)
-
-    grad_sheet = jnp.concatenate(
-        [joined(sums_one[:, :, k * span : (k + 1) * span]) for k in range(3)]
-        + [joined(sums_two[:, :, k * span : (k + 1) * span]) for k in range(3)]
-        + [sums_feed]
-        + [
-            joined(sums_two[:, :, 3 * span : 3 * span + text_width]),
-            joined(sums_two[:, :, 3 * span + text_width :]),
-        ]
-        + [gain_sums.astype(jnp.bfloat16)],
-        axis=1,
-    ).astype(jnp.float32)
-    squares = jnp.pad(jnp.sum(grad_sheet * grad_sheet).reshape(1, 1), ((0, 7), (0, 127)))
-    total_squares = jnp.sum(gather_everywhere(squares))
-    return (output[None], latent_grad[None]) + update(
-        grad_sheet, total_squares, sheet, first, second, length
-    )
-
-
-def update(grad_sheet, total_squares, sheet, first, second, length):
-    grad_norm = jnp.sqrt(total_squares)
-    clipped = grad_sheet / jnp.maximum(grad_norm, 1.0)
-    gain_grad = clipped[:, 6 * D + 3 * FF + 2 * CTXW :]
-    first_new = BETA_ONE * first + (1.0 - BETA_ONE) * clipped
-    second_new = BETA_TWO * second + (1.0 - BETA_TWO) * clipped * clipped
-    mean_hat = first_new / (1.0 - BETA_ONE**STEP)
-    square_hat = second_new / (1.0 - BETA_TWO**STEP)
-    rates = column_spread(length)[None, :]
-    sheet_new = sheet - rates * (
-        mean_hat / (jnp.sqrt(square_hat) + EPS_ADAM) + WEIGHT_DECAY * sheet
+    clipped, first_new, second_new, sheet_new, sheet_copy = sheet_update(
+        scale,
+        length,
+        sums_one,
+        sums_two,
+        sums_feed,
+        jnp.pad(gain_sums, ((0, 0), (0, 120))),
+        sheet,
+        first,
+        second,
     )
     return (
+        output[None],
+        latent_grad[None],
         grad_norm,
         clipped,
-        gain_grad,
+        gain_sums * scale,
         first_new,
         second_new,
         sheet_new,
-        sheet_new.astype(jnp.bfloat16),
+        sheet_copy,
     )
 
 

time: 708 us -> 669 us (0.945)
  matrix products: 124 us -> 79.5 us
    unnamed x181 -> x216, local copies, waits for them, and re-layouts: 26 us -> 59.2 us
    dot_general x8 -> x3, matrix products: 31.5 us -> 9.46 us  [matmul(): return jnp.dot(left, right, preferred_element_type=jnp.float32)]
    dot_general x8 -> x3, matrix products: 27.4 us -> 5.87 us  [contract_last(): lax.dot_general(left, right, (((1,), (1,)), ((), ())), preferred_element_...]
    convert_element_type x8 -> x1, other arithmetic: 18.4 us -> 0.98 us  [plane_plan(): hidden = (silu_gate * up_part).astype(jnp.bfloat16)]
    gather x8 -> x6, local copies, waits for them, and re-layouts: 27.8 us -> 10.4 us  [pick_blocks(): return blocks.at[order].get(mode='promise_in_bounds')]
    convert_element_type x7 -> x2, local copies, waits for them, and re-layouts: 8.41 us -> 0.45 us  [plane_plan(): grad.astype(jnp.bfloat16)]
    dot_general x6 -> x4, matrix products: 29.1 us -> 24.4 us  [contract_rows(): lax.dot_general(left, right, (((0,), (0,)), ((), ())), preferred_element_...]
    pallas_call x20 -> x10, Pallas kernels: 339 us -> 337 us  [the longest x5 129 us: back(): pl.pallas_call(functools.partial(back_kernel, plan), out_shape=tuple(outs...]
  transfers between devices with their start and end apart: 7 -> 8, of which waited for: 1 -> 1; matrix products, arithmetic and copies ran while one was open for 26% -> 22% of each run, Pallas kernels for 46% -> 49%
where the time goes in v3:
time: 669 us; the launch traced here: 658 us
  Pallas kernels  399 us (60%)
  local copies, waits for them, and re-layouts  95.1 us (14%)
  matrix products  79.5 us (12%)
  other arithmetic  51 us (8%)
  between operations  23.7 us (4%)
  waiting for transfers between devices  8.88 us (1%)
    pallas_call x5, Pallas kernels, back(): pl.pallas_call(functools.partial(back_kernel, plan), out_shape=tuple(outs...  129 us
    pallas_call x2, Pallas kernels, project(): pl.pallas_call(functools.partial(project_kernel, kind), out_shape=(whole,...  108 us
    unnamed x216, local copies, waits for them, and re-layouts  59.2 us
    pallas_call x1, Pallas kernels, first_gather(): pl.pallas_call(first_gather_kernel, out_shape=(jax.ShapeDtypeStruct((rows...  45.4 us
    pallas_call x1, Pallas kernels, feed(): pl.pallas_call(feed_kernel, out_shape=(jax.ShapeDtypeStruct((gu.shape[1],...  38.2 us
    pallas_call x1, Pallas kernels, opening(): pl.pallas_call(opening_kernel, out_shape=(jax.ShapeDtypeStruct(local.shap...  31.2 us
    pallas_call x1, Pallas kernels, closing(): pl.pallas_call(closing_kernel, out_shape=(jax.ShapeDtypeStruct(local.shap...  30.1 us
    dot_general x4, matrix products, contract_rows(): lax.dot_general(left, right, (((0,), (0,)), ((), ())), preferred_element_...  24.4 us
  transfers between devices with their start and end apart: 8, of which 1 were waited for; matrix products, arithmetic and copies ran while one was open for 22% of the time, Pallas kernels for 49%

profile of v3, /device:TPU:0, one launch (start us, length us, event | category | flops | bytes accessed | tf_op | source)
XLA Modules:
  0.0 657.9 jit_solution(5468904616705108817)
XLA Ops:
  18.2 31.2 %opening.1 = (bf16[128,3072]{1,0:T(8,128)(2,1)}, f32[4,8,8,128]{3,2,1,0:T(8,128)}, bf16[96,128]{1,0:T(8,128)(2,1)}, bf16[8,48,576]{2,1,0:T(8,128)(2,1)}, bf16[8,48,768]{2,1,0:T(8,128)(2,1)}) custom-call(bf16[128,3072]{1,0:T(8,128)(2,1)} %pad_maximum_fusion.4.x_ref, f32[8,128]{1,0:T(8,128)} %select_maximum_fusion.small_ref, bf16[768,128]{1,0:T(8,128)(2,1)} %bitcast.190, ...), custom_call_target="tpu_custom_call" | custom-call | bytes 1024 | tf_op jit(solution)/shard_map/opening/pallas_call | solution.py:1438
  65.7 45.4 %first_gather.1 = (bf16[1536,1024]{1,0:T(8,128)(2,1)}, bf16[8,48,1536]{2,1,0:T(8,128)(2,1)}, bf16[8,48,768]{2,1,0:T(8,128)(2,1)}) custom-call(bf16[1536,128]{1,0:T(8,128)(2,1)} %bitcast.186, bf16[48,29192]{1,0:T(8,128)(2,1)} %copy-done.64), custom_call_target="tpu_custom_call" | custom-call | bytes 1024 | tf_op jit(solution)/shard_map/first_gather/pallas_call | solution.py:1482
  117.6 4.5 fusion.66
  124.4 11.0 %fusion.64 = (f32[3,1024]{1,0:T(4,128)S(1)}, f32[3,1024,1024]{1,2,0:T(8,128)}) fusion(pred[1024,1024]{0,1:T(8,128)(4,1)} %broadcast_compare_fusion, bf16[3,32,1024]{2,1,0:T(8,128)(2,1)} %get-tuple-element.200, bf16[3,32,1024]{2,1,0:T(8,128)(2,1)} %get-tuple-element.201, bf16[3,32,1024]{2,1,0:T(8,128)(2,1)} %get-tuple-element.183, ...), kind=kOutput, calls=%fused_computation.184 | convolution fusion | flops 416809984 | bytes 14430208 | tf_op jit(solution)/shard_map/sub | solution.py:56
  135.3 6.6 fusion.18
  141.9 7.5 %all-gather.7.cloned.1.call-done = bf16[32,48,768]{2,1,0:T(8,128)(2,1)} async-done(((bf16[8,48,768]{2,1,0:T(8,128)(2,1)}), bf16[32,48,768]{2,1,0:T(8,128)(2,1)}) %all-gather.7.cloned.1.call-update) | async-done | bytes 2359312 | tf_op jit(solution)/shard_map/all_gather | solution.py:1742
  149.4 3.9 gather_fusion.2
  156.2 3.3 fusion.62
  169.7 47.3 %project_sum.1 = (bf16[1536,1024]{1,0:T(8,128)(2,1)S(1)}, f32[1536,128]{1,0:T(8,128)S(1)}, f32[1536,128]{1,0:T(8,128)S(1)}, f32[1,128]{1,0:T(1,128)S(1)}, bf16[1...) custom-call(s32[2,32]{1,0:T(2,128)S(1)} %pad_add_fusion.order_ref.refs_0_, bf16[192,1024]{1,0:T(8,128)(2,1)S(1)} %bitcast.161, ...), custom_call_target="tpu_custom_call" | custom-call | bytes 1024 | tf_op jit(solution)/shard_map/project_sum/pallas_call | solution.py:885
  229.2 60.3 %project_gather.1 = (bf16[1536,1024]{1,0:T(8,128)(2,1)S(1)}, f32[1536,128]{1,0:T(8,128)S(1)}, f32[1536,128]{1,0:T(8,128)S(1)}, f32[1,128]{1,0:T(1,128)S(1)}, bf1...) custom-call(s32[2,32]{1,0:T(2,128)S(1)} %pad_add_fusion.order_ref.refs_0_, bf16[192,1024]{1,0:T(8,128)(2,1)S(1)} %bitcast.162, ...), custom_call_target="tpu_custom_call" | custom-call | bytes 1024 | tf_op jit(solution)/shard_map/project_gather/pallas_call | solution.py:885
  295.4 7.9 %fusion.67 = f32[1536,1024]{1,0:T(8,128)S(1)} fusion(bf16[1536,1536]{1,0:T(8,128)(2,1)} %bitcast.175, bf16[1536,1024]{1,0:T(8,128)(2,1)} %copy-done.26), kind=kOutput, calls=%fused_computation.187 | convolution fusion | flops 4831838208 | bytes 14155776 | tf_op jit(solution)/shard_map/dot_general | solution.py:443
  307.7 3.9 convolution_convert_fusion.1
  312.1 8.7 %multiply_convert_fusion.2 = (bf16[768,1024]{1,0:T(8,128)(2,1)S(1)}, bf16[768,1024]{1,0:T(8,128)(2,1)S(1)}) fusion(f32[1536,1024]{1,0:T(8,128)} %copy-done.65, bf16[1536,768]{1,0:T(8,128)(2,1)} %bitcast.203, bf16[1536,1024]{1,0:T(8,128)(2,1)} %copy-done.61), kind=kOutput, calls=%fused_computation.24 | convolution fusion | flops 2426142720 | bytes 14942208 | tf_op jit(solution)/shard_map/dot_general | solution.py:443
  322.6 30.9 %back.5 = (f32[1536,128]{1,0:T(8,128)S(1)}, bf16[1536,1536]{1,0:T(8,128)(2,1)}, f32[8,1536]{1,0:T(8,128)S(1)}, bf16[192,1024]{1,0:T(8,128)(2,1)S(1)}) custom-call(s32[2,32]{1,0:T(2,128)S(1)} %pad_add_fusion.order_ref.refs_0_, bf16[1536,1536]{1,0:T(8,128)(2,1)} %bitcast.176, bf16[1536,1024]{1,0:T(8,128)(2,1)S(1)} %pad_maximum_fusion.refs_2_, ...), custom_call_target="tpu_custom_call" | custom-call | bytes 1024 | tf_op jit(solution)/shard_map/back/pallas_call | solution.py:1132
  358.1 20.5 %back.6 = (bf16[192,1024]{1,0:T(8,128)(2,1)S(1)}, bf16[1536,192]{1,0:T(8,128)(2,1)S(1)}) custom-call(s32[2,32]{1,0:T(2,128)S(1)} %pad_add_fusion.order_ref.refs_0_, bf16[1536,192]{1,0:T(8,128)(2,1)S(1)} %copy-done.7, bf16[192,1024]{1,0:T(8,128)(2,1)S(1)} %get-tuple-element.79.refs_2_, bf16[32,48,1024]{2,1,0:T(8,128)(2,1)S(1)} %bitcast.150), custom_call_target="tpu_custom_call" | custom-call | bytes 1024 | tf_op jit(solution)/shard_map/back/pallas_call | solution.py:1132
  389.0 34.2 %back.7 = (f32[1536,128]{1,0:T(8,128)S(1)}, bf16[1536,192]{1,0:T(8,128)(2,1)S(1)}, f32[8,1536]{1,0:T(8,128)S(1)}, bf16[192,1024]{1,0:T(8,128)(2,1)S(1)}, bf16[1536,256]{1,0:T(8,128)(2,1)S(1)}) custom-call(s32[2,32]{1,0:T(2,128)S(1)} %pad_add_fusion.order_ref.refs_0_, bf16[1536,192]{1,0:T(8,128)(2,1)S(1)} %copy-done.27, bf16[192,1024]{1,0:T(8,128)(2,1)S(1)} %bitcast.158, ...), custom_call_target="tpu_custom_call" | custom-call | bytes 1024 | tf_op jit(solution)/shard_map/back/pallas_call | solution.py:1132
  436.3 20.2 %back.8 = (bf16[192,1024]{1,0:T(8,128)(2,1)S(1)}, bf16[1536,192]{1,0:T(8,128)(2,1)S(1)}) custom-call(s32[2,32]{1,0:T(2,128)S(1)} %pad_add_fusion.order_ref.refs_0_, bf16[1536,192]{1,0:T(8,128)(2,1)S(1)} %copy-done.9, bf16[192,1024]{1,0:T(8,128)(2,1)S(1)} %copy-done.56, bf16[32,48,1024]{2,1,0:T(8,128)(2,1)S(1)} %bitcast.152, bf16[32,48,576]{2,1,0:T(8,128)(2,1)S(1)} %bitcast.144), custom_call_target="tpu_custom_call" | custom-call | bytes 1024 | tf_op jit(solution)/shard_map/back/pallas_call | solution.py:1132
  456.6 10.2 %multiply_reduce_fusion = (f32[3,1024]{1,0:T(4,128)S(1)}, f32[3,1024,1024]{1,2,0:T(8,128)}) fusion(f32[3,1024,1024]{1,2,0:T(8,128)} %get-tuple-element.212, f32[3,1024]{1,0:T(4,128)S(1)} %copy-done.93, bf16[3,64,1024]{2,1,0:T(8,128)(2,1)S(1)} %bitcast.163, bf16[3,64,1024]{2,1,0:T(8,128)(2,1)S(1)} %bitcast.193), kind=kOutput, calls=%fused_computation.12 | convolution fusion | flops 412087296 | bytes 25976832 | tf_op jit(solution)/shard_map/hdq,hdk->hqk/dot_general | solution.py:1998
  469.2 6.7 %multiply_convert_fusion = bf16[3,1024,1024]{1,2,0:T(8,128)(2,1)S(1)} fusion(f32[3,1024,1024]{1,2,0:T(8,128)} %get-tuple-element.218, f32[3,1024]{1,0:T(4,128)S(1)} %get-tuple-element.217, f32[3,1024,1024]{1,2,0:T(8,128)S(1)} %bitcast.174, f32[3,1024]{1,0:T(4,128)S(1)} %copy-done.93), kind=kLoop, calls=%fused_computation.11 | loop fusion | flops 12582912 | bytes 31481856 | tf_op jit(solution)/shard_map/convert_element_type | solution.py:2003
  485.8 23.2 %back.9 = (f32[1536,128]{1,0:T(8,128)S(1)}, bf16[1536,576]{1,0:T(8,128)(2,1)S(1)}, f32[8,1536]{1,0:T(8,128)S(1)}) custom-call(s32[2,32]{1,0:T(2,128)S(1)} %pad_add_fusion.order_ref.refs_0_, bf16[1536,576]{1,0:T(8,128)(2,1)S(1)} %bitcast.156, bf16[576,1024]{1,0:T(8,128)(2,1)S(1)} %bitcast.149, bf16[1536,1024]{1,0:T(8,128)(2,1)} %get-tuple-element.63.refs_3_, ...), custom_call_target="tpu_custom_call" | custom-call | bytes 1024 | tf_op jit(solution)/shard_map/back/pallas_call | solution.py:1132
  516.8 6.6 convolution_convert_fusion.p_ref
  530.5 38.2 %feed.1 = (bf16[48,18432]{1,0:T(8,128)(2,1)S(1)}, f32[1536,128]{1,0:T(8,128)S(1)}) custom-call(bf16[8,48,1536]{2,1,0:T(8,128)(2,1)S(1)} %copy-done.4, bf16[8,48,768]{2,1,0:T(8,128)(2,1)S(1)} %copy-done.16, bf16[1536,1024]{1,0:T(8,128)(2,1)S(1)} %copy-done.18, bf16[32,48,768]{2,1,0:T(8,128)(2,1)S(1)} %bitcast.142), custom_call_target="tpu_custom_call" | custom-call | bytes 1024 | tf_op jit(solution)/shard_map/feed/pallas_call | solution.py:1257
  585.1 30.1 %closing.1 = (bf16[128,3072]{1,0:T(8,128)(2,1)}, bf16[8,48,768]{2,1,0:T(8,128)(2,1)}, bf16[8,48,576]{2,1,0:T(8,128)(2,1)}, f32[8,8,1536]{2,1,0:T(8,128)}, f32[4,8,8,128]{3,2,1,0:T(8,128)}) custom-call(bf16[128,3072]{1,0:T(8,128)(2,1)} %pad_maximum_fusion.6.x_ref, bf16[8,48,768]{2,1,0:T(8,128)(2,1)} %reduce-scatter.9.cloned.1.call-done.w_ref, ...), custom_call_target="tpu_custom_call" | custom-call | bytes 1024 | tf_op jit(solution)/shard_map/closing/pallas_call | solution.py:1632
  632.5 17.0 %sheet_update.1 = (f32[48,29192]{1,0:T(8,128)}, f32[48,29192]{1,0:T(8,128)}, f32[48,29192]{1,0:T(8,128)}, f32[48,29192]{1,0:T(8,128)}, bf16[48,29192]{1,0:T(8,128)(2,1)}) custom-call(f32[1]{0:T(128)} %bitcast.65.scale_ref, f32[20]{0:T(128)S(1)} %gather_fusion.6, bf16[8,48,768]{2,1,0:T(8,128)(2,1)S(1)} %copy-done.51, bf16[8,48,576]{2,1,0:T(8,128)(2,1)S(1)} %copy-done.52, ...), custom_call_target="tpu_custom_call" | custom-call | tf_op jit(solution)/shard_map/sheet_update/pallas_call | solution.py:1710
  (372 shorter events, 154.9 us)
Async XLA Ops:
  7.2 110.4 %all-gather.5.cloned.1.call-start = ((), (), s32[]{:S(2)}) async-start(), calls=%async_computation.4 | async-start | bytes 2457600 | tf_op jit(solution)/shard_map/all_gather | solution.py:1747
  15.5 34.8 %copy-start.63 = (s32[32]{0:T(128)S(1)}, s32[32]{0:T(128)}, u32[]{:S(2)}) copy-start(s32[32]{0:T(128)} %param.15) | copy-start | bytes 388
  18.2 36.5 %copy-start.103 = (s32[4]{0:T(128)S(1)}, s32[4]{0:T(128)}, u32[]{:S(2)}) copy-start(s32[4]{0:T(128)} %param.14) | copy-start | bytes 52
  49.4 100.0 %all-gather.7.cloned.1.call-start = ((), (), s32[]{:S(2)}) async-start(), calls=%async_computation.5 | async-start | bytes 2949120 | tf_op jit(solution)/shard_map/all_gather | solution.py:1742
  50.2 245.2 %all-gather.9.cloned.1.call-start = ((), (), s32[]{:S(2)}) async-start(), calls=%async_computation.6 | async-start | bytes 5898240 | tf_op jit(solution)/shard_map/all_gather | solution.py:1747
  63.1 102.2 %copy-start.10 = (f32[1536,1]{1,0:T(8,128)}, f32[1536,1]{1,0:T(8,128)S(1)}, u32[]{:S(2)}) copy-start(f32[1536,1]{1,0:T(8,128)S(1)} %get-tuple-element.192.gain_ref.refs_6_) | copy-start | bytes 18436
  111.2 200.4 %all-gather.11.cloned.1.call-start = ((), (), s32[]{:S(2)}) async-start(), calls=%async_computation.7 | async-start | bytes 2949120 | tf_op jit(solution)/shard_map/all_gather | solution.py:1747
  111.7 271.9 %reduce-scatter.7.cloned.1.call-start = ((), (), s32[]{:S(2)}) async-start(), calls=%async_computation.9 | async-start | bytes 2949120 | tf_op jit(solution)/shard_map/reduce_scatter | solution.py:1760
  124.4 11.0 %copy-start.79 = (bf16[192,1024]{1,0:T(8,128)(2,1)S(1)}, bf16[192,1024]{1,0:T(8,128)(2,1)}, u32[]{:S(2)}) copy-start(bf16[192,1024]{1,0:T(8,128)(2,1)} %slice.292) | copy-start | bytes 1179652
  141.9 11.4 %copy-start.78 = (bf16[96,128]{1,0:T(8,128)(2,1)S(1)}, bf16[96,128]{1,0:T(8,128)(2,1)}, u32[]{:S(2)}) copy-start(bf16[96,128]{1,0:T(8,128)(2,1)} %get-tuple-element.65) | copy-start | bytes 73732
  311.6 170.2 %reduce-scatter.5.cloned.1.call-start = ((), (), s32[]{:S(2)}) async-start(), calls=%async_computation.8 | async-start | bytes 5898240 | tf_op jit(solution)/shard_map/reduce_scatter | solution.py:1760
  355.1 23.6 %copy-start.89 = (bf16[3,64,1,128]{3,2,1,0:T(2,128)(2,1)S(1)}, bf16[3,64,1,128]{3,2,1,0:T(2,128)(2,1)}, u32[]{:S(2)}) copy-start(bf16[3,64,1,128]{3,2,1,0:T(2,128)(2,1)} %copy-done.88) | copy-start | bytes 147460
  355.1 23.6 %copy-start.95 = (f32[3,1024]{1,0:T(4,128)S(1)}, f32[3,1024]{1,0:T(4,128)}, u32[]{:S(2)}) copy-start(f32[3,1024]{1,0:T(4,128)} %copy-done.94) | copy-start | bytes 36868
  355.1 170.5 %reduce-scatter.11.cloned.1.call-start = ((), (), s32[]{:S(2)}) async-start(), calls=%async_computation.11 | async-start | bytes 2457600 | tf_op jit(solution)/shard_map/reduce_scatter | solution.py:1760
  431.9 149.9 %reduce-scatter.9.cloned.1.call-start = ((), (), s32[]{:S(2)}) async-start(), calls=%async_computation.10 | async-start | bytes 2949120 | tf_op jit(solution)/shard_map/reduce_scatter | solution.py:1760
  436.3 20.2 %copy-start.80 = (bf16[192,1024]{1,0:T(8,128)(2,1)S(1)}, bf16[192,1024]{1,0:T(8,128)(2,1)}, u32[]{:S(2)}) copy-start(bf16[192,1024]{1,0:T(8,128)(2,1)} %slice.292) | copy-start | bytes 1179652
  436.3 20.2 %copy-start.93 = (f32[3,1024]{1,0:T(4,128)S(1)}, f32[3,1024]{1,0:T(4,128)}, u32[]{:S(2)}) copy-start(f32[3,1024]{1,0:T(4,128)} %copy-done.92) | copy-start | bytes 36868
  456.5 10.2 %slice-start = ((s8[12582912]{0:T(1024)(128)(4,1)}), s8[4194304]{0:T(1024)(128)(4,1)S(1)}, s32[]{:S(2)}) async-start(s8[12582912]{0:T(1024)(128)(4,1)} %bitcast.173), calls=%async_computation.12 | async-start | bytes 8388608
  456.5 11.5 %slice-start.1 = ((s8[12582912]{0:T(1024)(128)(4,1)}), s8[4194304]{0:T(1024)(128)(4,1)S(1)}, s32[]{:S(2)}) async-start(s8[12582912]{0:T(1024)(128)(4,1)} %bitcast.173), calls=%async_computation.13 | async-start | bytes 8388608
  456.5 12.7 %slice-start.2 = ((s8[12582912]{0:T(1024)(128)(4,1)}), s8[4194304]{0:T(1024)(128)(4,1)S(1)}, s32[]{:S(2)}) async-start(s8[12582912]{0:T(1024)(128)(4,1)} %bitcast.173), calls=%async_computation.14 | async-start | bytes 8388608
  516.8 10.8 %copy-start.1 = (bf16[1536,768]{1,0:T(8,128)(2,1)S(1)}, bf16[1536,768]{1,0:T(8,128)(2,1)}, u32[]{:S(2)}) copy-start(bf16[1536,768]{1,0:T(8,128)(2,1)} %pad_maximum_fusion.1) | copy-start | bytes 7077892
  516.8 10.8 %copy-start.4 = (bf16[8,48,1536]{2,1,0:T(8,128)(2,1)S(1)}, bf16[8,48,1536]{2,1,0:T(8,128)(2,1)}, u32[]{:S(2)}) copy-start(bf16[8,48,1536]{2,1,0:T(8,128)(2,1)} %reduce-scatter.5.cloned.1.call-done.refs_8_.gu_ref) | copy-start | bytes 3538948
  581.8 42.9 %copy-start.35 = (bf16[48,18432]{1,0:T(8,128)(2,1)S(1)}, bf16[48,18432]{1,0:T(8,128)(2,1)}, u32[]{:S(2)}) copy-start(bf16[48,18432]{1,0:T(8,128)(2,1)} %copy-done.34) | copy-start | bytes 5308420
  615.2 9.4 %copy-start.51 = (bf16[8,48,768]{2,1,0:T(8,128)(2,1)S(1)}, bf16[8,48,768]{2,1,0:T(8,128)(2,1)}, u32[]{:S(2)}) copy-start(bf16[8,48,768]{2,1,0:T(8,128)(2,1)} %get-tuple-element.102.one_ref) | copy-start | bytes 1769476
  (91 other events, 248.4 us)
Sparse Core Ops, SparseCore 0:
  49.5 48.8 all-gather.4
  100.0 49.3 all-gather.6
  151.0 88.2 all-gather.8
  240.7 48.9 all-gather.10
  311.7 45.8 reduce-scatter.6
  359.8 84.7 reduce-scatter.4
  447.5 41.9 reduce-scatter.10
  511.0 45.8 reduce-scatter.8

commit v4 on v3

--- a/solution.py
+++ b/solution.py
@@ -423,19 +423,6 @@
         grad_normed
         - jnp.mean(grad_normed, axis=0, keepdims=True)
         - normed * jnp.mean(grad_normed * normed, axis=0, keepdims=True)
-    )
-
-
-def rotate_columns(values, cosine, sine_table):
-    half_dim = HEAD // 2
-    first_half = values[:, :half_dim]
-    second_half = values[:, half_dim:]
-    return jnp.concatenate(
-        [
-            first_half * cosine - second_half * sine_table,
-            second_half * cosine + first_half * sine_table,
-        ],
-        axis=1,
     )
 
 
@@ -779,8 +766,11 @@
     return plane_scatter_call(partial, (rows, width), place, jnp.bfloat16, "scatter rows", after)
 
 
-def project_kernel(kind, order_ref, s_ref, w_ref, base_ref, gain_ref, side_ref, *refs):
-    full_ref, x_ref, n_ref, i_ref, h_ref, side_out, *refs = refs
+def project_kernel(kind, column, order_ref, s_ref, w_ref, base_ref, gain_ref, *refs):
+    if kind == "sum":
+        side_ref, full_ref, x_ref, n_ref, i_ref, h_ref, side_out, *refs = refs
+    else:
+        full_ref, x_ref, n_ref, i_ref, h_ref, *refs = refs
     full, total, part, landed, shard, by_block, base, gain, residual, normed, *refs = refs
     heads, weight, *bufs, local_sem, send_sem, recv_sem = refs
     rows, length = s_ref.shape
@@ -807,24 +797,18 @@
     total[...] = jnp.zeros_like(total)
 
     def add(member):
-        first = pl.multiple_of(member * rows, 16)
+        of = pl.ds(pl.multiple_of(member * rows, 16), rows)
 
         @pl.loop(0, length // 256)
         def _(i):
             at = pl.ds(pl.multiple_of(i * 256, 256), 256)
-            total[:, at] += jnp.dot(
-                weight[member], full[pl.ds(first, rows), at], preferred_element_type=jnp.float32
-            )
+            total[:, at] += contract_rows(weight[of, column : column + rows], full[of, at])
 
     gathered = gather_steps(
         member_rows(rows), heads, full, local_sem.at[0], mover(send_sem, recv_sem), add
     )
     if kind == "sum":
         chips()
-    else:
-        side_done = gather_steps(
-            member_lanes(width), side_ref, side_out, local_sem.at[7], side
-        )
     gathered()
     kept = pltpu.make_async_copy(full, full_ref, local_sem.at[0])
     kept.start()
@@ -847,7 +831,7 @@
     normed[...] = standard
     i_ref[...] = inverse_std
     scaled = (standard * gain[...]).astype(shard.dtype)
-    if kind == "gather":
+    if kind == "slots":
         by_block[...] = scaled.reshape(by_block.shape)
         reorder_blocks(by_block, shard, lambda b: order_ref[0, b])
     else:
@@ -861,33 +845,29 @@
     n_copy.start()
     if kind == "sum":
         side_out[...] = finish().astype(side_out.dtype)
-    else:
-        side_done()
     gathered()
     kept.wait()
     x_copy.wait()
     n_copy.wait()
 
 
-def project(kind, orders, heads, weight, base, gain, side):
+def project(kind, column, orders, heads, weight, base, gain, *side):
     rows, length = heads.shape
     features, width = base.shape
-    by_member = weight.reshape(8, rows, rows).swapaxes(1, 2)
     whole = jax.ShapeDtypeStruct((features, length), jnp.bfloat16)
     frames = jax.ShapeDtypeStruct(base.shape, jnp.float32)
+    side_outs, bufs = (), []
     if kind == "sum":
-        side_out = jax.ShapeDtypeStruct((side.shape[0] // 8, side.shape[1]), side.dtype)
-        bufs, at = scatter_bufs(*side_out.shape), IN_VMEM
-        bufs.append(pltpu.VMEM(side.shape, side.dtype))
-    else:
-        side_out, bufs, at = whole, [], IN_HBM
+        (text,) = side
+        side_outs = (jax.ShapeDtypeStruct((text.shape[0] // 8, text.shape[1]), text.dtype),)
+        bufs = scatter_bufs(*side_outs[0].shape) + [pltpu.VMEM(text.shape, text.dtype)]
     low, high = pltpu.VMEM(base.shape, jnp.bfloat16), pltpu.VMEM(base.shape, jnp.float32)
     return pl.pallas_call(
-        functools.partial(project_kernel, kind),
+        functools.partial(project_kernel, kind, column),
         out_shape=(whole, frames, frames, jax.ShapeDtypeStruct((1, width), jnp.float32), whole)
-        + (side_out,),
-        in_specs=[IN_SMEM] + [IN_HBM] * 5,
-        out_specs=(IN_HBM, IN_HBM, IN_HBM, IN_VMEM, IN_HBM, at),
+        + side_outs,
+        in_specs=[IN_SMEM] + [IN_HBM] * (4 + len(side)),
+        out_specs=(IN_HBM, IN_HBM, IN_HBM, IN_VMEM, IN_HBM) + (IN_VMEM,) * len(side),
         scratch_shapes=[
             pltpu.VMEM((features, length), jnp.bfloat16),
             pltpu.VMEM((rows, length), jnp.float32),
@@ -900,7 +880,7 @@
             high,
             high,
             pltpu.VMEM(heads.shape, heads.dtype),
-            pltpu.VMEM(by_member.shape, by_member.dtype),
+            pltpu.VMEM(weight.shape, weight.dtype),
         ]
         + bufs
         + [
@@ -915,11 +895,11 @@
         ),
         cost_estimate=BRIEF,
         name="project_" + kind,
-    )(orders, heads, by_member, base, gain, side)
+    )(orders, heads, weight, base, gain, *side)
 
 
 def back_kernel(plan, *refs):
-    by_rows, send_rows, text, in_slots, after = plan
+    by_rows, send_rows, text, in_slots, column, beside, after = plan
     refs = list(refs)
 
     def take(count):
@@ -930,6 +910,7 @@
     order_ref = take(1)[0]
     sources = take(3 if by_rows else 7)
     text_ref = take(1)[0] if text else None
+    beside_refs = take(4 if beside else 0)
     take(after)
     o_ref, own_out = take(2)
     sum_ref = None if by_rows else take(1)[0]
@@ -939,10 +920,11 @@
     w_ref, g_ref, act, *norms = held
     results = take(0 if by_rows else 2)
     mine, theirs, pair, from_x, from_y, relay, shard, slots, own_ref = take(9)
+    besides = take(4 if beside else 0)
     local_sem, send_sem, recv_sem = refs
     fetches = [
         pltpu.make_async_copy(ref, here, local_sem.at[4 + k])
-        for k, (ref, here) in enumerate(zip(sources, held))
+        for k, (ref, here) in enumerate(zip(sources + beside_refs, held + besides))
     ]
     for fetch in fetches:
         fetch.start()
@@ -951,6 +933,7 @@
     beyond = across + along - group
     sibling, by_x, by_y = {"core": 1 - core}, {"dp": across}, {"dp": along}
     rows, width = mine.shape[1:]
+    columns = slice(column, column + g_ref.shape[0])
     half = rows // 2
     low, high = pl.ds(0, half), pl.ds(half, half)
     copy = mover(send_sem, recv_sem)
@@ -975,7 +958,7 @@
             def _(i):
                 at = pl.ds(pl.multiple_of(i * 256, 256), 256)
                 both = jnp.dot(
-                    w_ref[pl.ds(pl.multiple_of(owner * 2 * rows, 16), 2 * rows), :],
+                    w_ref[pl.ds(pl.multiple_of(owner * 2 * rows, 16), 2 * rows), columns],
                     g_ref[:, at],
                     preferred_element_type=jnp.float32,
                 )
@@ -987,7 +970,7 @@
             def _(i):
                 at = pl.ds(pl.multiple_of(i * 256, 256), 256)
                 both = jnp.dot(
-                    w_ref[at, :],
+                    w_ref[at, columns],
                     g_ref[:, pl.ds(pl.multiple_of(owner * 2 * width, 256), 2 * width)],
                     preferred_element_type=jnp.float32,
                 )
@@ -1038,6 +1021,29 @@
             local_sem.at[1],
             mover(send_sem, recv_sem, 17),
         )
+    def put_beside():
+        cq, co, text_grad, text_mine = besides
+        count, rows = g_ref.shape[0], text_grad.shape[1]
+        part = text_mine.shape[0]
+        tokens = text_mine.shape[1]
+
+        @pl.loop(0, text_grad.shape[0])
+        def _(b):
+            at = pl.ds(pl.multiple_of(b * rows, 16), rows)
+            own_ref[at, count : 2 * count] = cq[at, :]
+            own_ref[at, 2 * count : 3 * count] = co[at, :]
+            slots[at, : 2 * tokens] = text_grad[order_ref[0, b]]
+
+        @pl.loop(0, 6)
+        def _(i):
+            at = pl.ds(pl.multiple_of(i * 256, 256), 256)
+            for k in range(2):
+                grads = contract_last(
+                    slots[at, k * tokens : (k + 1) * tokens], text_mine[...]
+                )
+                start = 3 * count + k * part
+                own_ref[at, start : start + part] = grads.astype(own_ref.dtype)
+
     fetches[2].wait()
     if not in_slots:
         reorder_blocks(act, slots, lambda b: order_ref[0, b])
@@ -1050,6 +1056,12 @@
     send(9, mine.at[2, low], from_y.at[low], by_y)
     both_cores(3)
     weight_grads(2, 6)
+    if beside:
+        for fetch in fetches[len(sources) :]:
+            fetch.wait()
+        put_beside()
+    if text:
+        text_done()
     own_copy = pltpu.make_async_copy(own_ref, own_out, local_sem.at[2])
     own_copy.start()
     arrived(6, from_x.at[low])
@@ -1062,7 +1074,7 @@
         result_copy = pltpu.make_async_copy(shard, o_ref, local_sem.at[3])
         result_copy.start()
     else:
-        for fetch in fetches[3:]:
+        for fetch in fetches[3 : len(sources)]:
             fetch.wait()
         normed, inverse_std, gain, base = norms
         result, by_block = results
@@ -1096,18 +1108,29 @@
             rows_done()
     result_copy.wait()
     own_copy.wait()
-    if text:
-        text_done()
     for moving in sent:
         moving.wait_send()
 
 
-def back(orders, weight, grad, act, norm=None, send_rows=False, text=None, in_slots=False, after=()):
+def back(
+    orders,
+    weight,
+    grad,
+    act,
+    norm=None,
+    column=0,
+    send_rows=False,
+    text=None,
+    in_slots=False,
+    beside=(),
+    after=(),
+):
     by_rows = norm is None
     features, length = weight.shape[0], grad.shape[1]
     shape = (features // 8, length) if by_rows else (features, length // 8)
     small = jnp.bfloat16
-    own = jax.ShapeDtypeStruct((features, grad.shape[0]), small)
+    own_width = grad.shape[0] * (4 if beside else 1)
+    own = jax.ShapeDtypeStruct((features, own_width), small)
     outs = [jax.ShapeDtypeStruct(shape, small if by_rows else jnp.float32), own]
     specs = [IN_HBM, IN_HBM]
     if not by_rows:
@@ -1125,8 +1148,12 @@
         operands.append(text)
         outs.append(jax.ShapeDtypeStruct((8 * text.shape[0], text.shape[1]), text.dtype))
         specs.append(IN_HBM)
+    if beside:
+        cq, co, text_grad, text_mine = beside
+        beside = (cq, co, text_grad.reshape(count, features // count, -1), text_mine)
+        operands += list(beside)
     operands += list(after)
-    plan = (by_rows, send_rows, text is not None, in_slots, len(after))
+    plan = (by_rows, send_rows, text is not None, in_slots, column, bool(beside), len(after))
     rows, width = shape
     four, slot = pltpu.VMEM((4, rows, width), small), pltpu.VMEM((rows, width), small)
     return pl.pallas_call(
@@ -1147,6 +1174,9 @@
         + [
             pltpu.VMEM((16, 128) if in_slots else (features, length), small),
             pltpu.VMEM(own.shape, small),
+        ]
+        + [pltpu.VMEM(array.shape, array.dtype) for array in beside]
+        + [
             pltpu.SemaphoreType.DMA((11,)),
             pltpu.SemaphoreType.DMA((31,)),
             pltpu.SemaphoreType.DMA((31,)),
@@ -1226,23 +1256,38 @@
     return lambda ref, member: lanes(ref.at[member], start, width)
 
 
-def feed_kernel(gu_ref, down_ref, p_ref, *refs):
-    o_ref, y_ref, part, summed, *bufs, local_sem, send_sem, recv_sem = refs[-12:]
+def feed_kernel(gu_ref, down_ref, w_ref, h_ref, *refs):
+    o_ref, y_ref, weight, hidden, part, summed, *bufs, local_sem, send_sem, recv_sem = refs[-14:]
     width = down_ref.shape[-1]
-    fetch = pltpu.make_async_copy(p_ref, part, local_sem.at[3])
-    fetch.start()
+    fetches = [
+        pltpu.make_async_copy(w_ref, weight, local_sem.at[3]),
+        pltpu.make_async_copy(h_ref, hidden, local_sem.at[5]),
+    ]
+    for fetch in fetches:
+        fetch.start()
     greet([member_at(peer) for peer in plane_peers()])
-    cores, chips, relays, ended = scatter_steps(
-        member_lanes(y_ref.shape[1]), part, bufs, mover(send_sem, recv_sem, 21)
-    )
-    fetch.wait()
-    cores()
-    chips()
     finish = []
     for k, (ref, start) in enumerate(((gu_ref, 0), (gu_ref, width), (down_ref, 0))):
         source, target = block_part(start, width), sheet_part(8 * k * width, width)
         copy = mover(send_sem, recv_sem, 7 * k)
         finish.append(exchange_steps(source, target, ref, o_ref, local_sem.at[k], copy))
+    for fetch in fetches:
+        fetch.wait()
+
+    @pl.loop(0, part.shape[0] // 256)
+    def _(i):
+        at = pl.ds(pl.multiple_of(i * 256, 256), 256)
+        for j in range(0, part.shape[1], 256):
+            product = jnp.dot(
+                weight[at, :], hidden[:, j : j + 256], preferred_element_type=jnp.float32
+            )
+            part[at, j : j + 256] = product.astype(part.dtype)
+
+    cores, chips, relays, ended = scatter_steps(
+        member_lanes(y_ref.shape[1]), part, bufs, mover(send_sem, recv_sem, 21)
+    )
+    cores()
+    chips()
     relays()
     summed[...] = ended()
     kept = pltpu.make_async_copy(summed, y_ref, local_sem.at[4])
@@ -1252,52 +1297,72 @@
     kept.wait()
 
 
-def feed(gu, down, partial, after=()):
-    rows, width = partial.shape[0], partial.shape[1] // 8
+def feed(gu, down, weight, hidden, after=()):
+    rows, length = weight.shape[0], hidden.shape[1]
+    width = length // 8
     return pl.pallas_call(
         feed_kernel,
         out_shape=(
             jax.ShapeDtypeStruct((gu.shape[1], 24 * down.shape[-1]), gu.dtype),
             jax.ShapeDtypeStruct((rows, width), jnp.float32),
         ),
-        in_specs=[IN_HBM] * (3 + len(after)),
+        in_specs=[IN_HBM] * (4 + len(after)),
         out_specs=(IN_HBM, IN_HBM),
         scratch_shapes=[
-            pltpu.VMEM(partial.shape, partial.dtype),
+            pltpu.VMEM(weight.shape, weight.dtype),
+            pltpu.VMEM(hidden.shape, hidden.dtype),
+            pltpu.VMEM((rows, length), jnp.bfloat16),
             pltpu.VMEM((rows, width), jnp.float32),
         ]
         + scatter_bufs(rows, width)
         + [
-            pltpu.SemaphoreType.DMA((5,)),
+            pltpu.SemaphoreType.DMA((6,)),
             pltpu.SemaphoreType.DMA((31,)),
             pltpu.SemaphoreType.DMA((31,)),
         ],
         compiler_params=pltpu.CompilerParams(
-            collective_id=identity_of("feed", gu, down, *after),
+            collective_id=identity_of("feed", gu, down, weight, *after),
             has_side_effects=True,
-            vmem_limit_bytes=24 * 2**20,
+            vmem_limit_bytes=28 * 2**20,
         ),
         cost_estimate=BRIEF,
         name="feed",
-    )(gu, down, partial, *after)
+    )(gu, down, weight, hidden, *after)
 
 
 def opening_kernel(
-    x_ref,
+    latents_ref,
+    cotangent_ref,
     small_ref,
     text_ref,
-    w_ref,
-    v_ref,
+    sheet_ref,
     t_ref,
     all_ref,
     mine_ref,
-    wo_ref,
-    vo_ref,
+    one_ref,
+    x_ref,
     held,
+    columns,
+    one,
     local_sem,
     send_sem,
     recv_sem,
 ):
+    features = latents_ref.shape[1]
+    part, text = D // 8, CTXW // 8
+    tail = 6 * D + 3 * FF
+    fetches = [
+        pltpu.make_async_copy(latents_ref, x_ref.at[:, :features], local_sem.at[5]),
+        pltpu.make_async_copy(cotangent_ref, x_ref.at[:, features:], local_sem.at[6]),
+        pltpu.make_async_copy(
+            sheet_ref.at[:, : 6 * D], columns.at[:, : 6 * D], local_sem.at[7]
+        ),
+        pltpu.make_async_copy(
+            sheet_ref.at[:, tail : tail + 2 * CTXW], columns.at[:, 6 * D :], local_sem.at[8]
+        ),
+    ]
+    for fetch in fetches:
+        fetch.start()
     group, core, _, _ = near()
     member = group * 2 + core
     plane = lax.axis_index("z")
@@ -1311,6 +1376,9 @@
     peers = plane_peers()
     line = [lax.rem(plane + k, 4) for k in range(1, 4)]
     greet([member_at(peer) for peer in peers] + [{"z": there} for there in line])
+
+    fetches[0].wait()
+    fetches[1].wait()
 
     near_copy = mover(send_sem, recv_sem)
     line_copy = mover(send_sem, recv_sem, 7)
@@ -1356,11 +1424,19 @@
         pl.when(row == plane)(stay.start)
         pl.when(row != plane)(rise(row).start)
 
-    first_done = exchange_steps(
-        block, block, w_ref, wo_ref, local_sem.at[2], mover(send_sem, recv_sem, 14)
-    )
-    second_done = exchange_steps(
-        block, block, v_ref, vo_ref, local_sem.at[5], mover(send_sem, recv_sem, 32)
+    fetches[2].wait()
+    fetches[3].wait()
+
+    def move(m, at, start, width):
+        one[m, :, at : at + width] = columns[:, start : start + width].astype(one.dtype)
+
+    for m in range(8):
+        for k in range(6):
+            move(m, (4 * part if k < 3 else -3 * part) + k * part, k * D + m * part, part)
+        for k in range(2):
+            move(m, 3 * part + k * text, 6 * D + k * CTXW + m * text, text)
+    weights_done = exchange_steps(
+        block, block, one, one_ref, local_sem.at[2], mover(send_sem, recv_sem, 14)
     )
 
     def text_copy(k, peer):
@@ -1413,8 +1489,7 @@
             device_id_type=MESH_ID,
         ).wait_recv()
     stay.wait()
-    first_done()
-    second_done()
+    weights_done()
 
     @pl.when(teacher)
     def _():
@@ -1434,90 +1509,124 @@
         rise(there).wait_send()
 
 
-def opening(local, small, text, first, second):
+def opening(latents, cotangent, small, text, sheet):
+    frames, features = latents.shape
+    local = (frames, 2 * features)
+    one = (8, sheet.shape[0], (6 * D + 2 * CTXW) // 8)
+    low = jnp.bfloat16
     return pl.pallas_call(
         opening_kernel,
         out_shape=(
-            jax.ShapeDtypeStruct(local.shape, local.dtype),
+            jax.ShapeDtypeStruct(local, low),
             jax.ShapeDtypeStruct((4, 8) + small.shape, small.dtype),
             jax.ShapeDtypeStruct((text.shape[0] // 8, text.shape[1]), text.dtype),
-            jax.ShapeDtypeStruct(first.shape, first.dtype),
-            jax.ShapeDtypeStruct(second.shape, second.dtype),
+            jax.ShapeDtypeStruct(one, low),
         ),
         in_specs=[IN_HBM] * 5,
-        out_specs=(IN_HBM,) * 5,
+        out_specs=(IN_HBM,) * 4,
         scratch_shapes=[
-            pltpu.VMEM(local.shape, local.dtype),
-            pltpu.SemaphoreType.DMA((6,)),
-            pltpu.SemaphoreType.DMA((39,)),
-            pltpu.SemaphoreType.DMA((39,)),
+            pltpu.VMEM(local, low),
+            pltpu.VMEM(local, low),
+            pltpu.VMEM((sheet.shape[0], 6 * D + 2 * CTXW), jnp.float32),
+            pltpu.VMEM(one, low),
+            pltpu.SemaphoreType.DMA((9,)),
+            pltpu.SemaphoreType.DMA((32,)),
+            pltpu.SemaphoreType.DMA((32,)),
         ],
         compiler_params=pltpu.CompilerParams(
-            collective_id=identity_of("opening", local), has_side_effects=True
+            collective_id=identity_of("opening", sheet),
+            has_side_effects=True,
+            vmem_limit_bytes=16 * 2**20,
         ),
         cost_estimate=BRIEF,
         name="opening",
-    )(local, small, text, first, second)
+    )(latents, cotangent, small, text, sheet)
 
 
 def first_gather_kernel(
-    x_ref, sheet_ref, o_ref, w_ref, v_ref, local_sem, send_sem, recv_sem
+    x_ref, y_ref, sheet_ref, ox_ref, oy_ref, gu_ref, down_ref, local_sem, send_sem, recv_sem
 ):
     place = member_lanes(x_ref.shape[1])
     width = FF // 8
     greet([member_at(peer) for peer in plane_peers()])
     finish = [
-        gather_steps(place, x_ref, o_ref, local_sem.at[0], mover(send_sem, recv_sem))
+        gather_steps(place, x_ref, ox_ref, local_sem.at[0], mover(send_sem, recv_sem)),
+        gather_steps(place, y_ref, oy_ref, local_sem.at[1], mover(send_sem, recv_sem, 14)),
     ]
-    for k, (ref, start) in enumerate(((w_ref, 0), (w_ref, width), (v_ref, 0))):
+    for k, (ref, start) in enumerate(((gu_ref, 0), (gu_ref, width), (down_ref, 0))):
         source, target = sheet_part(6 * D + k * FF, width), block_part(start, width)
-        copy = mover(send_sem, recv_sem, 14 + 7 * k)
-        finish.append(exchange_steps(source, target, sheet_ref, ref, local_sem.at[1 + k], copy))
+        copy = mover(send_sem, recv_sem, 28 + 7 * k)
+        finish.append(exchange_steps(source, target, sheet_ref, ref, local_sem.at[2 + k], copy))
     for end in finish:
         end()
 
 
-def first_gather(shard, sheet):
+def first_gather(shard, other, sheet):
     rows, width = shard.shape
+    whole = jax.ShapeDtypeStruct((rows, 8 * width), shard.dtype)
     return pl.pallas_call(
         first_gather_kernel,
         out_shape=(
-            jax.ShapeDtypeStruct((rows, 8 * width), shard.dtype),
+            whole,
+            whole,
             jax.ShapeDtypeStruct((8, sheet.shape[0], FF // 4), sheet.dtype),
             jax.ShapeDtypeStruct((8, sheet.shape[0], FF // 8), sheet.dtype),
         ),
-        in_specs=[IN_HBM] * 2,
-        out_specs=(IN_HBM,) * 3,
+        in_specs=[IN_HBM] * 3,
+        out_specs=(IN_HBM,) * 4,
         scratch_shapes=[
-            pltpu.SemaphoreType.DMA((4,)),
-            pltpu.SemaphoreType.DMA((35,)),
-            pltpu.SemaphoreType.DMA((35,)),
+            pltpu.SemaphoreType.DMA((5,)),
+            pltpu.SemaphoreType.DMA((49,)),
+            pltpu.SemaphoreType.DMA((49,)),
         ],
         compiler_params=pltpu.CompilerParams(
             collective_id=identity_of("first gather", shard, sheet), has_side_effects=True
         ),
         cost_estimate=BRIEF,
         name="first_gather",
-    )(shard, sheet)
+    )(shard, other, sheet)
 
 
 def closing_kernel(
-    x_ref,
+    order_ref,
+    y_ref,
+    base_ref,
+    grad_ref,
     w_ref,
     v_ref,
+    gu_ref,
+    down_ref,
     g_ref,
-    q_ref,
     t_ref,
     o_ref,
     vo_ref,
     s_ref,
     all_ref,
+    by_block,
+    sorted_y,
+    base,
+    grad,
+    x_ref,
     held,
     tall,
+    q_ref,
+    one,
+    two,
+    gu,
+    down,
     local_sem,
     send_sem,
     recv_sem,
 ):
+    fetches = [
+        pltpu.make_async_copy(ref, here, local_sem.at[7 + k])
+        for k, (ref, here) in enumerate(
+            [(y_ref, by_block), (base_ref, base), (grad_ref, grad)]
+            + [(w_ref, one), (v_ref, two), (gu_ref, gu), (down_ref, down)]
+        )
+    ]
+    for fetch in fetches:
+        fetch.start()
     group, core, _, _ = near()
     member = group * 2 + core
     plane = lax.axis_index("z")
@@ -1536,17 +1645,15 @@
     gain_plane = mover(send_sem, recv_sem, 17)
     square_plane = mover(send_sem, recv_sem, 24)
     square_line = mover(send_sem, recv_sem, 31)
-    square_local = pltpu.make_async_copy(q_ref, all_ref.at[plane, member], local_sem.at[5])
-    square_local.start()
-    shown = [
-        square_plane(k, q_ref, all_ref.at[plane, member], member_at(peer))
-        for k, peer in enumerate(peers)
-    ]
-    for moving in shown:
-        moving.start()
     gain_local = pltpu.make_async_copy(g_ref, tall.at[plane], local_sem.at[3])
     gain_local.start()
     sent = [gain_line(k, g_ref, tall.at[plane], {"z": there}) for k, there in enumerate(line)]
+    for fetch in fetches[:3]:
+        fetch.wait()
+    reorder_blocks(by_block, sorted_y, lambda b: order_ref[1, b])
+    features = base.shape[0]
+    x_ref[:, :features] = (base[...] + sorted_y[...]).T.astype(x_ref.dtype)
+    x_ref[:, features:] = grad[...].T.astype(x_ref.dtype)
     local = pltpu.make_async_copy(frames(x_ref, plane), frames(held, plane), local_sem.at[0])
     local.start()
     sent += [
@@ -1562,6 +1669,23 @@
         block, block, v_ref, vo_ref, local_sem.at[6], mover(send_sem, recv_sem, 34)
     )
 
+    for fetch in fetches[3:]:
+        fetch.wait()
+    total = jnp.zeros((), jnp.float32)
+    for ref in (one, two, gu, down):
+        line_sum = jnp.zeros((1, ref.shape[2]), jnp.float32)
+        for m in range(8):
+            line_sum += jnp.sum(jnp.square(wide(ref.at[m])), axis=0, keepdims=True)
+        total += jnp.sum(line_sum)
+    q_ref[...] = jnp.full(q_ref.shape, total, jnp.float32)
+    square_local = pltpu.make_async_copy(q_ref, all_ref.at[plane, member], local_sem.at[5])
+    square_local.start()
+    shown = [
+        square_plane(k, q_ref, all_ref.at[plane, member], member_at(peer))
+        for k, peer in enumerate(peers)
+    ]
+    for moving in shown:
+        moving.start()
     gain_local.wait()
     for k, origin in enumerate(back):
         gain_line(k, tall.at[origin], tall.at[origin], {"z": origin}).wait_recv()
@@ -1628,45 +1752,210 @@
         onward(origin).wait_send()
 
 
-def closing(local, weights, others, gains, squares):
+def closing(orders, y, base, grad, one, two, gu, down, gains):
+    features, width = base.shape
+    blocks = orders.shape[1]
+    frames = (width, 2 * features)
+    parts = (one, two, gu, down)
     return pl.pallas_call(
         closing_kernel,
         out_shape=(
-            jax.ShapeDtypeStruct(local.shape, local.dtype),
-            jax.ShapeDtypeStruct(weights.shape, weights.dtype),
-            jax.ShapeDtypeStruct(others.shape, others.dtype),
+            jax.ShapeDtypeStruct(frames, jnp.bfloat16),
+            jax.ShapeDtypeStruct(one.shape, one.dtype),
+            jax.ShapeDtypeStruct(two.shape, two.dtype),
             jax.ShapeDtypeStruct((8,) + gains.shape, gains.dtype),
-            jax.ShapeDtypeStruct((4, 8) + squares.shape, squares.dtype),
+            jax.ShapeDtypeStruct((4, 8, 8, 128), jnp.float32),
         ),
-        in_specs=[IN_HBM] * 5,
+        in_specs=[IN_SMEM] + [IN_HBM] * 8,
         out_specs=(IN_HBM,) * 5,
-        scratch_shapes=[
-            pltpu.VMEM(local.shape, local.dtype),
+        scratch_shapes=[pltpu.VMEM((blocks, features // blocks, width), jnp.float32)]
+        + [pltpu.VMEM(base.shape, jnp.float32)] * 3
+        + [pltpu.VMEM(frames, jnp.bfloat16)] * 2
+        + [
             pltpu.VMEM((5,) + gains.shape, gains.dtype),
-            pltpu.SemaphoreType.DMA((7,)),
+            pltpu.VMEM((8, 128), jnp.float32),
+        ]
+        + [pltpu.VMEM(part.shape, part.dtype) for part in parts]
+        + [
+            pltpu.SemaphoreType.DMA((14,)),
             pltpu.SemaphoreType.DMA((41,)),
             pltpu.SemaphoreType.DMA((41,)),
         ],
         compiler_params=pltpu.CompilerParams(
-            collective_id=identity_of("closing", local), has_side_effects=True
+            collective_id=identity_of("closing", y),
+            has_side_effects=True,
+            vmem_limit_bytes=24 * 2**20,
         ),
         cost_estimate=BRIEF,
         name="closing",
-    )(local, weights, others, gains, squares)
+    )(orders, y.reshape(blocks, -1, width), base, grad, one, two, gu, down, gains)
+
+
+def turned(values, cosine, sine_table):
+    half = HEAD // 2
+    first_half, second_half = values[:half], values[half:]
+    return jnp.concatenate(
+        [
+            first_half * cosine - second_half * sine_table,
+            second_half * cosine + first_half * sine_table,
+        ],
+        axis=0,
+    )
+
+
+def attend_kernel(
+    w_ref, h_ref, cos_ref, sin_ref, seg_ref, column_ref, part_ref, p_ref, o_ref, joint_ref
+):
+    heads, length = joint_ref.shape[1], joint_ref.shape[3]
+    span = heads * HEAD
+    cosine, sine_table = cos_ref[...], sin_ref[...]
+    for k in range(3):
+        by_row = w_ref[:, (4 + k) * span : (5 + k) * span].T
+
+        @pl.loop(0, length // 256)
+        def _(i, k=k, by_row=by_row):
+            at = pl.ds(pl.multiple_of(i * 256, 256), 256)
+            part = jnp.dot(by_row, h_ref[:, at], preferred_element_type=jnp.float32)
+            for h in range(heads):
+                joint_ref[k, h, :, at] = part[h * HEAD : (h + 1) * HEAD]
+
+    for h in range(heads):
+        queries = turned(joint_ref[0, h], cosine, sine_table)
+        part_ref[0, h] = queries.astype(part_ref.dtype)
+        keys = turned(joint_ref[1, h], cosine, sine_table)
+        part_ref[1, h] = keys.astype(part_ref.dtype)
+        part_ref[2, h] = joint_ref[2, h].astype(part_ref.dtype)
+        by_key = keys.T.astype(part_ref.dtype)
+
+        @pl.loop(0, length // 256)
+        def _(i, h=h, by_key=by_key):
+            at = pl.ds(pl.multiple_of(i * 256, 256), 256)
+            scores = jnp.dot(
+                by_key, part_ref[0, h, :, at], preferred_element_type=jnp.float32
+            ) * (HEAD**-0.5)
+            scores = jnp.where(column_ref[...] == seg_ref[:, at], scores, MASKED_SCORE)
+            exponent = jnp.exp(scores - jnp.max(scores, axis=0, keepdims=True))
+            probs = exponent * (1.0 / jnp.sum(exponent, axis=0, keepdims=True))
+            p_ref[h, :, at] = probs.astype(p_ref.dtype)
+            out = jnp.dot(part_ref[2, h], p_ref[h, :, at], preferred_element_type=jnp.float32)
+            o_ref[h * HEAD : (h + 1) * HEAD, at] = out.astype(o_ref.dtype)
+
+
+def attend(weight, frames, cosine, sine_table, segments):
+    heads, length = D // HEAD // 8, frames.shape[1]
+    joint = (3, heads, HEAD, length)
+    small = jnp.bfloat16
+    return pl.pallas_call(
+        attend_kernel,
+        out_shape=(
+            jax.ShapeDtypeStruct(joint, small),
+            jax.ShapeDtypeStruct((heads, length, length), small),
+            jax.ShapeDtypeStruct((heads * HEAD, length), small),
+        ),
+        in_specs=[IN_VMEM] * 6,
+        out_specs=(IN_VMEM,) * 3,
+        scratch_shapes=[pltpu.VMEM(joint, jnp.float32)],
+        compiler_params=pltpu.CompilerParams(vmem_limit_bytes=32 * 2**20),
+        name="attend",
+    )(weight, frames, cosine, sine_table, segments[None, :], segments[:, None])
+
+
+def attend_back_kernel(part_ref, p_ref, grad_ref, cos_ref, sin_ref, o_ref, dq_ref, dk_ref, dv_ref):
+    heads, length = part_ref.shape[1], part_ref.shape[3]
+    cosine, sine_table = cos_ref[...], -sin_ref[...]
+    scale = HEAD**-0.5
+    for h in range(heads):
+        of = slice(h * HEAD, (h + 1) * HEAD)
+        by_key = wide(part_ref.at[2, h]).T.astype(part_ref.dtype)
+        dk_ref[...] = jnp.zeros_like(dk_ref)
+        dv_ref[...] = jnp.zeros_like(dv_ref)
+
+        @pl.loop(0, length // 256)
+        def _(i, h=h, of=of, by_key=by_key):
+            at = pl.ds(pl.multiple_of(i * 256, 256), 256)
+            grad_out = grad_ref[of, at]
+            grad_probs = jnp.dot(by_key, grad_out, preferred_element_type=jnp.float32)
+            low_probs = p_ref[h, :, at]
+            probs = low_probs.astype(jnp.float32)
+            weighted = jnp.sum(probs * grad_probs, axis=0, keepdims=True)
+            grad_scores = (probs * (grad_probs - weighted)).astype(part_ref.dtype)
+            dq_ref[:, at] = jnp.dot(
+                part_ref[1, h], grad_scores, preferred_element_type=jnp.float32
+            )
+            dk_ref[...] += contract_last(part_ref[0, h, :, at], grad_scores)
+            dv_ref[...] += contract_last(grad_out, low_probs)
+
+        span = heads * HEAD
+        grad_queries = turned(dq_ref[...] * scale, cosine, sine_table)
+        grad_keys = turned(dk_ref[...] * scale, cosine, sine_table)
+        o_ref[of, :] = grad_queries.astype(o_ref.dtype)
+        o_ref[span + of.start : span + of.stop, :] = grad_keys.astype(o_ref.dtype)
+        o_ref[2 * span + of.start : 2 * span + of.stop, :] = dv_ref[...].astype(o_ref.dtype)
+
+
+def attend_back(parts, probs, grad, cosine, sine_table):
+    _, heads, _, length = parts.shape
+    return pl.pallas_call(
+        attend_back_kernel,
+        out_shape=jax.ShapeDtypeStruct((3 * heads * HEAD, length), jnp.bfloat16),
+        in_specs=[IN_VMEM] * 5,
+        out_specs=IN_VMEM,
+        scratch_shapes=[pltpu.VMEM((HEAD, length), jnp.float32)] * 3,
+        compiler_params=pltpu.CompilerParams(vmem_limit_bytes=32 * 2**20),
+        name="attend_back",
+    )(parts, probs, grad, cosine, sine_table)
 
 
 def update_kernel(
-    scale_ref, rate_ref, one_ref, two_ref, feed_ref, gain_ref, sheet_ref, first_ref, second_ref, *refs
+    block_ref,
+    rate_ref,
+    one_ref,
+    two_ref,
+    feed_ref,
+    all_ref,
+    gain_ref,
+    sheet_ref,
+    first_ref,
+    second_ref,
+    grad_out,
+    first_out,
+    second_out,
+    sheet_out,
+    copy_out,
+    norm_out,
+    gain_out,
+    grad,
+    gain,
+    scale,
 ):
-    grad_out, first_out, second_out, sheet_out, copy_out, grad = refs
     step = pl.program_id(0)
     part = D // 8
     text = CTXW // 8
+
+    @pl.when(step == 0)
+    def _():
+        summed = jnp.sum(gain_ref[...], axis=0)
+        rows = grad.shape[0]
+        here = lax.broadcasted_iota(jnp.int32, (rows, D), 1) == (
+            lax.broadcasted_iota(jnp.int32, (rows, D), 0) + block_ref[0] * rows
+        )
+        gain[...] = lax.dot_general(
+            here.astype(jnp.float32),
+            summed,
+            (((1,), (1,)), ((), ())),
+            precision=HIGHEST,
+            preferred_element_type=jnp.float32,
+        )
+        norm = jnp.sqrt(jnp.sum(all_ref[:, :, 0:1, 0:1]) + jnp.sum(summed * summed))
+        norm_out[0] = norm
+        scale[0] = 1.0 / jnp.maximum(norm, 1.0)
+        gain_out[...] = gain[...] * scale[0]
+
     for k in range(6):
 
         @pl.when(step == k)
         def _(k=k):
-            ref, start = (one_ref, k * part) if k < 4 else (two_ref, (k - 4) * part)
+            ref, start = (one_ref, k * part) if k < 3 else (two_ref, (k - 3) * part)
             for m in range(8):
                 grad[:, m * part : (m + 1) * part] = wide(ref.at[m, :, start : start + part])
 
@@ -1678,20 +1967,20 @@
     def _():
         for m in range(8):
             for k in range(2):
-                start = 2 * part + k * text
+                start = 3 * part + k * text
                 place = k * CTXW + m * text
                 grad[:, place : place + text] = wide(two_ref.at[m, :, start : start + text])
 
     @pl.when(step == 19)
     def _():
-        grad[:, :128] = gain_ref[...]
-
-    clipped = grad[...] * scale_ref[0]
+        grad[:, :8] = gain[...]
+
+    clipped = grad[...] * scale[0]
     sheet = sheet_ref[...]
     first_new = BETA_ONE * first_ref[...] + (1.0 - BETA_ONE) * clipped
     second_new = BETA_TWO * second_ref[...] + (1.0 - BETA_TWO) * clipped * clipped
-    mean_hat = first_new / (1.0 - BETA_ONE**STEP)
-    square_hat = second_new / (1.0 - BETA_TWO**STEP)
+    mean_hat = first_new * (1.0 / (1.0 - BETA_ONE**STEP))
+    square_hat = second_new * (1.0 / (1.0 - BETA_TWO**STEP))
     sheet_new = sheet - rate_ref[step] * (
         mean_hat / (jnp.sqrt(square_hat) + EPS_ADAM) + WEIGHT_DECAY * sheet
     )
@@ -1702,36 +1991,44 @@
     copy_out[...] = sheet_new.astype(copy_out.dtype)
 
 
-def sheet_update(scale, length, one, two, feed_part, gains, sheet, first, second):
+def sheet_update(block_index, length, one, two, feed_part, squares, gains, sheet, first, second):
     rows = sheet.shape[0]
     rates = column_spread(length)[jnp.minimum(jnp.arange(20) * D, SHEET - 1)]
     column_block = pl.BlockSpec((rows, D), lambda i: (0, i))
     like = jax.ShapeDtypeStruct(sheet.shape, sheet.dtype)
+
+    def whole(array):
+        return pl.BlockSpec(array.shape, lambda i: (0,) * array.ndim)
+
+    sheet, first, second = (
+        pltpu.with_memory_space_constraint(array, pltpu.HBM) for array in (sheet, first, second)
+    )
     return pl.pallas_call(
         update_kernel,
         grid=(20,),
-        out_shape=(like, like, like, like, jax.ShapeDtypeStruct(sheet.shape, jnp.bfloat16)),
+        out_shape=(like, like, like, like, jax.ShapeDtypeStruct(sheet.shape, jnp.bfloat16))
+        + (jax.ShapeDtypeStruct((1,), jnp.float32), jax.ShapeDtypeStruct((rows, 8), jnp.float32)),
         in_specs=[
             IN_SMEM,
             IN_SMEM,
-            pl.BlockSpec(one.shape, lambda i: (0, 0, 0)),
-            pl.BlockSpec(two.shape, lambda i: (0, 0, 0)),
+            whole(one),
+            whole(two),
             pl.BlockSpec((rows, D), lambda i: (0, jnp.clip(i - 6, 0, 11))),
-            pl.BlockSpec(gains.shape, lambda i: (0, 0)),
+            whole(squares),
+            whole(gains),
             column_block,
             column_block,
             column_block,
         ],
-        out_specs=(column_block,) * 5,
-        scratch_shapes=[pltpu.VMEM((rows, D), jnp.float32)],
+        out_specs=(column_block,) * 5 + (IN_SMEM, pl.BlockSpec((rows, 8), lambda i: (0, 0))),
+        scratch_shapes=[
+            pltpu.VMEM((rows, D), jnp.float32),
+            pltpu.VMEM((rows, 8), jnp.float32),
+            pltpu.SMEM((1,), jnp.float32),
+        ],
         compiler_params=pltpu.CompilerParams(vmem_limit_bytes=24 * 2**20),
         name="sheet_update",
-    )(scale.reshape(1), rates, one, two, feed_part, gains, sheet, first, second)
-
-
-def split_columns(block, members):
-    rows, columns = block.shape
-    return block.reshape(rows, members, columns // members)
+    )(block_index, rates, one, two, feed_part, squares, gains, sheet, first, second)
 
 
 def pick_blocks(blocks, order):
@@ -1789,41 +2086,24 @@
     to_slots = jnp.take(owners, slot)
 
     orders = jnp.stack([to_slots, to_logical])
-    low_sheet = sheet.astype(jnp.bfloat16)
-
-    def columns_of(start, width):
-        return split_columns(low_sheet[:, start : start + width], members)
-
-    def member_blocks(*pieces):
-        return jnp.swapaxes(jnp.concatenate(pieces, axis=2), 0, 1)
-
-    blocks_qkv = member_blocks(*[columns_of(k * D, D) for k in range(3)])
-    blocks_two = member_blocks(
-        columns_of(3 * D, D),
-        columns_of(4 * D, D),
-        columns_of(5 * D, D),
-        columns_of(tail_col, CTXW),
-        columns_of(tail_col + CTXW, CTXW),
-    )
     small = jnp.concatenate(
         [
-            jnp.pad(low_sheet[:, gain_col:].astype(jnp.float32).T, ((0, 0), (0, 64 - rows))),
+            jnp.pad(
+                sheet[:, gain_col:].astype(jnp.bfloat16).astype(jnp.float32).T,
+                ((0, 0), (0, 64 - rows)),
+            ),
             jnp.pad(clip_starts.astype(jnp.float32), ((0, 7), (0, 64 - clip_starts.shape[1]))),
         ],
         axis=1,
     )
-    both, small, text_mine, mine_qkv, mine_two = opening(
-        jnp.concatenate([latents[0], cotangent[0]], axis=1),
-        small,
-        context[0].T,
-        blocks_qkv,
-        blocks_two,
-    )
-    weight_qkv = gather_slots(mine_qkv)
-    weight_two = gather_line(mine_two, to_logical)
-    weight_ao = weight_two[:, :span]
+    both, small, text_mine, mine_one = opening(
+        latents[0], cotangent[0], small, context[0].T, sheet
+    )
+    mine_one, later = lax.optimization_barrier((mine_one, sheet))
+    low_sheet = later.astype(jnp.bfloat16)
+    weight_one = gather_slots(mine_one)
+    weight_two = sort_blocks(weight_one[:, : 4 * span], to_logical)
     weight_cq = weight_two[:, span : 2 * span]
-    weight_co = weight_two[:, 2 * span : 3 * span]
     weight_text = weight_two[:, 3 * span :]
     gains = pick_blocks(small[..., :rows].reshape(blocks, 8, rows), to_logical)
     gains = gains.swapaxes(1, 2).reshape(D, 8)
@@ -1848,32 +2128,24 @@
     place = jnp.arange(length, dtype=jnp.int32).reshape(planes, cores, groups, rest)
     positions = place.transpose(2, 1, 0, 3).reshape(-1)
     segments = segment_ids(starts, positions)
-    same_clip = segments[:, None] == segments[None, :]
     frequency = jnp.exp(
         -math.log(10000.0) * jnp.arange(HEAD // 2, dtype=jnp.float32) / (HEAD // 2)
     )
     angles = frequency[:, None] * positions.astype(jnp.float32)[None, :]
-    cosine = jnp.cos(angles)[None]
-    sine_table = jnp.sin(angles)[None]
+    cosine = jnp.cos(angles)
+    sine_table = jnp.sin(angles)
 
     normed_one, inverse_one = norm_columns(tokens)
     scaled_one = gain_one * time_gain
-    h_one, mine_gu, mine_down = first_gather(
-        sort_blocks((normed_one * scaled_one).astype(jnp.bfloat16), to_slots), low_sheet
+    h_one, grad_ff, mine_gu, mine_down = first_gather(
+        sort_blocks((normed_one * scaled_one).astype(jnp.bfloat16), to_slots),
+        sort_blocks(grad_out.astype(jnp.bfloat16), to_slots),
+        low_sheet,
     )
     weight_gu = gather_slots(mine_gu)
     line_down = gather_slots(mine_down)
 
-    joint = contract_rows(weight_qkv, h_one).reshape(3, head_count, HEAD, length)
-    queries = rotate_columns(joint[0], cosine, sine_table).astype(jnp.bfloat16)
-    keys = rotate_columns(joint[1], cosine, sine_table).astype(jnp.bfloat16)
-    values = joint[2].astype(jnp.bfloat16)
-    scores = (
-        jnp.einsum("hdq,hdk->hqk", queries, keys, preferred_element_type=jnp.float32) * score_scale
-    )
-    attn_probs = softmax_rows(jnp.where(same_clip[None], scores, MASKED_SCORE))
-    probs_low = attn_probs.astype(jnp.bfloat16)
-    attn_out = jnp.einsum("hqk,hdk->hdq", probs_low, values, preferred_element_type=jnp.float32)
+    parts, probs, attn_out = attend(weight_one, h_one, cosine, sine_table, segments)
     text_width = CTXW // members
     text_kv = jnp.stack(
         [
@@ -1884,9 +2156,10 @@
     ).reshape(D, 2 * CTX)
     attn_out, x_one, normed_two, inverse_two, h_two, text_kv = project(
         "sum",
+        0,
         orders,
-        attn_out.reshape(span, length).astype(jnp.bfloat16),
-        weight_ao,
+        attn_out,
+        weight_two,
         tokens,
         gain_two,
         text_kv.astype(jnp.bfloat16),
@@ -1905,14 +2178,14 @@
     cross_out = jnp.einsum(
         "hqk,hdk->hdq", cross_low, text_values, preferred_element_type=jnp.float32
     )
-    cross_out, x_two, normed_three, inverse_three, h_three, grad_ff = project(
-        "gather",
+    cross_out, x_two, normed_three, inverse_three, h_three = project(
+        "slots",
+        2 * span,
         orders,
         cross_out.reshape(span, length).astype(jnp.bfloat16),
-        weight_co,
+        weight_two,
         x_one,
         gain_three,
-        sort_blocks(grad_out.astype(jnp.bfloat16), to_slots),
     )
 
     gate_up = contract_rows(weight_gu, h_three)
@@ -1942,7 +2215,7 @@
     grad_blocks_gu = as_blocks(grad_weight_gu, to_slots)
     sums_gu = scatter_line(grad_blocks_gu)
     grad_cross_out, grad_weight_co = back(
-        orders, weight_co, grad_cross, cross_out
+        orders, weight_two, grad_cross, cross_out, column=2 * span
     )
     grad_cross_out = grad_cross_out.reshape(head_count, HEAD, length)
     grad_cross_probs = jnp.einsum(
@@ -1969,77 +2242,44 @@
     )
     grad_x_one, grad_weight_cq, sum_two, grad_attn, grad_text = back(
         orders,
-        weight_cq,
+        weight_two,
         grad_cross_q,
         h_two,
         (normed_two, inverse_two, gain_two, grad_x_two),
+        column=span,
         send_rows=True,
         text=grad_text.astype(jnp.bfloat16),
         after=[sums_down],
     )
-    grad_text = sort_blocks(grad_text, to_slots)
-    grad_weight_text = [
-        contract_last(grad_text[:, :CTX], text_mine),
-        contract_last(grad_text[:, CTX:], text_mine),
-    ]
-    grad_blocks_two = as_blocks(
-        jnp.concatenate(
-            [grad_weight_cq, grad_weight_co]
-            + [grad.astype(jnp.bfloat16) for grad in grad_weight_text],
-            axis=1,
-        ),
-        to_slots,
-    )
+    grad_attn_out, grad_weight_two = back(
+        orders,
+        weight_two,
+        grad_attn,
+        attn_out,
+        beside=(grad_weight_cq, grad_weight_co, grad_text, text_mine),
+    )
+    grad_blocks_two = as_blocks(grad_weight_two, to_slots)
     sums_two = scatter_line(grad_blocks_two)
-    grad_attn_out, grad_weight_ao = back(
-        orders, weight_ao, grad_attn, attn_out, after=[grad_blocks_two]
-    )
-    grad_attn_out = grad_attn_out.reshape(head_count, HEAD, length)
-    grad_probs = jnp.einsum(
-        "hdq,hdk->hqk", grad_attn_out, values, preferred_element_type=jnp.float32
-    )
-    grad_scores = (
-        attn_probs * (grad_probs - jnp.sum(attn_probs * grad_probs, axis=-1, keepdims=True))
-    ).astype(jnp.bfloat16)
-    grad_queries = (
-        jnp.einsum("hqk,hdk->hdq", grad_scores, keys, preferred_element_type=jnp.float32)
-        * score_scale
-    )
-    grad_keys = (
-        jnp.einsum("hqk,hdq->hdk", grad_scores, queries, preferred_element_type=jnp.float32)
-        * score_scale
-    )
-    grad_values = jnp.einsum(
-        "hqk,hdq->hdk", probs_low, grad_attn_out, preferred_element_type=jnp.float32
-    )
-    grad_qkv = jnp.stack(
-        [
-            rotate_columns(grad_queries, cosine, -sine_table),
-            rotate_columns(grad_keys, cosine, -sine_table),
-            grad_values,
-        ]
-    )
-    grad_qkv = grad_qkv.reshape(3 * span, length).astype(jnp.bfloat16)
+    grad_qkv = attend_back(parts, probs, grad_attn_out, cosine, sine_table)
     latent_grad, grad_weight_qkv, sum_one = back(
         orders,
-        weight_qkv,
+        weight_one,
         grad_qkv,
         h_one,
         (normed_one, inverse_one, scaled_one, grad_x_one),
+        column=4 * span,
         in_slots=True,
         after=[sums_gu],
     )
-    grad_blocks_one = as_blocks(
-        jnp.concatenate([grad_weight_qkv, grad_weight_ao], axis=1), to_slots
-    )
+    grad_blocks_one = as_blocks(grad_weight_qkv, to_slots)
     sums_one = scatter_line(grad_blocks_one)
     sums_feed, ff_out = feed(
         sums_gu,
         sums_down,
-        matmul(weight_down, hidden).astype(jnp.bfloat16),
+        weight_down,
+        hidden,
         [grad_blocks_one],
     )
-    result = x_two + sort_blocks(ff_out, to_logical)
     sum_one = sum_one[0:1]
     grad_gain_one = sum_one * time_gain.T
     grad_time = sum_one * gain_one.T
@@ -2052,33 +2292,20 @@
         ],
         axis=0,
     )
-    squares = sum(
-        jnp.sum(jnp.square(part.astype(jnp.float32)))
-        for part in (sums_gu, sums_down, sums_two, sums_one)
-    )
     out_pair, sums_one, sums_two, gain_sums, squares = closing(
-        jnp.concatenate([result.T, latent_grad.T], axis=1).astype(jnp.bfloat16),
-        sums_one,
-        sums_two,
-        gain_grads,
-        jnp.pad(squares.reshape(1, 1), ((0, 7), (0, 127))),
+        orders, ff_out, x_two, latent_grad, sums_one, sums_two, sums_gu, sums_down, gain_grads
     )
     output = out_pair[:, :D]
     latent_grad = out_pair[:, D:].astype(jnp.float32)
     place = lax.axis_index("dp") * (planes * cores) + plane * cores + lax.axis_index("core")
-    gain_sums = jnp.sum(gain_sums, axis=0)
-    grad_norm = jnp.sqrt(jnp.sum(squares) + jnp.sum(gain_sums * gain_sums))
-    scale = 1.0 / jnp.maximum(grad_norm, 1.0)
-    gain_sums = lax.dynamic_index_in_dim(
-        gain_sums.reshape(8, blocks, rows), owners[place], 1, False
-    ).T
-    clipped, first_new, second_new, sheet_new, sheet_copy = sheet_update(
-        scale,
+    clipped, first_new, second_new, sheet_new, sheet_copy, grad_norm, gain_grad = sheet_update(
+        lax.dynamic_slice_in_dim(owners, place, 1),
         length,
         sums_one,
         sums_two,
         sums_feed,
-        jnp.pad(gain_sums, ((0, 0), (0, 120))),
+        squares,
+        gain_sums,
         sheet,
         first,
         second,
@@ -2086,9 +2313,9 @@
     return (
         output[None],
         latent_grad[None],
-        grad_norm,
+        grad_norm[0],
         clipped,
-        gain_sums * scale,
+        gain_grad,
         first_new,
         second_new,
         sheet_new,

time: 669 us -> 612 us (0.915)
  matrix products: 79.5 us -> 30.6 us
  Pallas kernels: 399 us -> 444 us
  other arithmetic: 51 us -> 19 us
  local copies, waits for them, and re-layouts: 95.1 us -> 80.2 us
  between operations: 23.7 us -> 16.1 us
    pallas_call x5 -> x7, Pallas kernels: 214 us -> 254 us  [the longest x2 92.5 us: project(): pl.pallas_call(functools.partial(project_kernel, kind, column), out_shape...]
    dot_general x5 -> x0, matrix products: 22 us -> none  [the longest x1 10.2 us: plane_plan(): jnp.einsum('hdq,hdk->hqk', grad_attn_out, values, preferred_element_type=...]
    sub x2 -> x1, matrix products: 12.9 us -> 3.41 us  [softmax_rows(): exponent = jnp.exp(scores - row_max)]
    reduce_sum x7 -> x0, other arithmetic: 9.41 us -> none  [the longest x4 6.15 us: plane_plan(): jnp.sum(jnp.square(part.astype(jnp.float32)))]
    dot_general x3 -> x2, matrix products: 9.46 us -> 0.78 us  [matmul(): return jnp.dot(left, right, preferred_element_type=jnp.float32)]
    pallas_call x1, Pallas kernels: 17 us -> 24.9 us  [sheet_update(): pl.pallas_call(update_kernel, grid=(20,), out_shape=(like, like, like, li...]
    all_gather x1 -> x0, waiting for transfers between devices: 7.51 us -> none  [gather_line(): blocks = lax.all_gather(mine, 'z', axis=0, tiled=True)]
    reduce_scatter x4, waiting for transfers between devices: 0.05 us -> 7.5 us  [scatter_line(): return lax.psum_scatter(blocks, 'z', scatter_dimension=0, tiled=True)]
  transfers between devices with their start and end apart: 8 -> 7, of which waited for: 1 -> 2; matrix products, arithmetic and copies ran while one was open for 22% -> 11% of each run, Pallas kernels for 49% -> 59%
where the time goes in v4:
time: 612 us; the launch traced here: 601 us
  Pallas kernels  444 us (73%)
  local copies, waits for them, and re-layouts  80.2 us (13%)
  matrix products  30.6 us (5%)
  other arithmetic  19 us (3%)
  between operations  16.1 us (3%)
  waiting for transfers between devices  11.4 us (2%)
    pallas_call x5, Pallas kernels, back(): pl.pallas_call(functools.partial(back_kernel, plan), out_shape=tuple(outs...  128 us
    pallas_call x2, Pallas kernels, project(): pl.pallas_call(functools.partial(project_kernel, kind, column), out_shape...  92.5 us
    pallas_call x1, Pallas kernels, first_gather(): pl.pallas_call(first_gather_kernel, out_shape=(whole, whole, jax.ShapeDty...  62.4 us
    unnamed x161, local copies, waits for them, and re-layouts  60.5 us
    pallas_call x1, Pallas kernels, feed(): pl.pallas_call(feed_kernel, out_shape=(jax.ShapeDtypeStruct((gu.shape[1],...  36.7 us
    pallas_call x1, Pallas kernels, closing(): pl.pallas_call(closing_kernel, out_shape=(jax.ShapeDtypeStruct(frames, jn...  35.5 us
    pallas_call x1, Pallas kernels, opening(): pl.pallas_call(opening_kernel, out_shape=(jax.ShapeDtypeStruct(local, low...  31 us
    pallas_call x1, Pallas kernels, sheet_update(): pl.pallas_call(update_kernel, grid=(20,), out_shape=(like, like, like, li...  24.9 us
  transfers between devices with their start and end apart: 7, of which 2 were waited for; matrix products, arithmetic and copies ran while one was open for 11% of the time, Pallas kernels for 59%

profile of v4, /device:TPU:0, one launch (start us, length us, event | category | flops | bytes accessed | tf_op | source)
XLA Modules:
  0.0 601.2 jit_solution(9477870171806973826)
XLA Ops:
  14.5 31.0 %opening.1 = (bf16[128,3072]{1,0:T(8,128)(2,1)S(1)}, f32[4,8,8,128]{3,2,1,0:T(8,128)S(1)}, bf16[96,128]{1,0:T(8,128)(2,1)S(1)}, bf16[8,48,1344]{2,1,0:T(8,128)(2,1)}) custom-call(bf16[128,1536]{1,0:T(8,128)(2,1)S(1)} %bitcast.120, bf16[128,1536]{1,0:T(8,128)(2,1)S(1)} %bitcast.121, f32[8,128]{1,0:T(8,128)S(1)} %select_maximum_fusion.small_ref, ...), custom_call_target="tpu_custom_call" | custom-call | bytes 1024 | tf_op jit(solution)/shard_map/opening/pallas_call | solution.py:1517
  59.9 4.7 convert_element_type.102.sheet_ref
  64.7 62.4 %first_gather.1 = (bf16[1536,1024]{1,0:T(8,128)(2,1)}, bf16[1536,1024]{1,0:T(8,128)(2,1)}, bf16[8,48,1536]{2,1,0:T(8,128)(2,1)}, bf16[8,48,768]{2,1,0:T(8,128)(2,1)}) custom-call(bf16[1536,128]{1,0:T(8,128)(2,1)} %bitcast.138, bf16[1536,128]{1,0:T(8,128)(2,1)} %bitcast.137, bf16[48,29192]{1,0:T(8,128)(2,1)} %convert_element_type.102.sheet_ref), custom_call_target="tpu_custom_call" | custom-call | bytes 1024 | tf_op jit(solution)/shard_map/first_gather/pallas_call | solution.py:1567
  130.7 3.2 all-gather.8.cloned.1.call-done
  133.9 3.2 slice.111
  149.0 17.7 %attend.1 = (bf16[3,3,64,1024]{3,2,1,0:T(8,128)(2,1)S(1)}, bf16[3,1024,1024]{2,1,0:T(8,128)(2,1)S(1)}, bf16[192,1024]{1,0:T(8,128)(2,1)S(1)}) custom-call(bf16[1536,1344]{1,0:T(8,128)(2,1)S(1)} %bitcast.107, bf16[1536,1024]{1,0:T(8,128)(2,1)S(1)} %copy-done.2, f32[32,1024]{1,0:T(8,128)S(1)} %get-tuple-element.192.cos_ref, ...), custom_call_target="tpu_custom_call" | custom-call | tf_op jit(solution)/shard_map/attend/pallas_call | solution.py:1848
  169.3 47.8 %project_sum.1 = (bf16[1536,1024]{1,0:T(8,128)(2,1)S(1)}, f32[1536,128]{1,0:T(8,128)S(1)}, f32[1536,128]{1,0:T(8,128)S(1)}, f32[1,128]{1,0:T(1,128)S(1)}, bf16[1...) custom-call(s32[2,32]{1,0:T(2,128)S(1)} %pad_add_fusion.order_ref.refs_0_, ...), custom_call_target="tpu_custom_call" | custom-call | bytes 1024 | tf_op jit(solution)/shard_map/project_sum/pallas_call | solution.py:865
  223.0 2.8 convolution_convert_fusion.3
  225.8 3.4 fusion.27
  231.1 44.7 %project_slots.1 = (bf16[1536,1024]{1,0:T(8,128)(2,1)S(1)}, f32[1536,128]{1,0:T(8,128)S(1)}, f32[1536,128]{1,0:T(8,128)S(1)}, f32[1,128]{1,0:T(1,128)S(1)}, bf16[1536,1024]{1,0:T(8,128)(2,1)S(1)}) custom-call(s32[2,32]{1,0:T(2,128)S(1)} %pad_add_fusion.order_ref.refs_0_, bf16[192,1024]{1,0:T(8,128)(2,1)S(1)} %bitcast.122, bf16[1536,768]{1,0:T(8,128)(2,1)S(1)} %bitcast.101, ...), custom_call_target="tpu_custom_call" | custom-call | bytes 1024 | tf_op jit(solution)/shard_map/project_slots/pallas_call | solution.py:865
  281.0 8.1 %fusion.28 = f32[1536,1024]{1,0:T(8,128)S(1)} fusion(bf16[1536,1536]{1,0:T(8,128)(2,1)} %bitcast.131, bf16[1536,1024]{1,0:T(8,128)(2,1)} %copy-done.21), kind=kOutput, calls=%fused_computation.116 | convolution fusion | flops 4831838208 | bytes 14155776 | tf_op jit(solution)/shard_map/dot_general | solution.py:430
  293.2 3.9 convolution_convert_fusion
  298.4 8.4 %multiply_convert_fusion.1 = (bf16[768,1024]{1,0:T(8,128)(2,1)S(1)}, bf16[768,1024]{1,0:T(8,128)(2,1)S(1)}) fusion(f32[1536,1024]{1,0:T(8,128)} %copy-done.64, bf16[1536,768]{1,0:T(8,128)(2,1)} %bitcast.114, bf16[1536,1024]{1,0:T(8,128)(2,1)} %get-tuple-element.72), kind=kOutput, calls=%fused_computation.11 | convolution fusion | flops 2426142720 | bytes 14942208 | tf_op jit(solution)/shard_map/dot_general | solution.py:430
  308.8 30.8 %back.5 = (f32[1536,128]{1,0:T(8,128)S(1)}, bf16[1536,1536]{1,0:T(8,128)(2,1)}, f32[8,1536]{1,0:T(8,128)S(1)}, bf16[192,1024]{1,0:T(8,128)(2,1)S(1)}) custom-call(s32[2,32]{1,0:T(2,128)S(1)} %pad_add_fusion.order_ref.refs_0_, bf16[1536,1536]{1,0:T(8,128)(2,1)} %bitcast.132, bf16[1536,1024]{1,0:T(8,128)(2,1)S(1)} %pad_maximum_fusion.refs_2_, ...), custom_call_target="tpu_custom_call" | custom-call | bytes 1024 | tf_op jit(solution)/shard_map/back/pallas_call | solution.py:1159
  343.1 20.6 %back.6 = (bf16[192,1024]{1,0:T(8,128)(2,1)S(1)}, bf16[1536,192]{1,0:T(8,128)(2,1)S(1)}) custom-call(s32[2,32]{1,0:T(2,128)S(1)} %pad_add_fusion.order_ref.refs_0_, bf16[1536,768]{1,0:T(8,128)(2,1)S(1)} %bitcast.102, bf16[192,1024]{1,0:T(8,128)(2,1)S(1)} %get-tuple-element.88.refs_2_, bf16[32,48,1024]{2,1,0:T(8,128)(2,1)S(1)} %bitcast.112), custom_call_target="tpu_custom_call" | custom-call | bytes 1024 | tf_op jit(solution)/shard_map/back/pallas_call | solution.py:1159
  371.7 31.9 %back.7 = (f32[1536,128]{1,0:T(8,128)S(1)}, bf16[1536,192]{1,0:T(8,128)(2,1)S(1)}, f32[8,1536]{1,0:T(8,128)S(1)}, bf16[192,1024]{1,0:T(8,128)(2,1)S(1)}, bf16[1536,256]{1,0:T(8,128)(2,1)S(1)}) custom-call(s32[2,32]{1,0:T(2,128)S(1)} %pad_add_fusion.order_ref.refs_0_, bf16[1536,768]{1,0:T(8,128)(2,1)S(1)} %bitcast.103, bf16[192,1024]{1,0:T(8,128)(2,1)S(1)} %bitcast.116, ...), custom_call_target="tpu_custom_call" | custom-call | bytes 1024 | tf_op jit(solution)/shard_map/back/pallas_call | solution.py:1159
  404.4 20.9 %back.8 = (bf16[192,1024]{1,0:T(8,128)(2,1)S(1)}, bf16[1536,768]{1,0:T(8,128)(2,1)S(1)}) custom-call(s32[2,32]{1,0:T(2,128)S(1)} %pad_add_fusion.order_ref.refs_0_, bf16[1536,768]{1,0:T(8,128)(2,1)S(1)} %bitcast.104, bf16[192,1024]{1,0:T(8,128)(2,1)S(1)} %get-tuple-element.94.refs_2_, bf16[32,48,1024]{2,1,0:T(8,128)(2,1)} %bitcast.110, ...), custom_call_target="tpu_custom_call" | custom-call | bytes 1024 | tf_op jit(solution)/shard_map/back/pallas_call | solution.py:1159
  428.1 2.8 copy-done.9
  430.9 15.3 %attend_back.1.refs_2_ = bf16[576,1024]{1,0:T(8,128)(2,1)S(1)} custom-call(bf16[3,3,64,1024]{3,2,1,0:T(8,128)(2,1)S(1)} %copy-done.34, bf16[3,1024,1024]{2,1,0:T(8,128)(2,1)S(1)} %copy-done.9, bf16[192,1024]{1,0:T(8,128)(2,1)S(1)} %get-tuple-element.99.grad_ref, f32[32,1024]{1,0:T(8,128)S(1)} %copy-done.32, f32[32,1024]{1,0:T(8,128)S(1)} %copy-done.30), custom_call_target="tpu_custom_call" | custom-call | tf_op jit(solution)/shard_map/attend_back/pallas_call | solution.py:1898
  450.9 23.5 %back.9 = (f32[1536,128]{1,0:T(8,128)S(1)}, bf16[1536,576]{1,0:T(8,128)(2,1)}, f32[8,1536]{1,0:T(8,128)S(1)}) custom-call(s32[2,32]{1,0:T(2,128)S(1)} %pad_add_fusion.order_ref.refs_0_, bf16[1536,1344]{1,0:T(8,128)(2,1)} %bitcast.106, bf16[576,1024]{1,0:T(8,128)(2,1)S(1)} %attend_back.1.refs_2_, bf16[1536,1024]{1,0:T(8,128)(2,1)} %get-tuple-element.74.h_ref.refs_3_, ...), custom_call_target="tpu_custom_call" | custom-call | bytes 1024 | tf_op jit(solution)/shard_map/back/pallas_call | solution.py:1159
  479.9 36.7 %feed.1 = (bf16[48,18432]{1,0:T(8,128)(2,1)S(1)}, f32[1536,128]{1,0:T(8,128)S(1)}) custom-call(bf16[8,48,1536]{2,1,0:T(8,128)(2,1)S(1)} %copy-done.4, bf16[8,48,768]{2,1,0:T(8,128)(2,1)S(1)} %copy-done.13, bf16[1536,768]{1,0:T(8,128)(2,1)S(1)} %bitcast.115, bf16[768,1024]{1,0:T(8,128)(2,1)S(1)} %copy-done.11, bf16[32,48,576]{2,1,0:T(8,128)(2,1)} %bitcast.43.refs_0_), custom_call_target="tpu_custom_call" | custom-call | bytes 1024 | tf_op jit(solution)/shard_map/feed/pallas_call | solution.py:1303
  518.9 7.4 %reduce-scatter.9.cloned.1.call-done.w_ref = bf16[8,48,576]{2,1,0:T(8,128)(2,1)} async-done(((bf16[32,48,576]{2,1,0:T(8,128)(2,1)}), bf16[8,48,576]{2,1,0:T(8,128)(2,1)}) %reduce-scatter.9.cloned.1.call-update) | async-done | bytes 442384 | tf_op jit(solution)/shard_map/reduce_scatter | solution.py:2057
  531.8 35.5 %closing.1 = (bf16[128,3072]{1,0:T(8,128)(2,1)S(1)}, bf16[8,48,576]{2,1,0:T(8,128)(2,1)S(1)}, bf16[8,48,768]{2,1,0:T(8,128)(2,1)S(1)}, f32[8,8,1536]{2,1,0:T(8,128)S(1)}, f32[4,8,8,128]{3,2,1,0:T(8,128)S(1)}) custom-call(s32[2,32]{1,0:T(2,128)S(1)} %pad_add_fusion.order_ref.refs_0_, f32[32,48,128]{2,1,0:T(8,128)S(1)} %bitcast.119, ...), custom_call_target="tpu_custom_call" | custom-call | bytes 1024 | tf_op jit(solution)/shard_map/closing/pallas_call | solution.py:1760
  568.4 24.9 %sheet_update.1 = (f32[48,29192]{1,0:T(8,128)}, f32[48,29192]{1,0:T(8,128)}, f32[48,29192]{1,0:T(8,128)}, f32[48,29192]{1,0:T(8,128)}, bf16[48,29192]{1,0:T(8,128)(2,1)}, /*index=5*/f32[1]{0:T(128)}, f32[48,8]{1,0:T(8,128)S(1)}) custom-call(s32[1]{0:T(128)} %dynamic_slice.12.block_ref, f32[20]{0:T(128)S(1)} %gather_fusion.4, ...), custom_call_target="tpu_custom_call" | custom-call | tf_op jit(solution)/shard_map/sheet_update/pallas_call | solution.py:2006
  (252 shorter events, 93.7 us)
Async XLA Ops:
  7.2 126.7 %all-gather.8.cloned.1.call-start = ((), (), s32[]{:S(2)}) async-start(), calls=%async_computation.6 | async-start | bytes 5406720 | tf_op jit(solution)/shard_map/all_gather | solution.py:2044
  14.5 31.6 %copy-start.62 = (s32[32]{0:T(128)S(1)}, s32[32]{0:T(128)}, u32[]{:S(2)}) copy-start(s32[32]{0:T(128)} %param.15) | copy-start | bytes 388
  45.5 94.4 %copy-start.58 = (bf16[96,128]{1,0:T(8,128)(2,1)}, bf16[96,128]{1,0:T(8,128)(2,1)S(1)}, u32[]{:S(2)}) copy-start(bf16[96,128]{1,0:T(8,128)(2,1)S(1)} %get-tuple-element.76.refs_7_) | copy-start | bytes 73732
  45.5 235.5 %all-gather.4.cloned.1.call-start = ((), (), s32[]{:S(2)}) async-start(), calls=%async_computation.4 | async-start | bytes 5898240 | tf_op jit(solution)/shard_map/all_gather | solution.py:2044
  127.1 171.2 %all-gather.6.cloned.1.call-start = ((), (), s32[]{:S(2)}) async-start(), calls=%async_computation.5 | async-start | bytes 2949120 | tf_op jit(solution)/shard_map/all_gather | solution.py:2044
  127.8 239.5 %reduce-scatter.7.cloned.1.call-start = ((), (), s32[]{:S(2)}) async-start(), calls=%async_computation.8 | async-start | bytes 2949120 | tf_op jit(solution)/shard_map/reduce_scatter | solution.py:2057
  169.3 47.8 %copy-start.33 = (bf16[3,3,64,1024]{3,2,1,0:T(8,128)(2,1)}, bf16[3,3,64,1024]{3,2,1,0:T(8,128)(2,1)S(1)}, u32[]{:S(2)}) copy-start(bf16[3,3,64,1024]{3,2,1,0:T(8,128)(2,1)S(1)} %get-tuple-element.86.part_ref) | copy-start | bytes 3538948
  298.3 147.9 %reduce-scatter.5.cloned.1.call-start = ((), (), s32[]{:S(2)}) async-start(), calls=%async_computation.7 | async-start | bytes 5898240 | tf_op jit(solution)/shard_map/reduce_scatter | solution.py:2057
  341.1 22.6 %copy-start.69 = (bf16[3,64,1,128]{3,2,1,0:T(2,128)(2,1)S(1)}, bf16[3,64,1,128]{3,2,1,0:T(2,128)(2,1)}, u32[]{:S(2)}) copy-start(bf16[3,64,1,128]{3,2,1,0:T(2,128)(2,1)} %get-tuple-element.188) | copy-start | bytes 147460
  341.1 22.6 %copy-start.73 = (f32[3,1024]{1,0:T(4,128)S(1)}, f32[3,1024]{1,0:T(4,128)}, u32[]{:S(2)}) copy-start(f32[3,1024]{1,0:T(4,128)} %get-tuple-element.195) | copy-start | bytes 36868
  341.1 177.7 %reduce-scatter.11.cloned.1.call-start = ((), (), s32[]{:S(2)}) async-start(), calls=%async_computation.10 | async-start | bytes 2949120 | tf_op jit(solution)/shard_map/reduce_scatter | solution.py:2057
  371.7 32.8 %copy-start.44 = (bf16[1536,192]{1,0:T(8,128)(2,1)S(1)}, bf16[1536,192]{1,0:T(8,128)(2,1)}, u32[]{:S(2)}) copy-start(bf16[1536,192]{1,0:T(8,128)(2,1)} %copy-done.43) | copy-start | bytes 1769476
  371.7 32.8 %copy-start.59 = (bf16[96,128]{1,0:T(8,128)(2,1)S(1)}, bf16[96,128]{1,0:T(8,128)(2,1)}, u32[]{:S(2)}) copy-start(bf16[96,128]{1,0:T(8,128)(2,1)} %copy-done.58) | copy-start | bytes 73732
  404.4 21.0 %copy-start.61 = (f32[8,1536]{1,0:T(8,128)}, f32[8,1536]{1,0:T(8,128)S(1)}, u32[]{:S(2)}) copy-start(f32[8,1536]{1,0:T(8,128)S(1)} %get-tuple-element.107) | copy-start | bytes 147460
  404.4 22.5 %copy-start.30 = (f32[32,1024]{1,0:T(8,128)S(1)}, f32[32,1024]{1,0:T(8,128)}, u32[]{:S(2)}) copy-start(f32[32,1024]{1,0:T(8,128)} %copy-done.29) | copy-start | bytes 393220
  404.4 22.5 %copy-start.32 = (f32[32,1024]{1,0:T(8,128)S(1)}, f32[32,1024]{1,0:T(8,128)}, u32[]{:S(2)}) copy-start(f32[32,1024]{1,0:T(8,128)} %copy-done.31) | copy-start | bytes 393220
  426.8 99.5 %reduce-scatter.9.cloned.1.call-start = ((), (), s32[]{:S(2)}) async-start(), calls=%async_computation.9 | async-start | bytes 2457600 | tf_op jit(solution)/shard_map/reduce_scatter | solution.py:2057
  450.9 24.4 %copy-start.63 = (s32[32]{0:T(128)S(1)}, s32[32]{0:T(128)}, u32[]{:S(2)}) copy-start(s32[32]{0:T(128)} %param.15) | copy-start | bytes 388
  450.9 27.4 %copy-start.11 = (bf16[768,1024]{1,0:T(8,128)(2,1)S(1)}, bf16[768,1024]{1,0:T(8,128)(2,1)}, u32[]{:S(2)}) copy-start(bf16[768,1024]{1,0:T(8,128)(2,1)} %copy-done.10) | copy-start | bytes 4718596
  450.9 27.4 %copy-start.13 = (bf16[8,48,768]{2,1,0:T(8,128)(2,1)S(1)}, bf16[8,48,768]{2,1,0:T(8,128)(2,1)}, u32[]{:S(2)}) copy-start(bf16[8,48,768]{2,1,0:T(8,128)(2,1)} %reduce-scatter.7.cloned.1.call-done.refs_9_.down_ref) | copy-start | bytes 1769476
  479.9 38.8 %copy-start.71 = (f32[1536]{0:T(1024)S(1)}, f32[1536]{0:T(1024)}, u32[]{:S(2)}) copy-start(f32[1536]{0:T(1024)} %copy-done.70) | copy-start | bytes 18436
  479.9 38.8 %copy-start.72 = (f32[1536]{0:T(1024)S(1)}, f32[1536]{0:T(1024)}, u32[]{:S(2)}) copy-start(f32[1536]{0:T(1024)} %get-tuple-element.179) | copy-start | bytes 18436
  479.9 38.8 %copy-start.76 = (f32[5]{0:T(128)S(1)}, f32[5]{0:T(128)}, u32[]{:S(2)}) copy-start(f32[5]{0:T(128)} %copy-done.75) | copy-start | bytes 64
  531.8 36.6 %copy-start.28 = (bf16[48,18432]{1,0:T(8,128)(2,1)S(1)}, bf16[48,18432]{1,0:T(8,128)(2,1)}, u32[]{:S(2)}) copy-start(bf16[48,18432]{1,0:T(8,128)(2,1)} %copy-done.27) | copy-start | bytes 5308420
  (62 other events, 196.4 us)
Sparse Core Ops, SparseCore 0:
  45.6 88.1 all-gather.7
  135.4 87.9 all-gather.3
  225.0 48.9 all-gather.5
  298.4 46.2 reduce-scatter.6
  346.8 84.7 reduce-scatter.4
  434.4 48.5 reduce-scatter.10
  485.3 40.9 reduce-scatter.8

commit v5 on v4

--- a/solution.py
+++ b/solution.py
@@ -457,12 +457,42 @@
 BRIEF = pl.CostEstimate(flops=0, bytes_accessed=1024, transcendentals=0)
 
 
-def reorder_blocks(source, target, order):
+def kernel_call(kernel, *, out_shape, in_specs, out_specs, **options):
+    single = not isinstance(out_shape, tuple)
+    shapes = (out_shape,) if single else out_shape
+    places = (out_specs,) if single else out_specs
+    shapes = tuple(
+        pltpu.HBM(shape.shape, shape.dtype) if place is IN_HBM else shape
+        for shape, place in zip(shapes, places)
+    )
+    call = pl.pallas_call(
+        kernel,
+        out_shape=shapes[0] if single else shapes,
+        in_specs=in_specs,
+        out_specs=out_specs,
+        **options,
+    )
+
+    def run(*operands):
+        return call(
+            *[
+                pltpu.with_memory_space_constraint(operand, pltpu.HBM)
+                if place is IN_HBM
+                else operand
+                for operand, place in zip(operands, in_specs)
+            ]
+        )
+
+    return run
+
+
+def reorder_blocks(source, target, order, column=0):
     rows = source.shape[1]
+    columns = slice(column, column + target.shape[1])
 
     @pl.loop(0, source.shape[0])
     def _(b):
-        target[pl.ds(pl.multiple_of(b * rows, 16), rows), :] = source[order(b)]
+        target[pl.ds(pl.multiple_of(b * rows, 16), rows), :] = source[order(b), :, columns]
 
 
 def wide(ref):
@@ -628,7 +658,7 @@
 
 
 def plane_gather_call(shard, shape, place, kind, after):
-    return pl.pallas_call(
+    return kernel_call(
         functools.partial(gather_kernel, place),
         out_shape=jax.ShapeDtypeStruct(shape, shard.dtype),
         in_specs=[IN_HBM] * (1 + len(after)),
@@ -734,7 +764,7 @@
 
 def plane_scatter_call(partial, shape, place, dtype, kind, after):
     rows, width = shape
-    return pl.pallas_call(
+    return kernel_call(
         functools.partial(scatter_kernel, place),
         out_shape=jax.ShapeDtypeStruct(shape, dtype),
         in_specs=[IN_VMEM] + [IN_HBM] * len(after),
@@ -772,14 +802,14 @@
     else:
         full_ref, x_ref, n_ref, i_ref, h_ref, *refs = refs
     full, total, part, landed, shard, by_block, base, gain, residual, normed, *refs = refs
-    heads, weight, *bufs, local_sem, send_sem, recv_sem = refs
+    heads, slots, weight, *bufs, local_sem, send_sem, recv_sem = refs
     rows, length = s_ref.shape
     width = base_ref.shape[1]
     fetches = [
         pltpu.make_async_copy(ref, held, local_sem.at[8 + k])
         for k, (ref, held) in enumerate(
-            [(s_ref, heads), (w_ref, weight), (base_ref, base), (gain_ref, gain)]
-            + ([(side_ref, bufs[-1])] if kind == "sum" else [])
+            [(s_ref, heads), (w_ref.at[:, :, : slots.shape[2]], slots)]
+            + [(base_ref, base), (gain_ref, gain)]
         )
     ]
     for fetch in fetches:
@@ -788,12 +818,27 @@
     side = mover(send_sem, recv_sem, 35)
     if kind == "sum":
         cores, chips, relays, finish = scatter_steps(
-            member_rows(side_out.shape[0]), bufs[-1], bufs[:-1], side
+            member_rows(side_out.shape[0]), bufs[-1], bufs[:-2], side
         )
-        fetches[4].wait()
+        text_weight = bufs[-2]
+        fetches[1].wait()
+        reorder_blocks(slots, text_weight, lambda b: order_ref[1, b], 3 * rows)
+        tokens = side_ref.shape[1]
+
+        @pl.loop(0, text_weight.shape[0] // 256)
+        def _(i):
+            at = pl.ds(pl.multiple_of(i * 256, 256), 256)
+            for k in range(2):
+                half = slice(k * side_ref.shape[0], (k + 1) * side_ref.shape[0])
+                bufs[-1][at, k * tokens : (k + 1) * tokens] = jnp.dot(
+                    text_weight[at, half], side_ref[...], preferred_element_type=jnp.float32
+                ).astype(jnp.bfloat16)
+
         cores()
+    else:
+        fetches[1].wait()
+    reorder_blocks(slots, weight, lambda b: order_ref[1, b], column)
     fetches[0].wait()
-    fetches[1].wait()
     total[...] = jnp.zeros_like(total)
 
     def add(member):
@@ -802,7 +847,7 @@
         @pl.loop(0, length // 256)
         def _(i):
             at = pl.ds(pl.multiple_of(i * 256, 256), 256)
-            total[:, at] += contract_rows(weight[of, column : column + rows], full[of, at])
+            total[:, at] += contract_rows(weight[of, :], full[of, at])
 
     gathered = gather_steps(
         member_rows(rows), heads, full, local_sem.at[0], mover(send_sem, recv_sem), add
@@ -830,12 +875,8 @@
     standard, inverse_std = norm_columns(residual[...])
     normed[...] = standard
     i_ref[...] = inverse_std
-    scaled = (standard * gain[...]).astype(shard.dtype)
-    if kind == "slots":
-        by_block[...] = scaled.reshape(by_block.shape)
-        reorder_blocks(by_block, shard, lambda b: order_ref[0, b])
-    else:
-        shard[...] = scaled
+    by_block[...] = (standard * gain[...]).astype(shard.dtype).reshape(by_block.shape)
+    reorder_blocks(by_block, shard, lambda b: order_ref[0, b])
     gathered = gather_steps(
         member_lanes(width), shard, h_ref, local_sem.at[4], mover(send_sem, recv_sem, 21)
     )
@@ -858,15 +899,18 @@
     frames = jax.ShapeDtypeStruct(base.shape, jnp.float32)
     side_outs, bufs = (), []
     if kind == "sum":
-        (text,) = side
-        side_outs = (jax.ShapeDtypeStruct((text.shape[0] // 8, text.shape[1]), text.dtype),)
-        bufs = scatter_bufs(*side_outs[0].shape) + [pltpu.VMEM(text.shape, text.dtype)]
+        tokens = side[0].shape[1]
+        side_outs = (jax.ShapeDtypeStruct((rows, 2 * tokens), jnp.bfloat16),)
+        bufs = scatter_bufs(rows, 2 * tokens) + [
+            pltpu.VMEM((features, rows), jnp.bfloat16),
+            pltpu.VMEM((features, 2 * tokens), jnp.bfloat16),
+        ]
     low, high = pltpu.VMEM(base.shape, jnp.bfloat16), pltpu.VMEM(base.shape, jnp.float32)
-    return pl.pallas_call(
+    return kernel_call(
         functools.partial(project_kernel, kind, column),
         out_shape=(whole, frames, frames, jax.ShapeDtypeStruct((1, width), jnp.float32), whole)
         + side_outs,
-        in_specs=[IN_SMEM] + [IN_HBM] * (4 + len(side)),
+        in_specs=[IN_SMEM] + [IN_HBM] * 4 + [IN_VMEM] * len(side),
         out_specs=(IN_HBM, IN_HBM, IN_HBM, IN_VMEM, IN_HBM) + (IN_VMEM,) * len(side),
         scratch_shapes=[
             pltpu.VMEM((features, length), jnp.bfloat16),
@@ -880,7 +924,8 @@
             high,
             high,
             pltpu.VMEM(heads.shape, heads.dtype),
-            pltpu.VMEM(weight.shape, weight.dtype),
+            pltpu.VMEM((orders.shape[1], features // orders.shape[1], 4 * rows), weight.dtype),
+            pltpu.VMEM((features, rows), weight.dtype),
         ]
         + bufs
         + [
@@ -895,7 +940,7 @@
         ),
         cost_estimate=BRIEF,
         name="project_" + kind,
-    )(orders, heads, weight, base, gain, *side)
+    )(orders, heads, weight.reshape(orders.shape[1], -1, weight.shape[1]), base, gain, *side)
 
 
 def back_kernel(plan, *refs):
@@ -921,7 +966,15 @@
     results = take(0 if by_rows else 2)
     mine, theirs, pair, from_x, from_y, relay, shard, slots, own_ref = take(9)
     besides = take(4 if beside else 0)
+    by_head = take(1 if by_rows else 0)
     local_sem, send_sem, recv_sem = refs
+    if by_rows:
+        w_slots, w_ref = w_ref, by_head[0]
+    source = sources[0]
+    if by_rows:
+        sources[0] = source.at[:, :, : w_slots.shape[2]]
+    elif w_ref.shape[1] < source.shape[1]:
+        sources[0] = source.at[:, : w_ref.shape[1]]
     fetches = [
         pltpu.make_async_copy(ref, here, local_sem.at[4 + k])
         for k, (ref, here) in enumerate(zip(sources + beside_refs, held + besides))
@@ -933,7 +986,7 @@
     beyond = across + along - group
     sibling, by_x, by_y = {"core": 1 - core}, {"dp": across}, {"dp": along}
     rows, width = mine.shape[1:]
-    columns = slice(column, column + g_ref.shape[0])
+    columns = slice(0, g_ref.shape[0]) if by_rows else slice(column, column + g_ref.shape[0])
     half = rows // 2
     low, high = pl.ds(0, half), pl.ds(half, half)
     copy = mover(send_sem, recv_sem)
@@ -1000,6 +1053,8 @@
     else:
         greet([by_x, by_y, sibling])
     fetches[0].wait()
+    if by_rows:
+        reorder_blocks(w_slots, w_ref, lambda b: order_ref[1, b], column)
     fetches[1].wait()
     for k, owner in enumerate((beyond, across, along, group)):
         work_out(k, owner)
@@ -1142,6 +1197,12 @@
     count = orders.shape[1]
     if not in_slots:
         act = act.reshape(count, features // count, length)
+    few = weight.shape[1] if column + grad.shape[0] > 4 * (features // 8) else 4 * (features // 8)
+    if by_rows:
+        weight = weight.reshape(count, features // count, weight.shape[1])
+        held = jax.ShapeDtypeStruct((count, features // count, few), small)
+    else:
+        held = jax.ShapeDtypeStruct((features, few), small)
     sources = [weight, grad, act] + list(norm or ())
     operands = [orders] + sources
     if text is not None:
@@ -1156,12 +1217,12 @@
     plan = (by_rows, send_rows, text is not None, in_slots, column, bool(beside), len(after))
     rows, width = shape
     four, slot = pltpu.VMEM((4, rows, width), small), pltpu.VMEM((rows, width), small)
-    return pl.pallas_call(
+    return kernel_call(
         functools.partial(back_kernel, plan),
         out_shape=tuple(outs),
         in_specs=[IN_SMEM] + [IN_HBM] * (len(operands) - 1),
         out_specs=tuple(specs),
-        scratch_shapes=[pltpu.VMEM(array.shape, array.dtype) for array in sources]
+        scratch_shapes=[pltpu.VMEM(array.shape, array.dtype) for array in [held] + sources[1:]]
         + (
             []
             if by_rows
@@ -1176,6 +1237,7 @@
             pltpu.VMEM(own.shape, small),
         ]
         + [pltpu.VMEM(array.shape, array.dtype) for array in beside]
+        + ([pltpu.VMEM((features, grad.shape[0]), small)] if by_rows else [])
         + [
             pltpu.SemaphoreType.DMA((11,)),
             pltpu.SemaphoreType.DMA((31,)),
@@ -1198,7 +1260,7 @@
 
 
 def exchange(array, shape, source, target, kind, after=()):
-    return pl.pallas_call(
+    return kernel_call(
         functools.partial(exchange_kernel, source, target),
         out_shape=jax.ShapeDtypeStruct(shape, array.dtype),
         in_specs=[IN_HBM] * (1 + len(after)),
@@ -1300,7 +1362,7 @@
 def feed(gu, down, weight, hidden, after=()):
     rows, length = weight.shape[0], hidden.shape[1]
     width = length // 8
-    return pl.pallas_call(
+    return kernel_call(
         feed_kernel,
         out_shape=(
             jax.ShapeDtypeStruct((gu.shape[1], 24 * down.shape[-1]), gu.dtype),
@@ -1514,7 +1576,7 @@
     local = (frames, 2 * features)
     one = (8, sheet.shape[0], (6 * D + 2 * CTXW) // 8)
     low = jnp.bfloat16
-    return pl.pallas_call(
+    return kernel_call(
         opening_kernel,
         out_shape=(
             jax.ShapeDtypeStruct(local, low),
@@ -1564,7 +1626,7 @@
 def first_gather(shard, other, sheet):
     rows, width = shard.shape
     whole = jax.ShapeDtypeStruct((rows, 8 * width), shard.dtype)
-    return pl.pallas_call(
+    return kernel_call(
         first_gather_kernel,
         out_shape=(
             whole,
@@ -1757,7 +1819,7 @@
     blocks = orders.shape[1]
     frames = (width, 2 * features)
     parts = (one, two, gu, down)
-    return pl.pallas_call(
+    return kernel_call(
         closing_kernel,
         out_shape=(
             jax.ShapeDtypeStruct(frames, jnp.bfloat16),
@@ -1804,21 +1866,46 @@
 
 
 def attend_kernel(
-    w_ref, h_ref, cos_ref, sin_ref, seg_ref, column_ref, part_ref, p_ref, o_ref, joint_ref
+    w_ref,
+    h_ref,
+    cos_ref,
+    sin_ref,
+    seg_ref,
+    column_ref,
+    part_out,
+    p_out,
+    o_ref,
+    weight,
+    frames,
+    joint_ref,
+    part_ref,
+    p_ref,
+    sems,
 ):
     heads, length = joint_ref.shape[1], joint_ref.shape[3]
     span = heads * HEAD
+    tiles = length // 256
+    fetches = [pltpu.make_async_copy(w_ref, weight, sems.at[0])]
+    fetches += [
+        pltpu.make_async_copy(
+            h_ref.at[:, i * 256 : (i + 1) * 256], frames.at[:, i * 256 : (i + 1) * 256], sems.at[1 + i]
+        )
+        for i in range(tiles)
+    ]
+    for fetch in fetches:
+        fetch.start()
     cosine, sine_table = cos_ref[...], sin_ref[...]
-    for k in range(3):
-        by_row = w_ref[:, (4 + k) * span : (5 + k) * span].T
-
-        @pl.loop(0, length // 256)
-        def _(i, k=k, by_row=by_row):
-            at = pl.ds(pl.multiple_of(i * 256, 256), 256)
-            part = jnp.dot(by_row, h_ref[:, at], preferred_element_type=jnp.float32)
+    fetches[0].wait()
+    by_row = [weight[:, (4 + k) * span : (5 + k) * span].T for k in range(3)]
+    for i in range(tiles):
+        fetches[1 + i].wait()
+        at = slice(i * 256, (i + 1) * 256)
+        for k in range(3):
+            part = jnp.dot(by_row[k], frames[:, at], preferred_element_type=jnp.float32)
             for h in range(heads):
                 joint_ref[k, h, :, at] = part[h * HEAD : (h + 1) * HEAD]
 
+    kept = []
     for h in range(heads):
         queries = turned(joint_ref[0, h], cosine, sine_table)
         part_ref[0, h] = queries.astype(part_ref.dtype)
@@ -1827,7 +1914,7 @@
         part_ref[2, h] = joint_ref[2, h].astype(part_ref.dtype)
         by_key = keys.T.astype(part_ref.dtype)
 
-        @pl.loop(0, length // 256)
+        @pl.loop(0, tiles)
         def _(i, h=h, by_key=by_key):
             at = pl.ds(pl.multiple_of(i * 256, 256), 256)
             scores = jnp.dot(
@@ -1840,35 +1927,158 @@
             out = jnp.dot(part_ref[2, h], p_ref[h, :, at], preferred_element_type=jnp.float32)
             o_ref[h * HEAD : (h + 1) * HEAD, at] = out.astype(o_ref.dtype)
 
+        kept.append(pltpu.make_async_copy(p_ref.at[h], p_out.at[h], sems.at[1 + tiles + h]))
+        kept[-1].start()
+    kept.append(pltpu.make_async_copy(part_ref, part_out, sems.at[1 + tiles + heads]))
+    kept[-1].start()
+    for keep in kept:
+        keep.wait()
+
 
 def attend(weight, frames, cosine, sine_table, segments):
     heads, length = D // HEAD // 8, frames.shape[1]
     joint = (3, heads, HEAD, length)
     small = jnp.bfloat16
-    return pl.pallas_call(
+    return kernel_call(
         attend_kernel,
         out_shape=(
             jax.ShapeDtypeStruct(joint, small),
             jax.ShapeDtypeStruct((heads, length, length), small),
             jax.ShapeDtypeStruct((heads * HEAD, length), small),
         ),
-        in_specs=[IN_VMEM] * 6,
-        out_specs=(IN_VMEM,) * 3,
-        scratch_shapes=[pltpu.VMEM(joint, jnp.float32)],
-        compiler_params=pltpu.CompilerParams(vmem_limit_bytes=32 * 2**20),
+        in_specs=[IN_HBM] * 2 + [IN_VMEM] * 4,
+        out_specs=(IN_HBM, IN_HBM, IN_VMEM),
+        scratch_shapes=[
+            pltpu.VMEM(weight.shape, small),
+            pltpu.VMEM(frames.shape, small),
+            pltpu.VMEM(joint, jnp.float32),
+            pltpu.VMEM(joint, small),
+            pltpu.VMEM((heads, length, length), small),
+            pltpu.SemaphoreType.DMA((2 + length // 256 + heads,)),
+        ],
+        compiler_params=pltpu.CompilerParams(vmem_limit_bytes=36 * 2**20),
         name="attend",
     )(weight, frames, cosine, sine_table, segments[None, :], segments[:, None])
 
 
-def attend_back_kernel(part_ref, p_ref, grad_ref, cos_ref, sin_ref, o_ref, dq_ref, dk_ref, dv_ref):
+def cross_kernel(w_ref, h_ref, kv_ref, cq_ref, p_ref, o_ref, weight, frames, sems):
+    heads, text, length = p_ref.shape
+    span = heads * HEAD
+    tiles = length // 256
+    fetches = [pltpu.make_async_copy(w_ref.at[:, 128:384], weight, sems.at[0])]
+    fetches += [
+        pltpu.make_async_copy(
+            h_ref.at[:, i * 256 : (i + 1) * 256], frames.at[:, i * 256 : (i + 1) * 256], sems.at[1 + i]
+        )
+        for i in range(tiles)
+    ]
+    for fetch in fetches:
+        fetch.start()
+    keys = [
+        wide(kv_ref.at[h * HEAD : (h + 1) * HEAD, :text]).T.astype(cq_ref.dtype)
+        for h in range(heads)
+    ]
+    fetches[0].wait()
+    by_row = weight[:, span - 128 : 2 * span - 128].T
+    for i in range(tiles):
+        fetches[1 + i].wait()
+        at = slice(i * 256, (i + 1) * 256)
+        cq_ref[:, at] = jnp.dot(
+            by_row, frames[:, at], preferred_element_type=jnp.float32
+        ).astype(cq_ref.dtype)
+        for h in range(heads):
+            of = slice(h * HEAD, (h + 1) * HEAD)
+            scores = jnp.dot(keys[h], cq_ref[of, at], preferred_element_type=jnp.float32) * (
+                HEAD**-0.5
+            )
+            exponent = jnp.exp(scores - jnp.max(scores, axis=0, keepdims=True))
+            probs = exponent * (1.0 / jnp.sum(exponent, axis=0, keepdims=True))
+            p_ref[h, :, at] = probs.astype(p_ref.dtype)
+            out = jnp.dot(
+                kv_ref[of, text:], p_ref[h, :, at], preferred_element_type=jnp.float32
+            )
+            o_ref[of, at] = out.astype(o_ref.dtype)
+
+
+def cross(weight, frames, text_kv):
+    rows, length = text_kv.shape[0], frames.shape[1]
+    text, small = text_kv.shape[1] // 2, jnp.bfloat16
+    return kernel_call(
+        cross_kernel,
+        out_shape=(
+            jax.ShapeDtypeStruct((rows, length), small),
+            jax.ShapeDtypeStruct((rows // HEAD, text, length), small),
+            jax.ShapeDtypeStruct((rows, length), small),
+        ),
+        in_specs=[IN_HBM, IN_HBM, IN_VMEM],
+        out_specs=(IN_VMEM,) * 3,
+        scratch_shapes=[
+            pltpu.VMEM((weight.shape[0], 256), small),
+            pltpu.VMEM(frames.shape, small),
+            pltpu.SemaphoreType.DMA((1 + length // 256,)),
+        ],
+        compiler_params=pltpu.CompilerParams(vmem_limit_bytes=16 * 2**20),
+        name="cross",
+    )(weight, frames, text_kv)
+
+
+def cross_back_kernel(cq_ref, p_ref, kv_ref, grad_ref, dq_ref, dkv_ref):
+    heads, text, length = p_ref.shape
+    scale = HEAD**-0.5
+    for h in range(heads):
+        of = slice(h * HEAD, (h + 1) * HEAD)
+        by_key = wide(kv_ref.at[of, text:]).T.astype(cq_ref.dtype)
+        grad_out = grad_ref[of, :]
+        grad_probs = jnp.dot(by_key, grad_out, preferred_element_type=jnp.float32)
+        probs = wide(p_ref.at[h])
+        weighted = jnp.sum(probs * grad_probs, axis=0, keepdims=True)
+        grad_scores = (probs * (grad_probs - weighted)).astype(cq_ref.dtype)
+        dq_ref[of, :] = (
+            jnp.dot(kv_ref[of, :text], grad_scores, preferred_element_type=jnp.float32) * scale
+        ).astype(dq_ref.dtype)
+        dkv_ref[of, :text] = (contract_last(cq_ref[of, :], grad_scores) * scale).astype(
+            dkv_ref.dtype
+        )
+        dkv_ref[of, text:] = contract_last(grad_out, p_ref[h]).astype(dkv_ref.dtype)
+
+
+def cross_back(cross_q, probs, text_kv, grad):
+    return kernel_call(
+        cross_back_kernel,
+        out_shape=(
+            jax.ShapeDtypeStruct(cross_q.shape, cross_q.dtype),
+            jax.ShapeDtypeStruct(text_kv.shape, text_kv.dtype),
+        ),
+        in_specs=[IN_VMEM] * 4,
+        out_specs=(IN_VMEM,) * 2,
+        compiler_params=pltpu.CompilerParams(vmem_limit_bytes=16 * 2**20),
+        name="cross_back",
+    )(cross_q, probs, text_kv, grad)
+
+
+def attend_back_kernel(
+    part_in, p_in, g_in, cos_ref, sin_ref, o_ref, part_ref, p_ref, grad_ref, dq_ref, dk_ref, dv_ref, sems
+):
     heads, length = part_ref.shape[1], part_ref.shape[3]
+    fetches = [
+        pltpu.make_async_copy(part_in, part_ref, sems.at[0]),
+        pltpu.make_async_copy(g_in, grad_ref, sems.at[1]),
+    ]
+    fetches += [
+        pltpu.make_async_copy(p_in.at[h], p_ref.at[h], sems.at[2 + h]) for h in range(heads)
+    ]
+    for fetch in fetches:
+        fetch.start()
     cosine, sine_table = cos_ref[...], -sin_ref[...]
     scale = HEAD**-0.5
+    fetches[0].wait()
+    fetches[1].wait()
     for h in range(heads):
         of = slice(h * HEAD, (h + 1) * HEAD)
         by_key = wide(part_ref.at[2, h]).T.astype(part_ref.dtype)
         dk_ref[...] = jnp.zeros_like(dk_ref)
         dv_ref[...] = jnp.zeros_like(dv_ref)
+        fetches[2 + h].wait()
 
         @pl.loop(0, length // 256)
         def _(i, h=h, of=of, by_key=by_key):
@@ -1895,12 +2105,14 @@
 
 def attend_back(parts, probs, grad, cosine, sine_table):
     _, heads, _, length = parts.shape
-    return pl.pallas_call(
+    return kernel_call(
         attend_back_kernel,
         out_shape=jax.ShapeDtypeStruct((3 * heads * HEAD, length), jnp.bfloat16),
-        in_specs=[IN_VMEM] * 5,
+        in_specs=[IN_HBM] * 3 + [IN_VMEM] * 2,
         out_specs=IN_VMEM,
-        scratch_shapes=[pltpu.VMEM((HEAD, length), jnp.float32)] * 3,
+        scratch_shapes=[pltpu.VMEM(array.shape, array.dtype) for array in (parts, probs, grad)]
+        + [pltpu.VMEM((HEAD, length), jnp.float32)] * 3
+        + [pltpu.SemaphoreType.DMA((2 + heads,))],
         compiler_params=pltpu.CompilerParams(vmem_limit_bytes=32 * 2**20),
         name="attend_back",
     )(parts, probs, grad, cosine, sine_table)
@@ -1914,6 +2126,7 @@
     feed_ref,
     all_ref,
     gain_ref,
+    pair_ref,
     sheet_ref,
     first_ref,
     second_ref,
@@ -1924,6 +2137,8 @@
     copy_out,
     norm_out,
     gain_out,
+    output_out,
+    latent_out,
     grad,
     gain,
     scale,
@@ -1950,85 +2165,95 @@
         norm_out[0] = norm
         scale[0] = 1.0 / jnp.maximum(norm, 1.0)
         gain_out[...] = gain[...] * scale[0]
+        output_out[...] = pair_ref[:, :D]
+        latent_out[...] = wide(pair_ref.at[:, D:])
 
     for k in range(6):
 
-        @pl.when(step == k)
+        @pl.when(step == k // 2)
         def _(k=k):
             ref, start = (one_ref, k * part) if k < 3 else (two_ref, (k - 3) * part)
             for m in range(8):
-                grad[:, m * part : (m + 1) * part] = wide(ref.at[m, :, start : start + part])
-
-    @pl.when(jnp.logical_and(step >= 6, step < 18))
+                at = (k % 2) * D + m * part
+                grad[:, at : at + part] = wide(ref.at[m, :, start : start + part])
+
+    @pl.when(jnp.logical_and(step >= 3, step < 9))
     def _():
         grad[...] = wide(feed_ref)
 
-    @pl.when(step == 18)
+    @pl.when(step == 9)
     def _():
         for m in range(8):
             for k in range(2):
                 start = 3 * part + k * text
-                place = k * CTXW + m * text
-                grad[:, place : place + text] = wide(two_ref.at[m, :, start : start + text])
-
-    @pl.when(step == 19)
-    def _():
-        grad[:, :8] = gain[...]
-
-    clipped = grad[...] * scale[0]
-    sheet = sheet_ref[...]
-    first_new = BETA_ONE * first_ref[...] + (1.0 - BETA_ONE) * clipped
-    second_new = BETA_TWO * second_ref[...] + (1.0 - BETA_TWO) * clipped * clipped
-    mean_hat = first_new * (1.0 / (1.0 - BETA_ONE**STEP))
-    square_hat = second_new * (1.0 / (1.0 - BETA_TWO**STEP))
-    sheet_new = sheet - rate_ref[step] * (
-        mean_hat / (jnp.sqrt(square_hat) + EPS_ADAM) + WEIGHT_DECAY * sheet
-    )
-    grad_out[...] = clipped
-    first_out[...] = first_new
-    second_out[...] = second_new
-    sheet_out[...] = sheet_new
-    copy_out[...] = sheet_new.astype(copy_out.dtype)
-
-
-def sheet_update(block_index, length, one, two, feed_part, squares, gains, sheet, first, second):
+                at = k * CTXW + m * text
+                grad[:, at : at + text] = wide(two_ref.at[m, :, start : start + text])
+        grad[:, D : D + 8] = gain[...]
+
+    for half in range(2):
+        at = slice(half * D, (half + 1) * D)
+        clipped = grad[:, at] * scale[0]
+        sheet = sheet_ref[:, at]
+        first_new = BETA_ONE * first_ref[:, at] + (1.0 - BETA_ONE) * clipped
+        second_new = BETA_TWO * second_ref[:, at] + (1.0 - BETA_TWO) * clipped * clipped
+        mean_hat = first_new * (1.0 / (1.0 - BETA_ONE**STEP))
+        square_hat = second_new * (1.0 / (1.0 - BETA_TWO**STEP))
+        sheet_new = sheet - rate_ref[2 * step + half] * (
+            mean_hat / (jnp.sqrt(square_hat) + EPS_ADAM) + WEIGHT_DECAY * sheet
+        )
+        grad_out[:, at] = clipped
+        first_out[:, at] = first_new
+        second_out[:, at] = second_new
+        sheet_out[:, at] = sheet_new
+        copy_out[:, at] = sheet_new.astype(copy_out.dtype)
+
+
+def sheet_update(block_index, length, one, two, feed_part, squares, gains, pair, sheet, first, second):
     rows = sheet.shape[0]
+    frames = (pair.shape[0], D)
     rates = column_spread(length)[jnp.minimum(jnp.arange(20) * D, SHEET - 1)]
-    column_block = pl.BlockSpec((rows, D), lambda i: (0, i))
+    column_block = pl.BlockSpec((rows, 2 * D), lambda i: (0, i))
     like = jax.ShapeDtypeStruct(sheet.shape, sheet.dtype)
 
-    def whole(array):
-        return pl.BlockSpec(array.shape, lambda i: (0,) * array.ndim)
-
-    sheet, first, second = (
-        pltpu.with_memory_space_constraint(array, pltpu.HBM) for array in (sheet, first, second)
+    def whole(shape):
+        return pl.BlockSpec(shape, lambda i: (0,) * len(shape))
+
+    sheet, first, second, feed_part = (
+        pltpu.with_memory_space_constraint(array, pltpu.HBM)
+        for array in (sheet, first, second, feed_part)
     )
     return pl.pallas_call(
         update_kernel,
-        grid=(20,),
+        grid=(10,),
         out_shape=(like, like, like, like, jax.ShapeDtypeStruct(sheet.shape, jnp.bfloat16))
-        + (jax.ShapeDtypeStruct((1,), jnp.float32), jax.ShapeDtypeStruct((rows, 8), jnp.float32)),
+        + (jax.ShapeDtypeStruct((1,), jnp.float32), jax.ShapeDtypeStruct((rows, 8), jnp.float32))
+        + (
+            jax.ShapeDtypeStruct(frames, jnp.bfloat16),
+            jax.ShapeDtypeStruct(frames, jnp.float32),
+        ),
         in_specs=[
             IN_SMEM,
             IN_SMEM,
-            whole(one),
-            whole(two),
-            pl.BlockSpec((rows, D), lambda i: (0, jnp.clip(i - 6, 0, 11))),
-            whole(squares),
-            whole(gains),
+            whole(one.shape),
+            whole(two.shape),
+            pl.BlockSpec((rows, 2 * D), lambda i: (0, jnp.clip(i - 3, 0, 5))),
+            whole(squares.shape),
+            whole(gains.shape),
+            whole(pair.shape),
             column_block,
             column_block,
             column_block,
         ],
-        out_specs=(column_block,) * 5 + (IN_SMEM, pl.BlockSpec((rows, 8), lambda i: (0, 0))),
+        out_specs=(column_block,) * 5
+        + (IN_SMEM, whole((rows, 8)), whole(frames), whole(frames)),
         scratch_shapes=[
-            pltpu.VMEM((rows, D), jnp.float32),
+            pltpu.VMEM((rows, 2 * D), jnp.float32),
             pltpu.VMEM((rows, 8), jnp.float32),
             pltpu.SMEM((1,), jnp.float32),
         ],
-        compiler_params=pltpu.CompilerParams(vmem_limit_bytes=24 * 2**20),
+        compiler_params=pltpu.CompilerParams(vmem_limit_bytes=32 * 2**20),
         name="sheet_update",
-    )(block_index, rates, one, two, feed_part, squares, gains, sheet, first, second)
+    )(block_index, rates, one, two, feed_part, squares, gains, pair, sheet, first, second)
 
 
 def pick_blocks(blocks, order):
@@ -2102,9 +2327,6 @@
     mine_one, later = lax.optimization_barrier((mine_one, sheet))
     low_sheet = later.astype(jnp.bfloat16)
     weight_one = gather_slots(mine_one)
-    weight_two = sort_blocks(weight_one[:, : 4 * span], to_logical)
-    weight_cq = weight_two[:, span : 2 * span]
-    weight_text = weight_two[:, 3 * span :]
     gains = pick_blocks(small[..., :rows].reshape(blocks, 8, rows), to_logical)
     gains = gains.swapaxes(1, 2).reshape(D, 8)
     starts = lax.dynamic_index_in_dim(
@@ -2146,44 +2368,24 @@
     line_down = gather_slots(mine_down)
 
     parts, probs, attn_out = attend(weight_one, h_one, cosine, sine_table, segments)
-    text_width = CTXW // members
-    text_kv = jnp.stack(
-        [
-            matmul(weight_text[:, :text_width], text_mine),
-            matmul(weight_text[:, text_width:], text_mine),
-        ],
-        axis=1,
-    ).reshape(D, 2 * CTX)
     attn_out, x_one, normed_two, inverse_two, h_two, text_kv = project(
         "sum",
         0,
         orders,
         attn_out,
-        weight_two,
+        weight_one,
         tokens,
         gain_two,
-        text_kv.astype(jnp.bfloat16),
-    )
-
-    text_kv = text_kv.reshape(head_count, HEAD, 2, CTX)
-    text_keys = text_kv[:, :, 0]
-    text_values = text_kv[:, :, 1]
-    cross_q = contract_rows(weight_cq, h_two).astype(jnp.bfloat16).reshape(head_count, HEAD, length)
-    cross_scores = (
-        jnp.einsum("hdq,hdk->hqk", cross_q, text_keys, preferred_element_type=jnp.float32)
-        * score_scale
-    )
-    cross_probs = softmax_rows(cross_scores)
-    cross_low = cross_probs.astype(jnp.bfloat16)
-    cross_out = jnp.einsum(
-        "hqk,hdk->hdq", cross_low, text_values, preferred_element_type=jnp.float32
-    )
+        text_mine,
+    )
+
+    cross_q, cross_probs, cross_out = cross(weight_one, h_two, text_kv)
     cross_out, x_two, normed_three, inverse_three, h_three = project(
         "slots",
         2 * span,
         orders,
-        cross_out.reshape(span, length).astype(jnp.bfloat16),
-        weight_two,
+        cross_out,
+        weight_one,
         x_one,
         gain_three,
     )
@@ -2215,45 +2417,24 @@
     grad_blocks_gu = as_blocks(grad_weight_gu, to_slots)
     sums_gu = scatter_line(grad_blocks_gu)
     grad_cross_out, grad_weight_co = back(
-        orders, weight_two, grad_cross, cross_out, column=2 * span
-    )
-    grad_cross_out = grad_cross_out.reshape(head_count, HEAD, length)
-    grad_cross_probs = jnp.einsum(
-        "hdq,hdk->hqk", grad_cross_out, text_values, preferred_element_type=jnp.float32
-    )
-    grad_cross_scores = (
-        cross_probs
-        * (grad_cross_probs - jnp.sum(cross_probs * grad_cross_probs, axis=-1, keepdims=True))
-    ).astype(jnp.bfloat16)
-    grad_cross_q = (
-        jnp.einsum("hqk,hdk->hdq", grad_cross_scores, text_keys, preferred_element_type=jnp.float32)
-        * score_scale
-    )
-    grad_cross_q = grad_cross_q.reshape(span, length).astype(jnp.bfloat16)
-    grad_text_keys = (
-        jnp.einsum("hqk,hdq->hdk", grad_cross_scores, cross_q, preferred_element_type=jnp.float32)
-        * score_scale
-    )
-    grad_text_values = jnp.einsum(
-        "hqk,hdq->hdk", cross_low, grad_cross_out, preferred_element_type=jnp.float32
-    )
-    grad_text = jnp.concatenate(
-        [grad_text_keys.reshape(span, CTX), grad_text_values.reshape(span, CTX)], axis=1
-    )
+        orders, weight_one, grad_cross, cross_out, column=2 * span
+    )
+    grad_cross_q, grad_text = cross_back(cross_q, cross_probs, text_kv, grad_cross_out)
     grad_x_one, grad_weight_cq, sum_two, grad_attn, grad_text = back(
         orders,
-        weight_two,
+        weight_one,
         grad_cross_q,
         h_two,
         (normed_two, inverse_two, gain_two, grad_x_two),
         column=span,
         send_rows=True,
-        text=grad_text.astype(jnp.bfloat16),
+        text=grad_text,
+        in_slots=True,
         after=[sums_down],
     )
     grad_attn_out, grad_weight_two = back(
         orders,
-        weight_two,
+        weight_one,
         grad_attn,
         attn_out,
         beside=(grad_weight_cq, grad_weight_co, grad_text, text_mine),
@@ -2295,10 +2476,18 @@
     out_pair, sums_one, sums_two, gain_sums, squares = closing(
         orders, ff_out, x_two, latent_grad, sums_one, sums_two, sums_gu, sums_down, gain_grads
     )
-    output = out_pair[:, :D]
-    latent_grad = out_pair[:, D:].astype(jnp.float32)
     place = lax.axis_index("dp") * (planes * cores) + plane * cores + lax.axis_index("core")
-    clipped, first_new, second_new, sheet_new, sheet_copy, grad_norm, gain_grad = sheet_update(
+    (
+        clipped,
+        first_new,
+        second_new,
+        sheet_new,
+        sheet_copy,
+        grad_norm,
+        gain_grad,
+        output,
+        latent_grad,
+    ) = sheet_update(
         lax.dynamic_slice_in_dim(owners, place, 1),
         length,
         sums_one,
@@ -2306,6 +2495,7 @@
         sums_feed,
         squares,
         gain_sums,
+        out_pair,
         sheet,
         first,
         second,

time: 612 us -> 581 us (0.949)
  local copies, waits for them, and re-layouts: 80.2 us -> 25.2 us
  waiting for transfers between devices: 11.4 us -> 28.9 us
  Pallas kernels: 444 us -> 461 us
  matrix products: 30.6 us -> 20.4 us
    unnamed x161 -> x43, local copies, waits for them, and re-layouts: 60.5 us -> 15.7 us
    reduce_scatter x4, waiting for transfers between devices: 7.5 us -> 25.4 us  [scatter_line(): return lax.psum_scatter(blocks, 'z', scatter_dimension=0, tiled=True)]
    pallas_call x14 -> x16, Pallas kernels: 444 us -> 461 us  [the longest x15 440 us: run(): call(*[pltpu.with_memory_space_constraint(operand, pltpu.HBM) if place is...]
    dot_general x3 -> x2, matrix products: 19.2 us -> 16.5 us  [contract_rows(): lax.dot_general(left, right, (((0,), (0,)), ((), ())), preferred_element_...]
  transfers between devices with their start and end apart: 7 -> 7, of which waited for: 2 -> 2; matrix products, arithmetic and copies ran while one was open for 11% -> 8% of each run, Pallas kernels for 59% -> 66%
where the time goes in v5:
time: 581 us; the launch traced here: 570 us
  Pallas kernels  461 us (79%)
  waiting for transfers between devices  28.9 us (5%)
  local copies, waits for them, and re-layouts  25.2 us (4%)
  matrix products  20.4 us (4%)
  other arithmetic  18.9 us (3%)
  between operations  15.8 us (3%)
    pallas_call x15, Pallas kernels, run(): call(*[pltpu.with_memory_space_constraint(operand, pltpu.HBM) if place is...  440 us
    reduce_scatter x4, waiting for transfers between devices, scatter_line(): return lax.psum_scatter(blocks, 'z', scatter_dimension=0, tiled=True)  25.4 us
    pallas_call x1, Pallas kernels, sheet_update(): pl.pallas_call(update_kernel, grid=(10,), out_shape=(like, like, like, li...  21.3 us
    dot_general x2, matrix products, contract_rows(): lax.dot_general(left, right, (((0,), (0,)), ((), ())), preferred_element_...  16.5 us
    unnamed x43, local copies, waits for them, and re-layouts  15.7 us
  transfers between devices with their start and end apart: 7, of which 2 were waited for; matrix products, arithmetic and copies ran while one was open for 8% of the time, Pallas kernels for 66%

profile of v5, /device:TPU:0, one launch (start us, length us, event | category | flops | bytes accessed | tf_op | source)
XLA Modules:
  0.0 570.5 jit_solution(8432354451426617712)
XLA Ops:
  11.1 31.1 %opening.1 = (bf16[128,3072]{1,0:T(8,128)(2,1)}, f32[4,8,8,128]{3,2,1,0:T(8,128)}, bf16[96,128]{1,0:T(8,128)(2,1)}, bf16[8,48,1344]{2,1,0:T(8,128)(2,1)}) custom-call(bf16[128,1536]{1,0:T(8,128)(2,1)} %bitcast.85, bf16[128,1536]{1,0:T(8,128)(2,1)} %bitcast.86, f32[8,128]{1,0:T(8,128)} %select_maximum_fusion.small_ref, bf16[768,128]{1,0:T(8,128)(2,1)} %bitcast.81, ...), custom_call_target="tpu_custom_call" | custom-call | bytes 1024 | tf_op jit(solution)/shard_map/opening/pallas_call | solution.py:477
  53.5 2.1 slice_reduce_fusion
  58.0 4.5 convert_element_type.78.sheet_ref
  62.5 62.7 %first_gather.1 = (bf16[1536,1024]{1,0:T(8,128)(2,1)}, bf16[1536,1024]{1,0:T(8,128)(2,1)}, bf16[8,48,1536]{2,1,0:T(8,128)(2,1)}, bf16[8,48,768]{2,1,0:T(8,128)(2,1)}) custom-call(bf16[1536,128]{1,0:T(8,128)(2,1)} %bitcast.80, bf16[1536,128]{1,0:T(8,128)(2,1)} %bitcast.79, bf16[48,29192]{1,0:T(8,128)(2,1)} %convert_element_type.78.sheet_ref), custom_call_target="tpu_custom_call" | custom-call | bytes 1024 | tf_op jit(solution)/shard_map/first_gather/pallas_call | solution.py:477
  128.0 2.6 all-gather.8.cloned.1.call-done.w_ref.refs_1_
  130.7 20.4 %attend.1 = (bf16[3,3,64,1024]{3,2,1,0:T(8,128)(2,1)}, bf16[3,1024,1024]{2,1,0:T(8,128)(2,1)}, bf16[192,1024]{1,0:T(8,128)(2,1)S(1)}) custom-call(bf16[1536,1344]{1,0:T(8,128)(2,1)} %bitcast.59, bf16[1536,1024]{1,0:T(8,128)(2,1)} %get-tuple-element.81.h_ref.refs_3_, f32[32,1024]{1,0:T(8,128)S(1)} %get-tuple-element.202.cos_ref, ...), custom_call_target="tpu_custom_call" | custom-call | tf_op jit(solution)/shard_map/attend/pallas_call | solution.py:477
  151.8 51.5 %project_sum.1 = (bf16[1536,1024]{1,0:T(8,128)(2,1)}, f32[1536,128]{1,0:T(8,128)}, f32[1536,128]{1,0:T(8,128)}, f32[1,128]{1,0:T(1,128)S(1)}, bf16[1536,1024]{1,0:T(8,128)(2,1)}, /*index=5*/bf16[192,256]{1,0:T(8,128)(2,1)S(1)}) custom-call(s32[2,32]{1,0:T(2,128)S(1)} %pad_add_fusion.order_ref.refs_0_, bf16[192,1024]{1,0:T(8,128)(2,1)} %copy-done.7, ...), custom_call_target="tpu_custom_call" | custom-call | bytes 1024 | tf_op jit(solution)/shard_map/project_sum/pallas_call | solution.py:477
  203.3 6.7 %cross.1 = (bf16[192,1024]{1,0:T(8,128)(2,1)S(1)}, bf16[3,128,1024]{2,1,0:T(8,128)(2,1)S(1)}, bf16[192,1024]{1,0:T(8,128)(2,1)S(1)}) custom-call(bf16[1536,1344]{1,0:T(8,128)(2,1)} %bitcast.60, bf16[1536,1024]{1,0:T(8,128)(2,1)} %get-tuple-element.84.h_ref.refs_3_, bf16[192,256]{1,0:T(8,128)(2,1)S(1)} %get-tuple-element.85.kv_ref), custom_call_target="tpu_custom_call" | custom-call | tf_op jit(solution)/shard_map/cross/pallas_call | solution.py:477
  210.8 44.8 %project_slots.1 = (bf16[1536,1024]{1,0:T(8,128)(2,1)}, f32[1536,128]{1,0:T(8,128)}, f32[1536,128]{1,0:T(8,128)}, f32[1,128]{1,0:T(1,128)S(1)}, bf16[1536,1024]{1,0:T(8,128)(2,1)}) custom-call(s32[2,32]{1,0:T(2,128)S(1)} %pad_add_fusion.order_ref.refs_0_, bf16[192,1024]{1,0:T(8,128)(2,1)} %copy-done.8, ...), custom_call_target="tpu_custom_call" | custom-call | bytes 1024 | tf_op jit(solution)/shard_map/project_slots/pallas_call | solution.py:477
  255.6 8.2 %fusion.11 = f32[1536,1024]{1,0:T(8,128)S(1)} fusion(bf16[1536,1536]{1,0:T(8,128)(2,1)} %bitcast.69, bf16[1536,1024]{1,0:T(8,128)(2,1)} %get-tuple-element.88.refs_3_), kind=kOutput, calls=%fused_computation.81 | convolution fusion | flops 4831838208 | bytes 14155776 | tf_op jit(solution)/shard_map/dot_general | solution.py:430
  264.9 2.2 copy-done.15
  268.1 3.9 convolution_convert_fusion
  272.1 8.3 %multiply_convert_fusion.1 = (bf16[768,1024]{1,0:T(8,128)(2,1)S(1)}, bf16[768,1024]{1,0:T(8,128)(2,1)S(1)}) fusion(f32[1536,1024]{1,0:T(8,128)} %copy-done.15, bf16[1536,768]{1,0:T(8,128)(2,1)} %bitcast.75, bf16[1536,1024]{1,0:T(8,128)(2,1)} %get-tuple-element.79), kind=kOutput, calls=%fused_computation.9 | convolution fusion | flops 2426142720 | bytes 14942208 | tf_op jit(solution)/shard_map/dot_general | solution.py:430
  280.3 2.0 pad_maximum_fusion.refs_2_
  282.3 32.1 %back.5 = (f32[1536,128]{1,0:T(8,128)}, bf16[1536,1536]{1,0:T(8,128)(2,1)}, f32[8,1536]{1,0:T(8,128)S(1)}, bf16[192,1024]{1,0:T(8,128)(2,1)}) custom-call(s32[2,32]{1,0:T(2,128)S(1)} %pad_add_fusion.order_ref.refs_0_, bf16[1536,1536]{1,0:T(8,128)(2,1)} %bitcast.70, bf16[1536,1024]{1,0:T(8,128)(2,1)} %pad_maximum_fusion.refs_2_, ...), custom_call_target="tpu_custom_call" | custom-call | bytes 1024 | tf_op jit(solution)/shard_map/back/pallas_call | solution.py:477
  314.5 21.6 %back.6 = (bf16[192,1024]{1,0:T(8,128)(2,1)}, bf16[1536,192]{1,0:T(8,128)(2,1)}) custom-call(s32[2,32]{1,0:T(2,128)S(1)} %pad_add_fusion.order_ref.refs_0_, bf16[32,48,1344]{2,1,0:T(8,128)(2,1)} %all-gather.8.cloned.1.call-done.w_ref.refs_1_, bf16[192,1024]{1,0:T(8,128)(2,1)} %get-tuple-element.98.refs_2_, bf16[32,48,1024]{2,1,0:T(8,128)(2,1)} %bitcast.73), custom_call_target="tpu_custom_call" | custom-call | bytes 1024 | tf_op jit(solution)/shard_map/back/pallas_call | solution.py:477
  340.0 32.3 %back.7 = (f32[1536,128]{1,0:T(8,128)}, bf16[1536,192]{1,0:T(8,128)(2,1)}, f32[8,1536]{1,0:T(8,128)S(1)}, bf16[192,1024]{1,0:T(8,128)(2,1)}, bf16[1536,256]{1,0:T(8,128)(2,1)}) custom-call(s32[2,32]{1,0:T(2,128)S(1)} %pad_add_fusion.order_ref.refs_0_, bf16[1536,1344]{1,0:T(8,128)(2,1)} %bitcast.61, bf16[192,1024]{1,0:T(8,128)(2,1)} %copy-done.4, ...), custom_call_target="tpu_custom_call" | custom-call | bytes 1024 | tf_op jit(solution)/shard_map/back/pallas_call | solution.py:477
  372.3 21.7 %back.8 = (bf16[192,1024]{1,0:T(8,128)(2,1)}, bf16[1536,768]{1,0:T(8,128)(2,1)}) custom-call(s32[2,32]{1,0:T(2,128)S(1)} %pad_add_fusion.order_ref.refs_0_, bf16[32,48,1344]{2,1,0:T(8,128)(2,1)} %all-gather.8.cloned.1.call-done.w_ref.refs_1_, bf16[192,1024]{1,0:T(8,128)(2,1)} %get-tuple-element.106.refs_2_, bf16[32,48,1024]{2,1,0:T(8,128)(2,1)} %bitcast.72, ...), custom_call_target="tpu_custom_call" | custom-call | bytes 1024 | tf_op jit(solution)/shard_map/back/pallas_call | solution.py:477
  394.1 17.1 %attend_back.1.refs_2_ = bf16[576,1024]{1,0:T(8,128)(2,1)S(1)} custom-call(bf16[3,3,64,1024]{3,2,1,0:T(8,128)(2,1)} %get-tuple-element.94.part_in, bf16[3,1024,1024]{2,1,0:T(8,128)(2,1)} %get-tuple-element.95.p_in, bf16[192,1024]{1,0:T(8,128)(2,1)} %get-tuple-element.111.g_in, f32[32,1024]{1,0:T(8,128)S(1)} %get-tuple-element.202.cos_ref, ...), custom_call_target="tpu_custom_call" | custom-call | tf_op jit(solution)/shard_map/attend_back/pallas_call | solution.py:477
  412.3 24.1 %back.9 = (f32[1536,128]{1,0:T(8,128)}, bf16[1536,576]{1,0:T(8,128)(2,1)}, f32[8,1536]{1,0:T(8,128)S(1)}) custom-call(s32[2,32]{1,0:T(2,128)S(1)} %pad_add_fusion.order_ref.refs_0_, bf16[1536,1344]{1,0:T(8,128)(2,1)} %bitcast.62, bf16[576,1024]{1,0:T(8,128)(2,1)} %copy-done, bf16[1536,1024]{1,0:T(8,128)(2,1)} %get-tuple-element.81.h_ref.refs_3_, ...), custom_call_target="tpu_custom_call" | custom-call | bytes 1024 | tf_op jit(solution)/shard_map/back/pallas_call | solution.py:477
  437.8 37.3 %feed.1 = (bf16[48,18432]{1,0:T(8,128)(2,1)}, f32[1536,128]{1,0:T(8,128)}) custom-call(bf16[8,48,1536]{2,1,0:T(8,128)(2,1)} %reduce-scatter.5.cloned.1.call-done.refs_8_.gu_ref, bf16[8,48,768]{2,1,0:T(8,128)(2,1)} %reduce-scatter.7.cloned.1.call-done.refs_9_.down_ref, bf16[1536,768]{1,0:T(8,128)(2,1)} %bitcast.76, bf16[768,1024]{1,0:T(8,128)(2,1)} %copy-done.16, ...), custom_call_target="tpu_custom_call" | custom-call | bytes 1024 | tf_op jit(solution)/shard_map/feed/pallas_call | solution.py:477
  475.9 25.4 %reduce-scatter.9.cloned.1.call-done.w_ref = bf16[8,48,576]{2,1,0:T(8,128)(2,1)} async-done(((bf16[32,48,576]{2,1,0:T(8,128)(2,1)}), bf16[8,48,576]{2,1,0:T(8,128)(2,1)}) %reduce-scatter.9.cloned.1.call-update) | async-done | bytes 442384 | tf_op jit(solution)/shard_map/reduce_scatter | solution.py:2282
  501.3 34.8 %closing.1 = (bf16[128,3072]{1,0:T(8,128)(2,1)}, bf16[8,48,576]{2,1,0:T(8,128)(2,1)}, bf16[8,48,768]{2,1,0:T(8,128)(2,1)}, f32[8,8,1536]{2,1,0:T(8,128)}, f32[4,8,8,128]{3,2,1,0:T(8,128)}) custom-call(s32[2,32]{1,0:T(2,128)S(1)} %pad_add_fusion.order_ref.refs_0_, f32[32,48,128]{2,1,0:T(8,128)} %bitcast.83, f32[1536,128]{1,0:T(8,128)} %get-tuple-element.115.base_ref, ...), custom_call_target="tpu_custom_call" | custom-call | bytes 1024 | tf_op jit(solution)/shard_map/closing/pallas_call | solution.py:477
  541.2 21.3 %sheet_update.1 = (f32[48,29192]{1,0:T(8,128)}, f32[48,29192]{1,0:T(8,128)}, f32[48,29192]{1,0:T(8,128)}, f32[48,29192]{1,0:T(8,128)}, bf16[48,29192]{1,0:T(8,12...) custom-call(s32[1]{0:T(128)} %dynamic_slice.10.block_ref, ...), custom_call_target="tpu_custom_call" | custom-call | tf_op jit(solution)/shard_map/sheet_update/pallas_call | solution.py:2225
  (118 shorter events, 36.1 us)
Async XLA Ops:
  7.2 123.5 %all-gather.8.cloned.1.call-start = ((), (), s32[]{:S(2)}) async-start(), calls=%async_computation.6 | async-start | bytes 5406720 | tf_op jit(solution)/shard_map/all_gather | solution.py:2269
  11.1 32.8 %copy-start.14 = (s32[32]{0:T(128)S(1)}, s32[32]{0:T(128)}, u32[]{:S(2)}) copy-start(s32[32]{0:T(128)} %param.15) | copy-start | bytes 388
  42.2 3.4 copy-start.17
  42.2 4.3 copy-start.19
  42.3 213.4 %all-gather.4.cloned.1.call-start = ((), (), s32[]{:S(2)}) async-start(), calls=%async_computation.4 | async-start | bytes 5898240 | tf_op jit(solution)/shard_map/all_gather | solution.py:2269
  125.2 146.8 %all-gather.6.cloned.1.call-start = ((), (), s32[]{:S(2)}) async-start(), calls=%async_computation.5 | async-start | bytes 2949120 | tf_op jit(solution)/shard_map/all_gather | solution.py:2269
  126.0 214.1 %reduce-scatter.7.cloned.1.call-start = ((), (), s32[]{:S(2)}) async-start(), calls=%async_computation.8 | async-start | bytes 2949120 | tf_op jit(solution)/shard_map/reduce_scatter | solution.py:2282
  130.7 21.2 %copy-start.11 = (bf16[96,128]{1,0:T(8,128)(2,1)S(1)}, bf16[96,128]{1,0:T(8,128)(2,1)}, u32[]{:S(2)}) copy-start(bf16[96,128]{1,0:T(8,128)(2,1)} %get-tuple-element.83.refs_0_.refs_7_) | copy-start | bytes 73732
  151.1 0.7 copy-start.7
  203.3 6.7 %copy-start.13 = (f32[1,128]{1,0:T(1,128)}, f32[1,128]{1,0:T(1,128)S(1)}, u32[]{:S(2)}) copy-start(f32[1,128]{1,0:T(1,128)S(1)} %get-tuple-element.103.refs_5_) | copy-start | bytes 1540
  255.6 8.3 %copy-start.12 = (f32[1,128]{1,0:T(1,128)}, f32[1,128]{1,0:T(1,128)S(1)}, u32[]{:S(2)}) copy-start(f32[1,128]{1,0:T(1,128)S(1)} %get-tuple-element.91.refs_5_) | copy-start | bytes 1540
  263.9 3.2 copy-start.15
  263.9 4.2 copy-start.18
  267.1 4.9 copy-start.16
  272.0 140.3 %reduce-scatter.5.cloned.1.call-start = ((), (), s32[]{:S(2)}) async-start(), calls=%async_computation.7 | async-start | bytes 5898240 | tf_op jit(solution)/shard_map/reduce_scatter | solution.py:2282
  314.4 161.5 %reduce-scatter.11.cloned.1.call-start = ((), (), s32[]{:S(2)}) async-start(), calls=%async_computation.10 | async-start | bytes 2949120 | tf_op jit(solution)/shard_map/reduce_scatter | solution.py:2282
  336.0 1.0 copy-start.5
  394.1 107.2 %reduce-scatter.9.cloned.1.call-start = ((), (), s32[]{:S(2)}) async-start(), calls=%async_computation.9 | async-start | bytes 2457600 | tf_op jit(solution)/shard_map/reduce_scatter | solution.py:2282
  411.3 1.0 copy-start
  536.1 1.1 copy-start.1
  537.3 1.1 copy-start.2
  538.3 1.0 copy-start.3
  539.3 1.0 copy-start.6
  540.3 0.9 copy-start.9
  (3 other events, 2.1 us)
Sparse Core Ops, SparseCore 0:
  42.4 88.2 all-gather.7
  132.2 87.9 all-gather.3
  221.8 48.9 all-gather.5
  273.5 46.8 reduce-scatter.6
  322.5 84.7 reduce-scatter.4
  409.5 48.5 reduce-scatter.10
  460.3 40.9 reduce-scatter.8

commit v6 on v5

--- a/solution.py
+++ b/solution.py
@@ -1425,7 +1425,7 @@
     ]
     for fetch in fetches:
         fetch.start()
-    group, core, _, _ = near()
+    group, core, across, along = near()
     member = group * 2 + core
     plane = lax.axis_index("z")
     step = x_ref.shape[0] // 4
@@ -1453,38 +1453,50 @@
     for moving in first:
         moving.start()
 
-    others = [lax.rem(group + k, 4) for k in range(1, 4)]
+    others = [across, along, across + along - group]
     keep = pltpu.make_async_copy(frames(x_ref, group), frames(held, group), local_sem.at[1])
     keep.start()
 
-    def spread(owner, landing):
+    def piece(ref, j, a):
+        at = pl.ds(pl.multiple_of(j * step, 16), step)
+        return ref.at[at, a * features : (a + 1) * features]
+
+    def spread(owner, landing, a):
         return pltpu.make_async_remote_copy(
-            src_ref=frames(x_ref, owner),
-            dst_ref=frames(held, landing),
-            send_sem=send_sem.at[10 + owner],
-            recv_sem=recv_sem.at[10 + landing],
+            src_ref=piece(x_ref, owner, a),
+            dst_ref=piece(held, landing, a),
+            send_sem=send_sem.at[(10, 36)[a] + owner],
+            recv_sem=recv_sem.at[(10, 36)[a] + landing],
             device_id={"dp": owner},
             device_id_type=MESH_ID,
         )
 
-    for owner in others:
-        spread(owner, group).start()
-
-    def rise(row):
+    for a in range(2):
+        for owner in others:
+            spread(owner, group, a).start()
+
+    def rise(row, a):
         return pltpu.make_async_remote_copy(
-            src_ref=frames(held, row),
-            dst_ref=frames(t_ref, plane),
-            send_sem=send_sem.at[28 + row],
-            recv_sem=recv_sem.at[28 + plane],
+            src_ref=piece(held, row, a),
+            dst_ref=piece(t_ref, plane, a),
+            send_sem=send_sem.at[(28, 32)[a] + row],
+            recv_sem=recv_sem.at[(28, 32)[a] + plane],
             device_id={"z": row},
             device_id_type=MESH_ID,
         )
 
-    stay = pltpu.make_async_copy(frames(held, plane), frames(t_ref, plane), local_sem.at[4])
-
-    def pass_on(row):
-        pl.when(row == plane)(stay.start)
-        pl.when(row != plane)(rise(row).start)
+    stay = [
+        pltpu.make_async_copy(piece(held, plane, a), piece(t_ref, plane, a), local_sem.at[(4, 9)[a]])
+        for a in range(2)
+    ]
+
+    def pass_on(row, a):
+        pl.when(row == plane)(stay[a].start)
+        pl.when(row != plane)(rise(row, a).start)
+
+    keep.wait()
+    for a in range(2):
+        pass_on(group, a)
 
     fetches[2].wait()
     fetches[3].wait()
@@ -1497,6 +1509,9 @@
             move(m, (4 * part if k < 3 else -3 * part) + k * part, k * D + m * part, part)
         for k in range(2):
             move(m, 3 * part + k * text, 6 * D + k * CTXW + m * text, text)
+    for owner in others:
+        spread(owner, owner, 0).wait_recv()
+        pass_on(owner, 0)
     weights_done = exchange_steps(
         block, block, one, one_ref, local_sem.at[2], mover(send_sem, recv_sem, 14)
     )
@@ -1520,11 +1535,9 @@
         for k, peer in enumerate(peers):
             text_copy(k, peer).start()
 
-    keep.wait()
-    pass_on(group)
     for owner in others:
-        spread(owner, owner).wait_recv()
-        pass_on(owner)
+        spread(owner, owner, 1).wait_recv()
+        pass_on(owner, 1)
 
     for k in range(7):
         landed = all_ref.at[plane, lax.rem(member + 7 - k, 8)]
@@ -1540,17 +1553,18 @@
         landed = all_ref.at[lax.rem(plane + 3 - k, 4)]
         line_copy(k, landed, landed, {"z": line[k]}).wait_recv()
 
-    for there in line:
-        landed = frames(t_ref, there)
-        pltpu.make_async_remote_copy(
-            src_ref=landed,
-            dst_ref=landed,
-            send_sem=send_sem.at[28 + there],
-            recv_sem=recv_sem.at[28 + there],
-            device_id={"z": there},
-            device_id_type=MESH_ID,
-        ).wait_recv()
-    stay.wait()
+    for a in range(2):
+        for there in line:
+            landed = piece(t_ref, there, a)
+            pltpu.make_async_remote_copy(
+                src_ref=landed,
+                dst_ref=landed,
+                send_sem=send_sem.at[(28, 32)[a] + there],
+                recv_sem=recv_sem.at[(28, 32)[a] + there],
+                device_id={"z": there},
+                device_id_type=MESH_ID,
+            ).wait_recv()
+        stay[a].wait()
     weights_done()
 
     @pl.when(teacher)
@@ -1565,10 +1579,11 @@
 
     for moving in first + second:
         moving.wait_send()
-    for owner in others:
-        spread(owner, group).wait_send()
-    for there in line:
-        rise(there).wait_send()
+    for a in range(2):
+        for owner in others:
+            spread(owner, group, a).wait_send()
+        for there in line:
+            rise(there, a).wait_send()
 
 
 def opening(latents, cotangent, small, text, sheet):
@@ -1591,9 +1606,9 @@
             pltpu.VMEM(local, low),
             pltpu.VMEM((sheet.shape[0], 6 * D + 2 * CTXW), jnp.float32),
             pltpu.VMEM(one, low),
-            pltpu.SemaphoreType.DMA((9,)),
-            pltpu.SemaphoreType.DMA((32,)),
-            pltpu.SemaphoreType.DMA((32,)),
+            pltpu.SemaphoreType.DMA((10,)),
+            pltpu.SemaphoreType.DMA((40,)),
+            pltpu.SemaphoreType.DMA((40,)),
         ],
         compiler_params=pltpu.CompilerParams(
             collective_id=identity_of("opening", sheet),
@@ -1649,98 +1664,147 @@
     )(shard, other, sheet)
 
 
+def prepare_kernel(order_ref, y_ref, base_ref, grad_ref, gu_ref, down_ref, two_ref, x_ref, q_ref, y):
+    features = base_ref.shape[0]
+    reorder_blocks(y_ref, y, lambda b: order_ref[1, b])
+    x_ref[:, :features] = (base_ref[...] + y[...]).T.astype(x_ref.dtype)
+    x_ref[:, features:] = grad_ref[...].T.astype(x_ref.dtype)
+    q_ref[...] = jnp.full(q_ref.shape, square_sum((gu_ref, down_ref, two_ref)), jnp.float32)
+
+
+def prepare(orders, y, base, grad, gu, down, two):
+    features, width = base.shape
+    return kernel_call(
+        prepare_kernel,
+        out_shape=(
+            jax.ShapeDtypeStruct((width, 2 * features), jnp.bfloat16),
+            jax.ShapeDtypeStruct((8, 128), jnp.float32),
+        ),
+        in_specs=[IN_SMEM] + [IN_VMEM] * 6,
+        out_specs=(IN_VMEM,) * 2,
+        scratch_shapes=[pltpu.VMEM(base.shape, jnp.float32)],
+        compiler_params=pltpu.CompilerParams(vmem_limit_bytes=16 * 2**20),
+        name="prepare",
+    )(orders, y.reshape(orders.shape[1], -1, width), base, grad, gu, down, two)
+
+
+def square_sum(refs):
+    total = jnp.zeros((), jnp.float32)
+    for ref in refs:
+        line_sum = jnp.zeros((1, ref.shape[2]), jnp.float32)
+        for m in range(8):
+            line_sum += jnp.sum(jnp.square(wide(ref.at[m])), axis=0, keepdims=True)
+        total += jnp.sum(line_sum)
+    return total
+
+
 def closing_kernel(
-    order_ref,
-    y_ref,
-    base_ref,
-    grad_ref,
+    x_ref,
+    p_ref,
     w_ref,
-    v_ref,
-    gu_ref,
-    down_ref,
     g_ref,
+    _,
     t_ref,
     o_ref,
-    vo_ref,
     s_ref,
     all_ref,
-    by_block,
-    sorted_y,
-    base,
-    grad,
-    x_ref,
     held,
     tall,
     q_ref,
     one,
-    two,
-    gu,
-    down,
     local_sem,
     send_sem,
     recv_sem,
 ):
-    fetches = [
-        pltpu.make_async_copy(ref, here, local_sem.at[7 + k])
-        for k, (ref, here) in enumerate(
-            [(y_ref, by_block), (base_ref, base), (grad_ref, grad)]
-            + [(w_ref, one), (v_ref, two), (gu_ref, gu), (down_ref, down)]
-        )
-    ]
-    for fetch in fetches:
-        fetch.start()
-    group, core, _, _ = near()
+    fetch = pltpu.make_async_copy(w_ref, one, local_sem.at[0])
+    fetch.start()
+    group, core, across, along = near()
     member = group * 2 + core
     plane = lax.axis_index("z")
-    step = x_ref.shape[0] // 4
-    line = [lax.rem(plane + k, 4) for k in range(1, 4)]
-    back = [lax.rem(plane + 3 - k, 4) for k in range(3)]
-    groups = [lax.rem(group + k, 4) for k in range(1, 4)]
+    step, features = x_ref.shape[0] // 4, x_ref.shape[1] // 2
+    groups = [across, along, across + along - group]
+    inner = lax.div(plane * (3 - plane), 2)
+    two_off, mirrored = lax.rem(plane + 2, 4), 3 - plane
+    line = [
+        plane + 1 - 2 * lax.rem(plane, 2),
+        inner * mirrored + (1 - inner) * two_off,
+        inner * two_off + (1 - inner) * mirrored,
+    ]
     peers = plane_peers()
     greet([member_at(peer) for peer in peers] + [{"z": there} for there in line])
 
-    def frames(ref, j):
-        return ref.at[pl.ds(pl.multiple_of(j * step, 16), step), :]
-
-    copy = mover(send_sem, recv_sem)
-    gain_line = mover(send_sem, recv_sem, 14)
-    gain_plane = mover(send_sem, recv_sem, 17)
-    square_plane = mover(send_sem, recv_sem, 24)
-    square_line = mover(send_sem, recv_sem, 31)
+    def piece(ref, j, a):
+        at = pl.ds(pl.multiple_of(j * step, 16), step)
+        return ref.at[at, a * features : (a + 1) * features]
+
+    def cross_line(there, a):
+        return pltpu.make_async_remote_copy(
+            src_ref=piece(x_ref, there, a),
+            dst_ref=piece(held, plane, a),
+            send_sem=send_sem.at[4 * a + there],
+            recv_sem=recv_sem.at[4 * a + plane],
+            device_id={"z": there},
+            device_id_type=MESH_ID,
+        )
+
+    def onward(owner, a):
+        return pltpu.make_async_remote_copy(
+            src_ref=piece(held, owner, a),
+            dst_ref=piece(t_ref, group, a),
+            send_sem=send_sem.at[8 + 4 * a + owner],
+            recv_sem=recv_sem.at[8 + 4 * a + group],
+            device_id={"dp": owner},
+            device_id_type=MESH_ID,
+        )
+
+    def landed(ref, j, a, sem, peer):
+        at = piece(ref, j, a)
+        pltpu.make_async_remote_copy(
+            src_ref=at,
+            dst_ref=at,
+            send_sem=send_sem.at[sem],
+            recv_sem=recv_sem.at[sem],
+            device_id=peer,
+            device_id_type=MESH_ID,
+        ).wait_recv()
+
+    keep = [
+        pltpu.make_async_copy(piece(held, group, a), piece(t_ref, group, a), local_sem.at[1 + a])
+        for a in range(2)
+    ]
+
+    def pass_on(owner, a):
+        pl.when(owner == group)(keep[a].start)
+        pl.when(owner != group)(onward(owner, a).start)
+
+    gain_line = mover(send_sem, recv_sem, 23)
+    gain_plane = mover(send_sem, recv_sem, 26)
+    square_plane = mover(send_sem, recv_sem, 33)
+    square_line = mover(send_sem, recv_sem, 40)
+    turned_line = [lax.rem(plane + k, 4) for k in range(1, 4)]
+    back_line = [lax.rem(plane + 3 - k, 4) for k in range(3)]
     gain_local = pltpu.make_async_copy(g_ref, tall.at[plane], local_sem.at[3])
     gain_local.start()
-    sent = [gain_line(k, g_ref, tall.at[plane], {"z": there}) for k, there in enumerate(line)]
-    for fetch in fetches[:3]:
-        fetch.wait()
-    reorder_blocks(by_block, sorted_y, lambda b: order_ref[1, b])
-    features = base.shape[0]
-    x_ref[:, :features] = (base[...] + sorted_y[...]).T.astype(x_ref.dtype)
-    x_ref[:, features:] = grad[...].T.astype(x_ref.dtype)
-    local = pltpu.make_async_copy(frames(x_ref, plane), frames(held, plane), local_sem.at[0])
-    local.start()
-    sent += [
-        copy(k, frames(x_ref, there), frames(held, plane), {"z": there})
-        for k, there in enumerate(line)
+    sent = [
+        gain_line(k, g_ref, tall.at[plane], {"z": there}) for k, there in enumerate(turned_line)
     ]
     for moving in sent:
         moving.start()
+    local = pltpu.make_async_copy(
+        x_ref.at[pl.ds(pl.multiple_of(plane * step, 16), step), :],
+        held.at[pl.ds(pl.multiple_of(plane * step, 16), step), :],
+        local_sem.at[4],
+    )
+    local.start()
+    for a in range(2):
+        for there in line:
+            cross_line(there, a).start()
+    fetch.wait()
     weights_done = exchange_steps(
-        block, block, w_ref, o_ref, local_sem.at[1], mover(send_sem, recv_sem, 7)
-    )
-    others_done = exchange_steps(
-        block, block, v_ref, vo_ref, local_sem.at[6], mover(send_sem, recv_sem, 34)
-    )
-
-    for fetch in fetches[3:]:
-        fetch.wait()
-    total = jnp.zeros((), jnp.float32)
-    for ref in (one, two, gu, down):
-        line_sum = jnp.zeros((1, ref.shape[2]), jnp.float32)
-        for m in range(8):
-            line_sum += jnp.sum(jnp.square(wide(ref.at[m])), axis=0, keepdims=True)
-        total += jnp.sum(line_sum)
-    q_ref[...] = jnp.full(q_ref.shape, total, jnp.float32)
-    square_local = pltpu.make_async_copy(q_ref, all_ref.at[plane, member], local_sem.at[5])
+        block, block, one, o_ref, local_sem.at[5], mover(send_sem, recv_sem, 16)
+    )
+    q_ref[...] = p_ref[...] + square_sum((one,))
+    square_local = pltpu.make_async_copy(q_ref, all_ref.at[plane, member], local_sem.at[6])
     square_local.start()
     shown = [
         square_plane(k, q_ref, all_ref.at[plane, member], member_at(peer))
@@ -1748,109 +1812,79 @@
     ]
     for moving in shown:
         moving.start()
+    local.wait()
+    for a in range(2):
+        pass_on(plane, a)
     gain_local.wait()
-    for k, origin in enumerate(back):
+    for k, origin in enumerate(back_line):
         gain_line(k, tall.at[origin], tall.at[origin], {"z": origin}).wait_recv()
     tall[4] = tall[0] + tall[1] + tall[2] + tall[3]
-    gain_keep = pltpu.make_async_copy(tall.at[4], s_ref.at[member], local_sem.at[4])
+    gain_keep = pltpu.make_async_copy(tall.at[4], s_ref.at[member], local_sem.at[7])
     gain_keep.start()
     given = [
         gain_plane(k, tall.at[4], s_ref.at[member], member_at(peer)) for k, peer in enumerate(peers)
     ]
     for moving in given:
         moving.start()
-
-    def onward(owner):
-        return pltpu.make_async_remote_copy(
-            src_ref=frames(held, owner),
-            dst_ref=frames(t_ref, group),
-            send_sem=send_sem.at[3 + owner],
-            recv_sem=recv_sem.at[3 + group],
-            device_id={"dp": owner},
-            device_id_type=MESH_ID,
-        )
-
-    keep = pltpu.make_async_copy(frames(held, group), frames(t_ref, group), local_sem.at[2])
-
-    def pass_on(owner):
-        pl.when(owner == group)(keep.start)
-        pl.when(owner != group)(onward(owner).start)
-
     square_local.wait()
     for k in range(7):
-        landed = all_ref.at[plane, lax.rem(member + 7 - k, 8)]
-        square_plane(k, landed, landed, member_at(peers[k])).wait_recv()
-    for k, there in enumerate(line):
+        shown_here = all_ref.at[plane, lax.rem(member + 7 - k, 8)]
+        square_plane(k, shown_here, shown_here, member_at(peers[k])).wait_recv()
+    for k, there in enumerate(turned_line):
         shown.append(square_line(k, all_ref.at[plane], all_ref.at[plane], {"z": there}))
         shown[-1].start()
-    local.wait()
-    pass_on(plane)
-    for k, origin in enumerate(back):
-        landed = frames(held, origin)
-        copy(k, landed, landed, {"z": origin}).wait_recv()
-        pass_on(origin)
-    for origin in groups:
-        landed = frames(t_ref, origin)
-        pltpu.make_async_remote_copy(
-            src_ref=landed,
-            dst_ref=landed,
-            send_sem=send_sem.at[3 + origin],
-            recv_sem=recv_sem.at[3 + origin],
-            device_id={"dp": origin},
-            device_id_type=MESH_ID,
-        ).wait_recv()
-    keep.wait()
+    for a in range(2):
+        for origin in line:
+            landed(held, origin, a, 4 * a + origin, {"z": origin})
+            pass_on(origin, a)
+    for a in range(2):
+        for origin in groups:
+            landed(t_ref, origin, a, 8 + 4 * a + origin, {"dp": origin})
+        keep[a].wait()
     weights_done()
-    others_done()
     gain_keep.wait()
     for k in range(7):
-        landed = s_ref.at[lax.rem(member + 7 - k, 8)]
-        gain_plane(k, landed, landed, member_at(peers[k])).wait_recv()
-    for k, origin in enumerate(back):
+        given_here = s_ref.at[lax.rem(member + 7 - k, 8)]
+        gain_plane(k, given_here, given_here, member_at(peers[k])).wait_recv()
+    for k, origin in enumerate(back_line):
         square_line(k, all_ref.at[origin], all_ref.at[origin], {"z": origin}).wait_recv()
     for moving in sent + given + shown:
         moving.wait_send()
-    for origin in groups:
-        onward(origin).wait_send()
-
-
-def closing(orders, y, base, grad, one, two, gu, down, gains):
-    features, width = base.shape
-    blocks = orders.shape[1]
-    frames = (width, 2 * features)
-    parts = (one, two, gu, down)
+    for a in range(2):
+        for there in line:
+            cross_line(there, a).wait_send()
+        for owner in groups:
+            onward(owner, a).wait_send()
+
+
+def closing(local, squares, one, gains, after):
     return kernel_call(
         closing_kernel,
         out_shape=(
-            jax.ShapeDtypeStruct(frames, jnp.bfloat16),
+            jax.ShapeDtypeStruct(local.shape, local.dtype),
             jax.ShapeDtypeStruct(one.shape, one.dtype),
-            jax.ShapeDtypeStruct(two.shape, two.dtype),
             jax.ShapeDtypeStruct((8,) + gains.shape, gains.dtype),
-            jax.ShapeDtypeStruct((4, 8, 8, 128), jnp.float32),
+            jax.ShapeDtypeStruct((4, 8) + squares.shape, jnp.float32),
         ),
-        in_specs=[IN_SMEM] + [IN_HBM] * 8,
-        out_specs=(IN_HBM,) * 5,
-        scratch_shapes=[pltpu.VMEM((blocks, features // blocks, width), jnp.float32)]
-        + [pltpu.VMEM(base.shape, jnp.float32)] * 3
-        + [pltpu.VMEM(frames, jnp.bfloat16)] * 2
-        + [
+        in_specs=[IN_VMEM, IN_VMEM] + [IN_HBM] * 3,
+        out_specs=(IN_VMEM,) * 4,
+        scratch_shapes=[
+            pltpu.VMEM(local.shape, local.dtype),
             pltpu.VMEM((5,) + gains.shape, gains.dtype),
-            pltpu.VMEM((8, 128), jnp.float32),
-        ]
-        + [pltpu.VMEM(part.shape, part.dtype) for part in parts]
-        + [
-            pltpu.SemaphoreType.DMA((14,)),
-            pltpu.SemaphoreType.DMA((41,)),
-            pltpu.SemaphoreType.DMA((41,)),
+            pltpu.VMEM(squares.shape, jnp.float32),
+            pltpu.VMEM(one.shape, one.dtype),
+            pltpu.SemaphoreType.DMA((8,)),
+            pltpu.SemaphoreType.DMA((43,)),
+            pltpu.SemaphoreType.DMA((43,)),
         ],
         compiler_params=pltpu.CompilerParams(
-            collective_id=identity_of("closing", y),
+            collective_id=identity_of("closing", one),
             has_side_effects=True,
-            vmem_limit_bytes=24 * 2**20,
+            vmem_limit_bytes=8 * 2**20,
         ),
         cost_estimate=BRIEF,
         name="closing",
-    )(orders, y.reshape(blocks, -1, width), base, grad, one, two, gu, down, gains)
+    )(local, squares, one, gains, after)
 
 
 def turned(values, cosine, sine_table):
@@ -2234,12 +2268,12 @@
         in_specs=[
             IN_SMEM,
             IN_SMEM,
-            whole(one.shape),
-            whole(two.shape),
+            IN_VMEM,
+            IN_VMEM,
             pl.BlockSpec((rows, 2 * D), lambda i: (0, jnp.clip(i - 3, 0, 5))),
-            whole(squares.shape),
-            whole(gains.shape),
-            whole(pair.shape),
+            IN_VMEM,
+            IN_VMEM,
+            IN_VMEM,
             column_block,
             column_block,
             column_block,
@@ -2473,8 +2507,12 @@
         ],
         axis=0,
     )
-    out_pair, sums_one, sums_two, gain_sums, squares = closing(
-        orders, ff_out, x_two, latent_grad, sums_one, sums_two, sums_gu, sums_down, gain_grads
+    pair, squares = prepare(
+        orders, ff_out, x_two, latent_grad, sums_gu, sums_down, sums_two
+    )
+    sums_two = exchange_blocks(sums_two, [sums_feed])
+    out_pair, sums_one, gain_sums, squares = closing(
+        pair, squares, sums_one, gain_grads, sums_two
     )
     place = lax.axis_index("dp") * (planes * cores) + plane * cores + lax.axis_index("core")
     (

time: 581 us -> 566 us (0.974)
  waiting for transfers between devices: 28.9 us -> 14.1 us
    reduce_scatter x4, waiting for transfers between devices: 25.4 us -> 10.4 us  [scatter_line(): return lax.psum_scatter(blocks, 'z', scatter_dimension=0, tiled=True)]
    pallas_call x15 -> x17, Pallas kernels: 440 us -> 442 us  [run(): call(*[pltpu.with_memory_space_constraint(operand, pltpu.HBM) if place is...]
    unnamed x43 -> x51, local copies, waits for them, and re-layouts: 15.7 us -> 16 us
  transfers between devices with their start and end apart: 7 -> 7, of which waited for: 2 -> 2; matrix products, arithmetic and copies ran while one was open for 8% -> 8% of each run, Pallas kernels for 66% -> 68%
where the time goes in v6:
time: 566 us; the launch traced here: 559 us
  Pallas kernels  464 us (82%)
  local copies, waits for them, and re-layouts  25.6 us (5%)
  matrix products  20.3 us (4%)
  other arithmetic  18.8 us (3%)
  between operations  15.8 us (3%)
  waiting for transfers between devices  14.1 us (2%)
    pallas_call x17, Pallas kernels, run(): call(*[pltpu.with_memory_space_constraint(operand, pltpu.HBM) if place is...  442 us
    pallas_call x1, Pallas kernels, sheet_update(): pl.pallas_call(update_kernel, grid=(10,), out_shape=(like, like, like, li...  21.3 us
    dot_general x2, matrix products, contract_rows(): lax.dot_general(left, right, (((0,), (0,)), ((), ())), preferred_element_...  16.4 us
    unnamed x51, local copies, waits for them, and re-layouts  16 us
  transfers between devices with their start and end apart: 7, of which 2 were waited for; matrix products, arithmetic and copies ran while one was open for 8% of the time, Pallas kernels for 68%

profile of v6, /device:TPU:0, one launch (start us, length us, event | category | flops | bytes accessed | tf_op | source)
XLA Modules:
  0.0 558.7 jit_solution(18338133295456122591)
XLA Ops:
  11.1 28.1 %opening.1 = (bf16[128,3072]{1,0:T(8,128)(2,1)}, f32[4,8,8,128]{3,2,1,0:T(8,128)}, bf16[96,128]{1,0:T(8,128)(2,1)}, bf16[8,48,1344]{2,1,0:T(8,128)(2,1)}) custom-call(bf16[128,1536]{1,0:T(8,128)(2,1)} %bitcast.85, bf16[128,1536]{1,0:T(8,128)(2,1)} %bitcast.86, f32[8,128]{1,0:T(8,128)} %select_maximum_fusion.small_ref, bf16[768,128]{1,0:T(8,128)(2,1)} %bitcast.82, ...), custom_call_target="tpu_custom_call" | custom-call | bytes 1024 | tf_op jit(solution)/shard_map/opening/pallas_call | solution.py:477
  50.5 2.1 slice_reduce_fusion
  55.1 4.5 convert_element_type.78.sheet_ref
  59.5 59.1 %first_gather.1 = (bf16[1536,1024]{1,0:T(8,128)(2,1)}, bf16[1536,1024]{1,0:T(8,128)(2,1)}, bf16[8,48,1536]{2,1,0:T(8,128)(2,1)}, bf16[8,48,768]{2,1,0:T(8,128)(2,1)}) custom-call(bf16[1536,128]{1,0:T(8,128)(2,1)} %bitcast.81, bf16[1536,128]{1,0:T(8,128)(2,1)} %bitcast.80, bf16[48,29192]{1,0:T(8,128)(2,1)} %convert_element_type.78.sheet_ref), custom_call_target="tpu_custom_call" | custom-call | bytes 1024 | tf_op jit(solution)/shard_map/first_gather/pallas_call | solution.py:477
  121.5 2.9 all-gather.8.cloned.1.call-done.w_ref.refs_1_
  124.4 20.4 %attend.1 = (bf16[3,3,64,1024]{3,2,1,0:T(8,128)(2,1)}, bf16[3,1024,1024]{2,1,0:T(8,128)(2,1)}, bf16[192,1024]{1,0:T(8,128)(2,1)S(1)}) custom-call(bf16[1536,1344]{1,0:T(8,128)(2,1)} %bitcast.60, bf16[1536,1024]{1,0:T(8,128)(2,1)} %get-tuple-element.82.h_ref.refs_3_, f32[32,1024]{1,0:T(8,128)S(1)} %get-tuple-element.204.cos_ref, ...), custom_call_target="tpu_custom_call" | custom-call | tf_op jit(solution)/shard_map/attend/pallas_call | solution.py:477
  145.6 51.5 %project_sum.1 = (bf16[1536,1024]{1,0:T(8,128)(2,1)}, f32[1536,128]{1,0:T(8,128)}, f32[1536,128]{1,0:T(8,128)}, f32[1,128]{1,0:T(1,128)S(1)}, bf16[1536,1024]{1,0:T(8,128)(2,1)}, /*index=5*/bf16[192,256]{1,0:T(8,128)(2,1)S(1)}) custom-call(s32[2,32]{1,0:T(2,128)S(1)} %pad_add_fusion.order_ref.refs_0_, bf16[192,1024]{1,0:T(8,128)(2,1)} %copy-done.12, ...), custom_call_target="tpu_custom_call" | custom-call | bytes 1024 | tf_op jit(solution)/shard_map/project_sum/pallas_call | solution.py:477
  197.1 6.7 %cross.1 = (bf16[192,1024]{1,0:T(8,128)(2,1)S(1)}, bf16[3,128,1024]{2,1,0:T(8,128)(2,1)S(1)}, bf16[192,1024]{1,0:T(8,128)(2,1)S(1)}) custom-call(bf16[1536,1344]{1,0:T(8,128)(2,1)} %bitcast.61, bf16[1536,1024]{1,0:T(8,128)(2,1)} %get-tuple-element.85.h_ref.refs_3_, bf16[192,256]{1,0:T(8,128)(2,1)S(1)} %get-tuple-element.86.kv_ref), custom_call_target="tpu_custom_call" | custom-call | tf_op jit(solution)/shard_map/cross/pallas_call | solution.py:477
  204.5 44.8 %project_slots.1 = (bf16[1536,1024]{1,0:T(8,128)(2,1)}, f32[1536,128]{1,0:T(8,128)}, f32[1536,128]{1,0:T(8,128)}, f32[1,128]{1,0:T(1,128)S(1)}, bf16[1536,1024]{1,0:T(8,128)(2,1)}) custom-call(s32[2,32]{1,0:T(2,128)S(1)} %pad_add_fusion.order_ref.refs_0_, bf16[192,1024]{1,0:T(8,128)(2,1)} %copy-done.13, ...), custom_call_target="tpu_custom_call" | custom-call | bytes 1024 | tf_op jit(solution)/shard_map/project_slots/pallas_call | solution.py:477
  249.4 8.1 %fusion.11 = f32[1536,1024]{1,0:T(8,128)S(1)} fusion(bf16[1536,1536]{1,0:T(8,128)(2,1)} %bitcast.70, bf16[1536,1024]{1,0:T(8,128)(2,1)} %get-tuple-element.89.refs_3_), kind=kOutput, calls=%fused_computation.81 | convolution fusion | flops 4831838208 | bytes 14155776 | tf_op jit(solution)/shard_map/dot_general | solution.py:430
  258.5 2.2 copy-done.19
  261.7 3.9 convolution_convert_fusion
  265.7 8.3 %multiply_convert_fusion.1 = (bf16[768,1024]{1,0:T(8,128)(2,1)S(1)}, bf16[768,1024]{1,0:T(8,128)(2,1)S(1)}) fusion(f32[1536,1024]{1,0:T(8,128)} %copy-done.19, bf16[1536,768]{1,0:T(8,128)(2,1)} %bitcast.76, bf16[1536,1024]{1,0:T(8,128)(2,1)} %get-tuple-element.80), kind=kOutput, calls=%fused_computation.9 | convolution fusion | flops 2426142720 | bytes 14942208 | tf_op jit(solution)/shard_map/dot_general | solution.py:430
  275.9 32.1 %back.5 = (f32[1536,128]{1,0:T(8,128)}, bf16[1536,1536]{1,0:T(8,128)(2,1)}, f32[8,1536]{1,0:T(8,128)S(1)}, bf16[192,1024]{1,0:T(8,128)(2,1)}) custom-call(s32[2,32]{1,0:T(2,128)S(1)} %pad_add_fusion.order_ref.refs_0_, bf16[1536,1536]{1,0:T(8,128)(2,1)} %bitcast.71, bf16[1536,1024]{1,0:T(8,128)(2,1)} %pad_maximum_fusion.refs_2_, ...), custom_call_target="tpu_custom_call" | custom-call | bytes 1024 | tf_op jit(solution)/shard_map/back/pallas_call | solution.py:477
  308.1 21.6 %back.6 = (bf16[192,1024]{1,0:T(8,128)(2,1)}, bf16[1536,192]{1,0:T(8,128)(2,1)}) custom-call(s32[2,32]{1,0:T(2,128)S(1)} %pad_add_fusion.order_ref.refs_0_, bf16[32,48,1344]{2,1,0:T(8,128)(2,1)} %all-gather.8.cloned.1.call-done.w_ref.refs_1_, bf16[192,1024]{1,0:T(8,128)(2,1)} %get-tuple-element.99.refs_2_, bf16[32,48,1024]{2,1,0:T(8,128)(2,1)} %bitcast.74), custom_call_target="tpu_custom_call" | custom-call | bytes 1024 | tf_op jit(solution)/shard_map/back/pallas_call | solution.py:477
  333.7 32.3 %back.7 = (f32[1536,128]{1,0:T(8,128)}, bf16[1536,192]{1,0:T(8,128)(2,1)}, f32[8,1536]{1,0:T(8,128)S(1)}, bf16[192,1024]{1,0:T(8,128)(2,1)}, bf16[1536,256]{1,0:T(8,128)(2,1)}) custom-call(s32[2,32]{1,0:T(2,128)S(1)} %pad_add_fusion.order_ref.refs_0_, bf16[1536,1344]{1,0:T(8,128)(2,1)} %bitcast.62, bf16[192,1024]{1,0:T(8,128)(2,1)} %copy-done.10, ...), custom_call_target="tpu_custom_call" | custom-call | bytes 1024 | tf_op jit(solution)/shard_map/back/pallas_call | solution.py:477
  365.9 21.7 %back.8 = (bf16[192,1024]{1,0:T(8,128)(2,1)}, bf16[1536,768]{1,0:T(8,128)(2,1)}) custom-call(s32[2,32]{1,0:T(2,128)S(1)} %pad_add_fusion.order_ref.refs_0_, bf16[32,48,1344]{2,1,0:T(8,128)(2,1)} %all-gather.8.cloned.1.call-done.w_ref.refs_1_, bf16[192,1024]{1,0:T(8,128)(2,1)} %get-tuple-element.107.refs_2_, bf16[32,48,1024]{2,1,0:T(8,128)(2,1)} %bitcast.73, ...), custom_call_target="tpu_custom_call" | custom-call | bytes 1024 | tf_op jit(solution)/shard_map/back/pallas_call | solution.py:477
  387.8 17.2 %attend_back.1.refs_2_ = bf16[576,1024]{1,0:T(8,128)(2,1)S(1)} custom-call(bf16[3,3,64,1024]{3,2,1,0:T(8,128)(2,1)} %get-tuple-element.95.part_in, bf16[3,1024,1024]{2,1,0:T(8,128)(2,1)} %get-tuple-element.96.p_in, bf16[192,1024]{1,0:T(8,128)(2,1)} %get-tuple-element.112.g_in, f32[32,1024]{1,0:T(8,128)S(1)} %get-tuple-element.204.cos_ref, ...), custom_call_target="tpu_custom_call" | custom-call | tf_op jit(solution)/shard_map/attend_back/pallas_call | solution.py:477
  405.9 24.1 %back.9 = (f32[1536,128]{1,0:T(8,128)}, bf16[1536,576]{1,0:T(8,128)(2,1)}, f32[8,1536]{1,0:T(8,128)S(1)}) custom-call(s32[2,32]{1,0:T(2,128)S(1)} %pad_add_fusion.order_ref.refs_0_, bf16[1536,1344]{1,0:T(8,128)(2,1)} %bitcast.63, bf16[576,1024]{1,0:T(8,128)(2,1)} %copy-done.3, bf16[1536,1024]{1,0:T(8,128)(2,1)} %get-tuple-element.82.h_ref.refs_3_, ...), custom_call_target="tpu_custom_call" | custom-call | bytes 1024 | tf_op jit(solution)/shard_map/back/pallas_call | solution.py:477
  431.5 37.3 %feed.1 = (bf16[48,18432]{1,0:T(8,128)(2,1)}, f32[1536,128]{1,0:T(8,128)}) custom-call(bf16[8,48,1536]{2,1,0:T(8,128)(2,1)} %reduce-scatter.5.cloned.1.call-done.refs_8_.gu_ref, bf16[8,48,768]{2,1,0:T(8,128)(2,1)} %reduce-scatter.7.cloned.1.call-done.refs_9_.down_ref, bf16[1536,768]{1,0:T(8,128)(2,1)} %bitcast.77, bf16[768,1024]{1,0:T(8,128)(2,1)} %copy-done.20, ...), custom_call_target="tpu_custom_call" | custom-call | bytes 1024 | tf_op jit(solution)/shard_map/feed/pallas_call | solution.py:477
  468.8 9.4 %plane_exchange.1._.two_ref = bf16[8,48,768]{2,1,0:T(8,128)(2,1)} custom-call(bf16[8,48,768]{2,1,0:T(8,128)(2,1)} %reduce-scatter.9.cloned.1.call-done.two_ref.x_ref, bf16[48,18432]{1,0:T(8,128)(2,1)} %get-tuple-element.124.refs_0_.feed_ref), custom_call_target="tpu_custom_call" | custom-call | bytes 1024 | tf_op jit(solution)/shard_map/plane_exchange/pallas_call | solution.py:477
  484.8 10.3 %reduce-scatter.11.cloned.1.call-done.w_ref = bf16[8,48,576]{2,1,0:T(8,128)(2,1)} async-done(((bf16[32,48,576]{2,1,0:T(8,128)(2,1)}), bf16[8,48,576]{2,1,0:T(8,128)(2,1)}) %reduce-scatter.11.cloned.1.call-update) | async-done | bytes 442384 | tf_op jit(solution)/shard_map/reduce_scatter | solution.py:2316
  496.2 33.2 %closing.1 = (bf16[128,3072]{1,0:T(8,128)(2,1)S(1)}, bf16[8,48,576]{2,1,0:T(8,128)(2,1)S(1)}, f32[8,8,1536]{2,1,0:T(8,128)S(1)}, f32[4,8,8,128]{3,2,1,0:T(8,128)S(1)}) custom-call(bf16[128,3072]{1,0:T(8,128)(2,1)S(1)} %copy-done.9, f32[8,128]{1,0:T(8,128)S(1)} %get-tuple-element.120.p_ref, bf16[8,48,576]{2,1,0:T(8,128)(2,1)} %reduce-scatter.11.cloned.1.call-done.w_ref, ...), custom_call_target="tpu_custom_call" | custom-call | bytes 1024 | tf_op jit(solution)/shard_map/closing/pallas_call | solution.py:477
  529.4 21.3 %sheet_update.1 = (f32[48,29192]{1,0:T(8,128)}, f32[48,29192]{1,0:T(8,128)}, f32[48,29192]{1,0:T(8,128)}, f32[48,29192]{1,0:T(8,128)}, bf16[48,29192]{1,0:T(8,12...) custom-call(s32[1]{0:T(128)} %dynamic_slice.10.block_ref, ...), custom_call_target="tpu_custom_call" | custom-call | tf_op jit(solution)/shard_map/sheet_update/pallas_call | solution.py:2259
  (128 shorter events, 39.8 us)
Async XLA Ops:
  7.2 117.2 %all-gather.8.cloned.1.call-start = ((), (), s32[]{:S(2)}) async-start(), calls=%async_computation.6 | async-start | bytes 5406720 | tf_op jit(solution)/shard_map/all_gather | solution.py:2303
  11.1 29.9 %copy-start.18 = (s32[32]{0:T(128)S(1)}, s32[32]{0:T(128)}, u32[]{:S(2)}) copy-start(s32[32]{0:T(128)} %param.15) | copy-start | bytes 388
  39.3 3.4 copy-start.21
  39.3 4.3 copy-start.23
  39.3 210.0 %all-gather.4.cloned.1.call-start = ((), (), s32[]{:S(2)}) async-start(), calls=%async_computation.4 | async-start | bytes 5898240 | tf_op jit(solution)/shard_map/all_gather | solution.py:2303
  118.7 146.9 %all-gather.6.cloned.1.call-start = ((), (), s32[]{:S(2)}) async-start(), calls=%async_computation.5 | async-start | bytes 2949120 | tf_op jit(solution)/shard_map/all_gather | solution.py:2303
  119.4 214.2 %reduce-scatter.7.cloned.1.call-start = ((), (), s32[]{:S(2)}) async-start(), calls=%async_computation.8 | async-start | bytes 2949120 | tf_op jit(solution)/shard_map/reduce_scatter | solution.py:2316
  124.4 21.2 %copy-start.15 = (bf16[96,128]{1,0:T(8,128)(2,1)S(1)}, bf16[96,128]{1,0:T(8,128)(2,1)}, u32[]{:S(2)}) copy-start(bf16[96,128]{1,0:T(8,128)(2,1)} %get-tuple-element.84.refs_0_.refs_7_) | copy-start | bytes 73732
  197.1 6.7 %copy-start.17 = (f32[1,128]{1,0:T(1,128)}, f32[1,128]{1,0:T(1,128)S(1)}, u32[]{:S(2)}) copy-start(f32[1,128]{1,0:T(1,128)S(1)} %get-tuple-element.104.refs_5_) | copy-start | bytes 1540
  249.3 8.2 %copy-start.16 = (f32[1,128]{1,0:T(1,128)}, f32[1,128]{1,0:T(1,128)S(1)}, u32[]{:S(2)}) copy-start(f32[1,128]{1,0:T(1,128)S(1)} %get-tuple-element.92.refs_5_) | copy-start | bytes 1540
  257.5 3.2 copy-start.19
  257.5 4.2 copy-start.22
  260.7 4.9 copy-start.20
  265.6 140.3 %reduce-scatter.5.cloned.1.call-start = ((), (), s32[]{:S(2)}) async-start(), calls=%async_computation.7 | async-start | bytes 5898240 | tf_op jit(solution)/shard_map/reduce_scatter | solution.py:2316
  308.0 160.8 %reduce-scatter.9.cloned.1.call-start = ((), (), s32[]{:S(2)}) async-start(), calls=%async_computation.9 | async-start | bytes 2949120 | tf_op jit(solution)/shard_map/reduce_scatter | solution.py:2316
  387.7 107.4 %reduce-scatter.11.cloned.1.call-start = ((), (), s32[]{:S(2)}) async-start(), calls=%async_computation.10 | async-start | bytes 2457600 | tf_op jit(solution)/shard_map/reduce_scatter | solution.py:2316
  468.7 9.5 %copy-start = (bf16[8,48,1536]{2,1,0:T(8,128)(2,1)S(1)}, bf16[8,48,1536]{2,1,0:T(8,128)(2,1)}, u32[]{:S(2)}) copy-start(bf16[8,48,1536]{2,1,0:T(8,128)(2,1)} %reduce-scatter.5.cloned.1.call-done.refs_8_.gu_ref) | copy-start | bytes 3538948
  468.8 9.5 %copy-start.1 = (bf16[8,48,768]{2,1,0:T(8,128)(2,1)S(1)}, bf16[8,48,768]{2,1,0:T(8,128)(2,1)}, u32[]{:S(2)}) copy-start(bf16[8,48,768]{2,1,0:T(8,128)(2,1)} %reduce-scatter.7.cloned.1.call-done.refs_9_.down_ref) | copy-start | bytes 1769476
  468.8 9.5 %copy-start.4 = (bf16[8,48,768]{2,1,0:T(8,128)(2,1)S(1)}, bf16[8,48,768]{2,1,0:T(8,128)(2,1)}, u32[]{:S(2)}) copy-start(bf16[8,48,768]{2,1,0:T(8,128)(2,1)} %reduce-scatter.9.cloned.1.call-done.two_ref.x_ref) | copy-start | bytes 1769476
  478.3 1.1 copy-start.5
  479.4 1.1 copy-start.6
  480.5 1.1 copy-start.7
  481.7 47.7 %copy-start.2 = (bf16[8,48,768]{2,1,0:T(8,128)(2,1)S(1)}, bf16[8,48,768]{2,1,0:T(8,128)(2,1)}, u32[]{:S(2)}) copy-start(bf16[8,48,768]{2,1,0:T(8,128)(2,1)} %plane_exchange.1._.two_ref) | copy-start | bytes 1769476
  495.1 1.1 copy-start.9
  (7 other events, 5.8 us)
Sparse Core Ops, SparseCore 0:
  39.4 84.9 all-gather.7
  126.0 87.9 all-gather.3
  215.5 48.9 all-gather.5
  267.2 46.8 reduce-scatter.6
  316.2 84.7 reduce-scatter.4
  403.2 48.5 reduce-scatter.8
  454.1 40.9 reduce-scatter.10

commit v7 on v6

--- a/solution.py
+++ b/solution.py
@@ -1318,22 +1318,33 @@
     return lambda ref, member: lanes(ref.at[member], start, width)
 
 
-def feed_kernel(gu_ref, down_ref, w_ref, h_ref, *refs):
-    o_ref, y_ref, weight, hidden, part, summed, *bufs, local_sem, send_sem, recv_sem = refs[-14:]
+def feed_kernel(gu_ref, down_ref, w_ref, h_ref, g_ref, *refs):
+    o_ref, y_ref, t_ref, weight, hidden, part, summed, grad, x_ref, held, *refs = refs[-18:]
+    *bufs, local_sem, send_sem, recv_sem = refs
     width = down_ref.shape[-1]
     fetches = [
         pltpu.make_async_copy(w_ref, weight, local_sem.at[3]),
         pltpu.make_async_copy(h_ref, hidden, local_sem.at[5]),
+        pltpu.make_async_copy(g_ref, grad, local_sem.at[6]),
     ]
     for fetch in fetches:
         fetch.start()
-    greet([member_at(peer) for peer in plane_peers()])
+    plane = lax.axis_index("z")
+    greet(
+        [member_at(peer) for peer in plane_peers()]
+        + [{"z": lax.rem(plane + k, 4)} for k in range(1, 4)]
+    )
+    depart, arrive, turned_back = turn_steps(
+        x_ref, held, t_ref, local_sem.at[pl.ds(7, 2)], send_sem, recv_sem, 31
+    )
+    fetches[2].wait()
+    x_ref[...] = grad[...].T.astype(x_ref.dtype)
     finish = []
     for k, (ref, start) in enumerate(((gu_ref, 0), (gu_ref, width), (down_ref, 0))):
         source, target = block_part(start, width), sheet_part(8 * k * width, width)
         copy = mover(send_sem, recv_sem, 7 * k)
         finish.append(exchange_steps(source, target, ref, o_ref, local_sem.at[k], copy))
-    for fetch in fetches:
+    for fetch in fetches[:2]:
         fetch.wait()
 
     @pl.loop(0, part.shape[0] // 256)
@@ -1351,15 +1362,18 @@
     cores()
     chips()
     relays()
+    depart()
     summed[...] = ended()
     kept = pltpu.make_async_copy(summed, y_ref, local_sem.at[4])
     kept.start()
+    arrive()
     for end in finish:
         end()
     kept.wait()
-
-
-def feed(gu, down, weight, hidden, after=()):
+    turned_back()
+
+
+def feed(gu, down, weight, hidden, grad, after=()):
     rows, length = weight.shape[0], hidden.shape[1]
     width = length // 8
     return kernel_call(
@@ -1367,20 +1381,24 @@
         out_shape=(
             jax.ShapeDtypeStruct((gu.shape[1], 24 * down.shape[-1]), gu.dtype),
             jax.ShapeDtypeStruct((rows, width), jnp.float32),
+            jax.ShapeDtypeStruct((width, rows), jnp.bfloat16),
         ),
-        in_specs=[IN_HBM] * (4 + len(after)),
-        out_specs=(IN_HBM, IN_HBM),
+        in_specs=[IN_HBM] * (5 + len(after)),
+        out_specs=(IN_HBM,) * 3,
         scratch_shapes=[
             pltpu.VMEM(weight.shape, weight.dtype),
             pltpu.VMEM(hidden.shape, hidden.dtype),
             pltpu.VMEM((rows, length), jnp.bfloat16),
             pltpu.VMEM((rows, width), jnp.float32),
+            pltpu.VMEM((rows, width), jnp.float32),
+            pltpu.VMEM((width, rows), jnp.bfloat16),
+            pltpu.VMEM((width, rows), jnp.bfloat16),
         ]
         + scatter_bufs(rows, width)
         + [
-            pltpu.SemaphoreType.DMA((6,)),
-            pltpu.SemaphoreType.DMA((31,)),
-            pltpu.SemaphoreType.DMA((31,)),
+            pltpu.SemaphoreType.DMA((9,)),
+            pltpu.SemaphoreType.DMA((39,)),
+            pltpu.SemaphoreType.DMA((39,)),
         ],
         compiler_params=pltpu.CompilerParams(
             collective_id=identity_of("feed", gu, down, weight, *after),
@@ -1389,7 +1407,7 @@
         ),
         cost_estimate=BRIEF,
         name="feed",
-    )(gu, down, weight, hidden, *after)
+    )(gu, down, weight, hidden, grad, *after)
 
 
 def opening_kernel(
@@ -1664,28 +1682,93 @@
     )(shard, other, sheet)
 
 
-def prepare_kernel(order_ref, y_ref, base_ref, grad_ref, gu_ref, down_ref, two_ref, x_ref, q_ref, y):
-    features = base_ref.shape[0]
+def turn_steps(x_ref, held, t_ref, local_sem, send_sem, recv_sem, first):
+    group, core, across, along = near()
+    plane = lax.axis_index("z")
+    step = x_ref.shape[0] // 4
+    groups = [across, along, across + along - group]
+    inner = lax.div(plane * (3 - plane), 2)
+    two_off, mirrored = lax.rem(plane + 2, 4), 3 - plane
+    line = [
+        plane + 1 - 2 * lax.rem(plane, 2),
+        inner * mirrored + (1 - inner) * two_off,
+        inner * two_off + (1 - inner) * mirrored,
+    ]
+
+    def frames(ref, j):
+        return ref.at[pl.ds(pl.multiple_of(j * step, 16), step), :]
+
+    def copy(source, target, sent, landed, peer):
+        return pltpu.make_async_remote_copy(
+            src_ref=source,
+            dst_ref=target,
+            send_sem=send_sem.at[first + sent],
+            recv_sem=recv_sem.at[first + landed],
+            device_id=peer,
+            device_id_type=MESH_ID,
+        )
+
+    def along_line(there):
+        return copy(frames(x_ref, there), frames(held, plane), there, plane, {"z": there})
+
+    def onward(owner):
+        return copy(
+            frames(held, owner), frames(t_ref, group), 4 + owner, 4 + group, {"dp": owner}
+        )
+
+    own = pltpu.make_async_copy(frames(x_ref, plane), frames(held, plane), local_sem.at[0])
+    keep = pltpu.make_async_copy(frames(held, group), frames(t_ref, group), local_sem.at[1])
+
+    def pass_on(owner):
+        pl.when(owner == group)(keep.start)
+        pl.when(owner != group)(onward(owner).start)
+
+    def start():
+        own.start()
+        for there in line:
+            along_line(there).start()
+        own.wait()
+        pass_on(plane)
+
+    def arrive():
+        for origin in line:
+            at = frames(held, origin)
+            copy(at, at, origin, origin, {"z": origin}).wait_recv()
+            pass_on(origin)
+
+    def finish():
+        for origin in groups:
+            at = frames(t_ref, origin)
+            copy(at, at, 4 + origin, 4 + origin, {"dp": origin}).wait_recv()
+        keep.wait()
+        for there in line:
+            along_line(there).wait_send()
+        for owner in groups:
+            onward(owner).wait_send()
+
+    return start, arrive, finish
+
+
+def prepare_kernel(order_ref, y_ref, base_ref, gu_ref, down_ref, two_ref, x_ref, q_ref, y):
     reorder_blocks(y_ref, y, lambda b: order_ref[1, b])
-    x_ref[:, :features] = (base_ref[...] + y[...]).T.astype(x_ref.dtype)
-    x_ref[:, features:] = grad_ref[...].T.astype(x_ref.dtype)
+    x_ref[...] = (base_ref[...] + y[...]).T.astype(x_ref.dtype)
     q_ref[...] = jnp.full(q_ref.shape, square_sum((gu_ref, down_ref, two_ref)), jnp.float32)
 
 
-def prepare(orders, y, base, grad, gu, down, two):
+def prepare(orders, y, base, gu, down, two):
     features, width = base.shape
     return kernel_call(
         prepare_kernel,
         out_shape=(
-            jax.ShapeDtypeStruct((width, 2 * features), jnp.bfloat16),
+            jax.ShapeDtypeStruct((width, features), jnp.bfloat16),
             jax.ShapeDtypeStruct((8, 128), jnp.float32),
         ),
-        in_specs=[IN_SMEM] + [IN_VMEM] * 6,
+        in_specs=[IN_SMEM] + [IN_VMEM] * 5,
         out_specs=(IN_VMEM,) * 2,
         scratch_shapes=[pltpu.VMEM(base.shape, jnp.float32)],
         compiler_params=pltpu.CompilerParams(vmem_limit_bytes=16 * 2**20),
         name="prepare",
-    )(orders, y.reshape(orders.shape[1], -1, width), base, grad, gu, down, two)
+    )(orders, y.reshape(orders.shape[1], -1, width), base, gu, down, two)
 
 
 def square_sum(refs):
@@ -1718,70 +1801,19 @@
 ):
     fetch = pltpu.make_async_copy(w_ref, one, local_sem.at[0])
     fetch.start()
-    group, core, across, along = near()
+    group, core, _, _ = near()
     member = group * 2 + core
     plane = lax.axis_index("z")
-    step, features = x_ref.shape[0] // 4, x_ref.shape[1] // 2
-    groups = [across, along, across + along - group]
-    inner = lax.div(plane * (3 - plane), 2)
-    two_off, mirrored = lax.rem(plane + 2, 4), 3 - plane
-    line = [
-        plane + 1 - 2 * lax.rem(plane, 2),
-        inner * mirrored + (1 - inner) * two_off,
-        inner * two_off + (1 - inner) * mirrored,
-    ]
+    turned_line = [lax.rem(plane + k, 4) for k in range(1, 4)]
     peers = plane_peers()
-    greet([member_at(peer) for peer in peers] + [{"z": there} for there in line])
-
-    def piece(ref, j, a):
-        at = pl.ds(pl.multiple_of(j * step, 16), step)
-        return ref.at[at, a * features : (a + 1) * features]
-
-    def cross_line(there, a):
-        return pltpu.make_async_remote_copy(
-            src_ref=piece(x_ref, there, a),
-            dst_ref=piece(held, plane, a),
-            send_sem=send_sem.at[4 * a + there],
-            recv_sem=recv_sem.at[4 * a + plane],
-            device_id={"z": there},
-            device_id_type=MESH_ID,
-        )
-
-    def onward(owner, a):
-        return pltpu.make_async_remote_copy(
-            src_ref=piece(held, owner, a),
-            dst_ref=piece(t_ref, group, a),
-            send_sem=send_sem.at[8 + 4 * a + owner],
-            recv_sem=recv_sem.at[8 + 4 * a + group],
-            device_id={"dp": owner},
-            device_id_type=MESH_ID,
-        )
-
-    def landed(ref, j, a, sem, peer):
-        at = piece(ref, j, a)
-        pltpu.make_async_remote_copy(
-            src_ref=at,
-            dst_ref=at,
-            send_sem=send_sem.at[sem],
-            recv_sem=recv_sem.at[sem],
-            device_id=peer,
-            device_id_type=MESH_ID,
-        ).wait_recv()
-
-    keep = [
-        pltpu.make_async_copy(piece(held, group, a), piece(t_ref, group, a), local_sem.at[1 + a])
-        for a in range(2)
-    ]
-
-    def pass_on(owner, a):
-        pl.when(owner == group)(keep[a].start)
-        pl.when(owner != group)(onward(owner, a).start)
-
+    greet([member_at(peer) for peer in peers] + [{"z": there} for there in turned_line])
+    start, arrive, finish = turn_steps(
+        x_ref, held, t_ref, local_sem.at[pl.ds(1, 2)], send_sem, recv_sem, 0
+    )
     gain_line = mover(send_sem, recv_sem, 23)
     gain_plane = mover(send_sem, recv_sem, 26)
     square_plane = mover(send_sem, recv_sem, 33)
     square_line = mover(send_sem, recv_sem, 40)
-    turned_line = [lax.rem(plane + k, 4) for k in range(1, 4)]
     back_line = [lax.rem(plane + 3 - k, 4) for k in range(3)]
     gain_local = pltpu.make_async_copy(g_ref, tall.at[plane], local_sem.at[3])
     gain_local.start()
@@ -1790,15 +1822,7 @@
     ]
     for moving in sent:
         moving.start()
-    local = pltpu.make_async_copy(
-        x_ref.at[pl.ds(pl.multiple_of(plane * step, 16), step), :],
-        held.at[pl.ds(pl.multiple_of(plane * step, 16), step), :],
-        local_sem.at[4],
-    )
-    local.start()
-    for a in range(2):
-        for there in line:
-            cross_line(there, a).start()
+    start()
     fetch.wait()
     weights_done = exchange_steps(
         block, block, one, o_ref, local_sem.at[5], mover(send_sem, recv_sem, 16)
@@ -1812,9 +1836,6 @@
     ]
     for moving in shown:
         moving.start()
-    local.wait()
-    for a in range(2):
-        pass_on(plane, a)
     gain_local.wait()
     for k, origin in enumerate(back_line):
         gain_line(k, tall.at[origin], tall.at[origin], {"z": origin}).wait_recv()
@@ -1833,14 +1854,8 @@
     for k, there in enumerate(turned_line):
         shown.append(square_line(k, all_ref.at[plane], all_ref.at[plane], {"z": there}))
         shown[-1].start()
-    for a in range(2):
-        for origin in line:
-            landed(held, origin, a, 4 * a + origin, {"z": origin})
-            pass_on(origin, a)
-    for a in range(2):
-        for origin in groups:
-            landed(t_ref, origin, a, 8 + 4 * a + origin, {"dp": origin})
-        keep[a].wait()
+    arrive()
+    finish()
     weights_done()
     gain_keep.wait()
     for k in range(7):
@@ -1850,12 +1865,6 @@
         square_line(k, all_ref.at[origin], all_ref.at[origin], {"z": origin}).wait_recv()
     for moving in sent + given + shown:
         moving.wait_send()
-    for a in range(2):
-        for there in line:
-            cross_line(there, a).wait_send()
-        for owner in groups:
-            onward(owner, a).wait_send()
-
 
 def closing(local, squares, one, gains, after):
     return kernel_call(
@@ -2160,7 +2169,8 @@
     feed_ref,
     all_ref,
     gain_ref,
-    pair_ref,
+    output_ref,
+    latent_ref,
     sheet_ref,
     first_ref,
     second_ref,
@@ -2199,8 +2209,8 @@
         norm_out[0] = norm
         scale[0] = 1.0 / jnp.maximum(norm, 1.0)
         gain_out[...] = gain[...] * scale[0]
-        output_out[...] = pair_ref[:, :D]
-        latent_out[...] = wide(pair_ref.at[:, D:])
+        output_out[...] = output_ref[...]
+        latent_out[...] = wide(latent_ref)
 
     for k in range(6):
 
@@ -2242,9 +2252,11 @@
         copy_out[:, at] = sheet_new.astype(copy_out.dtype)
 
 
-def sheet_update(block_index, length, one, two, feed_part, squares, gains, pair, sheet, first, second):
+def sheet_update(
+    block_index, length, one, two, feed_part, squares, gains, output, latent, sheet, first, second
+):
     rows = sheet.shape[0]
-    frames = (pair.shape[0], D)
+    frames = output.shape
     rates = column_spread(length)[jnp.minimum(jnp.arange(20) * D, SHEET - 1)]
     column_block = pl.BlockSpec((rows, 2 * D), lambda i: (0, i))
     like = jax.ShapeDtypeStruct(sheet.shape, sheet.dtype)
@@ -2274,6 +2286,7 @@
             IN_VMEM,
             IN_VMEM,
             IN_VMEM,
+            IN_VMEM,
             column_block,
             column_block,
             column_block,
@@ -2287,7 +2300,20 @@
         ],
         compiler_params=pltpu.CompilerParams(vmem_limit_bytes=32 * 2**20),
         name="sheet_update",
-    )(block_index, rates, one, two, feed_part, squares, gains, pair, sheet, first, second)
+    )(
+        block_index,
+        rates,
+        one,
+        two,
+        feed_part,
+        squares,
+        gains,
+        output,
+        latent,
+        sheet,
+        first,
+        second,
+    )
 
 
 def pick_blocks(blocks, order):
@@ -2488,11 +2514,12 @@
     )
     grad_blocks_one = as_blocks(grad_weight_qkv, to_slots)
     sums_one = scatter_line(grad_blocks_one)
-    sums_feed, ff_out = feed(
+    sums_feed, ff_out, latent_grad = feed(
         sums_gu,
         sums_down,
         weight_down,
         hidden,
+        latent_grad,
         [grad_blocks_one],
     )
     sum_one = sum_one[0:1]
@@ -2507,12 +2534,10 @@
         ],
         axis=0,
     )
-    pair, squares = prepare(
-        orders, ff_out, x_two, latent_grad, sums_gu, sums_down, sums_two
-    )
+    output, squares = prepare(orders, ff_out, x_two, sums_gu, sums_down, sums_two)
     sums_two = exchange_blocks(sums_two, [sums_feed])
-    out_pair, sums_one, gain_sums, squares = closing(
-        pair, squares, sums_one, gain_grads, sums_two
+    output, sums_one, gain_sums, squares = closing(
+        output, squares, sums_one, gain_grads, sums_two
     )
     place = lax.axis_index("dp") * (planes * cores) + plane * cores + lax.axis_index("core")
     (
@@ -2533,7 +2558,8 @@
         sums_feed,
         squares,
         gain_sums,
-        out_pair,
+        output,
+        latent_grad,
         sheet,
         first,
         second,

time: 566 us -> 561 us (level)
  waiting for transfers between devices: 14.1 us -> 4.41 us
  Pallas kernels: 464 us -> 470 us
    reduce_scatter x4, waiting for transfers between devices: 10.4 us -> 0.67 us  [scatter_line(): return lax.psum_scatter(blocks, 'z', scatter_dimension=0, tiled=True)]
    pallas_call x17, Pallas kernels: 442 us -> 449 us  [run(): call(*[pltpu.with_memory_space_constraint(operand, pltpu.HBM) if place is...]
    unnamed x51 -> x47, local copies, waits for them, and re-layouts: 16 us -> 13.9 us
  transfers between devices with their start and end apart: 7 -> 7, of which waited for: 2 -> 2; matrix products, arithmetic and copies ran while one was open for 8% -> 8% of each run, Pallas kernels for 68% -> 72%
where the time goes in v7:
time: 561 us; the launch traced here: 554 us
  Pallas kernels  470 us (84%)
  local copies, waits for them, and re-layouts  23.5 us (4%)
  matrix products  20.3 us (4%)
  other arithmetic  18.9 us (3%)
  between operations  15.8 us (3%)
    pallas_call x17, Pallas kernels, run(): call(*[pltpu.with_memory_space_constraint(operand, pltpu.HBM) if place is...  449 us
    pallas_call x1, Pallas kernels, sheet_update(): pl.pallas_call(update_kernel, grid=(10,), out_shape=(like, like, like, li...  21.3 us
    dot_general x2, matrix products, contract_rows(): lax.dot_general(left, right, (((0,), (0,)), ((), ())), preferred_element_...  16.4 us
    unnamed x47, local copies, waits for them, and re-layouts  13.9 us
  transfers between devices with their start and end apart: 7, of which 2 were waited for; matrix products, arithmetic and copies ran while one was open for 8% of the time, Pallas kernels for 72%

profile of v7, /device:TPU:0, one launch (start us, length us, event | category | flops | bytes accessed | tf_op | source)
XLA Modules:
  0.0 553.6 jit_solution(1867083045922374765)
XLA Ops:
  11.1 28.1 %opening.1 = (bf16[128,3072]{1,0:T(8,128)(2,1)}, f32[4,8,8,128]{3,2,1,0:T(8,128)}, bf16[96,128]{1,0:T(8,128)(2,1)}, bf16[8,48,1344]{2,1,0:T(8,128)(2,1)}) custom-call(bf16[128,1536]{1,0:T(8,128)(2,1)} %bitcast.85, bf16[128,1536]{1,0:T(8,128)(2,1)} %bitcast.86, f32[8,128]{1,0:T(8,128)} %select_maximum_fusion.small_ref, bf16[768,128]{1,0:T(8,128)(2,1)} %bitcast.82, ...), custom_call_target="tpu_custom_call" | custom-call | bytes 1024 | tf_op jit(solution)/shard_map/opening/pallas_call | solution.py:477
  50.5 2.1 slice_reduce_fusion
  55.1 4.5 convert_element_type.78.sheet_ref
  59.5 59.1 %first_gather.1 = (bf16[1536,1024]{1,0:T(8,128)(2,1)}, bf16[1536,1024]{1,0:T(8,128)(2,1)}, bf16[8,48,1536]{2,1,0:T(8,128)(2,1)}, bf16[8,48,768]{2,1,0:T(8,128)(2,1)}) custom-call(bf16[1536,128]{1,0:T(8,128)(2,1)} %bitcast.81, bf16[1536,128]{1,0:T(8,128)(2,1)} %bitcast.80, bf16[48,29192]{1,0:T(8,128)(2,1)} %convert_element_type.78.sheet_ref), custom_call_target="tpu_custom_call" | custom-call | bytes 1024 | tf_op jit(solution)/shard_map/first_gather/pallas_call | solution.py:477
  121.5 2.9 all-gather.8.cloned.1.call-done.w_ref.refs_1_
  124.4 20.4 %attend.1 = (bf16[3,3,64,1024]{3,2,1,0:T(8,128)(2,1)}, bf16[3,1024,1024]{2,1,0:T(8,128)(2,1)}, bf16[192,1024]{1,0:T(8,128)(2,1)S(1)}) custom-call(bf16[1536,1344]{1,0:T(8,128)(2,1)} %bitcast.60, bf16[1536,1024]{1,0:T(8,128)(2,1)} %get-tuple-element.83.h_ref.refs_3_, f32[32,1024]{1,0:T(8,128)S(1)} %get-tuple-element.206.cos_ref, ...), custom_call_target="tpu_custom_call" | custom-call | tf_op jit(solution)/shard_map/attend/pallas_call | solution.py:477
  145.6 51.5 %project_sum.1 = (bf16[1536,1024]{1,0:T(8,128)(2,1)}, f32[1536,128]{1,0:T(8,128)}, f32[1536,128]{1,0:T(8,128)}, f32[1,128]{1,0:T(1,128)S(1)}, bf16[1536,1024]{1,0:T(8,128)(2,1)}, /*index=5*/bf16[192,256]{1,0:T(8,128)(2,1)S(1)}) custom-call(s32[2,32]{1,0:T(2,128)S(1)} %pad_add_fusion.order_ref.refs_0_, bf16[192,1024]{1,0:T(8,128)(2,1)} %copy-done.10, ...), custom_call_target="tpu_custom_call" | custom-call | bytes 1024 | tf_op jit(solution)/shard_map/project_sum/pallas_call | solution.py:477
  197.1 6.7 %cross.1 = (bf16[192,1024]{1,0:T(8,128)(2,1)S(1)}, bf16[3,128,1024]{2,1,0:T(8,128)(2,1)S(1)}, bf16[192,1024]{1,0:T(8,128)(2,1)S(1)}) custom-call(bf16[1536,1344]{1,0:T(8,128)(2,1)} %bitcast.61, bf16[1536,1024]{1,0:T(8,128)(2,1)} %get-tuple-element.86.h_ref.refs_3_, bf16[192,256]{1,0:T(8,128)(2,1)S(1)} %get-tuple-element.87.kv_ref), custom_call_target="tpu_custom_call" | custom-call | tf_op jit(solution)/shard_map/cross/pallas_call | solution.py:477
  204.5 44.8 %project_slots.1 = (bf16[1536,1024]{1,0:T(8,128)(2,1)}, f32[1536,128]{1,0:T(8,128)}, f32[1536,128]{1,0:T(8,128)}, f32[1,128]{1,0:T(1,128)S(1)}, bf16[1536,1024]{1,0:T(8,128)(2,1)}) custom-call(s32[2,32]{1,0:T(2,128)S(1)} %pad_add_fusion.order_ref.refs_0_, bf16[192,1024]{1,0:T(8,128)(2,1)} %copy-done.11, ...), custom_call_target="tpu_custom_call" | custom-call | bytes 1024 | tf_op jit(solution)/shard_map/project_slots/pallas_call | solution.py:477
  249.4 8.1 %fusion.11 = f32[1536,1024]{1,0:T(8,128)S(1)} fusion(bf16[1536,1536]{1,0:T(8,128)(2,1)} %bitcast.70, bf16[1536,1024]{1,0:T(8,128)(2,1)} %get-tuple-element.90.refs_3_), kind=kOutput, calls=%fused_computation.81 | convolution fusion | flops 4831838208 | bytes 14155776 | tf_op jit(solution)/shard_map/dot_general | solution.py:430
  258.5 2.2 copy-done.17
  261.7 3.9 convolution_convert_fusion
  265.7 8.3 %multiply_convert_fusion.1 = (bf16[768,1024]{1,0:T(8,128)(2,1)S(1)}, bf16[768,1024]{1,0:T(8,128)(2,1)S(1)}) fusion(f32[1536,1024]{1,0:T(8,128)} %copy-done.17, bf16[1536,768]{1,0:T(8,128)(2,1)} %bitcast.76, bf16[1536,1024]{1,0:T(8,128)(2,1)} %get-tuple-element.81), kind=kOutput, calls=%fused_computation.9 | convolution fusion | flops 2426142720 | bytes 14942208 | tf_op jit(solution)/shard_map/dot_general | solution.py:430
  273.9 2.0 pad_maximum_fusion.refs_2_
  275.9 32.1 %back.5 = (f32[1536,128]{1,0:T(8,128)}, bf16[1536,1536]{1,0:T(8,128)(2,1)}, f32[8,1536]{1,0:T(8,128)S(1)}, bf16[192,1024]{1,0:T(8,128)(2,1)}) custom-call(s32[2,32]{1,0:T(2,128)S(1)} %pad_add_fusion.order_ref.refs_0_, bf16[1536,1536]{1,0:T(8,128)(2,1)} %bitcast.71, bf16[1536,1024]{1,0:T(8,128)(2,1)} %pad_maximum_fusion.refs_2_, ...), custom_call_target="tpu_custom_call" | custom-call | bytes 1024 | tf_op jit(solution)/shard_map/back/pallas_call | solution.py:477
  308.1 21.6 %back.6 = (bf16[192,1024]{1,0:T(8,128)(2,1)}, bf16[1536,192]{1,0:T(8,128)(2,1)}) custom-call(s32[2,32]{1,0:T(2,128)S(1)} %pad_add_fusion.order_ref.refs_0_, bf16[32,48,1344]{2,1,0:T(8,128)(2,1)} %all-gather.8.cloned.1.call-done.w_ref.refs_1_, bf16[192,1024]{1,0:T(8,128)(2,1)} %get-tuple-element.100.refs_2_, bf16[32,48,1024]{2,1,0:T(8,128)(2,1)} %bitcast.74), custom_call_target="tpu_custom_call" | custom-call | bytes 1024 | tf_op jit(solution)/shard_map/back/pallas_call | solution.py:477
  333.7 32.3 %back.7 = (f32[1536,128]{1,0:T(8,128)}, bf16[1536,192]{1,0:T(8,128)(2,1)}, f32[8,1536]{1,0:T(8,128)S(1)}, bf16[192,1024]{1,0:T(8,128)(2,1)}, bf16[1536,256]{1,0:T(8,128)(2,1)}) custom-call(s32[2,32]{1,0:T(2,128)S(1)} %pad_add_fusion.order_ref.refs_0_, bf16[1536,1344]{1,0:T(8,128)(2,1)} %bitcast.62, bf16[192,1024]{1,0:T(8,128)(2,1)} %copy-done.7, ...), custom_call_target="tpu_custom_call" | custom-call | bytes 1024 | tf_op jit(solution)/shard_map/back/pallas_call | solution.py:477
  366.0 21.7 %back.8 = (bf16[192,1024]{1,0:T(8,128)(2,1)}, bf16[1536,768]{1,0:T(8,128)(2,1)}) custom-call(s32[2,32]{1,0:T(2,128)S(1)} %pad_add_fusion.order_ref.refs_0_, bf16[32,48,1344]{2,1,0:T(8,128)(2,1)} %all-gather.8.cloned.1.call-done.w_ref.refs_1_, bf16[192,1024]{1,0:T(8,128)(2,1)} %get-tuple-element.108.refs_2_, bf16[32,48,1024]{2,1,0:T(8,128)(2,1)} %bitcast.73, ...), custom_call_target="tpu_custom_call" | custom-call | bytes 1024 | tf_op jit(solution)/shard_map/back/pallas_call | solution.py:477
  387.8 17.2 %attend_back.1.refs_2_ = bf16[576,1024]{1,0:T(8,128)(2,1)S(1)} custom-call(bf16[3,3,64,1024]{3,2,1,0:T(8,128)(2,1)} %get-tuple-element.96.part_in, bf16[3,1024,1024]{2,1,0:T(8,128)(2,1)} %get-tuple-element.97.p_in, bf16[192,1024]{1,0:T(8,128)(2,1)} %get-tuple-element.113.g_in, f32[32,1024]{1,0:T(8,128)S(1)} %get-tuple-element.206.cos_ref, ...), custom_call_target="tpu_custom_call" | custom-call | tf_op jit(solution)/shard_map/attend_back/pallas_call | solution.py:477
  406.0 24.1 %back.9 = (f32[1536,128]{1,0:T(8,128)}, bf16[1536,576]{1,0:T(8,128)(2,1)}, f32[8,1536]{1,0:T(8,128)S(1)}) custom-call(s32[2,32]{1,0:T(2,128)S(1)} %pad_add_fusion.order_ref.refs_0_, bf16[1536,1344]{1,0:T(8,128)(2,1)} %bitcast.63, bf16[576,1024]{1,0:T(8,128)(2,1)} %copy-done.3, bf16[1536,1024]{1,0:T(8,128)(2,1)} %get-tuple-element.83.h_ref.refs_3_, ...), custom_call_target="tpu_custom_call" | custom-call | bytes 1024 | tf_op jit(solution)/shard_map/back/pallas_call | solution.py:477
  431.4 49.2 %feed.1 = (bf16[48,18432]{1,0:T(8,128)(2,1)}, f32[1536,128]{1,0:T(8,128)}, bf16[128,1536]{1,0:T(8,128)(2,1)}) custom-call(bf16[8,48,1536]{2,1,0:T(8,128)(2,1)} %reduce-scatter.5.cloned.1.call-done.refs_8_.gu_ref, bf16[8,48,768]{2,1,0:T(8,128)(2,1)} %reduce-scatter.7.cloned.1.call-done.refs_9_.down_ref, bf16[1536,768]{1,0:T(8,128)(2,1)} %bitcast.77, ...), custom_call_target="tpu_custom_call" | custom-call | bytes 1024 | tf_op jit(solution)/shard_map/feed/pallas_call | solution.py:477
  480.7 13.0 %plane_exchange.1._.two_ref = bf16[8,48,768]{2,1,0:T(8,128)(2,1)} custom-call(bf16[8,48,768]{2,1,0:T(8,128)(2,1)} %reduce-scatter.9.cloned.1.call-done.two_ref.x_ref, bf16[48,18432]{1,0:T(8,128)(2,1)} %get-tuple-element.125.refs_0_.feed_ref), custom_call_target="tpu_custom_call" | custom-call | bytes 1024 | tf_op jit(solution)/shard_map/plane_exchange/pallas_call | solution.py:477
  498.9 24.4 %closing.1 = (bf16[128,1536]{1,0:T(8,128)(2,1)S(1)}, bf16[8,48,576]{2,1,0:T(8,128)(2,1)S(1)}, f32[8,8,1536]{2,1,0:T(8,128)S(1)}, f32[4,8,8,128]{3,2,1,0:T(8,128)S(1)}) custom-call(bf16[128,1536]{1,0:T(8,128)(2,1)S(1)} %get-tuple-element.120.x_ref, f32[8,128]{1,0:T(8,128)S(1)} %get-tuple-element.121.p_ref, ...), custom_call_target="tpu_custom_call" | custom-call | bytes 1024 | tf_op jit(solution)/shard_map/closing/pallas_call | solution.py:477
  524.3 21.3 %sheet_update.1 = (f32[48,29192]{1,0:T(8,128)}, f32[48,29192]{1,0:T(8,128)}, f32[48,29192]{1,0:T(8,128)}, f32[48,29192]{1,0:T(8,128)}, bf16[48,29192]{1,0:T(8,12...) custom-call(s32[1]{0:T(128)} %dynamic_slice.10.block_ref, ...), custom_call_target="tpu_custom_call" | custom-call | tf_op jit(solution)/shard_map/sheet_update/pallas_call | solution.py:2271
  (124 shorter events, 36.3 us)
Async XLA Ops:
  7.2 117.2 %all-gather.8.cloned.1.call-start = ((), (), s32[]{:S(2)}) async-start(), calls=%async_computation.6 | async-start | bytes 5406720 | tf_op jit(solution)/shard_map/all_gather | solution.py:2329
  11.1 29.9 %copy-start.16 = (s32[32]{0:T(128)S(1)}, s32[32]{0:T(128)}, u32[]{:S(2)}) copy-start(s32[32]{0:T(128)} %param.15) | copy-start | bytes 388
  39.3 3.4 copy-start.19
  39.3 4.3 copy-start.21
  39.3 210.0 %all-gather.4.cloned.1.call-start = ((), (), s32[]{:S(2)}) async-start(), calls=%async_computation.4 | async-start | bytes 5898240 | tf_op jit(solution)/shard_map/all_gather | solution.py:2329
  118.7 146.9 %all-gather.6.cloned.1.call-start = ((), (), s32[]{:S(2)}) async-start(), calls=%async_computation.5 | async-start | bytes 2949120 | tf_op jit(solution)/shard_map/all_gather | solution.py:2329
  119.4 214.3 %reduce-scatter.7.cloned.1.call-start = ((), (), s32[]{:S(2)}) async-start(), calls=%async_computation.8 | async-start | bytes 2949120 | tf_op jit(solution)/shard_map/reduce_scatter | solution.py:2342
  124.4 21.2 %copy-start.13 = (bf16[96,128]{1,0:T(8,128)(2,1)S(1)}, bf16[96,128]{1,0:T(8,128)(2,1)}, u32[]{:S(2)}) copy-start(bf16[96,128]{1,0:T(8,128)(2,1)} %get-tuple-element.85.refs_0_.refs_7_) | copy-start | bytes 73732
  197.1 6.7 %copy-start.15 = (f32[1,128]{1,0:T(1,128)}, f32[1,128]{1,0:T(1,128)S(1)}, u32[]{:S(2)}) copy-start(f32[1,128]{1,0:T(1,128)S(1)} %get-tuple-element.105.refs_5_) | copy-start | bytes 1540
  249.3 8.2 %copy-start.14 = (f32[1,128]{1,0:T(1,128)}, f32[1,128]{1,0:T(1,128)S(1)}, u32[]{:S(2)}) copy-start(f32[1,128]{1,0:T(1,128)S(1)} %get-tuple-element.93.refs_5_) | copy-start | bytes 1540
  257.5 3.2 copy-start.17
  257.5 4.2 copy-start.20
  260.7 4.9 copy-start.18
  265.6 140.3 %reduce-scatter.5.cloned.1.call-start = ((), (), s32[]{:S(2)}) async-start(), calls=%async_computation.7 | async-start | bytes 5898240 | tf_op jit(solution)/shard_map/reduce_scatter | solution.py:2342
  308.0 172.7 %reduce-scatter.9.cloned.1.call-start = ((), (), s32[]{:S(2)}) async-start(), calls=%async_computation.9 | async-start | bytes 2949120 | tf_op jit(solution)/shard_map/reduce_scatter | solution.py:2342
  329.7 1.0 copy-start.8
  387.7 111.2 %reduce-scatter.11.cloned.1.call-start = ((), (), s32[]{:S(2)}) async-start(), calls=%async_computation.10 | async-start | bytes 2457600 | tf_op jit(solution)/shard_map/reduce_scatter | solution.py:2342
  404.9 1.0 copy-start.3
  480.7 13.1 %copy-start = (bf16[8,48,1536]{2,1,0:T(8,128)(2,1)S(1)}, bf16[8,48,1536]{2,1,0:T(8,128)(2,1)}, u32[]{:S(2)}) copy-start(bf16[8,48,1536]{2,1,0:T(8,128)(2,1)} %reduce-scatter.5.cloned.1.call-done.refs_8_.gu_ref) | copy-start | bytes 3538948
  480.7 13.1 %copy-start.1 = (bf16[8,48,768]{2,1,0:T(8,128)(2,1)S(1)}, bf16[8,48,768]{2,1,0:T(8,128)(2,1)}, u32[]{:S(2)}) copy-start(bf16[8,48,768]{2,1,0:T(8,128)(2,1)} %reduce-scatter.7.cloned.1.call-done.refs_9_.down_ref) | copy-start | bytes 1769476
  480.7 13.1 %copy-start.4 = (bf16[8,48,768]{2,1,0:T(8,128)(2,1)S(1)}, bf16[8,48,768]{2,1,0:T(8,128)(2,1)}, u32[]{:S(2)}) copy-start(bf16[8,48,768]{2,1,0:T(8,128)(2,1)} %reduce-scatter.9.cloned.1.call-done.two_ref.x_ref) | copy-start | bytes 1769476
  493.8 29.6 %copy-start.2 = (bf16[8,48,768]{2,1,0:T(8,128)(2,1)S(1)}, bf16[8,48,768]{2,1,0:T(8,128)(2,1)}, u32[]{:S(2)}) copy-start(bf16[8,48,768]{2,1,0:T(8,128)(2,1)} %plane_exchange.1._.two_ref) | copy-start | bytes 1769476
  493.8 1.2 copy-start.5
  495.0 1.1 copy-start.6
  (5 other events, 3.9 us)
Sparse Core Ops, SparseCore 0:
  39.4 84.9 all-gather.7
  126.0 87.9 all-gather.3
  215.5 48.9 all-gather.5
  267.2 46.8 reduce-scatter.6
  316.2 84.7 reduce-scatter.4
  403.2 48.5 reduce-scatter.8
  454.1 44.7 reduce-scatter.10

commit v8 on v7

--- a/solution.py
+++ b/solution.py
@@ -815,6 +815,20 @@
     for fetch in fetches:
         fetch.start()
     greet([member_at(peer) for peer in plane_peers()])
+    total[...] = jnp.zeros_like(total)
+
+    def add(member):
+        of = pl.ds(pl.multiple_of(member * rows, 16), rows)
+
+        @pl.loop(0, length // 256)
+        def _(i):
+            at = pl.ds(pl.multiple_of(i * 256, 256), 256)
+            total[:, at] += contract_rows(weight[of, :], full[of, at])
+
+    fetches[0].wait()
+    gathered = gather_steps(
+        member_rows(rows), heads, full, local_sem.at[0], mover(send_sem, recv_sem), add
+    )
     side = mover(send_sem, recv_sem, 35)
     if kind == "sum":
         cores, chips, relays, finish = scatter_steps(
@@ -838,20 +852,6 @@
     else:
         fetches[1].wait()
     reorder_blocks(slots, weight, lambda b: order_ref[1, b], column)
-    fetches[0].wait()
-    total[...] = jnp.zeros_like(total)
-
-    def add(member):
-        of = pl.ds(pl.multiple_of(member * rows, 16), rows)
-
-        @pl.loop(0, length // 256)
-        def _(i):
-            at = pl.ds(pl.multiple_of(i * 256, 256), 256)
-            total[:, at] += contract_rows(weight[of, :], full[of, at])
-
-    gathered = gather_steps(
-        member_rows(rows), heads, full, local_sem.at[0], mover(send_sem, recv_sem), add
-    )
     if kind == "sum":
         chips()
     gathered()
@@ -1424,6 +1424,8 @@
     held,
     columns,
     one,
+    tokens,
+    by_feature,
     local_sem,
     send_sem,
     recv_sem,
@@ -1440,6 +1442,7 @@
         pltpu.make_async_copy(
             sheet_ref.at[:, tail : tail + 2 * CTXW], columns.at[:, 6 * D :], local_sem.at[8]
         ),
+        pltpu.make_async_copy(text_ref, tokens, local_sem.at[10]),
     ]
     for fetch in fetches:
         fetch.start()
@@ -1534,9 +1537,12 @@
         block, block, one, one_ref, local_sem.at[2], mover(send_sem, recv_sem, 14)
     )
 
+    fetches[4].wait()
+    by_feature[...] = wide(tokens).T.astype(by_feature.dtype)
+
     def text_copy(k, peer):
         return pltpu.make_async_remote_copy(
-            src_ref=text_ref.at[pl.ds(pl.multiple_of(peer * text_rows, 16), text_rows), :],
+            src_ref=by_feature.at[pl.ds(pl.multiple_of(peer * text_rows, 16), text_rows), :],
             dst_ref=mine_ref,
             send_sem=send_sem.at[21 + k],
             recv_sem=recv_sem.at[21],
@@ -1544,7 +1550,7 @@
             device_id_type=MESH_ID,
         )
 
-    own_text = text_ref.at[pl.ds(pl.multiple_of(member * text_rows, 16), text_rows), :]
+    own_text = by_feature.at[pl.ds(pl.multiple_of(member * text_rows, 16), text_rows), :]
     text_local = pltpu.make_async_copy(own_text, mine_ref, local_sem.at[3])
 
     @pl.when(teacher)
@@ -1614,7 +1620,7 @@
         out_shape=(
             jax.ShapeDtypeStruct(local, low),
             jax.ShapeDtypeStruct((4, 8) + small.shape, small.dtype),
-            jax.ShapeDtypeStruct((text.shape[0] // 8, text.shape[1]), text.dtype),
+            jax.ShapeDtypeStruct((text.shape[1] // 8, text.shape[0]), text.dtype),
             jax.ShapeDtypeStruct(one, low),
         ),
         in_specs=[IN_HBM] * 5,
@@ -1624,7 +1630,9 @@
             pltpu.VMEM(local, low),
             pltpu.VMEM((sheet.shape[0], 6 * D + 2 * CTXW), jnp.float32),
             pltpu.VMEM(one, low),
-            pltpu.SemaphoreType.DMA((10,)),
+            pltpu.VMEM(text.shape, low),
+            pltpu.VMEM(text.shape[::-1], low),
+            pltpu.SemaphoreType.DMA((11,)),
             pltpu.SemaphoreType.DMA((40,)),
             pltpu.SemaphoreType.DMA((40,)),
         ],
@@ -2382,7 +2390,7 @@
         axis=1,
     )
     both, small, text_mine, mine_one = opening(
-        latents[0], cotangent[0], small, context[0].T, sheet
+        latents[0], cotangent[0], small, context[0], sheet
     )
     mine_one, later = lax.optimization_barrier((mine_one, sheet))
     low_sheet = later.astype(jnp.bfloat16)

time: 561 us -> 558 us (level)
  Pallas kernels: 470 us -> 464 us
    pallas_call x17, Pallas kernels: 449 us -> 443 us  [run(): call(*[pltpu.with_memory_space_constraint(operand, pltpu.HBM) if place is...]
    unnamed x47 -> x46, local copies, waits for them, and re-layouts: 13.9 us -> 12.2 us
  transfers between devices with their start and end apart: 7 -> 7, of which waited for: 2 -> 3; matrix products, arithmetic and copies ran while one was open for 8% -> 8% of each run, Pallas kernels for 72% -> 71%
where the time goes in v8:
time: 558 us; the launch traced here: 551 us
  Pallas kernels  464 us (83%)
  local copies, waits for them, and re-layouts  21.7 us (4%)
  matrix products  20.3 us (4%)
  other arithmetic  18.9 us (3%)
  between operations  15.8 us (3%)
  waiting for transfers between devices  9.6 us (2%)
    pallas_call x17, Pallas kernels, run(): call(*[pltpu.with_memory_space_constraint(operand, pltpu.HBM) if place is...  443 us
    pallas_call x1, Pallas kernels, sheet_update(): pl.pallas_call(update_kernel, grid=(10,), out_shape=(like, like, like, li...  21.3 us
    dot_general x2, matrix products, contract_rows(): lax.dot_general(left, right, (((0,), (0,)), ((), ())), preferred_element_...  16.4 us
    unnamed x46, local copies, waits for them, and re-layouts  12.2 us
  transfers between devices with their start and end apart: 7, of which 3 were waited for; matrix products, arithmetic and copies ran while one was open for 8% of the time, Pallas kernels for 71%

profile of v8, /device:TPU:0, one launch (start us, length us, event | category | flops | bytes accessed | tf_op | source)
XLA Modules:
  0.0 550.6 jit_solution(395077767853870252)
XLA Ops:
  9.4 28.2 %opening.1 = (bf16[128,3072]{1,0:T(8,128)(2,1)}, f32[4,8,8,128]{3,2,1,0:T(8,128)}, bf16[96,128]{1,0:T(8,128)(2,1)}, bf16[8,48,1344]{2,1,0:T(8,128)(2,1)}) custom-call(bf16[128,1536]{1,0:T(8,128)(2,1)} %bitcast.82, bf16[128,1536]{1,0:T(8,128)(2,1)} %bitcast.83, f32[8,128]{1,0:T(8,128)} %select_maximum_fusion.small_ref, bf16[128,768]{1,0:T(8,128)(2,1)} %bitcast.84, ...), custom_call_target="tpu_custom_call" | custom-call | bytes 1024 | tf_op jit(solution)/shard_map/opening/pallas_call | solution.py:477
  53.4 4.5 convert_element_type.78.sheet_ref
  57.8 59.1 %first_gather.1 = (bf16[1536,1024]{1,0:T(8,128)(2,1)}, bf16[1536,1024]{1,0:T(8,128)(2,1)}, bf16[8,48,1536]{2,1,0:T(8,128)(2,1)}, bf16[8,48,768]{2,1,0:T(8,128)(2,1)}) custom-call(bf16[1536,128]{1,0:T(8,128)(2,1)} %bitcast.79, bf16[1536,128]{1,0:T(8,128)(2,1)} %bitcast.78, bf16[48,29192]{1,0:T(8,128)(2,1)} %convert_element_type.78.sheet_ref), custom_call_target="tpu_custom_call" | custom-call | bytes 1024 | tf_op jit(solution)/shard_map/first_gather/pallas_call | solution.py:477
  119.8 2.9 all-gather.8.cloned.1.call-done.w_ref.refs_1_
  122.7 20.4 %attend.1 = (bf16[3,3,64,1024]{3,2,1,0:T(8,128)(2,1)}, bf16[3,1024,1024]{2,1,0:T(8,128)(2,1)}, bf16[192,1024]{1,0:T(8,128)(2,1)S(1)}) custom-call(bf16[1536,1344]{1,0:T(8,128)(2,1)} %bitcast.58, bf16[1536,1024]{1,0:T(8,128)(2,1)} %get-tuple-element.83.h_ref.refs_3_, f32[32,1024]{1,0:T(8,128)S(1)} %get-tuple-element.206.cos_ref, ...), custom_call_target="tpu_custom_call" | custom-call | tf_op jit(solution)/shard_map/attend/pallas_call | solution.py:477
  143.9 47.4 %project_sum.1 = (bf16[1536,1024]{1,0:T(8,128)(2,1)}, f32[1536,128]{1,0:T(8,128)}, f32[1536,128]{1,0:T(8,128)}, f32[1,128]{1,0:T(1,128)S(1)}, bf16[1536,1024]{1,0:T(8,128)(2,1)}, /*index=5*/bf16[192,256]{1,0:T(8,128)(2,1)S(1)}) custom-call(s32[2,32]{1,0:T(2,128)S(1)} %pad_add_fusion.order_ref.refs_0_, bf16[192,1024]{1,0:T(8,128)(2,1)} %copy-done.10, ...), custom_call_target="tpu_custom_call" | custom-call | bytes 1024 | tf_op jit(solution)/shard_map/project_sum/pallas_call | solution.py:477
  191.3 6.7 %cross.1 = (bf16[192,1024]{1,0:T(8,128)(2,1)S(1)}, bf16[3,128,1024]{2,1,0:T(8,128)(2,1)S(1)}, bf16[192,1024]{1,0:T(8,128)(2,1)S(1)}) custom-call(bf16[1536,1344]{1,0:T(8,128)(2,1)} %bitcast.59, bf16[1536,1024]{1,0:T(8,128)(2,1)} %get-tuple-element.86.h_ref.refs_3_, bf16[192,256]{1,0:T(8,128)(2,1)S(1)} %get-tuple-element.87.kv_ref), custom_call_target="tpu_custom_call" | custom-call | tf_op jit(solution)/shard_map/cross/pallas_call | solution.py:477
  198.7 44.5 %project_slots.1 = (bf16[1536,1024]{1,0:T(8,128)(2,1)}, f32[1536,128]{1,0:T(8,128)}, f32[1536,128]{1,0:T(8,128)}, f32[1,128]{1,0:T(1,128)S(1)}, bf16[1536,1024]{1,0:T(8,128)(2,1)}) custom-call(s32[2,32]{1,0:T(2,128)S(1)} %pad_add_fusion.order_ref.refs_0_, bf16[192,1024]{1,0:T(8,128)(2,1)} %copy-done.11, ...), custom_call_target="tpu_custom_call" | custom-call | bytes 1024 | tf_op jit(solution)/shard_map/project_slots/pallas_call | solution.py:477
  243.3 8.1 %fusion.11 = f32[1536,1024]{1,0:T(8,128)S(1)} fusion(bf16[1536,1536]{1,0:T(8,128)(2,1)} %bitcast.68, bf16[1536,1024]{1,0:T(8,128)(2,1)} %get-tuple-element.90.refs_3_), kind=kOutput, calls=%fused_computation.81 | convolution fusion | flops 4831838208 | bytes 14155776 | tf_op jit(solution)/shard_map/dot_general | solution.py:430
  252.5 2.2 copy-done.17
  255.7 3.9 convolution_convert_fusion
  259.6 3.2 all-gather.6.cloned.1.call-done
  262.9 8.3 %multiply_convert_fusion.1 = (bf16[768,1024]{1,0:T(8,128)(2,1)S(1)}, bf16[768,1024]{1,0:T(8,128)(2,1)S(1)}) fusion(f32[1536,1024]{1,0:T(8,128)} %copy-done.17, bf16[1536,768]{1,0:T(8,128)(2,1)} %bitcast.74, bf16[1536,1024]{1,0:T(8,128)(2,1)} %get-tuple-element.81), kind=kOutput, calls=%fused_computation.9 | convolution fusion | flops 2426142720 | bytes 14942208 | tf_op jit(solution)/shard_map/dot_general | solution.py:430
  273.1 31.5 %back.5 = (f32[1536,128]{1,0:T(8,128)}, bf16[1536,1536]{1,0:T(8,128)(2,1)}, f32[8,1536]{1,0:T(8,128)S(1)}, bf16[192,1024]{1,0:T(8,128)(2,1)}) custom-call(s32[2,32]{1,0:T(2,128)S(1)} %pad_add_fusion.order_ref.refs_0_, bf16[1536,1536]{1,0:T(8,128)(2,1)} %bitcast.69, bf16[1536,1024]{1,0:T(8,128)(2,1)} %pad_maximum_fusion.refs_2_, ...), custom_call_target="tpu_custom_call" | custom-call | bytes 1024 | tf_op jit(solution)/shard_map/back/pallas_call | solution.py:477
  304.7 21.1 %back.6 = (bf16[192,1024]{1,0:T(8,128)(2,1)}, bf16[1536,192]{1,0:T(8,128)(2,1)}) custom-call(s32[2,32]{1,0:T(2,128)S(1)} %pad_add_fusion.order_ref.refs_0_, bf16[32,48,1344]{2,1,0:T(8,128)(2,1)} %all-gather.8.cloned.1.call-done.w_ref.refs_1_, bf16[192,1024]{1,0:T(8,128)(2,1)} %get-tuple-element.100.refs_2_, bf16[32,48,1024]{2,1,0:T(8,128)(2,1)} %bitcast.72), custom_call_target="tpu_custom_call" | custom-call | bytes 1024 | tf_op jit(solution)/shard_map/back/pallas_call | solution.py:477
  329.9 32.4 %back.7 = (f32[1536,128]{1,0:T(8,128)}, bf16[1536,192]{1,0:T(8,128)(2,1)}, f32[8,1536]{1,0:T(8,128)S(1)}, bf16[192,1024]{1,0:T(8,128)(2,1)}, bf16[1536,256]{1,0:T(8,128)(2,1)}) custom-call(s32[2,32]{1,0:T(2,128)S(1)} %pad_add_fusion.order_ref.refs_0_, bf16[1536,1344]{1,0:T(8,128)(2,1)} %bitcast.60, bf16[192,1024]{1,0:T(8,128)(2,1)} %copy-done.7, ...), custom_call_target="tpu_custom_call" | custom-call | bytes 1024 | tf_op jit(solution)/shard_map/back/pallas_call | solution.py:477
  362.2 21.6 %back.8 = (bf16[192,1024]{1,0:T(8,128)(2,1)}, bf16[1536,768]{1,0:T(8,128)(2,1)}) custom-call(s32[2,32]{1,0:T(2,128)S(1)} %pad_add_fusion.order_ref.refs_0_, bf16[32,48,1344]{2,1,0:T(8,128)(2,1)} %all-gather.8.cloned.1.call-done.w_ref.refs_1_, bf16[192,1024]{1,0:T(8,128)(2,1)} %get-tuple-element.108.refs_2_, bf16[32,48,1024]{2,1,0:T(8,128)(2,1)} %bitcast.71, ...), custom_call_target="tpu_custom_call" | custom-call | bytes 1024 | tf_op jit(solution)/shard_map/back/pallas_call | solution.py:477
  383.9 17.1 %attend_back.1.refs_2_ = bf16[576,1024]{1,0:T(8,128)(2,1)S(1)} custom-call(bf16[3,3,64,1024]{3,2,1,0:T(8,128)(2,1)} %get-tuple-element.96.part_in, bf16[3,1024,1024]{2,1,0:T(8,128)(2,1)} %get-tuple-element.97.p_in, bf16[192,1024]{1,0:T(8,128)(2,1)} %get-tuple-element.113.g_in, f32[32,1024]{1,0:T(8,128)S(1)} %get-tuple-element.206.cos_ref, ...), custom_call_target="tpu_custom_call" | custom-call | tf_op jit(solution)/shard_map/attend_back/pallas_call | solution.py:477
  402.0 24.4 %back.9 = (f32[1536,128]{1,0:T(8,128)}, bf16[1536,576]{1,0:T(8,128)(2,1)}, f32[8,1536]{1,0:T(8,128)S(1)}) custom-call(s32[2,32]{1,0:T(2,128)S(1)} %pad_add_fusion.order_ref.refs_0_, bf16[1536,1344]{1,0:T(8,128)(2,1)} %bitcast.61, bf16[576,1024]{1,0:T(8,128)(2,1)} %copy-done.3, bf16[1536,1024]{1,0:T(8,128)(2,1)} %get-tuple-element.83.h_ref.refs_3_, ...), custom_call_target="tpu_custom_call" | custom-call | bytes 1024 | tf_op jit(solution)/shard_map/back/pallas_call | solution.py:477
  427.8 48.8 %feed.1 = (bf16[48,18432]{1,0:T(8,128)(2,1)}, f32[1536,128]{1,0:T(8,128)}, bf16[128,1536]{1,0:T(8,128)(2,1)}) custom-call(bf16[8,48,1536]{2,1,0:T(8,128)(2,1)} %reduce-scatter.5.cloned.1.call-done.refs_8_.gu_ref, bf16[8,48,768]{2,1,0:T(8,128)(2,1)} %reduce-scatter.7.cloned.1.call-done.refs_9_.down_ref, bf16[1536,768]{1,0:T(8,128)(2,1)} %bitcast.75, ...), custom_call_target="tpu_custom_call" | custom-call | bytes 1024 | tf_op jit(solution)/shard_map/feed/pallas_call | solution.py:477
  476.6 11.9 %plane_exchange.1._.two_ref = bf16[8,48,768]{2,1,0:T(8,128)(2,1)} custom-call(bf16[8,48,768]{2,1,0:T(8,128)(2,1)} %reduce-scatter.9.cloned.1.call-done.two_ref.x_ref, bf16[48,18432]{1,0:T(8,128)(2,1)} %get-tuple-element.125.refs_0_.feed_ref), custom_call_target="tpu_custom_call" | custom-call | bytes 1024 | tf_op jit(solution)/shard_map/plane_exchange/pallas_call | solution.py:477
  493.0 2.6 reduce-scatter.11.cloned.1.call-done.w_ref
  495.6 24.7 %closing.1 = (bf16[128,1536]{1,0:T(8,128)(2,1)S(1)}, bf16[8,48,576]{2,1,0:T(8,128)(2,1)S(1)}, f32[8,8,1536]{2,1,0:T(8,128)S(1)}, f32[4,8,8,128]{3,2,1,0:T(8,128)S(1)}) custom-call(bf16[128,1536]{1,0:T(8,128)(2,1)S(1)} %get-tuple-element.120.x_ref, f32[8,128]{1,0:T(8,128)S(1)} %get-tuple-element.121.p_ref, ...), custom_call_target="tpu_custom_call" | custom-call | bytes 1024 | tf_op jit(solution)/shard_map/closing/pallas_call | solution.py:477
  521.3 21.3 %sheet_update.1 = (f32[48,29192]{1,0:T(8,128)}, f32[48,29192]{1,0:T(8,128)}, f32[48,29192]{1,0:T(8,128)}, f32[48,29192]{1,0:T(8,128)}, bf16[48,29192]{1,0:T(8,12...) custom-call(s32[1]{0:T(128)} %dynamic_slice.10.block_ref, ...), custom_call_target="tpu_custom_call" | custom-call | tf_op jit(solution)/shard_map/sheet_update/pallas_call | solution.py:2279
  (123 shorter events, 38.0 us)
Async XLA Ops:
  7.2 115.5 %all-gather.8.cloned.1.call-start = ((), (), s32[]{:S(2)}) async-start(), calls=%async_computation.6 | async-start | bytes 5406720 | tf_op jit(solution)/shard_map/all_gather | solution.py:2337
  9.4 29.9 %copy-start.16 = (s32[32]{0:T(128)S(1)}, s32[32]{0:T(128)}, u32[]{:S(2)}) copy-start(s32[32]{0:T(128)} %param.15) | copy-start | bytes 388
  37.5 3.4 copy-start.19
  37.6 4.3 copy-start.21
  37.6 205.7 %all-gather.4.cloned.1.call-start = ((), (), s32[]{:S(2)}) async-start(), calls=%async_computation.4 | async-start | bytes 5898240 | tf_op jit(solution)/shard_map/all_gather | solution.py:2337
  117.0 145.8 %all-gather.6.cloned.1.call-start = ((), (), s32[]{:S(2)}) async-start(), calls=%async_computation.5 | async-start | bytes 2949120 | tf_op jit(solution)/shard_map/all_gather | solution.py:2337
  117.7 212.2 %reduce-scatter.7.cloned.1.call-start = ((), (), s32[]{:S(2)}) async-start(), calls=%async_computation.8 | async-start | bytes 2949120 | tf_op jit(solution)/shard_map/reduce_scatter | solution.py:2350
  122.7 21.2 %copy-start.13 = (bf16[96,128]{1,0:T(8,128)(2,1)S(1)}, bf16[96,128]{1,0:T(8,128)(2,1)}, u32[]{:S(2)}) copy-start(bf16[96,128]{1,0:T(8,128)(2,1)} %get-tuple-element.85.refs_0_.refs_7_) | copy-start | bytes 73732
  191.3 6.7 %copy-start.15 = (f32[1,128]{1,0:T(1,128)}, f32[1,128]{1,0:T(1,128)S(1)}, u32[]{:S(2)}) copy-start(f32[1,128]{1,0:T(1,128)S(1)} %get-tuple-element.105.refs_5_) | copy-start | bytes 1540
  243.2 8.2 %copy-start.14 = (f32[1,128]{1,0:T(1,128)}, f32[1,128]{1,0:T(1,128)S(1)}, u32[]{:S(2)}) copy-start(f32[1,128]{1,0:T(1,128)S(1)} %get-tuple-element.93.refs_5_) | copy-start | bytes 1540
  251.5 3.2 copy-start.17
  251.5 4.2 copy-start.20
  254.6 4.9 copy-start.18
  262.8 139.2 %reduce-scatter.5.cloned.1.call-start = ((), (), s32[]{:S(2)}) async-start(), calls=%async_computation.7 | async-start | bytes 5898240 | tf_op jit(solution)/shard_map/reduce_scatter | solution.py:2350
  304.7 172.0 %reduce-scatter.9.cloned.1.call-start = ((), (), s32[]{:S(2)}) async-start(), calls=%async_computation.9 | async-start | bytes 2949120 | tf_op jit(solution)/shard_map/reduce_scatter | solution.py:2350
  325.8 1.0 copy-start.8
  383.8 111.8 %reduce-scatter.11.cloned.1.call-start = ((), (), s32[]{:S(2)}) async-start(), calls=%async_computation.10 | async-start | bytes 2457600 | tf_op jit(solution)/shard_map/reduce_scatter | solution.py:2350
  401.0 1.0 copy-start.3
  476.6 11.9 %copy-start = (bf16[8,48,1536]{2,1,0:T(8,128)(2,1)S(1)}, bf16[8,48,1536]{2,1,0:T(8,128)(2,1)}, u32[]{:S(2)}) copy-start(bf16[8,48,1536]{2,1,0:T(8,128)(2,1)} %reduce-scatter.5.cloned.1.call-done.refs_8_.gu_ref) | copy-start | bytes 3538948
  476.6 11.9 %copy-start.1 = (bf16[8,48,768]{2,1,0:T(8,128)(2,1)S(1)}, bf16[8,48,768]{2,1,0:T(8,128)(2,1)}, u32[]{:S(2)}) copy-start(bf16[8,48,768]{2,1,0:T(8,128)(2,1)} %reduce-scatter.7.cloned.1.call-done.refs_9_.down_ref) | copy-start | bytes 1769476
  476.6 11.9 %copy-start.4 = (bf16[8,48,768]{2,1,0:T(8,128)(2,1)S(1)}, bf16[8,48,768]{2,1,0:T(8,128)(2,1)}, u32[]{:S(2)}) copy-start(bf16[8,48,768]{2,1,0:T(8,128)(2,1)} %reduce-scatter.9.cloned.1.call-done.two_ref.x_ref) | copy-start | bytes 1769476
  488.5 31.8 %copy-start.2 = (bf16[8,48,768]{2,1,0:T(8,128)(2,1)S(1)}, bf16[8,48,768]{2,1,0:T(8,128)(2,1)}, u32[]{:S(2)}) copy-start(bf16[8,48,768]{2,1,0:T(8,128)(2,1)} %plane_exchange.1._.two_ref) | copy-start | bytes 1769476
  488.6 1.2 copy-start.5
  489.7 1.1 copy-start.6
  (5 other events, 3.9 us)
Sparse Core Ops, SparseCore 0:
  37.7 84.9 all-gather.7
  124.2 87.9 all-gather.3
  213.8 48.9 all-gather.5
  265.5 46.8 reduce-scatter.6
  314.6 84.7 reduce-scatter.4
  401.5 48.5 reduce-scatter.8
  452.4 43.1 reduce-scatter.10

commit v9 on v8

--- a/solution.py
+++ b/solution.py
@@ -1963,14 +1963,14 @@
         keys = turned(joint_ref[1, h], cosine, sine_table)
         part_ref[1, h] = keys.astype(part_ref.dtype)
         part_ref[2, h] = joint_ref[2, h].astype(part_ref.dtype)
-        by_key = keys.T.astype(part_ref.dtype)
+        by_key = (part_ref[1, h].astype(jnp.float32) * (HEAD**-0.5)).T.astype(part_ref.dtype)
 
         @pl.loop(0, tiles)
         def _(i, h=h, by_key=by_key):
             at = pl.ds(pl.multiple_of(i * 256, 256), 256)
             scores = jnp.dot(
                 by_key, part_ref[0, h, :, at], preferred_element_type=jnp.float32
-            ) * (HEAD**-0.5)
+            )
             scores = jnp.where(column_ref[...] == seg_ref[:, at], scores, MASKED_SCORE)
             exponent = jnp.exp(scores - jnp.max(scores, axis=0, keepdims=True))
             probs = exponent * (1.0 / jnp.sum(exponent, axis=0, keepdims=True))

time: 558 us -> 557 us (level)
  no operation moved by 1% of the time
where the time goes in v9:
time: 557 us; the launch traced here: 549 us
  Pallas kernels  462 us (83%)
  local copies, waits for them, and re-layouts  21.7 us (4%)
  matrix products  20.3 us (4%)
  other arithmetic  18.9 us (3%)
  between operations  15.8 us (3%)
  waiting for transfers between devices  9.52 us (2%)
    pallas_call x17, Pallas kernels, run(): call(*[pltpu.with_memory_space_constraint(operand, pltpu.HBM) if place is...  441 us
    pallas_call x1, Pallas kernels, sheet_update(): pl.pallas_call(update_kernel, grid=(10,), out_shape=(like, like, like, li...  21.3 us
    dot_general x2, matrix products, contract_rows(): lax.dot_general(left, right, (((0,), (0,)), ((), ())), preferred_element_...  16.4 us
    unnamed x46, local copies, waits for them, and re-layouts  12.2 us
  transfers between devices with their start and end apart: 7, of which 3 were waited for; matrix products, arithmetic and copies ran while one was open for 8% of the time, Pallas kernels for 71%

profile of v9, /device:TPU:0, one launch (start us, length us, event | category | flops | bytes accessed | tf_op | source)
XLA Modules:
  0.0 548.9 jit_solution(15956639399046344536)
XLA Ops:
  9.4 28.2 %opening.1 = (bf16[128,3072]{1,0:T(8,128)(2,1)}, f32[4,8,8,128]{3,2,1,0:T(8,128)}, bf16[96,128]{1,0:T(8,128)(2,1)}, bf16[8,48,1344]{2,1,0:T(8,128)(2,1)}) custom-call(bf16[128,1536]{1,0:T(8,128)(2,1)} %bitcast.82, bf16[128,1536]{1,0:T(8,128)(2,1)} %bitcast.83, f32[8,128]{1,0:T(8,128)} %select_maximum_fusion.small_ref, bf16[128,768]{1,0:T(8,128)(2,1)} %bitcast.84, ...), custom_call_target="tpu_custom_call" | custom-call | bytes 1024 | tf_op jit(solution)/shard_map/opening/pallas_call | solution.py:477
  53.3 4.5 convert_element_type.78.sheet_ref
  57.8 59.1 %first_gather.1 = (bf16[1536,1024]{1,0:T(8,128)(2,1)}, bf16[1536,1024]{1,0:T(8,128)(2,1)}, bf16[8,48,1536]{2,1,0:T(8,128)(2,1)}, bf16[8,48,768]{2,1,0:T(8,128)(2,1)}) custom-call(bf16[1536,128]{1,0:T(8,128)(2,1)} %bitcast.79, bf16[1536,128]{1,0:T(8,128)(2,1)} %bitcast.78, bf16[48,29192]{1,0:T(8,128)(2,1)} %convert_element_type.78.sheet_ref), custom_call_target="tpu_custom_call" | custom-call | bytes 1024 | tf_op jit(solution)/shard_map/first_gather/pallas_call | solution.py:477
  119.8 2.9 all-gather.8.cloned.1.call-done.w_ref.refs_1_
  122.7 20.5 %attend.1 = (bf16[3,3,64,1024]{3,2,1,0:T(8,128)(2,1)}, bf16[3,1024,1024]{2,1,0:T(8,128)(2,1)}, bf16[192,1024]{1,0:T(8,128)(2,1)S(1)}) custom-call(bf16[1536,1344]{1,0:T(8,128)(2,1)} %bitcast.58, bf16[1536,1024]{1,0:T(8,128)(2,1)} %get-tuple-element.83.h_ref.refs_3_, f32[32,1024]{1,0:T(8,128)S(1)} %get-tuple-element.206.cos_ref, ...), custom_call_target="tpu_custom_call" | custom-call | tf_op jit(solution)/shard_map/attend/pallas_call | solution.py:477
  143.9 47.4 %project_sum.1 = (bf16[1536,1024]{1,0:T(8,128)(2,1)}, f32[1536,128]{1,0:T(8,128)}, f32[1536,128]{1,0:T(8,128)}, f32[1,128]{1,0:T(1,128)S(1)}, bf16[1536,1024]{1,0:T(8,128)(2,1)}, /*index=5*/bf16[192,256]{1,0:T(8,128)(2,1)S(1)}) custom-call(s32[2,32]{1,0:T(2,128)S(1)} %pad_add_fusion.order_ref.refs_0_, bf16[192,1024]{1,0:T(8,128)(2,1)} %copy-done.10, ...), custom_call_target="tpu_custom_call" | custom-call | bytes 1024 | tf_op jit(solution)/shard_map/project_sum/pallas_call | solution.py:477
  191.3 6.7 %cross.1 = (bf16[192,1024]{1,0:T(8,128)(2,1)S(1)}, bf16[3,128,1024]{2,1,0:T(8,128)(2,1)S(1)}, bf16[192,1024]{1,0:T(8,128)(2,1)S(1)}) custom-call(bf16[1536,1344]{1,0:T(8,128)(2,1)} %bitcast.59, bf16[1536,1024]{1,0:T(8,128)(2,1)} %get-tuple-element.86.h_ref.refs_3_, bf16[192,256]{1,0:T(8,128)(2,1)S(1)} %get-tuple-element.87.kv_ref), custom_call_target="tpu_custom_call" | custom-call | tf_op jit(solution)/shard_map/cross/pallas_call | solution.py:477
  198.8 44.5 %project_slots.1 = (bf16[1536,1024]{1,0:T(8,128)(2,1)}, f32[1536,128]{1,0:T(8,128)}, f32[1536,128]{1,0:T(8,128)}, f32[1,128]{1,0:T(1,128)S(1)}, bf16[1536,1024]{1,0:T(8,128)(2,1)}) custom-call(s32[2,32]{1,0:T(2,128)S(1)} %pad_add_fusion.order_ref.refs_0_, bf16[192,1024]{1,0:T(8,128)(2,1)} %copy-done.11, ...), custom_call_target="tpu_custom_call" | custom-call | bytes 1024 | tf_op jit(solution)/shard_map/project_slots/pallas_call | solution.py:477
  243.3 8.2 %fusion.11 = f32[1536,1024]{1,0:T(8,128)S(1)} fusion(bf16[1536,1536]{1,0:T(8,128)(2,1)} %bitcast.68, bf16[1536,1024]{1,0:T(8,128)(2,1)} %get-tuple-element.90.refs_3_), kind=kOutput, calls=%fused_computation.81 | convolution fusion | flops 4831838208 | bytes 14155776 | tf_op jit(solution)/shard_map/dot_general | solution.py:430
  252.5 2.2 copy-done.17
  255.7 3.9 convolution_convert_fusion
  259.6 3.1 all-gather.6.cloned.1.call-done
  262.8 8.3 %multiply_convert_fusion.1 = (bf16[768,1024]{1,0:T(8,128)(2,1)S(1)}, bf16[768,1024]{1,0:T(8,128)(2,1)S(1)}) fusion(f32[1536,1024]{1,0:T(8,128)} %copy-done.17, bf16[1536,768]{1,0:T(8,128)(2,1)} %bitcast.74, bf16[1536,1024]{1,0:T(8,128)(2,1)} %get-tuple-element.81), kind=kOutput, calls=%fused_computation.9 | convolution fusion | flops 2426142720 | bytes 14942208 | tf_op jit(solution)/shard_map/dot_general | solution.py:430
  273.1 31.5 %back.5 = (f32[1536,128]{1,0:T(8,128)}, bf16[1536,1536]{1,0:T(8,128)(2,1)}, f32[8,1536]{1,0:T(8,128)S(1)}, bf16[192,1024]{1,0:T(8,128)(2,1)}) custom-call(s32[2,32]{1,0:T(2,128)S(1)} %pad_add_fusion.order_ref.refs_0_, bf16[1536,1536]{1,0:T(8,128)(2,1)} %bitcast.69, bf16[1536,1024]{1,0:T(8,128)(2,1)} %pad_maximum_fusion.refs_2_, ...), custom_call_target="tpu_custom_call" | custom-call | bytes 1024 | tf_op jit(solution)/shard_map/back/pallas_call | solution.py:477
  304.7 21.1 %back.6 = (bf16[192,1024]{1,0:T(8,128)(2,1)}, bf16[1536,192]{1,0:T(8,128)(2,1)}) custom-call(s32[2,32]{1,0:T(2,128)S(1)} %pad_add_fusion.order_ref.refs_0_, bf16[32,48,1344]{2,1,0:T(8,128)(2,1)} %all-gather.8.cloned.1.call-done.w_ref.refs_1_, bf16[192,1024]{1,0:T(8,128)(2,1)} %get-tuple-element.100.refs_2_, bf16[32,48,1024]{2,1,0:T(8,128)(2,1)} %bitcast.72), custom_call_target="tpu_custom_call" | custom-call | bytes 1024 | tf_op jit(solution)/shard_map/back/pallas_call | solution.py:477
  329.8 32.4 %back.7 = (f32[1536,128]{1,0:T(8,128)}, bf16[1536,192]{1,0:T(8,128)(2,1)}, f32[8,1536]{1,0:T(8,128)S(1)}, bf16[192,1024]{1,0:T(8,128)(2,1)}, bf16[1536,256]{1,0:T(8,128)(2,1)}) custom-call(s32[2,32]{1,0:T(2,128)S(1)} %pad_add_fusion.order_ref.refs_0_, bf16[1536,1344]{1,0:T(8,128)(2,1)} %bitcast.60, bf16[192,1024]{1,0:T(8,128)(2,1)} %copy-done.7, ...), custom_call_target="tpu_custom_call" | custom-call | bytes 1024 | tf_op jit(solution)/shard_map/back/pallas_call | solution.py:477
  362.2 21.6 %back.8 = (bf16[192,1024]{1,0:T(8,128)(2,1)}, bf16[1536,768]{1,0:T(8,128)(2,1)}) custom-call(s32[2,32]{1,0:T(2,128)S(1)} %pad_add_fusion.order_ref.refs_0_, bf16[32,48,1344]{2,1,0:T(8,128)(2,1)} %all-gather.8.cloned.1.call-done.w_ref.refs_1_, bf16[192,1024]{1,0:T(8,128)(2,1)} %get-tuple-element.108.refs_2_, bf16[32,48,1024]{2,1,0:T(8,128)(2,1)} %bitcast.71, ...), custom_call_target="tpu_custom_call" | custom-call | bytes 1024 | tf_op jit(solution)/shard_map/back/pallas_call | solution.py:477
  383.8 17.1 %attend_back.1.refs_2_ = bf16[576,1024]{1,0:T(8,128)(2,1)S(1)} custom-call(bf16[3,3,64,1024]{3,2,1,0:T(8,128)(2,1)} %get-tuple-element.96.part_in, bf16[3,1024,1024]{2,1,0:T(8,128)(2,1)} %get-tuple-element.97.p_in, bf16[192,1024]{1,0:T(8,128)(2,1)} %get-tuple-element.113.g_in, f32[32,1024]{1,0:T(8,128)S(1)} %get-tuple-element.206.cos_ref, ...), custom_call_target="tpu_custom_call" | custom-call | tf_op jit(solution)/shard_map/attend_back/pallas_call | solution.py:477
  401.9 24.4 %back.9 = (f32[1536,128]{1,0:T(8,128)}, bf16[1536,576]{1,0:T(8,128)(2,1)}, f32[8,1536]{1,0:T(8,128)S(1)}) custom-call(s32[2,32]{1,0:T(2,128)S(1)} %pad_add_fusion.order_ref.refs_0_, bf16[1536,1344]{1,0:T(8,128)(2,1)} %bitcast.61, bf16[576,1024]{1,0:T(8,128)(2,1)} %copy-done.3, bf16[1536,1024]{1,0:T(8,128)(2,1)} %get-tuple-element.83.h_ref.refs_3_, ...), custom_call_target="tpu_custom_call" | custom-call | bytes 1024 | tf_op jit(solution)/shard_map/back/pallas_call | solution.py:477
  427.8 48.8 %feed.1 = (bf16[48,18432]{1,0:T(8,128)(2,1)}, f32[1536,128]{1,0:T(8,128)}, bf16[128,1536]{1,0:T(8,128)(2,1)}) custom-call(bf16[8,48,1536]{2,1,0:T(8,128)(2,1)} %reduce-scatter.5.cloned.1.call-done.refs_8_.gu_ref, bf16[8,48,768]{2,1,0:T(8,128)(2,1)} %reduce-scatter.7.cloned.1.call-done.refs_9_.down_ref, bf16[1536,768]{1,0:T(8,128)(2,1)} %bitcast.75, ...), custom_call_target="tpu_custom_call" | custom-call | bytes 1024 | tf_op jit(solution)/shard_map/feed/pallas_call | solution.py:477
  476.6 11.9 %plane_exchange.1._.two_ref = bf16[8,48,768]{2,1,0:T(8,128)(2,1)} custom-call(bf16[8,48,768]{2,1,0:T(8,128)(2,1)} %reduce-scatter.9.cloned.1.call-done.two_ref.x_ref, bf16[48,18432]{1,0:T(8,128)(2,1)} %get-tuple-element.125.refs_0_.feed_ref), custom_call_target="tpu_custom_call" | custom-call | bytes 1024 | tf_op jit(solution)/shard_map/plane_exchange/pallas_call | solution.py:477
  493.0 2.6 reduce-scatter.11.cloned.1.call-done.w_ref
  495.6 23.0 %closing.1 = (bf16[128,1536]{1,0:T(8,128)(2,1)S(1)}, bf16[8,48,576]{2,1,0:T(8,128)(2,1)S(1)}, f32[8,8,1536]{2,1,0:T(8,128)S(1)}, f32[4,8,8,128]{3,2,1,0:T(8,128)S(1)}) custom-call(bf16[128,1536]{1,0:T(8,128)(2,1)S(1)} %get-tuple-element.120.x_ref, f32[8,128]{1,0:T(8,128)S(1)} %get-tuple-element.121.p_ref, ...), custom_call_target="tpu_custom_call" | custom-call | bytes 1024 | tf_op jit(solution)/shard_map/closing/pallas_call | solution.py:477
  519.7 21.3 %sheet_update.1 = (f32[48,29192]{1,0:T(8,128)}, f32[48,29192]{1,0:T(8,128)}, f32[48,29192]{1,0:T(8,128)}, f32[48,29192]{1,0:T(8,128)}, bf16[48,29192]{1,0:T(8,12...) custom-call(s32[1]{0:T(128)} %dynamic_slice.10.block_ref, ...), custom_call_target="tpu_custom_call" | custom-call | tf_op jit(solution)/shard_map/sheet_update/pallas_call | solution.py:2279
  (123 shorter events, 38.0 us)
Async XLA Ops:
  7.2 115.5 %all-gather.8.cloned.1.call-start = ((), (), s32[]{:S(2)}) async-start(), calls=%async_computation.6 | async-start | bytes 5406720 | tf_op jit(solution)/shard_map/all_gather | solution.py:2337
  9.4 29.9 %copy-start.16 = (s32[32]{0:T(128)S(1)}, s32[32]{0:T(128)}, u32[]{:S(2)}) copy-start(s32[32]{0:T(128)} %param.15) | copy-start | bytes 388
  37.5 3.4 copy-start.19
  37.6 4.3 copy-start.21
  37.6 205.7 %all-gather.4.cloned.1.call-start = ((), (), s32[]{:S(2)}) async-start(), calls=%async_computation.4 | async-start | bytes 5898240 | tf_op jit(solution)/shard_map/all_gather | solution.py:2337
  116.9 145.8 %all-gather.6.cloned.1.call-start = ((), (), s32[]{:S(2)}) async-start(), calls=%async_computation.5 | async-start | bytes 2949120 | tf_op jit(solution)/shard_map/all_gather | solution.py:2337
  117.7 212.1 %reduce-scatter.7.cloned.1.call-start = ((), (), s32[]{:S(2)}) async-start(), calls=%async_computation.8 | async-start | bytes 2949120 | tf_op jit(solution)/shard_map/reduce_scatter | solution.py:2350
  122.7 21.2 %copy-start.13 = (bf16[96,128]{1,0:T(8,128)(2,1)S(1)}, bf16[96,128]{1,0:T(8,128)(2,1)}, u32[]{:S(2)}) copy-start(bf16[96,128]{1,0:T(8,128)(2,1)} %get-tuple-element.85.refs_0_.refs_7_) | copy-start | bytes 73732
  191.3 6.7 %copy-start.15 = (f32[1,128]{1,0:T(1,128)}, f32[1,128]{1,0:T(1,128)S(1)}, u32[]{:S(2)}) copy-start(f32[1,128]{1,0:T(1,128)S(1)} %get-tuple-element.105.refs_5_) | copy-start | bytes 1540
  243.3 8.2 %copy-start.14 = (f32[1,128]{1,0:T(1,128)}, f32[1,128]{1,0:T(1,128)S(1)}, u32[]{:S(2)}) copy-start(f32[1,128]{1,0:T(1,128)S(1)} %get-tuple-element.93.refs_5_) | copy-start | bytes 1540
  251.5 3.2 copy-start.17
  251.5 4.2 copy-start.20
  254.7 4.9 copy-start.18
  262.8 139.1 %reduce-scatter.5.cloned.1.call-start = ((), (), s32[]{:S(2)}) async-start(), calls=%async_computation.7 | async-start | bytes 5898240 | tf_op jit(solution)/shard_map/reduce_scatter | solution.py:2350
  304.6 171.9 %reduce-scatter.9.cloned.1.call-start = ((), (), s32[]{:S(2)}) async-start(), calls=%async_computation.9 | async-start | bytes 2949120 | tf_op jit(solution)/shard_map/reduce_scatter | solution.py:2350
  325.8 1.0 copy-start.8
  383.8 111.8 %reduce-scatter.11.cloned.1.call-start = ((), (), s32[]{:S(2)}) async-start(), calls=%async_computation.10 | async-start | bytes 2457600 | tf_op jit(solution)/shard_map/reduce_scatter | solution.py:2350
  400.9 1.0 copy-start.3
  476.5 11.9 %copy-start = (bf16[8,48,1536]{2,1,0:T(8,128)(2,1)S(1)}, bf16[8,48,1536]{2,1,0:T(8,128)(2,1)}, u32[]{:S(2)}) copy-start(bf16[8,48,1536]{2,1,0:T(8,128)(2,1)} %reduce-scatter.5.cloned.1.call-done.refs_8_.gu_ref) | copy-start | bytes 3538948
  476.5 11.9 %copy-start.1 = (bf16[8,48,768]{2,1,0:T(8,128)(2,1)S(1)}, bf16[8,48,768]{2,1,0:T(8,128)(2,1)}, u32[]{:S(2)}) copy-start(bf16[8,48,768]{2,1,0:T(8,128)(2,1)} %reduce-scatter.7.cloned.1.call-done.refs_9_.down_ref) | copy-start | bytes 1769476
  476.6 11.9 %copy-start.4 = (bf16[8,48,768]{2,1,0:T(8,128)(2,1)S(1)}, bf16[8,48,768]{2,1,0:T(8,128)(2,1)}, u32[]{:S(2)}) copy-start(bf16[8,48,768]{2,1,0:T(8,128)(2,1)} %reduce-scatter.9.cloned.1.call-done.two_ref.x_ref) | copy-start | bytes 1769476
  488.5 30.2 %copy-start.2 = (bf16[8,48,768]{2,1,0:T(8,128)(2,1)S(1)}, bf16[8,48,768]{2,1,0:T(8,128)(2,1)}, u32[]{:S(2)}) copy-start(bf16[8,48,768]{2,1,0:T(8,128)(2,1)} %plane_exchange.1._.two_ref) | copy-start | bytes 1769476
  488.5 1.2 copy-start.5
  489.7 1.1 copy-start.6
  (5 other events, 3.9 us)
Sparse Core Ops, SparseCore 0:
  37.7 84.9 all-gather.7
  124.2 87.9 all-gather.3
  213.8 48.9 all-gather.5
  265.5 46.9 reduce-scatter.6
  314.6 84.7 reduce-scatter.4
  401.5 48.5 reduce-scatter.8
  452.4 43.1 reduce-scatter.10
